TPU v7x, 32 devices: a whole 2x2x4 slice. The times are simulated.
32 devices in a mesh: seq: 4 (over z), batch: 8 (over y, x, core).
Axes of the slice: x: 2, y: 2, z: 4, core: 2. Of those that a mesh axis runs over, the one named last changes fastest.
Arguments:
- inputs: float32 [8, 1024, 1024], P('batch', 'seq'), may hold values from -6 to 6
- targets: int32 [8, 1024], P('batch', 'seq'), may hold values from 0 to 267734, as said below
- neighbours: int32 [8, 1024, 1024], P('batch', 'seq'), may hold values from 0 to 16367, as said below
- neighbour_scores: float32 [8, 1024, 1024], P('batch', 'seq'), may hold values from -10 to 10
- loglik_grad: float32 [8, 1024], P('batch', 'seq'), may hold values from -6 to 6
- first_gain: float32 [1024], replicated, may hold values from 0.5 to 1.5
- first_shift: float32 [1024], replicated, may hold values from -1 to 1
- query_weight: bfloat16 [1024, 1024], replicated, may hold values from -0.1875 to 0.1875
- query_bias: float32 [1024], replicated, may hold values from -1 to 1
- key_weight: bfloat16 [1024, 1024], replicated, may hold values from -0.1875 to 0.1875
- value_weight: bfloat16 [1024, 1024], replicated, may hold values from -0.1875 to 0.1875
- value_bias: float32 [1024], replicated, may hold values from -1 to 1
- out_weight: bfloat16 [1024, 1024], replicated, may hold values from -0.75 to 0.75
- out_bias: float32 [1024], replicated, may hold values from -1 to 1
- second_gain: float32 [1024], replicated, may hold values from 0.5 to 1.5
- second_shift: float32 [1024], replicated, may hold values from -1 to 1
- inner_weight: bfloat16 [1024, 4096], replicated, may hold values from -0.1875 to 0.1875
- inner_bias: float32 [4096], replicated, may hold values from -1.5 to 1.5
- outer_weight: bfloat16 [4096, 1024], replicated, may hold values from -0.09375 to 0.09375
- outer_bias: float32 [1024], replicated, may hold values from -1 to 1
- final_gain: float32 [1024], replicated, may hold values from 0.5 to 1.5
- final_shift: float32 [1024], replicated, may hold values from -1 to 1
- head_table: bfloat16 [20000, 1024], P('batch'), may hold values from -0.375 to 0.375
- cluster_weight: bfloat16 [1024, 2], replicated, may hold values from -0.375 to 0.375
- middle_map: bfloat16 [1024, 256], replicated, may hold values from -0.1875 to 0.1875
- middle_table: bfloat16 [40000, 256], P('batch'), may hold values from -0.75 to 0.75
- tail_map: bfloat16 [1024, 64], replicated, may hold values from -0.1875 to 0.1875
- tail_table: bfloat16 [207736, 64], P('batch'), may hold values from -1.5 to 1.5
Outputs:
- loglik: float32 [8, 1024], P('batch', 'seq')
- input_grad: float32 [8, 1024, 1024], P('batch', 'seq')
- first_gain_grad: float32 [1024], P('batch')
- first_shift_grad: float32 [1024], P('batch')
- query_weight_grad: float32 [1024, 1024], P('batch')
- query_bias_grad: float32 [1024], P('batch')
- key_weight_grad: float32 [1024, 1024], P('batch')
- value_weight_grad: float32 [1024, 1024], P('batch')
- value_bias_grad: float32 [1024], P('batch')
- out_weight_grad: float32 [1024, 1024], P('batch')
- out_bias_grad: float32 [1024], P('batch')
- second_gain_grad: float32 [1024], P('batch')
- second_shift_grad: float32 [1024], P('batch')
- inner_weight_grad: float32 [1024, 4096], P('batch')
- inner_bias_grad: float32 [4096], P('batch')
- outer_weight_grad: float32 [4096, 1024], P('batch')
- outer_bias_grad: float32 [1024], P('batch')
- final_gain_grad: float32 [1024], P('batch')
- final_shift_grad: float32 [1024], P('batch')
- head_table_grad: float32 [20000, 1024], P('batch')
- cluster_weight_grad: float32 [1024, 2], P('batch')
- middle_map_grad: float32 [1024, 256], P('batch')
- middle_table_grad: float32 [40000, 256], P('batch')
- tail_map_grad: float32 [1024, 64], P('batch')
- tail_table_grad: float32 [207736, 64], P('batch')
Inputs may be any that keep to these rules, and one draw needn't show every extreme that they name: `targets`: target words; those from 20000 to 59999 form the middle band, higher ones the tail band. `neighbours`: 0 marks a neighbour whose word is the token's target.
All inputs are finite; a program needn't handle non-finite values.
Results may differ from a plain program's by a relative error of at most 0.033.
Values may be sent and summed in bfloat16 or wider, within the bound.
No kernel may reach another device: no remote copies, remote signals or barrier semaphores. Data moves between devices by JAX's collectives and lax.ppermute only.
A program may use at most 256 MiB of HBM per device.

v0:
```python
import math

import jax
import jax.numpy as jnp
from jax import lax
from jax.sharding import PartitionSpec as P

HEADS = 16
HEAD_WORDS = 20000
MID_WORDS = 40000
TAIL_WORDS = 207735


NEG_FILL = -1e30
EPSILON = 1e-05


def joined(value, axis, join):
    gathered = jax.tree.map(
        lambda a, kind: lax.all_gather(a.astype(kind), axis),
        value,
        jax.tree.map(lambda a: jnp.bfloat16 if a.dtype == jnp.float32 else a.dtype, value),
    )

    def take(source):
        return jax.tree.map(
            lambda a, own: lax.dynamic_index_in_dim(a, source, 0, False).astype(own.dtype),
            gathered,
            value,
        )

    return lax.fori_loop(
        1, lax.axis_size(axis), lambda source, state: join(state, take(source)), take(0)
    )


def layer_norm(values, gain_vector, shift_vector):
    average = jnp.mean(values, -1, keepdims=True)
    centred = values - average
    spread = jnp.mean(centred * centred, -1, keepdims=True)
    return centred * lax.rsqrt(spread + EPSILON) * gain_vector + shift_vector


def norm_back(values, gain_vector, shift_vector, upstream):
    unused, pullback = jax.vjp(layer_norm, values, gain_vector, shift_vector)
    return pullback(upstream)


def gelu_back(before, upstream):
    unused, pullback = jax.vjp(jax.nn.gelu, before)
    return pullback(upstream)[0]


def product(former, latter):
    return jnp.dot(former, latter, preferred_element_type=jnp.float32)


def product_tn(former, latter):
    return lax.dot_general(
        former, latter, (((0,), (0,)), ((), ())), preferred_element_type=jnp.float32
    )


def product_nt(former, latter):
    return lax.dot_general(
        former, latter, (((1,), (1,)), ((), ())), preferred_element_type=jnp.float32
    )


def lowered(values):
    return values.astype(jnp.bfloat16)


def pick_block(total_rows, other_rows):
    limit = max(1, (1 << 23) // other_rows)
    best_size = 1
    for candidate in range(1, min(total_rows, limit) + 1):
        if total_rows % candidate == 0:
            best_size = candidate
    return best_size


def add_rows(total_rows, part_rows, row_start):
    current = lax.dynamic_slice_in_dim(total_rows, row_start, part_rows.shape[0], 0)
    return lax.dynamic_update_slice_in_dim(total_rows, current + part_rows, row_start, 0)


def keep_state(state_in):
    return state_in


def key_blocks(key_piece, head_count):
    row_count = key_piece.shape[0]
    block_size = math.gcd(row_count, 1536)
    shaped = key_piece.reshape(
        row_count // block_size, block_size, head_count, key_piece.shape[1] // head_count
    )
    offsets = jnp.arange(row_count // block_size, dtype=jnp.int32) * block_size
    return (shaped, offsets)


def block_scores(queries, key_block, key_start, query_start):
    scale = queries.shape[2] ** (-0.5)
    raw_scores = (
        jnp.einsum("qhd,khd->hqk", queries, key_block, preferred_element_type=jnp.float32) * scale
    )
    query_pos = query_start + jnp.arange(queries.shape[0], dtype=jnp.int32)
    key_pos = key_start + jnp.arange(key_block.shape[0], dtype=jnp.int32)
    allowed = (key_pos[None, :] <= query_pos[:, None])[None]
    return (jnp.where(allowed, raw_scores, NEG_FILL), allowed)


def stats_fold(queries, query_start, state_in, key_piece, piece_start):
    shaped, offsets = key_blocks(key_piece, queries.shape[1])
    last_query = query_start + queries.shape[0] - 1

    def visit(running, inputs):
        key_block, block_start = inputs
        key_start = piece_start + block_start

        def compute(current):
            run_max, run_sum = current
            scores, allowed = block_scores(queries, key_block, key_start, query_start)
            new_max = jnp.maximum(run_max, jnp.max(scores, -1))
            exponent = jnp.where(allowed, jnp.exp(scores - new_max[..., None]), 0.0)
            return (new_max, run_sum * jnp.exp(run_max - new_max) + jnp.sum(exponent, -1))

        return (lax.cond(key_start <= last_query, compute, keep_state, running), None)

    result, unused = lax.scan(visit, state_in, (shaped, offsets))
    return result


def mix_fold(queries, query_start, totals, state_in, pieces, piece_start):
    key_piece, value_piece = pieces
    key_shaped, offsets = key_blocks(key_piece, queries.shape[1])
    value_shaped, unused = key_blocks(value_piece, queries.shape[1])
    last_query = query_start + queries.shape[0] - 1

    def visit(running, inputs):
        key_block, value_block, block_start = inputs
        key_start = piece_start + block_start

        def compute(current):
            scores, allowed = block_scores(queries, key_block, key_start, query_start)
            probabilities = jnp.where(allowed, jnp.exp(scores - totals[..., None]), 0.0)
            return current + jnp.einsum(
                "hqk,khd->qhd",
                lowered(probabilities),
                value_block,
                preferred_element_type=jnp.float32,
            )

        return (lax.cond(key_start <= last_query, compute, keep_state, running), None)

    result, unused = lax.scan(visit, state_in, (key_shaped, value_shaped, offsets))
    return result


def back_fold(queries, query_start, totals, out_grad, delta, state_in, pieces):
    key_piece, value_piece = pieces
    key_shaped, offsets = key_blocks(key_piece, queries.shape[1])
    value_shaped, unused = key_blocks(value_piece, queries.shape[1])
    last_query = query_start + queries.shape[0] - 1
    scale = queries.shape[2] ** (-0.5)
    feature_count = key_piece.shape[1]

    def visit(running, inputs):
        key_block, value_block, block_start = inputs

        def compute(current):
            query_grad, key_grads, value_grads = current
            scores, allowed = block_scores(queries, key_block, block_start, query_start)
            probabilities = jnp.where(allowed, jnp.exp(scores - totals[..., None]), 0.0)
            value_part = jnp.einsum(
                "hqk,qhd->khd", lowered(probabilities), out_grad, preferred_element_type=jnp.float32
            )
            prob_grad = jnp.einsum(
                "qhd,khd->hqk", out_grad, value_block, preferred_element_type=jnp.float32
            )
            score_grad = lowered(probabilities * (prob_grad - delta[..., None]))
            query_grad = (
                query_grad
                + jnp.einsum(
                    "hqk,khd->qhd", score_grad, key_block, preferred_element_type=jnp.float32
                )
                * scale
            )
            key_part = (
                jnp.einsum("hqk,qhd->khd", score_grad, queries, preferred_element_type=jnp.float32)
                * scale
            )
            key_grads = add_rows(key_grads, key_part.reshape(-1, feature_count), block_start)
            value_grads = add_rows(value_grads, value_part.reshape(-1, feature_count), block_start)
            return (query_grad, key_grads, value_grads)

        return (lax.cond(block_start <= last_query, compute, keep_state, running), None)

    result, unused = lax.scan(visit, state_in, (key_shaped, value_shaped, offsets))
    return result


def band_ids(token_ids):
    head_member = token_ids < HEAD_WORDS
    middle_member = (token_ids >= HEAD_WORDS) & (token_ids < HEAD_WORDS + MID_WORDS)
    tail_member = token_ids >= HEAD_WORDS + MID_WORDS
    return (
        (token_ids, head_member),
        (token_ids - HEAD_WORDS, middle_member),
        (token_ids - HEAD_WORDS - MID_WORDS, tail_member),
    )


def select_column(logits, columns, wanted):
    matches = columns[None, :] == wanted[:, None]
    return jnp.sum(jnp.where(matches, logits, 0.0), -1)


def band_stats(token_rows, local_ids, member, matrix, valid):
    token_count = token_rows.shape[0]
    row_count = matrix.shape[0]
    is_owned = member & (local_ids >= 0) & (local_ids < row_count)
    if token_count >= row_count:
        block_size = pick_block(token_count, row_count)
        all_columns = jnp.arange(row_count, dtype=jnp.int32)
        usable = (all_columns < valid)[None, :]

        def one_block(inputs):
            row_block, local_block, owned_block = inputs
            logits = jnp.where(usable, product_nt(row_block, matrix), NEG_FILL)
            top_value = jnp.max(logits, -1)
            exp_total = jnp.sum(jnp.where(usable, jnp.exp(logits - top_value[:, None]), 0.0), -1)
            target_pick = select_column(logits, all_columns, local_block)
            return (top_value, exp_total, jnp.where(owned_block, target_pick, 0.0))

        block_count = token_count // block_size
        parts = lax.map(
            one_block,
            (
                token_rows.reshape(block_count, block_size, -1),
                local_ids.reshape(block_count, block_size),
                is_owned.reshape(block_count, block_size),
            ),
        )
        return tuple((element.reshape(token_count) for element in parts))
    block_size = pick_block(row_count, token_count)

    def visit(running, inputs):
        top_value, exp_total, target_sum = running
        matrix_block, block_start = inputs
        columns = block_start + jnp.arange(block_size, dtype=jnp.int32)
        usable = (columns < valid)[None, :]
        logits = jnp.where(usable, product_nt(token_rows, matrix_block), NEG_FILL)
        new_top = jnp.maximum(top_value, jnp.max(logits, -1))
        exp_total = exp_total * jnp.exp(top_value - new_top) + jnp.sum(
            jnp.where(usable, jnp.exp(logits - new_top[:, None]), 0.0), -1
        )
        inside = is_owned & (local_ids >= block_start) & (local_ids < block_start + block_size)
        target_pick = select_column(logits, columns, local_ids)
        return ((new_top, exp_total, target_sum + jnp.where(inside, target_pick, 0.0)), None)

    starts = jnp.arange(row_count // block_size, dtype=jnp.int32) * block_size
    initial = (
        jnp.full((token_count,), NEG_FILL, jnp.float32),
        jnp.zeros((token_count,), jnp.float32),
        jnp.zeros((token_count,), jnp.float32),
    )
    result, unused = lax.scan(
        visit, initial, (matrix.reshape(row_count // block_size, block_size, -1), starts)
    )
    return result


def word_stats(states, token_ids, tables, offsets, valids):
    results = []
    target_logit = jnp.zeros(token_ids.shape, jnp.float32)
    for band_index, (band_local, member) in enumerate(band_ids(token_ids)):
        top_value, exp_total, target_part = band_stats(
            states[band_index],
            band_local - offsets[band_index],
            member,
            tables[band_index],
            valids[band_index],
        )
        results = results + [top_value, exp_total]
        target_logit = target_logit + target_part
    return (results[0], results[1], results[2], results[3], results[4], results[5], target_logit)


def merge_stats(former, latter):
    merged = []
    for band_index in range(3):
        former_top = former[2 * band_index]
        latter_top = latter[2 * band_index]
        top_value = jnp.maximum(former_top, latter_top)
        merged = merged + [
            top_value,
            former[2 * band_index + 1] * jnp.exp(former_top - top_value)
            + latter[2 * band_index + 1] * jnp.exp(latter_top - top_value),
        ]
    return (merged[0], merged[1], merged[2], merged[3], merged[4], merged[5], former[6] + latter[6])


def band_totals(stats, clusters):
    top_value = jnp.maximum(stats[0], jnp.max(clusters, -1))
    head_total = top_value + jnp.log(
        stats[1] * jnp.exp(stats[0] - top_value)
        + jnp.sum(jnp.exp(clusters - top_value[:, None]), -1)
    )
    return (head_total, stats[2] + jnp.log(stats[3]), stats[4] + jnp.log(stats[5]))


def mix_loss(target_logit, totals, clusters, token_ids, knn_prob):
    head_total, middle_total, tail_total = totals
    in_head = token_ids < HEAD_WORDS
    in_middle = (token_ids >= HEAD_WORDS) & (token_ids < HEAD_WORDS + MID_WORDS)
    model_logp = jnp.where(
        in_head,
        target_logit - head_total,
        jnp.where(
            in_middle,
            clusters[:, 0] - head_total + target_logit - middle_total,
            clusters[:, 1] - head_total + target_logit - tail_total,
        ),
    )
    ratio = 0.25 * knn_prob * jnp.exp(-model_logp)
    return (model_logp + jnp.log(0.75 + ratio), 0.75 / (0.75 + ratio))


def band_grads(token_rows, is_owned, local_ids, weights, band_total, matrix, valid):
    token_count = token_rows.shape[0]
    row_count = matrix.shape[0]

    def logit_grad(
        row_block, local_block, owned_block, weight_block, total_block, matrix_block, block_start
    ):
        logits = product_nt(row_block, matrix_block)
        columns = block_start + jnp.arange(matrix_block.shape[0], dtype=jnp.int32)
        probabilities = jnp.where(
            (columns < valid)[None, :], jnp.exp(logits - total_block[:, None]), 0.0
        )
        onehot = (columns[None, :] == local_block[:, None]) & owned_block[:, None]
        return lowered(weight_block[:, None] * (onehot.astype(jnp.float32) - probabilities))

    if token_count >= row_count:
        block_size = pick_block(token_count, row_count)
        block_count = token_count // block_size

        def visit(running, inputs):
            row_block, local_block, owned_block, weight_block, total_block = inputs
            grad_logits = logit_grad(
                row_block, local_block, owned_block, weight_block, total_block, matrix, 0
            )
            return (running + product_tn(grad_logits, row_block), product(grad_logits, matrix))

        table_grad, terms = lax.scan(
            visit,
            jnp.zeros(matrix.shape, jnp.float32),
            (
                token_rows.reshape(block_count, block_size, -1),
                local_ids.reshape(block_count, block_size),
                is_owned.reshape(block_count, block_size),
                weights.reshape(block_count, block_size),
                band_total.reshape(block_count, block_size),
            ),
        )
        return (terms.reshape(token_count, -1), table_grad)
    block_size = pick_block(row_count, token_count)

    def visit(running, inputs):
        matrix_block, block_start = inputs
        grad_logits = logit_grad(
            token_rows, local_ids, is_owned, weights, band_total, matrix_block, block_start
        )
        return (running + product(grad_logits, matrix_block), product_tn(grad_logits, token_rows))

    starts = jnp.arange(row_count // block_size, dtype=jnp.int32) * block_size
    terms, table_grad = lax.scan(
        visit,
        jnp.zeros((token_count, matrix.shape[1]), jnp.float32),
        (matrix.reshape(row_count // block_size, block_size, -1), starts),
    )
    return (terms, table_grad.reshape(row_count, -1))


def word_grads(states, token_ids, weights, totals, tables, offsets, valids):
    terms = []
    table_grads = []
    for band_index, (band_local, member) in enumerate(band_ids(token_ids)):
        local_ids = band_local - offsets[band_index]
        row_count = tables[band_index].shape[0]
        is_owned = member & (local_ids >= 0) & (local_ids < row_count)
        band_weights = weights if band_index == 0 else jnp.where(member, weights, 0.0)
        state_term, table_grad = band_grads(
            states[band_index],
            is_owned,
            local_ids,
            band_weights,
            totals[band_index],
            tables[band_index],
            valids[band_index],
        )
        terms = terms + [state_term]
        table_grads = table_grads + [table_grad]
    return ((terms[0], terms[1], terms[2]), (table_grads[0], table_grads[1], table_grads[2]))


def on_device(
    inputs,
    targets,
    neighbours,
    neighbour_scores,
    loglik_grad,
    first_gain,
    first_shift,
    query_weight,
    query_bias,
    key_weight,
    value_weight,
    value_bias,
    out_weight,
    out_bias,
    second_gain,
    second_shift,
    inner_weight,
    inner_bias,
    outer_weight,
    outer_bias,
    final_gain,
    final_shift,
    head_table,
    cluster_weight,
    middle_map,
    middle_table,
    tail_map,
    tail_table,
):
    tokens = inputs[0]
    token_ids = targets[0]
    token_count = tokens.shape[0]
    feature_count = tokens.shape[1]
    head_count = HEADS
    head_size = feature_count // head_count
    query_start = lax.axis_index("seq") * token_count
    full_length = lax.axis_size("seq") * token_count
    top_score = jnp.max(neighbour_scores[0], -1, keepdims=True)
    exponent = jnp.exp(neighbour_scores[0] - top_score)
    shares = exponent / jnp.sum(exponent, -1, keepdims=True)
    knn_prob = jnp.sum(jnp.where(neighbours[0] == 0, shares, 0.0), -1)
    normed_low = lowered(layer_norm(tokens, first_gain, first_shift))
    queries = lowered(product(normed_low, query_weight) + query_bias)
    key_rows = lowered(product(normed_low, key_weight))
    value_rows = lowered(product(normed_low, value_weight) + value_bias)
    query_heads = queries.reshape(token_count, head_count, head_size)
    whole_keys, whole_values = (
        lax.all_gather(key_rows, "seq", axis=0, tiled=True),
        lax.all_gather(value_rows, "seq", axis=0, tiled=True),
    )
    start_max = jnp.full((head_count, token_count), NEG_FILL, jnp.float32)
    start_sum = jnp.zeros((head_count, token_count), jnp.float32)
    run_max, run_sum = stats_fold(query_heads, query_start, (start_max, start_sum), whole_keys, 0)
    totals = run_max + jnp.log(run_sum)
    attended = mix_fold(
        query_heads,
        query_start,
        totals,
        jnp.zeros((token_count, head_count, head_size), jnp.float32),
        (whole_keys, whole_values),
        0,
    )
    attended_low = lowered(attended.reshape(token_count, feature_count))
    mixed = tokens + product(attended_low, out_weight) + out_bias
    second_low = lowered(layer_norm(mixed, second_gain, second_shift))
    before = product(second_low, inner_weight) + inner_bias
    hidden_low = lowered(jax.nn.gelu(before))
    final = mixed + product(hidden_low, outer_weight) + outer_bias
    state_low = lowered(layer_norm(final, final_gain, final_shift))
    middle_low = lowered(product(state_low, middle_map))
    tail_low = lowered(product(state_low, tail_map))
    clusters = product(state_low, cluster_weight)
    tables = (head_table, middle_table, tail_table)
    member = lax.axis_index("batch")
    all_states = (
        lax.all_gather(state_low, "batch", axis=0, tiled=True),
        lax.all_gather(middle_low, "batch", axis=0, tiled=True),
        lax.all_gather(tail_low, "batch", axis=0, tiled=True),
    )
    all_ids = lax.all_gather(token_ids, "batch", axis=0, tiled=True)
    offsets = (
        member * head_table.shape[0],
        member * middle_table.shape[0],
        member * tail_table.shape[0],
    )
    valids = (head_table.shape[0], middle_table.shape[0], TAIL_WORDS - offsets[2])
    merged = joined(word_stats(all_states, all_ids, tables, offsets, valids), "batch", merge_stats)
    all_clusters = product(all_states[0], cluster_weight)
    all_totals = band_totals(merged, all_clusters)
    own_totals = tuple(
        (
            lax.dynamic_slice_in_dim(element, member * token_count, token_count, 0)
            for element in all_totals
        )
    )
    own_target = lax.dynamic_slice_in_dim(merged[6], member * token_count, token_count, 0)
    loglik, slope = mix_loss(own_target, own_totals, clusters, token_ids, knn_prob)
    word_weight = loglik_grad[0] * slope
    all_weights = lax.all_gather(word_weight, "batch", axis=0, tiled=True)
    all_terms, table_grads = word_grads(
        all_states, all_ids, all_weights, all_totals, tables, offsets, valids
    )
    head_term, middle_term, tail_term = (
        lax.psum_scatter(
            all_terms[0].astype(jnp.bfloat16), "batch", scatter_dimension=0, tiled=True
        ).astype(jnp.float32),
        lax.psum_scatter(
            all_terms[1].astype(jnp.bfloat16), "batch", scatter_dimension=0, tiled=True
        ).astype(jnp.float32),
        lax.psum_scatter(
            all_terms[2].astype(jnp.bfloat16), "batch", scatter_dimension=0, tiled=True
        ).astype(jnp.float32),
    )
    in_middle = (token_ids >= HEAD_WORDS) & (token_ids < HEAD_WORDS + MID_WORDS)
    in_tail = token_ids >= HEAD_WORDS + MID_WORDS
    cluster_hit = jnp.stack([in_middle, in_tail], -1).astype(jnp.float32)
    cluster_grad = word_weight[:, None] * (cluster_hit - jnp.exp(clusters - own_totals[0][:, None]))
    middle_state = lowered(middle_term)
    tail_state = lowered(tail_term)
    state_grad = (
        head_term
        + product_nt(middle_state, middle_map)
        + product_nt(tail_state, tail_map)
        + product_nt(cluster_grad, cluster_weight.astype(jnp.float32))
    )
    middle_map_grad = product_tn(state_low, middle_state)
    tail_map_grad = product_tn(state_low, tail_state)
    cluster_weight_grad = product_tn(state_low.astype(jnp.float32), cluster_grad)
    final_grad, final_gain_grad, final_shift_grad = norm_back(
        final, final_gain, final_shift, state_grad
    )
    final_low = lowered(final_grad)
    outer_weight_grad = product_tn(hidden_low, final_low)
    outer_bias_grad = jnp.sum(final_grad, 0)
    before_grad = lowered(gelu_back(before, product_nt(final_low, outer_weight)))
    inner_weight_grad = product_tn(second_low, before_grad)
    inner_bias_grad = jnp.sum(before_grad.astype(jnp.float32), 0)
    second_in_grad, second_gain_grad, second_shift_grad = norm_back(
        mixed, second_gain, second_shift, product_nt(before_grad, inner_weight)
    )
    mixed_grad = final_grad + second_in_grad
    mixed_low = lowered(mixed_grad)
    out_weight_grad = product_tn(attended_low, mixed_low)
    out_bias_grad = jnp.sum(mixed_grad, 0)
    attended_grad = lowered(product_nt(mixed_low, out_weight)).reshape(
        token_count, head_count, head_size
    )
    delta = jnp.einsum("qhd,qhd->hq", attended_grad.astype(jnp.float32), attended)
    initial = (
        jnp.zeros((token_count, head_count, head_size), jnp.float32),
        jnp.zeros((full_length, feature_count), jnp.float32),
        jnp.zeros((full_length, feature_count), jnp.float32),
    )
    query_grad, key_grads, value_grads = back_fold(
        query_heads,
        query_start,
        totals,
        attended_grad,
        delta,
        initial,
        (
            lax.all_gather(key_rows, "seq", axis=0, tiled=True),
            lax.all_gather(value_rows, "seq", axis=0, tiled=True),
        ),
    )
    key_grad, value_grad = (
        lax.psum_scatter(
            key_grads.astype(jnp.bfloat16), "seq", scatter_dimension=0, tiled=True
        ).astype(jnp.float32),
        lax.psum_scatter(
            value_grads.astype(jnp.bfloat16), "seq", scatter_dimension=0, tiled=True
        ).astype(jnp.float32),
    )
    query_low = lowered(query_grad.reshape(token_count, feature_count))
    key_low = lowered(key_grad)
    value_low = lowered(value_grad)
    query_weight_grad = product_tn(normed_low, query_low)
    query_bias_grad = jnp.sum(query_low.astype(jnp.float32), 0)
    key_weight_grad = product_tn(normed_low, key_low)
    value_weight_grad = product_tn(normed_low, value_low)
    value_bias_grad = jnp.sum(value_low.astype(jnp.float32), 0)
    normed_grad = (
        product_nt(query_low, query_weight)
        + product_nt(key_low, key_weight)
        + product_nt(value_low, value_weight)
    )
    first_in_grad, first_gain_grad, first_shift_grad = norm_back(
        tokens, first_gain, first_shift, normed_grad
    )
    input_grad = mixed_grad + first_in_grad
    reduced = (
        lax.psum_scatter(
            first_gain_grad.astype(jnp.bfloat16), "batch", scatter_dimension=0, tiled=True
        ).astype(jnp.float32),
        lax.psum_scatter(
            first_shift_grad.astype(jnp.bfloat16), "batch", scatter_dimension=0, tiled=True
        ).astype(jnp.float32),
        lax.psum_scatter(
            query_weight_grad.astype(jnp.bfloat16), "batch", scatter_dimension=0, tiled=True
        ).astype(jnp.float32),
        lax.psum_scatter(
            query_bias_grad.astype(jnp.bfloat16), "batch", scatter_dimension=0, tiled=True
        ).astype(jnp.float32),
        lax.psum_scatter(
            key_weight_grad.astype(jnp.bfloat16), "batch", scatter_dimension=0, tiled=True
        ).astype(jnp.float32),
        lax.psum_scatter(
            value_weight_grad.astype(jnp.bfloat16), "batch", scatter_dimension=0, tiled=True
        ).astype(jnp.float32),
        lax.psum_scatter(
            value_bias_grad.astype(jnp.bfloat16), "batch", scatter_dimension=0, tiled=True
        ).astype(jnp.float32),
        lax.psum_scatter(
            out_weight_grad.astype(jnp.bfloat16), "batch", scatter_dimension=0, tiled=True
        ).astype(jnp.float32),
        lax.psum_scatter(
            out_bias_grad.astype(jnp.bfloat16), "batch", scatter_dimension=0, tiled=True
        ).astype(jnp.float32),
        lax.psum_scatter(
            second_gain_grad.astype(jnp.bfloat16), "batch", scatter_dimension=0, tiled=True
        ).astype(jnp.float32),
        lax.psum_scatter(
            second_shift_grad.astype(jnp.bfloat16), "batch", scatter_dimension=0, tiled=True
        ).astype(jnp.float32),
        lax.psum_scatter(
            inner_weight_grad.astype(jnp.bfloat16), "batch", scatter_dimension=0, tiled=True
        ).astype(jnp.float32),
        lax.psum_scatter(
            inner_bias_grad.astype(jnp.bfloat16), "batch", scatter_dimension=0, tiled=True
        ).astype(jnp.float32),
        lax.psum_scatter(
            outer_weight_grad.astype(jnp.bfloat16), "batch", scatter_dimension=0, tiled=True
        ).astype(jnp.float32),
        lax.psum_scatter(
            outer_bias_grad.astype(jnp.bfloat16), "batch", scatter_dimension=0, tiled=True
        ).astype(jnp.float32),
        lax.psum_scatter(
            final_gain_grad.astype(jnp.bfloat16), "batch", scatter_dimension=0, tiled=True
        ).astype(jnp.float32),
        lax.psum_scatter(
            final_shift_grad.astype(jnp.bfloat16), "batch", scatter_dimension=0, tiled=True
        ).astype(jnp.float32),
        lax.psum_scatter(
            cluster_weight_grad.astype(jnp.bfloat16), "batch", scatter_dimension=0, tiled=True
        ).astype(jnp.float32),
        lax.psum_scatter(
            middle_map_grad.astype(jnp.bfloat16), "batch", scatter_dimension=0, tiled=True
        ).astype(jnp.float32),
        lax.psum_scatter(
            tail_map_grad.astype(jnp.bfloat16), "batch", scatter_dimension=0, tiled=True
        ).astype(jnp.float32),
    )
    summed = (
        lax.psum(reduced[0].astype(jnp.bfloat16), "seq").astype(jnp.float32),
        lax.psum(reduced[1].astype(jnp.bfloat16), "seq").astype(jnp.float32),
        lax.psum(reduced[2].astype(jnp.bfloat16), "seq").astype(jnp.float32),
        lax.psum(reduced[3].astype(jnp.bfloat16), "seq").astype(jnp.float32),
        lax.psum(reduced[4].astype(jnp.bfloat16), "seq").astype(jnp.float32),
        lax.psum(reduced[5].astype(jnp.bfloat16), "seq").astype(jnp.float32),
        lax.psum(reduced[6].astype(jnp.bfloat16), "seq").astype(jnp.float32),
        lax.psum(reduced[7].astype(jnp.bfloat16), "seq").astype(jnp.float32),
        lax.psum(reduced[8].astype(jnp.bfloat16), "seq").astype(jnp.float32),
        lax.psum(reduced[9].astype(jnp.bfloat16), "seq").astype(jnp.float32),
        lax.psum(reduced[10].astype(jnp.bfloat16), "seq").astype(jnp.float32),
        lax.psum(reduced[11].astype(jnp.bfloat16), "seq").astype(jnp.float32),
        lax.psum(reduced[12].astype(jnp.bfloat16), "seq").astype(jnp.float32),
        lax.psum(reduced[13].astype(jnp.bfloat16), "seq").astype(jnp.float32),
        lax.psum(reduced[14].astype(jnp.bfloat16), "seq").astype(jnp.float32),
        lax.psum(reduced[15].astype(jnp.bfloat16), "seq").astype(jnp.float32),
        lax.psum(reduced[16].astype(jnp.bfloat16), "seq").astype(jnp.float32),
        lax.psum(reduced[17].astype(jnp.bfloat16), "seq").astype(jnp.float32),
        lax.psum(reduced[18].astype(jnp.bfloat16), "seq").astype(jnp.float32),
        lax.psum(reduced[19].astype(jnp.bfloat16), "seq").astype(jnp.float32),
        lax.psum(table_grads[0].astype(jnp.bfloat16), "seq").astype(jnp.float32),
        lax.psum(table_grads[1].astype(jnp.bfloat16), "seq").astype(jnp.float32),
        lax.psum(table_grads[2].astype(jnp.bfloat16), "seq").astype(jnp.float32),
    )
    return (
        loglik.reshape(1, token_count),
        input_grad.reshape(1, token_count, feature_count),
        summed[0],
        summed[1],
        summed[2],
        summed[3],
        summed[4],
        summed[5],
        summed[6],
        summed[7],
        summed[8],
        summed[9],
        summed[10],
        summed[11],
        summed[12],
        summed[13],
        summed[14],
        summed[15],
        summed[16],
        summed[20],
        summed[17],
        summed[18],
        summed[21],
        summed[19],
        summed[22],
    )


def solution(mesh):
    return jax.shard_map(
        on_device,
        mesh=mesh,
        in_specs=(
            P("batch", "seq", None),
            P("batch", "seq"),
            P("batch", "seq", None),
            P("batch", "seq", None),
            P("batch", "seq"),
            P(),
            P(),
            P(),
            P(),
            P(),
            P(),
            P(),
            P(),
            P(),
            P(),
            P(),
            P(),
            P(),
            P(),
            P(),
            P(),
            P(),
            P("batch", None),
            P(),
            P(),
            P("batch", None),
            P(),
            P("batch", None),
        ),
        out_specs=(
            P("batch", "seq"),
            P("batch", "seq", None),
            P("batch"),
            P("batch"),
            P("batch", None),
            P("batch"),
            P("batch", None),
            P("batch", None),
            P("batch"),
            P("batch", None),
            P("batch"),
            P("batch"),
            P("batch"),
            P("batch", None),
            P("batch"),
            P("batch", None),
            P("batch"),
            P("batch"),
            P("batch"),
            P("batch", None),
            P("batch", None),
            P("batch", None),
            P("batch", None),
            P("batch", None),
            P("batch", None),
        ),
        check_vma=False,
    )
```

profile of v0, /device:TPU:0, one launch (start us, length us, event | category | flops | bytes accessed | tf_op | source)
XLA Modules:
  0.0 2304.7 jit_solution(4209373856030237419)
XLA Ops:
  31.5 8.7 copy.95
  41.6 10.5 all-gather.2
  76.9 9.4 while.133
  86.4 25.4 %all-gather.16.cloned.1.call-done = bf16[1024,1024]{1,0:T(8,128)(2,1)} async-done(((bf16[256,1024]{1,0:T(8,128)(2,1)}), bf16[1024,1024]{1,0:T(8,128)(2,1)}) %all-gather.16.cloned.1.call-update) | async-done | bytes 2097168 | tf_op jit(solution)/shard_map/all_gather | solution.py:457
  124.7 10.5 while.134
  154.7 9.8 all_gather.72
  164.8 349.2 %while.138 = (s32[]{:T(128)}, f32[2048]{0:T(1024)S(1)}, f32[2048]{0:T(1024)S(1)}, f32[2048]{0:T(1024)S(1)}, s32[23]{0:T(128)S(1)}, /*index=5*/s32[]{:T(128)}, bf...) while((s32[]{:T(128)}, f32[2048]{0:T(1024)S(1)}, ...), condition=%wide.region_27.28_spmd.clone, body=%wide.region_23.27_spmd.clone.sunk | while | flops 314484032 | bytes 19220800 | solution.py:268
  514.1 9.0 all-gather.5
  533.3 49.9 %while.137 = (s32[]{:T(128)}, f32[2048]{0:T(1024)S(1)}, f32[2048]{0:T(1024)S(1)}, f32[2048]{0:T(1024)S(1)}, s32[2]{0:T(128)S(1)}, /*index=5*/bf16[2,2500,256]{2,...) while((s32[]{:T(128)}, f32[2048]{0:T(1024)S(1)}, ...), condition=%wide.region_22.23_spmd.clone, body=%wide.region_18.22_spmd.clone.sunk | while | flops 2667550208 | bytes 43475996 | solution.py:268
  534.9 10.4 select_reduce_fusion.7
  546.0 11.2 fusion.227
  559.8 10.2 select_reduce_fusion.7
  570.7 11.3 fusion.227
  583.3 9.0 all-gather.3
  592.3 8.2 all-gather.4
  600.5 18.3 select_reduce_fusion.4
  618.9 9.0 all-gather
  627.9 12.1 select_reduce_fusion.2
  640.2 8.5 all-gather.1
  648.7 9.0 all-gather.7
  671.9 55.7 %while.139 = (s32[]{:T(128)}, f32[2048,256]{1,0:T(8,128)}, bf16[2,2500,256]{2,1,0:T(8,128)(2,1)}, f32[2048]{0:T(1024)S(1)}, s32[2]{0:T(128)S(1)}, /*index=5*/s32...) while((s32[]{:T(128)}, f32[2048,256]{1,0:T(8,128)}, ...), condition=%wide.region_38.39_spmd.clone, body=%wide.region_37.38_spmd.clone.sunk | while | flops 7906335744 | bytes 103660192 | solution.py:378
  673.8 11.5 fusion.237
  685.3 9.3 convolution_add_fusion.14
  701.3 11.5 fusion.237
  712.8 10.0 convolution_add_fusion.14
  730.6 12.4 multiply_convert_fusion
  747.0 13.3 convolution_convert_fusion.3
  761.6 321.2 %while.140 = (s32[]{:T(128)}, f32[2048,64]{0,1:T(8,128)S(1)}, bf16[23,1129,64]{1,2,0:T(8,128)(2,1)}, f32[2048]{0:T(1024)S(1)}, s32[23]{0:T(128)S(1)}, /*index=5*...) while((s32[]{:T(128)}, f32[2048,64]{0,1:T(8,128)S(1)}, ...), condition=%wide.region_41.42_spmd.clone, body=%wide.region_40.41_spmd.clone.sunk | while | flops 906644800 | bytes 34886888 | solution.py:378
  1086.7 35.2 %reduce-scatter.23.cloned.1.call-done = bf16[256,64]{0,1:T(8,128)(2,1)} async-done(((bf16[2048,64]{0,1:T(8,128)(2,1)}), bf16[256,64]{0,1:T(8,128)(2,1)}) %reduce-scatter.23.cloned.1.call-update) | async-done | bytes 32784 | tf_op jit(solution)/shard_map/reduce_scatter | solution.py:518
  1151.3 50.4 %while.136 = (s32[]{:T(128)}, f32[256,16,64]{0,2,1:T(8,128)}, f32[1024,1024]{0,1:T(8,128)}, f32[1024,1024]{0,1:T(8,128)}, s32[2]{0:T(128)}, /*index=5*/s32[]{:T(...) while((s32[]{:T(128)}, f32[256,16,64]{0,2,1:T(8,128)}, ...), condition=%wide.region_50.51_spmd, body=%wide.region_47.50_spmd.sunk | while | flops 1369572096 | bytes 137813056 | solution.py:199
  1153.4 46.4 %conditional.8 = ((f32[256,16,64]{0,2,1:T(8,128)}, f32[1024,1024]{0,1:T(8,128)}, f32[1024,1024]{0,1:T(8,128)})) conditional(s32[]{:T(128)} %convert_element_type.710, (f32[256,16,64]{0,2,1:T(8,128)}, f32[1024,1024]{0,1:T(8,128)}, f32[1024,1024]{0,1:T(8,128)}) %tuple.268, (s32[]{:T(128)}, s32[]{:T(128)}, bf16[2,512,16,64]{1,3,2,0:T(8,128)(2,1)}, ...), branch_computations={%region_48.48_spmd, %region_49.49_spmd} | conditional | flops 1369572096 | bytes 137812768 | solution.py:197
  1178.0 10.9 dynamic_update_slice.19
  1188.9 11.0 dynamic_update_slice.20
  1220.4 74.0 %reduce-scatter.25.cloned.1.call-done = bf16[256,1024]{0,1:T(8,128)(2,1)} async-done(((bf16[1024,1024]{0,1:T(8,128)(2,1)}), bf16[256,1024]{0,1:T(8,128)(2,1)}) %reduce-scatter.25.cloned.1.call-update) | async-done | bytes 524304 | tf_op jit(solution)/shard_map/reduce_scatter | solution.py:575
  1297.7 42.8 %reduce-scatter.27.cloned.1.call-done = bf16[256,1024]{0,1:T(8,128)(2,1)} async-done(((bf16[1024,1024]{0,1:T(8,128)(2,1)}), bf16[256,1024]{0,1:T(8,128)(2,1)}) %reduce-scatter.27.cloned.1.call-update) | async-done | bytes 524304 | tf_op jit(solution)/shard_map/reduce_scatter | solution.py:578
  1351.7 8.9 convolution_convert_fusion
  1366.0 16.3 convolution_convert_fusion.2
  1397.5 24.9 %reduce-scatter.29.cloned.1.call-done = bf16[128,1024]{1,0:T(8,128)(2,1)} async-done(((bf16[1024,1024]{1,0:T(8,128)(2,1)}), bf16[128,1024]{1,0:T(8,128)(2,1)}) %reduce-scatter.29.cloned.1.call-update) | async-done | bytes 262160 | tf_op jit(solution)/shard_map/reduce_scatter | solution.py:606
  1422.4 44.4 %reduce-scatter.35.cloned.1.call-done = bf16[128,1024]{1,0:T(8,128)(2,1)} async-done(((bf16[1024,1024]{1,0:T(8,128)(2,1)}), bf16[128,1024]{1,0:T(8,128)(2,1)}) %reduce-scatter.35.cloned.1.call-update) | async-done | bytes 262160 | tf_op jit(solution)/shard_map/reduce_scatter | solution.py:621
  1466.8 45.5 %reduce-scatter.31.cloned.1.call-done = bf16[128,1024]{1,0:T(8,128)(2,1)} async-done(((bf16[1024,1024]{1,0:T(8,128)(2,1)}), bf16[128,1024]{1,0:T(8,128)(2,1)}) %reduce-scatter.31.cloned.1.call-update) | async-done | bytes 262160 | tf_op jit(solution)/shard_map/reduce_scatter | solution.py:612
  1512.3 45.0 %reduce-scatter.33.cloned.1.call-done = bf16[128,1024]{1,0:T(8,128)(2,1)} async-done(((bf16[1024,1024]{1,0:T(8,128)(2,1)}), bf16[128,1024]{1,0:T(8,128)(2,1)}) %reduce-scatter.33.cloned.1.call-update) | async-done | bytes 262160 | tf_op jit(solution)/shard_map/reduce_scatter | solution.py:615
  1557.2 75.0 %reduce-scatter.37.cloned.1.call-done = bf16[128,4096]{1,0:T(8,128)(2,1)} async-done(((bf16[1024,4096]{1,0:T(8,128)(2,1)}), bf16[128,4096]{1,0:T(8,128)(2,1)}) %reduce-scatter.37.cloned.1.call-update) | async-done | bytes 1048592 | tf_op jit(solution)/shard_map/reduce_scatter | solution.py:633
  1632.2 74.7 %reduce-scatter.39.cloned.1.call-done = bf16[512,1024]{1,0:T(8,128)(2,1)} async-done(((bf16[4096,1024]{1,0:T(8,128)(2,1)}), bf16[512,1024]{1,0:T(8,128)(2,1)}) %reduce-scatter.39.cloned.1.call-update) | async-done | bytes 1048592 | tf_op jit(solution)/shard_map/reduce_scatter | solution.py:639
  1710.0 34.2 %reduce-scatter.43.cloned.1.call-done = bf16[128,2]{1,0:T(8,128)(2,1)} async-done(((bf16[1024,2]{1,0:T(8,128)(2,1)}), bf16[128,2]{1,0:T(8,128)(2,1)}) %reduce-scatter.43.cloned.1.call-update) | async-done | bytes 528
  1745.1 36.3 %reduce-scatter.45.cloned.1.call-done = bf16[128,64]{1,0:T(8,128)(2,1)} async-done(((bf16[1024,64]{1,0:T(8,128)(2,1)}), bf16[128,64]{1,0:T(8,128)(2,1)}) %reduce-scatter.45.cloned.1.call-update) | async-done | bytes 16400
  1792.0 23.8 %all-reduce.11 = (bf16[1024]{0:T(1024)(128)(2,1)S(1)}, bf16[1024]{0:T(1024)(128)(2,1)S(1)}, bf16[1024]{0:T(1024)(128)(2,1)S(1)}, bf16[1024]{0:T(1024)(128)(2,1)S...) all-reduce(bf16[1024]{0:T(1024)(128)(2,1)S(1)} %get-tuple-element.1, ...), channel_id=15, replica_groups=mesh['seq'=4,'batch'=8] {'batch'}, use_global_device_ids=true, to_apply=%region_56.57.clone | all-reduce | flops 14336 | bytes 57344
  1816.7 22.1 all-reduce.12
  1849.7 424.2 %all-reduce.16.cloned.1.call-done = (bf16[128,1024]{1,0:T(8,128)(2,1)}, bf16[128,1024]{1,0:T(8,128)(2,1)}, bf16[128,1024]{1,0:T(8,128)(2,1)}, bf16[128,1024]{1,0...) async-done(((bf16[128,1024]{1,0:T(8,128)(2,1)}, ...) | async-done | bytes 14215056 | tf_op jit(solution)/shard_map/psum | solution.py:664
  (969 shorter events, 976.8 us)
Async XLA Ops:
  7.2 57.8 %all-gather.14.cloned.1.call-start = ((), (), s32[]{:S(2)}) async-start(), calls=%async_computation.14 | async-start | bytes 2621440 | tf_op jit(solution)/shard_map/all_gather | solution.py:456
  16.2 95.6 %all-gather.16.cloned.1.call-start = ((), (), s32[]{:S(2)}) async-start(), calls=%async_computation.15 | async-start | bytes 2621440 | tf_op jit(solution)/shard_map/all_gather | solution.py:457
  17.8 514.9 %all-gather.20.cloned.1.call-start = ((), (), s32[]{:S(2)}) async-start(), calls=%async_computation.17 | async-start | bytes 1179648 | tf_op jit(solution)/shard_map/all_gather | solution.py:485
  154.3 446.2 %all-gather.18.cloned.1.call-start = ((), (), s32[]{:S(2)}) async-start(), calls=%async_computation.16 | async-start | bytes 4718592 | tf_op jit(solution)/shard_map/all_gather | solution.py:484
  164.8 366.6 %copy-start.58 = (bf16[1024,2]{0,1:T(2,128)(2,1)S(1)}, bf16[1024,2]{0,1:T(2,128)(2,1)}, u32[]{:S(2)}) copy-start(bf16[1024,2]{0,1:T(2,128)(2,1)} %param.73) | copy-start | bytes 12292
  514.0 18.7 copy-start.7
  514.1 18.7 copy-start.37
  531.4 552.7 %reduce-scatter.21.cloned.1.call-start = ((), (), s32[]{:S(2)}) async-start(), calls=%async_computation.19 | async-start | bytes 1179648 | tf_op jit(solution)/shard_map/reduce_scatter | solution.py:515
  532.7 67.8 %copy-start.63 = (pred[2500]{0:T(1024)(128)(4,1)S(1)}, pred[2500]{0:T(1024)(128)(4,1)}, u32[]{:S(2)}) copy-start(pred[2500]{0:T(1024)(128)(4,1)} %iota_compare_fusion.1) | copy-start | bytes 7504
  600.5 27.4 %copy-start.44 = (s32[1,2048]{1,0:T(1,128)S(1)}, s32[1,2048]{1,0:T(1,128)}, u32[]{:S(2)}) copy-start(s32[1,2048]{1,0:T(1,128)} %copy-done.43) | copy-start | bytes 24580
  627.9 20.8 copy-start.75
  627.9 20.8 copy-start.106
  627.9 20.8 copy-start.107
  640.1 22.5 copy-start.95
  640.1 22.5 copy-start.117
  640.1 22.5 copy-start.118
  640.1 22.5 copy-start.119
  640.1 31.2 %copy-start.71 = (pred[2048]{0:T(1024)(128)(4,1)S(1)}, pred[2048]{0:T(1024)(128)(4,1)}, u32[]{:S(2)}) copy-start(pred[2048]{0:T(1024)(128)(4,1)} %copy-done.70) | copy-start | bytes 6148
  640.1 31.2 %copy-start.73 = (pred[2048]{0:T(1024)(128)(4,1)S(1)}, pred[2048]{0:T(1024)(128)(4,1)}, u32[]{:S(2)}) copy-start(pred[2048]{0:T(1024)(128)(4,1)} %copy-done.72) | copy-start | bytes 6148
  640.1 31.8 %copy-start.14 = (bf16[2048,256]{1,0:T(8,128)(2,1)S(1)}, bf16[2048,256]{1,0:T(8,128)(2,1)}, u32[]{:S(2)}) copy-start(bf16[2048,256]{1,0:T(8,128)(2,1)} %get-tuple-element.2567) | copy-start | bytes 3145732
  730.3 353.8 %reduce-scatter.19.cloned.1.call-start = ((), (), s32[]{:S(2)}) async-start(), calls=%async_computation.18 | async-start | bytes 4718592 | tf_op jit(solution)/shard_map/reduce_scatter | solution.py:512
  760.4 361.4 %reduce-scatter.23.cloned.1.call-start = ((), (), s32[]{:S(2)}) async-start(), calls=%async_computation.20 | async-start | bytes 294912 | tf_op jit(solution)/shard_map/reduce_scatter | solution.py:518
  761.6 360.2 %copy-start.42 = (bf16[1024,64]{0,1:T(8,128)(2,1)S(1)}, bf16[1024,64]{0,1:T(8,128)(2,1)}, u32[]{:S(2)}) copy-start(bf16[1024,64]{0,1:T(8,128)(2,1)} %param.76) | copy-start | bytes 393220
  1082.8 40.8 %copy-start.55 = (f32[1024]{0:T(1024)S(1)}, f32[1024]{0:T(1024)}, u32[]{:S(2)}) copy-start(f32[1024]{0:T(1024)} %param.70) | copy-start | bytes 12292
  1082.8 40.8 %copy-start.59 = (bf16[1024,2]{0,1:T(2,128)(2,1)S(1)}, bf16[1024,2]{0,1:T(2,128)(2,1)}, u32[]{:S(2)}) copy-start(bf16[1024,2]{0,1:T(2,128)(2,1)} %param.73) | copy-start | bytes 12292
  1082.8 40.8 %copy-start.61 = (f32[256,2]{0,1:T(2,128)S(1)}, f32[256,2]{0,1:T(2,128)}, u32[]{:S(2)}) copy-start(f32[256,2]{0,1:T(2,128)} %copy-done.60) | copy-start | bytes 6148
  1082.8 40.8 %copy-start.69 = (f32[256]{0:T(256)S(1)}, f32[256]{0:T(256)}, u32[]{:S(2)}) copy-start(f32[256]{0:T(256)} %copy-done.68) | copy-start | bytes 3076
  1082.8 40.8 %copy-start.80 = (f32[256]{0:T(256)S(1)}, f32[256]{0:T(256)}, u32[]{:S(2)}) copy-start(f32[256]{0:T(256)} %copy-done.79) | copy-start | bytes 3076
  1082.8 40.8 %copy-start.82 = (f32[256]{0:T(256)S(1)}, f32[256]{0:T(256)}, u32[]{:S(2)}) copy-start(f32[256]{0:T(256)} %copy-done.81) | copy-start | bytes 3076
  1082.8 40.8 %copy-start.89 = (f32[256]{0:T(256)S(1)}, f32[256]{0:T(256)}, u32[]{:S(2)}) copy-start(f32[256]{0:T(256)} %get-tuple-element.1598) | copy-start | bytes 3076
  1082.8 40.8 %copy-start.91 = (pred[256,1]{0,1:T(4,128)(4,1)S(1)}, pred[256,1]{0,1:T(4,128)(4,1)}, u32[]{:S(2)}) copy-start(pred[256,1]{0,1:T(4,128)(4,1)} %get-tuple-element.1606) | copy-start | bytes 772
  1082.8 40.8 %copy-start.93 = (pred[256,1]{0,1:T(4,128)(4,1)S(1)}, pred[256,1]{0,1:T(4,128)(4,1)}, u32[]{:S(2)}) copy-start(pred[256,1]{0,1:T(4,128)(4,1)} %get-tuple-element.1607) | copy-start | bytes 772
  1082.8 42.0 %copy-start.102 = (f32[256]{0:T(256)S(1)}, f32[256]{0:T(256)}, u32[]{:S(2)}) copy-start(f32[256]{0:T(256)} %copy-done.101) | copy-start | bytes 3076
  1083.6 40.1 %copy-start.19 = (f32[256,1024]{1,0:T(8,128)S(1)}, f32[256,1024]{1,0:T(8,128)}, u32[]{:S(2)}) copy-start(f32[256,1024]{1,0:T(8,128)} %copy-done.18) | copy-start | bytes 3145732
  1083.6 210.8 %reduce-scatter.25.cloned.1.call-start = ((), (), s32[]{:S(2)}) async-start(), calls=%async_computation.21 | async-start | bytes 2621440 | tf_op jit(solution)/shard_map/reduce_scatter | solution.py:575
  1205.7 134.9 %reduce-scatter.27.cloned.1.call-start = ((), (), s32[]{:S(2)}) async-start(), calls=%async_computation.22 | async-start | bytes 2621440 | tf_op jit(solution)/shard_map/reduce_scatter | solution.py:578
  1209.6 187.9 %reduce-scatter.41.cloned.1.call-start = ((), (), s32[]{:S(2)}) async-start(), calls=%async_computation.29 | async-start | bytes 589824 | tf_op jit(solution)/shard_map/reduce_scatter | solution.py:654
  1212.0 210.4 %reduce-scatter.29.cloned.1.call-start = ((), (), s32[]{:S(2)}) async-start(), calls=%async_computation.23 | async-start | bytes 2359296 | tf_op jit(solution)/shard_map/reduce_scatter | solution.py:606
  1216.6 250.2 %reduce-scatter.35.cloned.1.call-start = ((), (), s32[]{:S(2)}) async-start(), calls=%async_computation.26 | async-start | bytes 2359296 | tf_op jit(solution)/shard_map/reduce_scatter | solution.py:621
  1220.1 292.1 %reduce-scatter.31.cloned.1.call-start = ((), (), s32[]{:S(2)}) async-start(), calls=%async_computation.24 | async-start | bytes 2359296 | tf_op jit(solution)/shard_map/reduce_scatter | solution.py:612
  1297.7 46.3 %copy-start.51 = (f32[1024]{0:T(1024)S(1)}, f32[1024]{0:T(1024)}, u32[]{:S(2)}) copy-start(f32[1024]{0:T(1024)} %param.65) | copy-start | bytes 12292
  1297.7 259.5 %reduce-scatter.33.cloned.1.call-start = ((), (), s32[]{:S(2)}) async-start(), calls=%async_computation.25 | async-start | bytes 2359296 | tf_op jit(solution)/shard_map/reduce_scatter | solution.py:615
  1343.9 288.4 %reduce-scatter.37.cloned.1.call-start = ((), (), s32[]{:S(2)}) async-start(), calls=%async_computation.27 | async-start | bytes 9437184 | tf_op jit(solution)/shard_map/reduce_scatter | solution.py:633
  1351.7 355.2 %reduce-scatter.39.cloned.1.call-start = ((), (), s32[]{:S(2)}) async-start(), calls=%async_computation.28 | async-start | bytes 9437184 | tf_op jit(solution)/shard_map/reduce_scatter | solution.py:639
  1360.7 383.5 %reduce-scatter.43.cloned.1.call-start = ((), (), s32[]{:S(2)}) async-start(), calls=%async_computation.30 | async-start | bytes 294912
  1363.5 417.9 %reduce-scatter.45.cloned.1.call-start = ((), (), s32[]{:S(2)}) async-start(), calls=%async_computation.31 | async-start | bytes 294912
  1365.7 908.3 %all-reduce.16.cloned.1.call-start = ((), (), s32[]{:S(2)}) async-start(), calls=%async_computation.32 | async-start | bytes 28450816 | tf_op jit(solution)/shard_map/psum | solution.py:664
  1787.1 58.5 %copy-start.98 = (f32[256]{0:T(256)S(1)}, f32[256]{0:T(256)}, u32[]{:S(2)}) copy-start(f32[256]{0:T(256)} %copy-done.97) | copy-start | bytes 3076
  (131 other events, 680.6 us)
Sparse Core Ops, SparseCore 0:
  16.3 48.6 all-gather.13
  67.1 44.6 all-gather.15
  154.4 28.6 all-gather.19
  531.5 40.9 all-gather.17
  730.5 40.6 reduce-scatter.20
  774.4 51.2 reduce-scatter.18
  1083.7 38.0 reduce-scatter.22
  1205.8 88.5 reduce-scatter.24
  1297.4 43.1 reduce-scatter.26
  1344.1 33.4 reduce-scatter.40
  1381.2 41.2 reduce-scatter.28
  1425.5 41.1 reduce-scatter.34
  1471.0 41.2 reduce-scatter.30
  1516.0 41.1 reduce-scatter.32
  1560.9 71.2 reduce-scatter.36
  1635.5 71.2 reduce-scatter.38
  1710.6 33.5 reduce-scatter.42
  1747.7 33.6 reduce-scatter.44
  1787.0 486.9 all-reduce.15
where the time goes:
time: 2320 us; the launch traced here: 2300 us
  waiting for transfers between devices  988 us (43%)
  matrix products  637 us (27%)
  other arithmetic  342 us (15%)
  local copies, waits for them, and re-layouts  157 us (7%)
  blocking collectives  135 us (6%)
  loops' own time  26 us (1%)
    psum x1, waiting for transfers between devices, on_device(): lax.psum(reduced[2].astype(jnp.bfloat16), 'seq').astype(jnp.float32)  424 us
    dot_general x60, matrix products, product_nt(): lax.dot_general(former, latter, (((1,), (1,)), ((), ())), preferred_eleme...  368 us
    reduce_sum x26, other arithmetic, select_column(): return jnp.sum(jnp.where(matches, logits, 0.0), -1)  170 us
    dot_general x36, matrix products, product(): return jnp.dot(former, latter, preferred_element_type=jnp.float32)  141 us
    dot_general x35, matrix products, product_tn(): lax.dot_general(former, latter, (((0,), (0,)), ((), ())), preferred_eleme...  105 us
    reduce_scatter x1, waiting for transfers between devices, on_device(): lax.psum_scatter(inner_weight_grad.astype(jnp.bfloat16), 'batch', scatter...  75 us
    reduce_scatter x1, waiting for transfers between devices, on_device(): lax.psum_scatter(outer_weight_grad.astype(jnp.bfloat16), 'batch', scatter...  74.7 us
    reduce_scatter x1, waiting for transfers between devices, on_device(): lax.psum_scatter(key_grads.astype(jnp.bfloat16), 'seq', scatter_dimension...  74 us
  transfers between devices with their start and end apart: 19, of which 14 were waited for; matrix products, arithmetic and copies ran while one was open for 38% of the time, Pallas kernels for 0%

commit v1 on v0

v1 whole, which is shorter than its diff:
```python
import functools
import math

import jax
import jax.numpy as jnp
from jax import lax
from jax.experimental import pallas as pl
from jax.experimental.pallas import tpu as pltpu
from jax.sharding import PartitionSpec as P

HEADS = 16
HEAD_WORDS = 20000
MID_WORDS = 40000
TAIL_WORDS = 207735


NEG_FILL = -1e30
EPSILON = 1e-05
BLOCK = 256
SAFE = 1e30
VMEM_BYTES = 56 << 20
ONCE = dict(pipeline_mode=pl.Buffered(1))


def layer_norm(values, gain_vector, shift_vector):
    average = jnp.mean(values, -1, keepdims=True)
    centred = values - average
    spread = jnp.mean(centred * centred, -1, keepdims=True)
    return centred * lax.rsqrt(spread + EPSILON) * gain_vector + shift_vector


def norm_back(values, gain_vector, shift_vector, upstream):
    unused, pullback = jax.vjp(layer_norm, values, gain_vector, shift_vector)
    return pullback(upstream)


def gelu_back(before, upstream):
    unused, pullback = jax.vjp(jax.nn.gelu, before)
    return pullback(upstream)[0]


def product(former, latter):
    return jnp.dot(former, latter, preferred_element_type=jnp.float32)


def product_tn(former, latter):
    return lax.dot_general(
        former, latter, (((0,), (0,)), ((), ())), preferred_element_type=jnp.float32
    )


def product_nt(former, latter):
    return lax.dot_general(
        former, latter, (((1,), (1,)), ((), ())), preferred_element_type=jnp.float32
    )


def lowered(values):
    return values.astype(jnp.bfloat16)


def round_up(count, unit):
    return -(-count // unit) * unit


def thirds(values):
    high = lowered(values)
    rest = values - high.astype(jnp.float32)
    middle = lowered(rest)
    return [high, middle, lowered(rest - middle.astype(jnp.float32))]


def attend_kernel(start_ref, query_ref, key_ref, value_ref, out_ref):
    rows, keys = query_ref.shape[0], key_ref.shape[0]
    half = query_ref.shape[1] // 2
    query_pos = start_ref[0] + lax.broadcasted_iota(jnp.int32, (rows, keys), 0)
    allowed = lax.broadcasted_iota(jnp.int32, (rows, keys), 1) <= query_pos
    for part in range(2):
        cols = slice(part * half, part * half + half)
        scores = product_nt(query_ref[:, cols], key_ref[:, cols]) * half**-0.5
        scores = jnp.where(allowed, scores, NEG_FILL)
        weights = jnp.exp(scores - jnp.max(scores, 1, keepdims=True))
        weights = weights / jnp.sum(weights, 1, keepdims=True)
        out_ref[:, cols] = lowered(product(lowered(weights), value_ref[:, cols]))


def attend(start, queries, keys, values):
    rows, features = queries.shape
    width = 2 * features // HEADS
    own = pl.BlockSpec((rows, width), lambda i, s: (0, i))
    whole = pl.BlockSpec((keys.shape[0], width), lambda i, s: (0, i))
    return pl.pallas_call(
        attend_kernel,
        grid_spec=pltpu.PrefetchScalarGridSpec(
            num_scalar_prefetch=1,
            grid=(features // width,),
            in_specs=[own, whole, whole],
            out_specs=own,
        ),
        out_shape=jax.ShapeDtypeStruct((rows, features), jnp.bfloat16),
        compiler_params=pltpu.CompilerParams(vmem_limit_bytes=VMEM_BYTES),
        cost_estimate=pl.CostEstimate(
            flops=4 * rows * keys.shape[0] * features,
            bytes_accessed=4 * (rows + keys.shape[0]) * features,
            transcendentals=rows * keys.shape[0] * HEADS,
        ),
        name="attend",
    )(start, queries, keys, values)


def attend_back_kernel(
    start_ref, query_ref, key_ref, value_ref, up_ref, query_grad_ref, key_grad_ref, value_grad_ref
):
    rows, keys = query_ref.shape[0], key_ref.shape[0]
    half = query_ref.shape[1] // 2
    scale = half**-0.5
    query_pos = start_ref[0] + lax.broadcasted_iota(jnp.int32, (keys, rows), 1)
    allowed = lax.broadcasted_iota(jnp.int32, (keys, rows), 0) <= query_pos
    for part in range(2):
        cols = slice(part * half, part * half + half)
        query, key, value, up = (
            ref[:, cols] for ref in (query_ref, key_ref, value_ref, up_ref)
        )
        scores = jnp.where(allowed, product_nt(key, query) * scale, NEG_FILL)
        probs = jnp.exp(scores - jnp.max(scores, 0, keepdims=True))
        probs = probs / jnp.sum(probs, 0, keepdims=True)
        prob_grad = product_nt(value, up)
        delta = jnp.sum(probs * prob_grad, 0, keepdims=True)
        score_grad = lowered(probs * (prob_grad - delta))
        value_grad_ref[:, cols] = lowered(product(lowered(probs), up))
        key_grad_ref[:, cols] = lowered(product(score_grad, query) * scale)
        query_grad_ref[:, cols] = lowered(product_tn(score_grad, key) * scale)


def attend_back(start, queries, keys, values, upstream):
    rows, features = queries.shape
    count = keys.shape[0]
    width = 2 * features // HEADS
    own = pl.BlockSpec((rows, width), lambda i, s: (0, i))
    whole = pl.BlockSpec((count, width), lambda i, s: (0, i))
    return pl.pallas_call(
        attend_back_kernel,
        grid_spec=pltpu.PrefetchScalarGridSpec(
            num_scalar_prefetch=1,
            grid=(features // width,),
            in_specs=[own, whole, whole, own],
            out_specs=[own, whole, whole],
        ),
        out_shape=[
            jax.ShapeDtypeStruct((rows, features), jnp.bfloat16),
            jax.ShapeDtypeStruct((count, features), jnp.bfloat16),
            jax.ShapeDtypeStruct((count, features), jnp.bfloat16),
        ],
        compiler_params=pltpu.CompilerParams(vmem_limit_bytes=VMEM_BYTES),
        cost_estimate=pl.CostEstimate(
            flops=10 * rows * count * features,
            bytes_accessed=6 * (rows + count) * features,
            transcendentals=rows * count * HEADS,
        ),
        name="attend_back",
    )(start, queries, keys, values, upstream)


def pick_kernel(by_slot, index_ref, rows_ref, out_ref):
    count = rows_ref.shape[0]
    total = jnp.zeros(out_ref.shape, jnp.float32)
    base = pl.program_id(0) * BLOCK
    for at in range(0, count, BLOCK):
        if by_slot:
            place = base + lax.broadcasted_iota(jnp.int32, (BLOCK, BLOCK), 0)
            hit = index_ref[:, at : at + BLOCK] == place
        else:
            place = at + lax.broadcasted_iota(jnp.int32, (BLOCK, BLOCK), 1)
            hit = index_ref[...] == place
        onehot = lowered(jnp.where(hit, 1.0, 0.0))
        total = total + product(onehot, rows_ref[at : at + BLOCK, :])
    out_ref[...] = total.astype(out_ref.dtype)


def pick_rows(index, rows, out_count, by_slot, kind):
    count, width = rows.shape
    if by_slot:
        index = index.reshape(1, -1)
        index_spec = pl.BlockSpec(index.shape, lambda i: (0, 0))
    else:
        index = index.reshape(-1, 1)
        index_spec = pl.BlockSpec((BLOCK, 1), lambda i: (i, 0))
    return pl.pallas_call(
        functools.partial(pick_kernel, by_slot),
        grid=(out_count // BLOCK,),
        in_specs=[index_spec, pl.BlockSpec(rows.shape, lambda i: (0, 0), **ONCE)],
        out_specs=pl.BlockSpec((BLOCK, width), lambda i: (i, 0)),
        out_shape=jax.ShapeDtypeStruct((out_count, width), kind),
        compiler_params=pltpu.CompilerParams(vmem_limit_bytes=VMEM_BYTES),
        cost_estimate=pl.CostEstimate(
            flops=2 * out_count * count * max(width, 256),
            bytes_accessed=rows.size * 2 + out_count * width * 4,
            transcendentals=0,
        ),
        name="pick_rows",
    )(index, rows)


def band_kernel(chunk, per, words, sum_column, span_ref, rows_ref, table_ref, stat_ref, out_ref, mix_ref):
    step_id = pl.program_id(0)
    count, width = mix_ref.shape
    chunk_count = table_ref.shape[0] // chunk
    group_count = chunk_count // per
    active = (step_id >= span_ref[0]) & (step_id < span_ref[1])

    def put_stats(top, total):
        lane = lax.broadcasted_iota(jnp.int32, (count, 128), 1)
        both = jnp.where(lane == 0, top, jnp.where(lane == 1, total, 0.0))
        stat_ref[...] = both.T[:8, :]

    def logits_at(at, rows):
        return product_nt(rows, table_ref[pl.ds(at, chunk), :])

    def beyond(at, shape):
        return at + lax.broadcasted_iota(jnp.int32, shape, 1) >= words

    def run(rows, top):
        mix_ref[...] = jnp.zeros(mix_ref.shape, jnp.float32)

        def visit(group, total):
            for inner in range(per):
                at = (group * per + inner) * chunk
                checked = isinstance(at, int) and at + chunk > words
                if not isinstance(at, int):
                    at = pl.multiple_of(at, chunk)
                weights = jnp.exp(logits_at(at, rows) - top)
                if checked:
                    weights = jnp.where(beyond(at, weights.shape), 0.0, weights)
                if sum_column is None:
                    for lane in range(0, chunk, 128):
                        total = total + weights[:, lane : lane + 128]
                mix_ref[...] += product(lowered(weights), table_ref[pl.ds(at, chunk), :])
            return total

        lanes = jnp.zeros((count, 128), jnp.float32)
        lanes = visit(0, lanes) if group_count == 1 else lax.fori_loop(0, group_count, visit, lanes)
        if sum_column is None:
            return jnp.sum(lanes, 1, keepdims=True)
        return mix_ref[:, sum_column : sum_column + 1]

    @pl.when(active)
    def _():
        rows = rows_ref[...]
        first = product_nt(rows, table_ref[pl.ds(0, 128), :])
        top = jnp.max(first, 1, keepdims=True)
        total = run(rows, top)
        put_stats(top, total)

        @pl.when(jnp.logical_not(jnp.max(jnp.where(total < SAFE, 0.0, 1.0)) < 0.5))
        def _():
            def largest(index, top):
                at = pl.multiple_of(index * chunk, chunk)
                logits = logits_at(at, rows)
                if sum_column is None:
                    logits = jnp.where(beyond(at, logits.shape), NEG_FILL, logits)
                return jnp.maximum(top, jnp.max(logits, 1, keepdims=True))

            exact = lax.fori_loop(0, chunk_count, largest, jnp.full((count, 1), NEG_FILL))
            put_stats(exact, run(rows, exact))

        out_ref[...] = lowered(mix_ref[...])

    @pl.when(jnp.logical_not(active))
    def _():
        put_stats(jnp.full((count, 1), NEG_FILL), jnp.zeros((count, 1), jnp.float32))
        out_ref[...] = jnp.zeros(out_ref.shape, jnp.bfloat16)


def band_forward(span, rows, table, words, chunk, sum_column, share):
    count, width = rows.shape[0], table.shape[1]
    chunk_count = table.shape[0] // chunk
    per = chunk_count if chunk_count <= 4 else 4
    assert chunk_count % per == 0 and words >= 128
    return pl.pallas_call(
        functools.partial(band_kernel, chunk, per, words, sum_column),
        grid_spec=pltpu.PrefetchScalarGridSpec(
            num_scalar_prefetch=1,
            grid=(count // BLOCK,),
            in_specs=[
                pl.BlockSpec((BLOCK, width), lambda i, s: (i, 0)),
                pl.BlockSpec(table.shape, lambda i, s: (0, 0), **ONCE),
            ],
            out_specs=[
                pl.BlockSpec((8, BLOCK), lambda i, s: (0, i)),
                pl.BlockSpec((BLOCK, width), lambda i, s: (i, 0)),
            ],
            scratch_shapes=[pltpu.VMEM((BLOCK, width), jnp.float32)],
        ),
        out_shape=[
            jax.ShapeDtypeStruct((8, count), jnp.float32),
            jax.ShapeDtypeStruct((count, width), jnp.bfloat16),
        ],
        compiler_params=pltpu.CompilerParams(vmem_limit_bytes=VMEM_BYTES),
        cost_estimate=pl.CostEstimate(
            flops=int(share * 4 * count * table.shape[0] * max(width, 256)),
            bytes_accessed=table.size * 2 + count * width * 6,
            transcendentals=int(share * count * table.shape[0]),
        ),
        name="band_forward",
    )(span, rows, table)


def head_grad_kernel(chunk, lists, base_ref, table_ref, *refs):
    out_ref, sum_ref = refs[2 * lists :]
    words = table_ref.shape[0]
    base = base_ref[0] + pl.program_id(0) * words
    sum_ref[...] = jnp.zeros(sum_ref.shape, jnp.float32)
    for rows_ref, fact_ref in zip(refs[0 : 2 * lists : 2], refs[1 : 2 * lists : 2]):
        piece = min(rows_ref.shape[0], 1024)

        def visit(step, unused, rows_ref=rows_ref, fact_ref=fact_ref, piece=piece):
            at = pl.multiple_of(step * piece, piece)
            rows = rows_ref[pl.ds(at, piece), :]
            weight = fact_ref[0:1, pl.ds(at, piece)]
            total = fact_ref[1:2, pl.ds(at, piece)]
            ids = fact_ref[2:3, pl.ds(at, piece)].astype(jnp.int32)
            for start in range(0, words, chunk):
                probs = jnp.exp(product_nt(table_ref[start : start + chunk, :], rows) - total)
                word = base + start + lax.broadcasted_iota(jnp.int32, (chunk, 1), 0)
                grads = weight * (jnp.where(word == ids, 1.0, 0.0) - probs)
                sum_ref[start : start + chunk, :] += product(lowered(grads), rows)
            return unused

        lax.fori_loop(0, rows_ref.shape[0] // piece, visit, 0)
    out_ref[...] = lowered(sum_ref[...])


def head_grad(table, part, part_words, first_word, lists):
    width = table.shape[1]
    word_block = math.gcd(part_words, 640)
    steps = part_words // word_block
    chunk = word_block // 2 if word_block % 32 == 0 else word_block
    specs = []
    for rows, facts in lists:
        specs.append(pl.BlockSpec(rows.shape, lambda i, s: (0, 0), **ONCE))
        specs.append(pl.BlockSpec(facts.shape, lambda i, s: (0, 0), **ONCE))
    count = sum(rows.shape[0] for rows, facts in lists)
    scalars = jnp.stack([first_word + part * part_words, part * steps]).astype(jnp.int32)
    return pl.pallas_call(
        functools.partial(head_grad_kernel, chunk, len(lists)),
        grid_spec=pltpu.PrefetchScalarGridSpec(
            num_scalar_prefetch=1,
            grid=(steps,),
            in_specs=[pl.BlockSpec((word_block, width), lambda i, s: (s[1] + i, 0))] + specs,
            out_specs=pl.BlockSpec((word_block, width), lambda i, s: (i, 0)),
            scratch_shapes=[pltpu.VMEM((word_block, width), jnp.float32)],
        ),
        out_shape=jax.ShapeDtypeStruct((part_words, width), jnp.bfloat16),
        compiler_params=pltpu.CompilerParams(vmem_limit_bytes=VMEM_BYTES),
        cost_estimate=pl.CostEstimate(
            flops=4 * count * part_words * width,
            bytes_accessed=(count + part_words) * width * 2,
            transcendentals=count * part_words,
        ),
        name="head_grad",
    )(scalars, table, *[value for pair in lists for value in pair])


def band_grad_kernel(chunk, most, plan_ref, table_ref, rows_ref, fact_ref, out_ref, sum_ref):
    words = table_ref.shape[0]
    step_id = pl.program_id(0)
    base = plan_ref[most + 1] + step_id * words
    sum_ref[...] = jnp.zeros(sum_ref.shape, jnp.float32)

    def block_at(position):
        return pl.multiple_of(plan_ref[position] * BLOCK, BLOCK)

    def spread(starts):
        rows = [rows_ref[pl.ds(start, BLOCK), :] for start in starts]
        facts = [fact_ref[:, pl.ds(start, BLOCK)] for start in starts]
        rows = rows[0] if len(rows) == 1 else jnp.concatenate(rows, 0)
        facts = facts[0] if len(facts) == 1 else jnp.concatenate(facts, 1)
        weight, total = facts[0:1], facts[1:2]
        for start in range(0, words, chunk):
            probs = jnp.exp(product_nt(table_ref[start : start + chunk, :], rows) - total)
            sum_ref[start : start + chunk, :] -= product(lowered(weight * probs), rows)

    count = plan_ref[0]

    def pair(step, unused):
        spread([block_at(1 + 2 * step), block_at(2 + 2 * step)])
        return unused

    lax.fori_loop(0, count // 2, pair, 0)

    @pl.when(count % 2 == 1)
    def _():
        spread([block_at(count)])

    line = most + 2 + step_id * (most + 1)

    def hits(step, unused):
        at = block_at(line + 1 + step)
        rows = rows_ref[pl.ds(at, BLOCK), :]
        weight = fact_ref[0:1, pl.ds(at, BLOCK)]
        ids = fact_ref[2:3, pl.ds(at, BLOCK)].astype(jnp.int32)
        for start in range(0, words, chunk):
            word = base + start + lax.broadcasted_iota(jnp.int32, (chunk, 1), 0)
            chosen = lowered(jnp.where(word == ids, weight, 0.0))
            sum_ref[start : start + chunk, :] += product(chosen, rows)
        return unused

    lax.fori_loop(0, plan_ref[line], hits, 0)
    out_ref[...] = sum_ref[:, : out_ref.shape[1]].astype(out_ref.dtype)


def listed(flags):
    size = flags.shape[-1]
    order = jnp.cumsum(flags.astype(jnp.int32), -1)
    chosen = (order[..., None, :] == jnp.arange(1, size + 1)[:, None]) & flags[..., None, :]
    places = jnp.sum(jnp.where(chosen, jnp.arange(size), 0), -1)
    return jnp.concatenate([order[..., -1:], places], -1).astype(jnp.int32)


def band_grad(table, rows, facts, active, lowest, highest, part, part_words, first_word, width, chunk):
    count, full = rows.shape[0], table.shape[1]
    word_block = chunk
    steps = part_words // word_block
    most = count // BLOCK
    first = first_word + part * part_words
    low = first + jnp.arange(steps, dtype=jnp.int32)[:, None] * word_block
    step_hits = active[None, :] & (lowest[None, :] < low + word_block) & (highest[None, :] >= low)
    plan = jnp.concatenate(
        [
            listed(active),
            first.reshape(1).astype(jnp.int32),
            listed(step_hits).reshape(-1),
            (part * steps).reshape(1).astype(jnp.int32),
        ]
    )
    last = plan.shape[0] - 1
    return pl.pallas_call(
        functools.partial(band_grad_kernel, chunk // 2 if chunk > 832 else chunk, most),
        grid_spec=pltpu.PrefetchScalarGridSpec(
            num_scalar_prefetch=1,
            grid=(steps,),
            in_specs=[
                pl.BlockSpec((word_block, full), lambda i, s: (s[last] + i, 0)),
                pl.BlockSpec((count, full), lambda i, s: (0, 0), **ONCE),
                pl.BlockSpec(facts.shape, lambda i, s: (0, 0), **ONCE),
            ],
            out_specs=pl.BlockSpec((word_block, width), lambda i, s: (i, 0)),
            scratch_shapes=[pltpu.VMEM((word_block, full), jnp.float32)],
        ),
        out_shape=jax.ShapeDtypeStruct((part_words, width), jnp.bfloat16),
        compiler_params=pltpu.CompilerParams(vmem_limit_bytes=VMEM_BYTES),
        cost_estimate=pl.CostEstimate(
            flops=2 * count * part_words * 256,
            bytes_accessed=count * full * 2 + part_words * full * 4,
            transcendentals=count * part_words // 2,
        ),
        name="band_grad",
    )(plan, table, rows, facts)


def settle_kernel(
    member_ref,
    everyone_ref,
    fact_ref,
    head_mix_ref,
    middle_mix_ref,
    tail_mix_ref,
    head_hit_ref,
    middle_hit_ref,
    tail_hit_ref,
    term_ref,
    line_ref,
    slot_ref,
):
    step = pl.program_id(0)
    devices, _, slots = everyone_ref.shape
    tail_width = 64
    here = pl.ds(pl.multiple_of(step * BLOCK, BLOCK), BLOCK)

    def merged(read):
        lines = [read(device) for device in range(devices)]
        top = functools.reduce(jnp.maximum, [line[0] for line in lines])
        return top, sum(line[1] * jnp.exp(line[0] - top) for line in lines)

    head_top, head_sum = merged(
        lambda d: (everyone_ref[d, 0:1, here], everyone_ref[d, 1:2, here])
    )
    target = sum(everyone_ref[d, 2:3, here] for d in range(devices))
    slot_top, slot_sum = merged(lambda d: (everyone_ref[d, 3:4, :], everyone_ref[d, 4:5, :]))
    used = slot_sum > 0.0
    slot_total = jnp.where(used, slot_top + jnp.log(jnp.where(used, slot_sum, 1.0)), 0.0)
    member = member_ref[0]
    own_slot_top = jnp.where(used, everyone_ref[member, 3:4, :], 0.0)
    own_head_top = everyone_ref[member, 0:1, here]

    facts = fact_ref[...]
    slot, share, cotangent, first_cluster, second_cluster, band, word = (
        facts[index : index + 1] for index in range(7)
    )

    def as_columns(lines):
        square = jnp.concatenate(
            lines + [jnp.zeros((128 - len(lines), BLOCK), jnp.float32)], 0
        )
        return square.T

    def three(line):
        return [part.astype(jnp.float32) for part in thirds(line)]

    slot_column = as_columns([slot])[:, 0:1].astype(jnp.int32)
    hot = lowered(
        jnp.where(lax.broadcasted_iota(jnp.int32, (BLOCK, slots), 1) == slot_column, 1.0, 0.0)
    )
    lines = three(slot_total) + three(own_slot_top) + [jnp.zeros((10, slots), jnp.float32)]
    on_tokens = product_nt(lowered(jnp.concatenate(lines, 0)), hot)
    band_total = on_tokens[0:1] + on_tokens[1:2] + on_tokens[2:3]
    own_band_top = on_tokens[3:4] + on_tokens[4:5] + on_tokens[5:6]

    cluster_top = jnp.maximum(head_top, jnp.maximum(first_cluster, second_cluster))
    head_total = cluster_top + jnp.log(
        head_sum * jnp.exp(head_top - cluster_top)
        + jnp.exp(first_cluster - cluster_top)
        + jnp.exp(second_cluster - cluster_top)
    )
    in_head = band < 0.5
    cluster = jnp.where(band < 1.5, first_cluster, second_cluster)
    model_logp = target - head_total + jnp.where(in_head, 0.0, cluster - band_total)
    ratio = 0.25 * share * jnp.exp(-model_logp)
    weight = cotangent * 0.75 / (0.75 + ratio)
    head_scale = weight * jnp.exp(own_head_top - head_total)
    band_scale = weight * jnp.where(in_head, 0.0, jnp.exp(own_band_top - band_total))
    columns = as_columns([weight, head_scale, band_scale])
    weight_column, head_column, band_column = (columns[:, i : i + 1] for i in range(3))
    width = head_mix_ref.shape[1]
    term_ref[:, :width] = lowered(
        weight_column * head_hit_ref[...].astype(jnp.float32)
        - head_column * head_mix_ref[...].astype(jnp.float32)
    )
    narrow = tail_mix_ref.shape[1]
    kept = lax.broadcasted_iota(jnp.int32, (BLOCK, narrow), 1) < tail_width

    def widened(values):
        values = jnp.where(kept, values, 0.0)
        more = middle_mix_ref.shape[1] - narrow
        return jnp.concatenate([values, jnp.zeros((BLOCK, more), jnp.float32)], 1)

    band_mix = product(hot, middle_mix_ref[...]) + widened(product(hot, tail_mix_ref[...]))
    band_hit = middle_hit_ref[...].astype(jnp.float32) + widened(
        tail_hit_ref[...].astype(jnp.float32)
    )
    term_ref[:, width:] = lowered(weight_column * band_hit - band_column * band_mix)
    line_ref[...] = jnp.concatenate(
        [
            model_logp + jnp.log(0.75 + ratio),
            weight,
            head_total,
            word,
            jnp.zeros((4, BLOCK), jnp.float32),
        ],
        0,
    )

    @pl.when(step == 0)
    def _():
        slot_ref[...] = jnp.concatenate(
            [jnp.zeros((8, slots), jnp.float32), slot_total, jnp.zeros((7, slots), jnp.float32)], 0
        )

    sent = three(weight) + three(word) + [jnp.zeros((10, BLOCK), jnp.float32)]
    slot_ref[0:8, :] += product(lowered(jnp.concatenate(sent, 0)), hot)[0:8]


def settle(member, everyone, facts, head_mix, middle_mix, tail_mix, hits):
    count, width = head_mix.shape
    slots = middle_mix.shape[0]
    full = width + middle_mix.shape[1]

    def tokens(values):
        return pl.BlockSpec((BLOCK, values.shape[1]), lambda i, s: (i, 0))

    def whole(values):
        return pl.BlockSpec(values.shape, lambda i, s: (0,) * values.ndim, **ONCE)

    lines = pl.BlockSpec((8, BLOCK), lambda i, s: (0, i))
    return pl.pallas_call(
        settle_kernel,
        grid_spec=pltpu.PrefetchScalarGridSpec(
            num_scalar_prefetch=1,
            grid=(count // BLOCK,),
            in_specs=[whole(everyone), lines, tokens(head_mix), whole(middle_mix), whole(tail_mix)]
            + [tokens(hit) for hit in hits],
            out_specs=[
                pl.BlockSpec((BLOCK, full), lambda i, s: (i, 0)),
                lines,
                pl.BlockSpec((16, slots), lambda i, s: (0, 0)),
            ],
        ),
        out_shape=[
            jax.ShapeDtypeStruct((count, full), jnp.bfloat16),
            jax.ShapeDtypeStruct((8, count), jnp.float32),
            jax.ShapeDtypeStruct((16, slots), jnp.float32),
        ],
        compiler_params=pltpu.CompilerParams(vmem_limit_bytes=VMEM_BYTES),
        cost_estimate=pl.CostEstimate(
            flops=2 * count * slots * 1024,
            bytes_accessed=count * width * 12 + slots * full,
            transcendentals=slots * 64,
        ),
        name="settle",
    )(member.reshape(1).astype(jnp.int32), everyone, facts, head_mix, middle_mix, tail_mix, *hits)


def line_pieces(value, both=True):
    size = lax.axis_size("seq")
    before, behind = [value], [value]
    for step in range(1, size):
        before.append(
            lax.ppermute(before[-1], "seq", [(d, d + 1) for d in range(step - 1, size - 1)])
        )
        if both:
            behind.append(
                lax.ppermute(behind[-1], "seq", [(d, d - 1) for d in range(1, size - step + 1)])
            )
    return before, behind


def line_gather(value):
    size, place = lax.axis_size("seq"), lax.axis_index("seq")
    before, behind = line_pieces(value)
    return [value] + [
        jnp.where(place + k < size, behind[k], before[size - k]) for k in range(1, size)
    ]


def in_order(pieces):
    size, place = lax.axis_size("seq"), lax.axis_index("seq")
    joined = jnp.zeros((size,) + pieces[0].shape, pieces[0].dtype)
    for k, piece in enumerate(pieces):
        joined = lax.dynamic_update_index_in_dim(joined, piece, lax.rem(place + k, size), 0)
    return joined.reshape((-1,) + pieces[0].shape[1:])


def line_scatter(values, forward=True):
    size, place = lax.axis_size("seq"), lax.axis_index("seq")
    parts = values.reshape((size, -1) + values.shape[1:])

    def part(index):
        index = jnp.clip(index, 0, size - 1)
        return lax.dynamic_index_in_dim(parts, index, 0, False).astype(jnp.float32)

    ahead, back = 0.0, 0.0
    for step in range(1, size):
        if forward:
            sent = lowered(part(place + size - step) + ahead)
            ahead = lax.ppermute(sent, "seq", [(d, d + 1) for d in range(step)]).astype(jnp.float32)
        sent = lowered(part(place - size + step) + back)
        back = lax.ppermute(
            sent, "seq", [(d, d - 1) for d in range(size - step, size)]
        ).astype(jnp.float32)
    return part(place) + ahead + back


def line_sum(values):
    return in_order(line_gather(lowered(line_scatter(values)))).astype(jnp.float32)


def word_pad(rows, biggest, splits):
    chunk = min(biggest, round_up(rows, 128))
    chunks = -(-rows // chunk)
    if chunks > 4:
        chunks = round_up(chunks, 4)
    return chunk, chunks * chunk


def on_device(
    inputs,
    targets,
    neighbours,
    neighbour_scores,
    loglik_grad,
    first_gain,
    first_shift,
    query_weight,
    query_bias,
    key_weight,
    value_weight,
    value_bias,
    out_weight,
    out_bias,
    second_gain,
    second_shift,
    inner_weight,
    inner_bias,
    outer_weight,
    outer_bias,
    final_gain,
    final_shift,
    head_table,
    cluster_weight,
    middle_map,
    middle_table,
    tail_map,
    tail_table,
):
    nb = lax.axis_size("batch")
    nz = lax.axis_size("seq")
    member = lax.axis_index("batch")
    place = lax.axis_index("seq")
    tokens = inputs[0]
    own_ids = targets[0]
    token_count, feature_count = tokens.shape
    group_count = token_count * nb
    slot_count = group_count + BLOCK
    query_start = (place * token_count).reshape(1)

    normed_low = lowered(layer_norm(tokens, first_gain, first_shift))
    earlier, unused = line_pieces(normed_low, False)
    normed_parts = jnp.zeros((nz,) + normed_low.shape, jnp.bfloat16)
    for step in range(nz - 1, -1, -1):
        normed_parts = lax.dynamic_update_index_in_dim(
            normed_parts, earlier[step], jnp.maximum(place - step, 0), 0
        )
    normed_all = normed_parts.reshape(-1, feature_count)
    top_score = jnp.max(neighbour_scores[0], -1, keepdims=True)
    exponent = jnp.exp(neighbour_scores[0] - top_score)
    knn_prob = jnp.sum(jnp.where(neighbours[0] == 0, exponent, 0.0), -1) / jnp.sum(exponent, -1)
    early = jnp.stack([own_ids.astype(jnp.float32), knn_prob, loglik_grad[0]])
    early = lax.all_gather(early, "batch", axis=1, tiled=True)
    all_ids = early[0].astype(jnp.int32)
    all_knn, all_up = early[1], early[2]
    in_head = all_ids < HEAD_WORDS
    in_middle = (all_ids >= HEAD_WORDS) & (all_ids < HEAD_WORDS + MID_WORDS)
    in_tail = all_ids >= HEAD_WORDS + MID_WORDS
    order = jnp.arange(group_count, dtype=jnp.int32)
    ahead = (all_ids[None, :] < all_ids[:, None]) | (
        (all_ids[None, :] == all_ids[:, None]) & (order[None, :] < order[:, None])
    )
    rank = jnp.sum(ahead.astype(jnp.int32), -1)
    head_size = jnp.sum(in_head.astype(jnp.int32))
    middle_size = jnp.sum(in_middle.astype(jnp.int32))
    tail_size = group_count - head_size - middle_size
    middle_blocks = (middle_size + BLOCK - 1) // BLOCK
    tail_blocks = (tail_size + BLOCK - 1) // BLOCK
    slot = jnp.where(
        in_head,
        -1,
        rank - head_size + jnp.where(in_tail, middle_blocks * BLOCK - middle_size, 0),
    )
    zero_span = jnp.zeros((1,), jnp.int32)
    head_span = jnp.array([0, group_count // BLOCK], jnp.int32)
    middle_span = jnp.stack([0 * middle_blocks, middle_blocks]).astype(jnp.int32)
    tail_span = jnp.stack([middle_blocks, middle_blocks + tail_blocks]).astype(jnp.int32)
    slot_order = jnp.arange(slot_count, dtype=jnp.int32)
    slot_middle = slot_order < middle_size
    slot_tail = (slot_order >= middle_blocks * BLOCK) & (
        slot_order < middle_blocks * BLOCK + tail_size
    )
    slot_used = slot_middle | slot_tail
    band_id = all_ids - jnp.where(in_tail, HEAD_WORDS + MID_WORDS, HEAD_WORDS)

    tables = (head_table, middle_table, tail_table)
    sizes = tuple(table.shape[0] for table in tables)
    head_chunk, head_padded = word_pad(sizes[0], 1280, nz)
    middle_chunk, middle_padded = word_pad(sizes[1], 1280, nz)
    tail_chunk, tail_padded = word_pad(sizes[2], 1664, nz)
    tail_width = tail_table.shape[1]
    head_pad = jnp.pad(head_table, ((0, head_padded - sizes[0]), (0, 0)))
    middle_pad = jnp.pad(middle_table, ((0, middle_padded - sizes[1]), (0, 0)))
    tail_word = jnp.arange(tail_padded, dtype=jnp.int32)
    tail_bias = jnp.where(tail_word < jnp.minimum(TAIL_WORDS - member * sizes[2], sizes[2]), 0.0, NEG_FILL)
    tail_pad = jnp.concatenate(
        [
            jnp.pad(tail_table, ((0, tail_padded - sizes[2]), (0, 0))),
            jnp.ones((tail_padded, 1), jnp.bfloat16),
            lowered(tail_bias)[:, None],
            jnp.zeros((tail_padded, 126 - tail_width), jnp.bfloat16),
        ],
        1,
    )
    locals_ = (
        all_ids - member * sizes[0],
        all_ids - HEAD_WORDS - member * sizes[1],
        all_ids - HEAD_WORDS - MID_WORDS - member * sizes[2],
    )
    owned = tuple(
        inside & (local >= 0) & (local < size)
        for inside, local, size in zip((in_head, in_middle, in_tail), locals_, sizes)
    )
    hit_rows = tuple(
        jnp.where(
            own[:, None],
            jnp.take(table, jnp.clip(local, 0, size - 1), axis=0, mode="clip"),
            jnp.bfloat16(0),
        )
        for own, table, local, size in zip(owned, (head_pad, middle_pad, tail_pad), locals_, sizes)
    )

    queries = lowered(product(normed_low, query_weight) + query_bias)
    key_rows = lowered(product(normed_all, key_weight))
    value_rows = lowered(product(normed_all, value_weight) + value_bias)
    attended_low = attend(query_start, queries, key_rows, value_rows)
    mixed = tokens + product(attended_low, out_weight) + out_bias
    second_low = lowered(layer_norm(mixed, second_gain, second_shift))
    before = product(second_low, inner_weight) + inner_bias
    hidden_low = lowered(jax.nn.gelu(before))
    final = mixed + product(hidden_low, outer_weight) + outer_bias
    state_low = lowered(layer_norm(final, final_gain, final_shift))
    all_states = lax.all_gather(state_low, "batch", axis=0, tiled=True)

    middle_width = middle_map.shape[1]
    maps = jnp.pad(jnp.concatenate([middle_map, tail_map], 1), ((0, 0), (0, 128 - tail_width)))
    one_column = (jnp.arange(middle_width + 128) == middle_width + tail_width + 1).astype(jnp.float32)
    band_low = lowered(product(all_states, maps) + one_column)
    middle_low, tail_low = band_low[:, :middle_width], band_low[:, middle_width:]
    cluster_lines = product_nt(
        jnp.pad(cluster_weight.T, ((0, 6), (0, 0))), all_states
    )
    slot_full = pick_rows(slot, band_low, slot_count, True, jnp.bfloat16)
    first_tail = middle_blocks * BLOCK
    in_tail_slot = slot_order >= first_tail
    slot_low = jnp.where(
        in_tail_slot[:, None],
        jnp.pad(slot_full[:, middle_width:], ((0, 0), (0, middle_width - 128))),
        slot_full[:, :middle_width],
    )
    tail_stats, tail_mix = band_forward(
        tail_span, slot_low, tail_pad, tail_padded, tail_chunk, tail_width, 0.5
    )
    middle_stats, middle_mix = band_forward(
        middle_span, slot_low, middle_pad, sizes[1], middle_chunk, None, 0.25
    )
    head_stats, head_mix = band_forward(
        head_span, all_states, head_pad, sizes[0], head_chunk, None, 1.0
    )
    inner_lane = jnp.arange(128) < tail_width
    target_part = (
        jnp.sum(hit_rows[0].astype(jnp.float32) * all_states.astype(jnp.float32), -1)
        + jnp.sum(hit_rows[1].astype(jnp.float32) * middle_low.astype(jnp.float32), -1)
        + jnp.sum(
            jnp.where(inner_lane, hit_rows[2].astype(jnp.float32), 0.0)
            * tail_low.astype(jnp.float32),
            -1,
        )
    )
    slot_stats = jnp.where(in_tail_slot[None, :], tail_stats[:2], middle_stats[:2])
    extra = ((0, 0), (0, BLOCK))
    stats = jnp.concatenate(
        [
            jnp.pad(jnp.concatenate([head_stats[:2], target_part[None]], 0), extra),
            slot_stats,
            jnp.zeros((3, slot_count), jnp.float32),
        ],
        0,
    )
    everyone = lax.all_gather(stats, "batch")

    token_facts = jnp.concatenate(
        [
            slot.astype(jnp.float32)[None],
            early[1:3],
            cluster_lines[:2],
            jnp.where(in_head, 0.0, jnp.where(in_middle, 1.0, 2.0))[None],
            early[0:1],
            jnp.zeros((1, group_count), jnp.float32),
        ],
        0,
    )
    terms, lines, slot_lines = settle(
        member, everyone, token_facts, head_mix, middle_mix, tail_mix, hit_rows
    )
    own_terms = lax.psum_scatter(terms, "batch", scatter_dimension=0, tiled=True).astype(jnp.float32)

    def own_part(values):
        return lax.dynamic_slice_in_dim(values, member * token_count, token_count, 0)

    loglik = own_part(lines[0])

    split = 2 * nz * group_count * feature_count <= 24 << 20
    kind = jnp.where(slot_middle, 1.0, jnp.where(slot_tail, 2.0, 0.0))
    slot_facts = jnp.stack(
        [
            jnp.sum(slot_lines[0:3], 0),
            slot_lines[8],
            jnp.sum(slot_lines[3:6], 0),
            kind,
        ]
    )
    head_facts = jnp.concatenate([lines[1:4], jnp.zeros((1, group_count), jnp.float32)], 0)
    if split:
        piece = slot_count // nb
        slot_piece = lax.dynamic_slice_in_dim(slot_low, member * piece, piece, 0)
        other_states = jnp.concatenate(line_gather(state_low)[1:], 0)
        other_states = lax.all_gather(other_states, "batch", axis=0, tiled=True)
        other_slots = jnp.concatenate(line_gather(slot_piece)[1:], 0)
        other_slots = lax.all_gather(other_slots, "batch", axis=0, tiled=True)
        other_slots = (
            other_slots.reshape(nb, nz - 1, piece, middle_width)
            .transpose(1, 0, 2, 3)
            .reshape(-1, middle_width)
        )
        rows_all = jnp.concatenate([slot_low, other_slots], 0)
        fact_pieces = line_gather(jnp.concatenate([slot_facts, head_facts], 1))
        facts = jnp.concatenate([value[:, :slot_count] for value in fact_pieces], 1)
        other_facts = (
            jnp.stack([value[:, slot_count:] for value in fact_pieces[1:]], 1)
            .reshape(4, nz - 1, nb, token_count)
            .transpose(0, 2, 1, 3)
            .reshape(4, -1)
        )
        lists = [(all_states, head_facts), (other_states, other_facts)]
        part, parts = place, nz
    else:
        rows_all, facts, lists = slot_low, slot_facts, [(all_states, head_facts)]
        part, parts = 0 * place, 1
    head_part = head_grad(head_pad, part, head_padded // parts, member * sizes[0], lists)
    block_facts = facts[2:4].reshape(2, -1, BLOCK)
    block_kind = jnp.max(block_facts[1], -1)
    filled = block_facts[1] > 0
    lowest = jnp.min(jnp.where(filled, block_facts[0], 1e9), -1).astype(jnp.int32)
    highest = jnp.max(jnp.where(filled, block_facts[0], -1e9), -1).astype(jnp.int32)
    facts = jnp.concatenate(
        [facts[:2], jnp.where(facts[3:4] > 0, facts[2:3], -1e9), jnp.zeros_like(facts[:1])], 0
    )
    table_parts = [head_part]
    for band, table, padded, start, width, chunk in (
        (1, middle_pad, middle_padded, HEAD_WORDS, middle_width, middle_chunk),
        (2, tail_pad, tail_padded, HEAD_WORDS + MID_WORDS, tail_width, tail_chunk),
    ):
        part_words = padded // parts
        table_parts.append(
            band_grad(
                table,
                rows_all,
                facts,
                block_kind == band,
                lowest,
                highest,
                part,
                part_words,
                start + member * sizes[band],
                width,
                math.gcd(part_words, chunk),
            )
        )
    if split:
        table_sums = [in_order(line_gather(value)) for value in table_parts]
    else:
        table_sums = [lax.psum(value, "seq") for value in table_parts]
    head_table_grad, middle_table_grad, tail_table_grad = (
        value[:size].astype(jnp.float32) for value, size in zip(table_sums, sizes)
    )

    own_middle = own_part(in_middle)
    own_tail = own_part(in_tail)
    own_lines = lax.dynamic_slice_in_dim(lines, member * token_count, token_count, 1)
    own_weights, own_total = own_lines[1], own_lines[2]
    own_clusters = product(state_low, cluster_weight)
    band_state = own_terms[:, feature_count:]
    middle_state = lowered(jnp.where(own_middle[:, None], band_state, 0.0))
    tail_state = lowered(jnp.where(own_tail[:, None], band_state[:, :tail_width], 0.0))
    cluster_hit = jnp.stack([own_middle, own_tail], -1).astype(jnp.float32)
    cluster_grad = own_weights[:, None] * (
        cluster_hit - jnp.exp(own_clusters - own_total[:, None])
    )
    state_grad = (
        own_terms[:, :feature_count]
        + product_nt(middle_state, middle_map)
        + product_nt(tail_state, tail_map)
        + product_nt(cluster_grad, cluster_weight.astype(jnp.float32))
    )
    middle_map_grad = product_tn(state_low, middle_state)
    tail_map_rows = product_tn(tail_state, state_low)
    cluster_rows = product_tn(cluster_grad, state_low.astype(jnp.float32))
    final_grad, final_gain_grad, final_shift_grad = norm_back(
        final, final_gain, final_shift, state_grad
    )
    final_low = lowered(final_grad)
    outer_weight_grad = product_tn(hidden_low, final_low)
    outer_bias_grad = jnp.sum(final_grad, 0)
    outer_part = lax.psum_scatter(
        lowered(outer_weight_grad), "batch", scatter_dimension=0, tiled=True
    )
    before_grad = lowered(gelu_back(before, product_nt(final_low, outer_weight)))
    inner_weight_grad = product_tn(second_low, before_grad)
    inner_bias_grad = jnp.sum(before_grad.astype(jnp.float32), 0)
    inner_part = lax.psum_scatter(
        lowered(inner_weight_grad), "batch", scatter_dimension=0, tiled=True
    )
    second_in_grad, second_gain_grad, second_shift_grad = norm_back(
        mixed, second_gain, second_shift, product_nt(before_grad, inner_weight)
    )
    mixed_grad = final_grad + second_in_grad
    mixed_low = lowered(mixed_grad)
    out_weight_grad = product_tn(attended_low, mixed_low)
    out_bias_grad = jnp.sum(mixed_grad, 0)
    attended_grad = lowered(product_nt(mixed_low, out_weight))
    query_low, key_low, value_low = attend_back(
        query_start, queries, key_rows, value_rows, attended_grad
    )
    query_weight_grad = product_tn(normed_low, query_low)
    key_weight_grad = product_tn(normed_all, key_low)
    value_weight_grad = product_tn(normed_all, value_low)
    query_bias_grad = jnp.sum(query_low.astype(jnp.float32), 0)
    value_bias_grad = jnp.sum(value_low.astype(jnp.float32), 0)
    spread = product_nt(key_low, key_weight) + product_nt(value_low, value_weight)
    query_spread = product_nt(query_low, query_weight)
    first_shift_grad = jnp.sum(spread, 0) + jnp.sum(query_spread, 0)
    all_centred = (normed_all.astype(jnp.float32) - first_shift) / first_gain
    own_average = jnp.mean(tokens, -1, keepdims=True)
    own_spread = jnp.mean((tokens - own_average) ** 2, -1, keepdims=True)
    own_centred = (tokens - own_average) * lax.rsqrt(own_spread + EPSILON)
    first_gain_grad = jnp.sum(all_centred * spread, 0) + jnp.sum(own_centred * query_spread, 0)
    normed_grad = query_spread + line_scatter(lowered(spread), False)
    first_in_grad, unused, unused = norm_back(tokens, first_gain, first_shift, normed_grad)
    input_grad = mixed_grad + first_in_grad

    bias_rows = inner_bias_grad.shape[0] // feature_count
    inner_bias_rows = (
        inner_bias_grad.reshape(nb, bias_rows, -1).transpose(1, 0, 2).reshape(bias_rows, -1)
    )
    vectors = [
        first_gain_grad,
        first_shift_grad,
        query_bias_grad,
        value_bias_grad,
        out_bias_grad,
        second_gain_grad,
        second_shift_grad,
        outer_bias_grad,
        final_gain_grad,
        final_shift_grad,
    ]
    rows = [tail_map_rows, cluster_rows, inner_bias_rows] + [value[None] for value in vectors]
    edges = [0]
    for row in rows:
        edges.append(edges[-1] + row.shape[0])
    row_count = round_up(edges[-1], 128)
    rows.append(jnp.zeros((row_count - edges[-1], feature_count), jnp.float32))
    columns = [
        query_weight_grad,
        key_weight_grad,
        value_weight_grad,
        out_weight_grad,
        middle_map_grad,
        jnp.concatenate(rows, 0).T,
    ]
    rest_part = lax.psum_scatter(
        jnp.concatenate([lowered(column) for column in columns], 1),
        "batch",
        scatter_dimension=0,
        tiled=True,
    )
    outer_sum = line_sum(outer_part)
    inner_sum = line_sum(inner_part)
    rest_sum = lax.psum(rest_part, "seq").astype(jnp.float32)
    cut = [rest_sum[:, i * feature_count : (i + 1) * feature_count] for i in range(4)]
    middle_map_sum = rest_sum[:, 4 * feature_count : 4 * feature_count + middle_width]
    row_sum = rest_sum[:, 4 * feature_count + middle_width :].T
    tail_map_sum, cluster_sum, inner_bias_sum = (
        row_sum[low:high] for low, high in zip(edges[:3], edges[1:4])
    )
    lines = [row_sum[index] for index in range(edges[3], edges[3] + len(vectors))]
    return (
        loglik.reshape(1, token_count),
        input_grad.reshape(1, token_count, feature_count),
        lines[0],
        lines[1],
        cut[0],
        lines[2],
        cut[1],
        cut[2],
        lines[3],
        cut[3],
        lines[4],
        lines[5],
        lines[6],
        inner_sum,
        inner_bias_sum.reshape(-1),
        outer_sum,
        lines[7],
        lines[8],
        lines[9],
        head_table_grad,
        cluster_sum.T,
        middle_map_sum,
        middle_table_grad,
        tail_map_sum.T,
        tail_table_grad,
    )


def solution(mesh):
    return jax.shard_map(
        on_device,
        mesh=mesh,
        in_specs=(
            P("batch", "seq", None),
            P("batch", "seq"),
            P("batch", "seq", None),
            P("batch", "seq", None),
            P("batch", "seq"),
            P(),
            P(),
            P(),
            P(),
            P(),
            P(),
            P(),
            P(),
            P(),
            P(),
            P(),
            P(),
            P(),
            P(),
            P(),
            P(),
            P(),
            P("batch", None),
            P(),
            P(),
            P("batch", None),
            P(),
            P("batch", None),
        ),
        out_specs=(
            P("batch", "seq"),
            P("batch", "seq", None),
            P("batch"),
            P("batch"),
            P("batch", None),
            P("batch"),
            P("batch", None),
            P("batch", None),
            P("batch"),
            P("batch", None),
            P("batch"),
            P("batch"),
            P("batch"),
            P("batch", None),
            P("batch"),
            P("batch", None),
            P("batch"),
            P("batch"),
            P("batch"),
            P("batch", None),
            P("batch", None),
            P("batch", None),
            P("batch", None),
            P("batch", None),
            P("batch", None),
        ),
        check_vma=False,
    )
```

time: 2320 us -> 1070 us (0.46)
  waiting for transfers between devices: 988 us -> 182 us
  matrix products: 637 us -> 91.1 us
  Pallas kernels: 0 us -> 255 us
  other arithmetic: 342 us -> 127 us
  starting transfers between devices: 1.87 us -> 128 us
  blocking collectives: 135 us -> 20 us
  local copies, waits for them, and re-layouts: 157 us -> 230 us
  loops' own time: 26 us -> 0 us
    reduce_scatter x12 -> x3, waiting for transfers between devices: 461 us -> 0.02 us  [the longest x1 0.02 us: on_device(): lax.psum_scatter(terms, 'batch', scatter_dimension=0, tiled=True)]
    psum x1, waiting for transfers between devices: 424 us -> 48.3 us  [on_device(): rest_sum = lax.psum(rest_part, 'seq').astype(jnp.float32)]
    dot_general x60 -> x10, matrix products: 368 us -> 35.9 us  [product_nt(): lax.dot_general(former, latter, (((1,), (1,)), ((), ())), preferred_eleme...]
    pallas_call x0 -> x10, Pallas kernels: none -> 255 us  [the longest x3 90.4 us: band_forward(): pl.pallas_call(functools.partial(band_kernel, chunk, per, words, sum_colu...]
    reduce_sum x30 -> x10, other arithmetic: 176 us -> 19 us  [the longest x1 5.22 us: on_device(): rank = jnp.sum(ahead.astype(jnp.int32), -1)]
    ppermute x0 -> x66, waiting for transfers between devices: none -> 134 us  [the longest x24 107 us: line_pieces(): lax.ppermute(behind[-1], 'seq', [(d, d - 1) for d in range(1, size - step...]
    ppermute x0 -> x66, starting transfers between devices: none -> 128 us  [the longest x27 56 us: line_pieces(): lax.ppermute(before[-1], 'seq', [(d, d + 1) for d in range(step - 1, size...]
    dot_general x36 -> x8, matrix products: 141 us -> 24.5 us  [product(): return jnp.dot(former, latter, preferred_element_type=jnp.float32)]
  transfers between devices with their start and end apart: 19 -> 74, of which waited for: 14 -> 22; matrix products, arithmetic and copies ran while one was open for 38% -> 36% of each run, Pallas kernels for 0% -> 12%
where the time goes in v1:
time: 1070 us; the launch traced here: 1050 us
  Pallas kernels  255 us (24%)
  local copies, waits for them, and re-layouts  230 us (21%)
  waiting for transfers between devices  182 us (17%)
  starting transfers between devices  128 us (12%)
  other arithmetic  127 us (12%)
  matrix products  91.1 us (9%)
  blocking collectives  20 us (2%)
  between operations  19.9 us (2%)
    ppermute x24, waiting for transfers between devices, line_pieces(): lax.ppermute(behind[-1], 'seq', [(d, d - 1) for d in range(1, size - step...  107 us
    pallas_call x3, Pallas kernels, band_forward(): pl.pallas_call(functools.partial(band_kernel, chunk, per, words, sum_colu...  90.4 us
    dynamic_update_slice x6, local copies, waits for them, and re-layouts, in_order(): lax.dynamic_update_index_in_dim(joined, piece, lax.rem(place + k, size), 0)  83.2 us
    pallas_call x2, Pallas kernels, band_grad(): pl.pallas_call(functools.partial(band_grad_kernel, chunk // 2 if chunk >...  65.7 us
    ppermute x27, starting transfers between devices, line_pieces(): lax.ppermute(before[-1], 'seq', [(d, d + 1) for d in range(step - 1, size...  56 us
    psum x1, waiting for transfers between devices, on_device(): rest_sum = lax.psum(rest_part, 'seq').astype(jnp.float32)  48.3 us
    unnamed x252, local copies, waits for them, and re-layouts  41 us
    dot_general x10, matrix products, product_nt(): lax.dot_general(former, latter, (((1,), (1,)), ((), ())), preferred_eleme...  35.9 us
  transfers between devices with their start and end apart: 74, of which 22 were waited for; matrix products, arithmetic and copies ran while one was open for 36% of the time, Pallas kernels for 12%

profile of v1, /device:TPU:0, one launch (start us, length us, event | category | flops | bytes accessed | tf_op | source)
XLA Modules:
  0.0 1052.8 jit_solution(9266162893850232199)
XLA Ops:
  12.6 5.7 collective-permute-start
  20.8 9.1 all_gather.19
  50.4 7.4 copy.149
  59.0 5.5 pad.29.table_ref
  80.1 15.2 %attend.1 = bf16[256,1024]{1,0:T(8,128)(2,1)} custom-call(s32[1]{0:T(128)} %bitcast.2.start_ref, bf16[256,1024]{1,0:T(8,128)(2,1)} %fusion.18.query_ref, bf16[1024,1024]{1,0:T(8,128)(2,1)} %convolution_convert_fusion.2.key_ref, bf16[1024,1024]{1,0:T(8,128)(2,1)} %add_convert_fusion.value_ref), custom_call_target="tpu_custom_call" | custom-call | flops 1073741824 | bytes 5242880 | tf_op jit(solution)/shard_map/attend/pallas_call | solution.py:92
  98.4 6.0 convolution_add_fusion
  109.5 11.1 %fusion.5.table_ref = bf16[26624,128]{1,0:T(8,128)(2,1)} fusion(bf16[25967,64]{1,0:T(8,128)(2,1)} %copy.149, bf16[26624,1]{1,0:T(8,128)(2,1)} %select_convert_fusion, bf16[128]{0:T(256)(128)(2,1)S(1)} %copy-done.104, bf16[128]{0:T(256)(128)(2,1)S(1)} %copy-done.105), kind=kLoop, calls=%fused_computation.16 | loop fusion | flops 34078720 | bytes 10193280 | tf_op jit(solution)/shard_map/concatenate | solution.py:771
  120.6 11.5 %gather_fusion.2 = bf16[2048,128]{1,0:T(8,128)(2,1)} fusion(bf16[26624,128]{1,0:T(8,128)(2,1)} %fusion.5.table_ref, s32[2048]{0:T(1024)S(1)} %broadcast_clamp_fusion), kind=kCustom, calls=%fused_computation.2 | custom fusion | bytes 1056768 | tf_op jit(solution)/shard_map/jit(_take)/gather | solution.py:792
  132.1 14.1 %gather_fusion = bf16[2048,1024]{1,0:T(8,128)(2,1)} fusion(bf16[2560,1024]{1,0:T(8,128)(2,1)} %pad.29.table_ref, s32[2048]{0:T(1024)S(1)} %broadcast_clamp_fusion.2), kind=kCustom, calls=%fused_computation | custom fusion | bytes 8396800 | tf_op jit(solution)/shard_map/jit(_take)/gather | solution.py:792
  146.2 8.8 gather_fusion.1
  157.3 30.4 %band_forward.3 = (f32[8,2048]{1,0:T(8,128)}, bf16[2048,1024]{1,0:T(8,128)(2,1)}) custom-call(s32[2]{0:T(128)} %iota_multiply_fusion.span_ref, bf16[2048,1024]{1,0:T(8,128)(2,1)} %all-gather.5.cloned.1.call-done.rows_ref.refs_0_, bf16[2560,1024]{1,0:T(8,128)(2,1)} %pad.29.table_ref), custom_call_target="tpu_custom_call" | custom-call | flops 21474836480 | bytes 17825792 | tf_op jit(solution)/shard_map/band_forward/pallas_call | solution.py:279
  192.0 8.6 pick_rows.1
  204.8 47.7 %band_forward.4 = (f32[8,2304]{1,0:T(8,128)}, bf16[2304,128]{1,0:T(8,128)(2,1)}) custom-call(s32[2]{0:T(128)} %pad_add_fusion.1.span_ref, bf16[2304,256]{1,0:T(8,128)(2,1)} %slice_select_fusion.rows_ref, bf16[26624,128]{1,0:T(8,128)(2,1)} %fusion.5.table_ref), custom_call_target="tpu_custom_call" | custom-call | flops 31406948352 | bytes 8585216 | tf_op jit(solution)/shard_map/band_forward/pallas_call | solution.py:279
  252.6 12.2 %band_forward.5 = (f32[8,2304]{1,0:T(8,128)}, bf16[2304,256]{1,0:T(8,128)(2,1)}) custom-call(s32[2]{0:T(128)} %pad_add_fusion.2.span_ref, bf16[2304,256]{1,0:T(8,128)(2,1)} %slice_select_fusion.rows_ref, bf16[5120,256]{1,0:T(8,128)(2,1)} %pad.30.table_ref), custom_call_target="tpu_custom_call" | custom-call | flops 3019898880 | bytes 6160384 | tf_op jit(solution)/shard_map/band_forward/pallas_call | solution.py:279
  274.3 11.0 %all-gather = f32[64,2304]{1,0:T(8,128)} all-gather(f32[8,2304]{1,0:T(8,128)S(1)} %maximum_maximum_fusion), channel_id=2, replica_groups=mesh['seq'=4,'batch'=8] {'batch'}, dimensions={0}, use_global_device_ids=true | all-gather | bytes 663552 | tf_op jit(solution)/shard_map/all_gather | solution.py:855
  287.2 17.0 %settle.1 = (bf16[2048,1280]{1,0:T(8,128)(2,1)}, f32[8,2048]{1,0:T(8,128)}, f32[16,2304]{1,0:T(8,128)}) custom-call(s32[1]{0:T(128)} %bitcast.member_ref, f32[8,8,2304]{2,1,0:T(8,128)} %bitcast.286, f32[8,2048]{1,0:T(8,128)} %concatenate.60.fact_ref, bf16[2048,1024]{1,0:T(8,128)(2,1)} %get-tuple-element.40.head_mix_ref, ...), custom_call_target="tpu_custom_call" | custom-call | flops 9663676416 | bytes 28114944 | tf_op jit(solution)/shard_map/settle/pallas_call | solution.py:585
  306.7 11.7 %collective-permute-start.49 = (bf16[288,256]{1,0:T(8,128)(2,1)S(1)}, bf16[288,256]{1,0:T(8,128)(2,1)S(1)}, u32[]{:S(2)}, u32[]{:S(2)}) collective-permute-start(bf16[288,256]{1,0:T(8,128)(2,1)S(1)} %constant_dynamic-slice_fusion), channel_id=1, source_target_pairs={{0,8},{8,16},{16,24},{1,9},{9,17},{17,25},{2,10},{10,18},{18,26},{... | collective-permute-start | bytes 442376 | tf_op jit(solution)/shard_map/ppermute | solution.py:618
  322.8 5.5 collective-permute-done.52
  342.1 7.7 collective-permute-done.30
  351.8 10.7 %collective-permute-done.34 = bf16[256,1024]{1,0:T(8,128)(2,1)S(1)} collective-permute-done((bf16[256,1024]{1,0:T(8,128)(2,1)S(1)}, bf16[256,1024]{1,0:T(8,128)(2,1)S(1)}, u32[]{:S(2)}, u32[]{:S(2)}) %collective-permute-start.34) | collective-permute-done | bytes 524320 | tf_op jit(solution)/shard_map/ppermute | solution.py:622
  364.5 9.7 collective-permute-done.35
  406.7 8.0 fusion.84
  416.0 5.8 convolution_convert_fusion.1
  451.2 8.1 pad_maximum_fusion.rows_ref
  459.2 55.1 %band_grad.3 = bf16[6656,64]{1,0:T(8,128)(2,1)} custom-call(s32[187]{0:T(256)} %concatenate.73.plan_ref, bf16[26624,128]{1,0:T(8,128)(2,1)} %fusion.5.table_ref, bf16[9216,256]{1,0:T(8,128)(2,1)} %pad_maximum_fusion.rows_ref, f32[4,9216]{1,0:T(4,128)} %fusion.52.fact_ref), custom_call_target="tpu_custom_call" | custom-call | flops 31406948352 | bytes 5767168 | tf_op jit(solution)/shard_map/band_grad/pallas_call | solution.py:437
  518.2 5.8 collective-permute-start.61
  524.0 10.6 %band_grad.2 = bf16[1280,256]{1,0:T(8,128)(2,1)} custom-call(s32[76]{0:T(128)} %concatenate.68.plan_ref, bf16[5120,256]{1,0:T(8,128)(2,1)} %pad.30.table_ref, bf16[9216,256]{1,0:T(8,128)(2,1)} %pad_maximum_fusion.rows_ref, f32[4,9216]{1,0:T(4,128)} %fusion.52.fact_ref), custom_call_target="tpu_custom_call" | custom-call | flops 6039797760 | bytes 6029312 | tf_op jit(solution)/shard_map/band_grad/pallas_call | solution.py:437
  550.2 20.3 %dynamic_update_slice.98 = bf16[4,6656,64]{1,0,2:T(4,128)(2,1)} dynamic-update-slice(bf16[4,6656,64]{1,0,2:T(4,128)(2,1)} %broadcast_in_dim.467, bf16[1,6656,64]{1,0,2:T(2,128)(2,1)} %copy.157, s32[]{:T(128)S(6)} %select_n.386, s32[]{:T(128)} %constant.271.clone.1, s32[]{:T(128)} %constant.271.clone.1) | dynamic-update-slice | bytes 1703940 | tf_op jit(solution)/shard_map/jit(dynamic_update_index_in_dim)/dynamic_update_slice | solution.py:639
  580.0 6.7 multiply_reduce_fusion.4
  589.8 24.0 %attend_back.1 = (bf16[256,1024]{1,0:T(8,128)(2,1)}, bf16[1024,1024]{1,0:T(8,128)(2,1)}, bf16[1024,1024]{1,0:T(8,128)(2,1)}) custom-call(s32[1]{0:T(128)} %bitcast.2.start_ref, bf16[256,1024]{1,0:T(8,128)(2,1)} %fusion.18.query_ref, bf16[1024,1024]{1,0:T(8,128)(2,1)} %convolution_convert_fusion.2.key_ref, bf16[1024,1024]{1,0:T(8,128)(2,1)} %add_convert_fusion.value_ref, ...), custom_call_target="tpu_custom_call" | custom-call | flops 2684354560 | bytes 7864320 | tf_op jit(solution)/shard_map/attend_back/pallas_call | solution.py:141
  620.2 6.8 fusion.85
  626.9 5.3 convolution_convert_fusion
  632.5 6.1 convert_dynamic-update-slice_fusion.2
  669.0 15.5 %collective-permute-done.59 = bf16[1280,256]{1,0:T(8,128)(2,1)S(1)} collective-permute-done((bf16[1280,256]{1,0:T(8,128)(2,1)}, bf16[1280,256]{1,0:T(8,128)(2,1)S(1)}, u32[]{:S(2)}, u32[]{:S(2)}) %collective-permute-start.59) | collective-permute-done | bytes 655392 | tf_op jit(solution)/shard_map/ppermute | solution.py:622
  692.5 7.5 collective-permute-done.65
  706.5 20.3 %dynamic_update_slice.99 = bf16[4,6656,64]{1,0,2:T(4,128)(2,1)} dynamic-update-slice(bf16[4,6656,64]{1,0,2:T(4,128)(2,1)} %dynamic_update_slice.98, bf16[1,6656,64]{1,0,2:T(2,128)(2,1)} %copy.160, s32[]{:T(128)S(6)} %select_n.389, s32[]{:T(128)} %constant.271.clone.1, s32[]{:T(128)} %constant.271.clone.1) | dynamic-update-slice | bytes 1703940 | tf_op jit(solution)/shard_map/jit(dynamic_update_index_in_dim)/dynamic_update_slice | solution.py:639
  726.7 20.3 %dynamic_update_slice.100 = bf16[4,6656,64]{1,0,2:T(4,128)(2,1)} dynamic-update-slice(bf16[4,6656,64]{1,0,2:T(4,128)(2,1)} %dynamic_update_slice.99, bf16[1,6656,64]{1,0,2:T(2,128)(2,1)} %copy.161, s32[]{:T(128)S(6)} %select_n.392, s32[]{:T(128)} %constant.271.clone.1, s32[]{:T(128)} %constant.271.clone.1) | dynamic-update-slice | bytes 1703940 | tf_op jit(solution)/shard_map/jit(dynamic_update_index_in_dim)/dynamic_update_slice | solution.py:639
  747.0 20.3 %dynamic_update_slice.101 = bf16[4,6656,64]{1,0,2:T(4,128)(2,1)} dynamic-update-slice(bf16[4,6656,64]{1,0,2:T(4,128)(2,1)} %dynamic_update_slice.100, bf16[1,6656,64]{1,0,2:T(2,128)(2,1)} %copy.162, s32[]{:T(128)S(6)} %select_n.395, s32[]{:T(128)} %constant.271.clone.1, s32[]{:T(128)} %constant.271.clone.1) | dynamic-update-slice | bytes 1703940 | tf_op jit(solution)/shard_map/jit(dynamic_update_index_in_dim)/dynamic_update_slice | solution.py:639
  780.5 12.5 %copy.169 = bf16[1024,4480]{1,0:T(8,128)(2,1)} copy(bf16[1024,4480]{0,1:T(8,128)(2,1)} %bitcast_dynamic-update-slice_fusion.19) | data formatting | bytes 18350080
  793.1 33.9 %head_grad.1 = bf16[640,1024]{1,0:T(8,128)(2,1)} custom-call(s32[2]{0:T(128)} %pad_add_fusion.3.base_ref, bf16[2560,1024]{1,0:T(8,128)(2,1)} %pad.29.table_ref, bf16[2048,1024]{1,0:T(8,128)(2,1)} %all-gather.5.cloned.1.call-done.rows_ref.refs_0_, f32[4,2048]{1,0:T(4,128)} %copy-done.41, bf16[6144,1024]{1,0:T(8,128)(2,1)} %all-gather.7.cloned.1.call-done.refs_2_, ...), custom_call_target="tpu_custom_call" | custom-call | flops 21474836480 | bytes 18087936 | tf_op jit(solution)/shard_map/head_grad/pallas_call | solution.py:344
  841.4 9.6 collective-permute-done.43
  853.9 10.4 collective-permute-start.18
  873.8 8.2 collective-permute-start.19
  883.7 19.5 %collective-permute-done.46 = bf16[640,1024]{1,0:T(8,128)(2,1)S(1)} collective-permute-done((bf16[640,1024]{1,0:T(8,128)(2,1)}, bf16[640,1024]{1,0:T(8,128)(2,1)S(1)}, u32[]{:S(2)}, u32[]{:S(2)}) %collective-permute-start.46) | collective-permute-done | bytes 1310752 | tf_op jit(solution)/shard_map/ppermute | solution.py:622
  905.4 5.3 collective-permute-start.8
  920.5 15.6 %collective-permute-done.11 = bf16[32,4096]{1,0:T(8,128)(2,1)S(1)} collective-permute-done((bf16[32,4096]{1,0:T(8,128)(2,1)S(1)}, bf16[32,4096]{1,0:T(8,128)(2,1)S(1)}, u32[]{:S(2)}, u32[]{:S(2)}) %collective-permute-start.11) | collective-permute-done | bytes 262176 | tf_op jit(solution)/shard_map/ppermute | solution.py:657
  956.0 5.3 slice_convert_fusion
  983.2 48.3 %all-reduce.10.cloned.1.call-done = bf16[128,4480]{0,1:T(8,128)(2,1)} async-done(((bf16[128,4480]{0,1:T(8,128)(2,1)}), bf16[128,4480]{0,1:T(8,128)(2,1)}) %all-reduce.10.cloned.1.call-update) | async-done | bytes 1146896 | tf_op jit(solution)/shard_map/psum | solution.py:1055
  (626 shorter events, 351.5 us)
Async XLA Ops:
  7.2 150.0 %all-gather.5.cloned.1.call-start = ((), (), s32[]{:S(2)}) async-start(), calls=%async_computation.4 | async-start | bytes 4718592 | tf_op jit(solution)/shard_map/all_gather | solution.py:808
  12.6 25.6 %collective-permute-start = (bf16[256,1024]{1,0:T(8,128)(2,1)}, bf16[256,1024]{1,0:T(8,128)(2,1)}, u32[]{:S(2)}, u32[]{:S(2)}) collective-permute-start(bf16[256,1024]{1,0:T(8,128)(2,1)} %add_convert_fusion.5), channel_id=1, source_target_pairs={{0,8},{8,16},{16,24},{1,9},{9,17},{17,25},{2,10},{10,18},{18,26},{... | collective-permute-start | bytes 1572872 | tf_op jit(solution)/shard_map/ppermute | solution.py:618
  44.9 23.3 %collective-permute-start.2 = (bf16[256,1024]{1,0:T(8,128)(2,1)}, bf16[256,1024]{1,0:T(8,128)(2,1)}, u32[]{:S(2)}, u32[]{:S(2)}) collective-permute-start(bf16[256,1024]{1,0:T(8,128)(2,1)} %collective-permute-done.1), channel_id=1, source_target_pairs={{16,24},{17,25},{18,26},{19,27},{20,28},{21,29},{22,30},{23,31}} | collective-permute-start | bytes 1572872 | tf_op jit(solution)/shard_map/ppermute | solution.py:618
  109.4 290.5 %reduce-scatter.7.cloned.1.call-start = ((), (), s32[]{:S(2)}) async-start(), calls=%async_computation.5 | async-start | bytes 5898240 | tf_op jit(solution)/shard_map/reduce_scatter | solution.py:871
  304.3 144.5 %all-gather.9.cloned.1.call-start = ((), (), s32[]{:S(2)}) async-start(), calls=%async_computation.10 | async-start | bytes 3981312 | tf_op jit(solution)/shard_map/all_gather | solution.py:895
  305.4 15.4 %collective-permute-start.48 = (bf16[288,256]{1,0:T(8,128)(2,1)S(1)}, bf16[288,256]{1,0:T(8,128)(2,1)S(1)}, u32[]{:S(2)}, u32[]{:S(2)}) collective-permute-start(bf16[288,256]{1,0:T(8,128)(2,1)S(1)} %constant_dynamic-slice_fusion), channel_id=1, source_target_pairs={{8,0},{16,8},{24,16},{9,1},{17,9},{25,17},{10,2},{18,10},{26,18},{... | collective-permute-start | bytes 442376 | tf_op jit(solution)/shard_map/ppermute | solution.py:622
  306.7 15.4 %collective-permute-start.49 = (bf16[288,256]{1,0:T(8,128)(2,1)S(1)}, bf16[288,256]{1,0:T(8,128)(2,1)S(1)}, u32[]{:S(2)}, u32[]{:S(2)}) collective-permute-start(bf16[288,256]{1,0:T(8,128)(2,1)S(1)} %constant_dynamic-slice_fusion), channel_id=1, source_target_pairs={{0,8},{8,16},{16,24},{1,9},{9,17},{17,25},{2,10},{10,18},{18,26},{... | collective-permute-start | bytes 442376 | tf_op jit(solution)/shard_map/ppermute | solution.py:618
  336.1 457.0 %all-gather.7.cloned.1.call-start = ((), (), s32[]{:S(2)}) async-start(), calls=%async_computation.9 | async-start | bytes 14155776 | tf_op jit(solution)/shard_map/all_gather | solution.py:893
  336.2 13.5 %collective-permute-start.30 = (bf16[256,1024]{1,0:T(8,128)(2,1)S(1)}, bf16[256,1024]{1,0:T(8,128)(2,1)S(1)}, u32[]{:S(2)}, u32[]{:S(2)}) collective-permute-start(bf16[256,1024]{1,0:T(8,128)(2,1)S(1)} %copy-done.5), channel_id=1, source_target_pairs={{8,0},{16,8},{24,16},{9,1},{17,9},{25,17},{10,2},{18,10},{26,18},{... | collective-permute-start | bytes 1572872 | tf_op jit(solution)/shard_map/ppermute | solution.py:622
  337.5 13.5 %collective-permute-start.31 = (bf16[256,1024]{1,0:T(8,128)(2,1)S(1)}, bf16[256,1024]{1,0:T(8,128)(2,1)S(1)}, u32[]{:S(2)}, u32[]{:S(2)}) collective-permute-start(bf16[256,1024]{1,0:T(8,128)(2,1)S(1)} %copy-done.5), channel_id=1, source_target_pairs={{0,8},{8,16},{16,24},{1,9},{9,17},{17,25},{2,10},{10,18},{18,26},{... | collective-permute-start | bytes 1572872 | tf_op jit(solution)/shard_map/ppermute | solution.py:618
  349.8 12.7 %collective-permute-start.34 = (bf16[256,1024]{1,0:T(8,128)(2,1)S(1)}, bf16[256,1024]{1,0:T(8,128)(2,1)S(1)}, u32[]{:S(2)}, u32[]{:S(2)}) collective-permute-start(bf16[256,1024]{1,0:T(8,128)(2,1)S(1)} %collective-permute-done.30), channel_id=1, source_target_pairs={{8,0},{16,8},{9,1},{17,9},{10,2},{18,10},{11,3},{19,11},{12,4},{20... | collective-permute-start | bytes 1572872 | tf_op jit(solution)/shard_map/ppermute | solution.py:622
  375.7 460.5 %reduce-scatter.9.cloned.1.call-start = ((), (), s32[]{:S(2)}) async-start(), calls=%async_computation.7 | async-start | bytes 9437184 | tf_op jit(solution)/shard_map/reduce_scatter | solution.py:986
  398.3 23.7 %collective-permute-start.41 = (f32[4,4352]{1,0:T(4,128)S(1)}, f32[4,4352]{1,0:T(4,128)}, u32[]{:S(2)}, u32[]{:S(2)}) collective-permute-start(f32[4,4352]{1,0:T(4,128)S(1)} %collective-permute-done.40), channel_id=1, source_target_pairs={{8,0},{9,1},{10,2},{11,3},{12,4},{13,5},{14,6},{15,7}} | collective-permute-start | bytes 208904 | tf_op jit(solution)/shard_map/ppermute | solution.py:622
  421.9 430.8 %reduce-scatter.11.cloned.1.call-start = ((), (), s32[]{:S(2)}) async-start(), calls=%async_computation.8 | async-start | bytes 9437184 | tf_op jit(solution)/shard_map/reduce_scatter | solution.py:980
  516.9 60.1 %collective-permute-start.60 = (bf16[6656,64]{0,1:T(8,128)(2,1)}, bf16[6656,64]{0,1:T(8,128)(2,1)}, u32[]{:S(2)}, u32[]{:S(2)}) collective-permute-start(bf16[6656,64]{0,1:T(8,128)(2,1)} %copy.158), channel_id=1, source_target_pairs={{8,0},{16,8},{24,16},{9,1},{17,9},{25,17},{10,2},{18,10},{26,18},{... | collective-permute-start | bytes 2555912 | tf_op jit(solution)/shard_map/ppermute | solution.py:622
  518.2 60.2 %collective-permute-start.61 = (bf16[6656,64]{0,1:T(8,128)(2,1)}, bf16[6656,64]{0,1:T(8,128)(2,1)}, u32[]{:S(2)}, u32[]{:S(2)}) collective-permute-start(bf16[6656,64]{0,1:T(8,128)(2,1)} %copy.158), channel_id=1, source_target_pairs={{0,8},{8,16},{16,24},{1,9},{9,17},{17,25},{2,10},{10,18},{18,26},{... | collective-permute-start | bytes 2555912 | tf_op jit(solution)/shard_map/ppermute | solution.py:618
  534.6 39.5 %collective-permute-start.55 = (bf16[1280,256]{1,0:T(8,128)(2,1)}, bf16[1280,256]{1,0:T(8,128)(2,1)}, u32[]{:S(2)}, u32[]{:S(2)}) collective-permute-start(bf16[1280,256]{1,0:T(8,128)(2,1)} %band_grad.2), channel_id=1, source_target_pairs={{0,8},{8,16},{16,24},{1,9},{9,17},{17,25},{2,10},{10,18},{18,26},{... | collective-permute-start | bytes 1966088 | tf_op jit(solution)/shard_map/ppermute | solution.py:618
  538.5 37.3 %collective-permute-start.54 = (bf16[1280,256]{1,0:T(8,128)(2,1)}, bf16[1280,256]{1,0:T(8,128)(2,1)}, u32[]{:S(2)}, u32[]{:S(2)}) collective-permute-start(bf16[1280,256]{1,0:T(8,128)(2,1)} %band_grad.2), channel_id=1, source_target_pairs={{8,0},{16,8},{24,16},{9,1},{17,9},{25,17},{10,2},{18,10},{26,18},{... | collective-permute-start | bytes 1966088 | tf_op jit(solution)/shard_map/ppermute | solution.py:622
  574.1 81.9 %collective-permute-start.56 = (bf16[1280,256]{1,0:T(8,128)(2,1)}, bf16[1280,256]{1,0:T(8,128)(2,1)}, u32[]{:S(2)}, u32[]{:S(2)}) collective-permute-start(bf16[1280,256]{1,0:T(8,128)(2,1)} %collective-permute-done.55), channel_id=1, source_target_pairs={{8,16},{16,24},{9,17},{17,25},{10,18},{18,26},{11,19},{19,27},{12,... | collective-permute-start | bytes 1966088 | tf_op jit(solution)/shard_map/ppermute | solution.py:618
  575.7 81.0 %collective-permute-start.58 = (bf16[1280,256]{1,0:T(8,128)(2,1)}, bf16[1280,256]{1,0:T(8,128)(2,1)}, u32[]{:S(2)}, u32[]{:S(2)}) collective-permute-start(bf16[1280,256]{1,0:T(8,128)(2,1)} %collective-permute-done.54), channel_id=1, source_target_pairs={{8,0},{16,8},{9,1},{17,9},{10,2},{18,10},{11,3},{19,11},{12,4},{20... | collective-permute-start | bytes 1966088 | tf_op jit(solution)/shard_map/ppermute | solution.py:622
  577.0 81.0 %collective-permute-start.64 = (bf16[6656,64]{0,1:T(8,128)(2,1)}, bf16[6656,64]{0,1:T(8,128)(2,1)}, u32[]{:S(2)}, u32[]{:S(2)}) collective-permute-start(bf16[6656,64]{0,1:T(8,128)(2,1)} %collective-permute-done.60), channel_id=1, source_target_pairs={{8,0},{16,8},{9,1},{17,9},{10,2},{18,10},{11,3},{19,11},{12,4},{20... | collective-permute-start | bytes 2555912 | tf_op jit(solution)/shard_map/ppermute | solution.py:622
  578.4 79.7 %collective-permute-start.62 = (bf16[6656,64]{0,1:T(8,128)(2,1)}, bf16[6656,64]{0,1:T(8,128)(2,1)}, u32[]{:S(2)}, u32[]{:S(2)}) collective-permute-start(bf16[6656,64]{0,1:T(8,128)(2,1)} %collective-permute-done.61), channel_id=1, source_target_pairs={{8,16},{16,24},{9,17},{17,25},{10,18},{18,26},{11,19},{19,27},{12,... | collective-permute-start | bytes 2555912 | tf_op jit(solution)/shard_map/ppermute | solution.py:618
  632.3 344.1 %reduce-scatter.13.cloned.1.call-start = ((), (), s32[]{:S(2)}) async-start(), calls=%async_computation.11 | async-start | bytes 10321920
  646.9 17.0 %collective-permute-start.3 = (bf16[256,1024]{1,0:T(8,128)(2,1)S(1)}, bf16[256,1024]{1,0:T(8,128)(2,1)S(1)}, u32[]{:S(2)}, u32[]{:S(2)}) collective-permute-start(bf16[256,1024]{1,0:T(8,128)(2,1)S(1)} %dynamic-slice_bitcast_fusion), channel_id=1, source_target_pairs={{24,16},{25,17},{26,18},{27,19},{28,20},{29,21},{30,22},{31,23}} | collective-permute-start | bytes 1572872 | tf_op jit(solution)/shard_map/ppermute | solution.py:657
  656.8 27.8 %collective-permute-start.59 = (bf16[1280,256]{1,0:T(8,128)(2,1)}, bf16[1280,256]{1,0:T(8,128)(2,1)S(1)}, u32[]{:S(2)}, u32[]{:S(2)}) collective-permute-start(bf16[1280,256]{1,0:T(8,128)(2,1)} %collective-permute-done.58), channel_id=1, source_target_pairs={{8,0},{9,1},{10,2},{11,3},{12,4},{13,5},{14,6},{15,7}} | collective-permute-start | bytes 1966088 | tf_op jit(solution)/shard_map/ppermute | solution.py:622
  661.9 38.2 %collective-permute-start.65 = (bf16[6656,64]{0,1:T(8,128)(2,1)}, bf16[6656,64]{0,1:T(8,128)(2,1)S(1)}, u32[]{:S(2)}, u32[]{:S(2)}) collective-permute-start(bf16[6656,64]{0,1:T(8,128)(2,1)} %collective-permute-done.64), channel_id=1, source_target_pairs={{8,0},{9,1},{10,2},{11,3},{12,4},{13,5},{14,6},{15,7}} | collective-permute-start | bytes 2555912 | tf_op jit(solution)/shard_map/ppermute | solution.py:622
  663.1 37.0 %collective-permute-start.63 = (bf16[6656,64]{0,1:T(8,128)(2,1)}, bf16[6656,64]{0,1:T(8,128)(2,1)S(1)}, u32[]{:S(2)}, u32[]{:S(2)}) collective-permute-start(bf16[6656,64]{0,1:T(8,128)(2,1)} %collective-permute-done.62), channel_id=1, source_target_pairs={{16,24},{17,25},{18,26},{19,27},{20,28},{21,29},{22,30},{23,31}} | collective-permute-start | bytes 2555912 | tf_op jit(solution)/shard_map/ppermute | solution.py:618
  664.1 25.9 %collective-permute-start.4 = (bf16[256,1024]{1,0:T(8,128)(2,1)S(1)}, bf16[256,1024]{1,0:T(8,128)(2,1)S(1)}, u32[]{:S(2)}, u32[]{:S(2)}) collective-permute-start(bf16[256,1024]{1,0:T(8,128)(2,1)S(1)} %fusion.22), channel_id=1, source_target_pairs={{16,8},{24,16},{17,9},{25,17},{18,10},{26,18},{19,11},{27,19},{20,... | collective-permute-start | bytes 1572872 | tf_op jit(solution)/shard_map/ppermute | solution.py:657
  691.0 80.7 %collective-permute-start.5 = (bf16[256,1024]{1,0:T(8,128)(2,1)}, bf16[256,1024]{1,0:T(8,128)(2,1)}, u32[]{:S(2)}, u32[]{:S(2)}) collective-permute-start(bf16[256,1024]{1,0:T(8,128)(2,1)} %fusion.23), channel_id=1, source_target_pairs={{8,0},{16,8},{24,16},{9,1},{17,9},{25,17},{10,2},{18,10},{26,18},{... | collective-permute-start | bytes 1572872 | tf_op jit(solution)/shard_map/ppermute | solution.py:657
  793.0 238.4 %all-reduce.10.cloned.1.call-start = ((), (), s32[]{:S(2)}) async-start(), calls=%async_computation.6 | async-start | bytes 2293760 | tf_op jit(solution)/shard_map/psum | solution.py:1055
  827.0 23.9 %collective-permute-start.43 = (bf16[640,1024]{1,0:T(8,128)(2,1)}, bf16[640,1024]{1,0:T(8,128)(2,1)}, u32[]{:S(2)}, u32[]{:S(2)}) collective-permute-start(bf16[640,1024]{1,0:T(8,128)(2,1)} %head_grad.1), channel_id=1, source_target_pairs={{0,8},{8,16},{16,24},{1,9},{9,17},{17,25},{2,10},{10,18},{18,26},{... | collective-permute-start | bytes 3932168 | tf_op jit(solution)/shard_map/ppermute | solution.py:618
  838.1 26.9 %collective-permute-start.6 = (bf16[32,4096]{1,0:T(8,128)(2,1)}, bf16[32,4096]{1,0:T(8,128)(2,1)}, u32[]{:S(2)}, u32[]{:S(2)}) collective-permute-start(bf16[32,4096]{1,0:T(8,128)(2,1)} %get-tuple-element.259), channel_id=1, source_target_pairs={{0,8},{1,9},{2,10},{3,11},{4,12},{5,13},{6,14},{7,15}} | collective-permute-start | bytes 786440 | tf_op jit(solution)/shard_map/ppermute | solution.py:655
  840.1 30.9 %collective-permute-start.42 = (bf16[640,1024]{1,0:T(8,128)(2,1)}, bf16[640,1024]{1,0:T(8,128)(2,1)}, u32[]{:S(2)}, u32[]{:S(2)}) collective-permute-start(bf16[640,1024]{1,0:T(8,128)(2,1)} %head_grad.1), channel_id=1, source_target_pairs={{8,0},{16,8},{24,16},{9,1},{17,9},{25,17},{10,2},{18,10},{26,18},{... | collective-permute-start | bytes 3932168 | tf_op jit(solution)/shard_map/ppermute | solution.py:622
  851.0 21.3 %collective-permute-start.44 = (bf16[640,1024]{1,0:T(8,128)(2,1)}, bf16[640,1024]{1,0:T(8,128)(2,1)}, u32[]{:S(2)}, u32[]{:S(2)}) collective-permute-start(bf16[640,1024]{1,0:T(8,128)(2,1)} %collective-permute-done.43), channel_id=1, source_target_pairs={{8,16},{16,24},{9,17},{17,25},{10,18},{18,26},{11,19},{19,27},{12,... | collective-permute-start | bytes 3932168 | tf_op jit(solution)/shard_map/ppermute | solution.py:618
  853.9 19.1 %collective-permute-start.18 = (bf16[128,1024]{1,0:T(8,128)(2,1)S(1)}, bf16[128,1024]{1,0:T(8,128)(2,1)S(1)}, u32[]{:S(2)}, u32[]{:S(2)}) collective-permute-start(bf16[128,1024]{1,0:T(8,128)(2,1)S(1)} %get-tuple-element.255), channel_id=1, source_target_pairs={{0,8},{1,9},{2,10},{3,11},{4,12},{5,13},{6,14},{7,15}} | collective-permute-start | bytes 786440 | tf_op jit(solution)/shard_map/ppermute | solution.py:655
  866.1 15.9 %collective-permute-start.7 = (bf16[32,4096]{1,0:T(8,128)(2,1)S(1)}, bf16[32,4096]{1,0:T(8,128)(2,1)S(1)}, u32[]{:S(2)}, u32[]{:S(2)}) collective-permute-start(bf16[32,4096]{1,0:T(8,128)(2,1)S(1)} %fusion.43), channel_id=1, source_target_pairs={{0,8},{8,16},{1,9},{9,17},{2,10},{10,18},{3,11},{11,19},{4,12},{12... | collective-permute-start | bytes 786440 | tf_op jit(solution)/shard_map/ppermute | solution.py:655
  871.0 32.2 %collective-permute-start.46 = (bf16[640,1024]{1,0:T(8,128)(2,1)}, bf16[640,1024]{1,0:T(8,128)(2,1)S(1)}, u32[]{:S(2)}, u32[]{:S(2)}) collective-permute-start(bf16[640,1024]{1,0:T(8,128)(2,1)} %collective-permute-done.42), channel_id=1, source_target_pairs={{8,0},{16,8},{9,1},{17,9},{10,2},{18,10},{11,3},{19,11},{12,4},{20... | collective-permute-start | bytes 3932168 | tf_op jit(solution)/shard_map/ppermute | solution.py:622
  872.3 39.7 %collective-permute-start.45 = (bf16[640,1024]{1,0:T(8,128)(2,1)}, bf16[640,1024]{1,0:T(8,128)(2,1)S(1)}, u32[]{:S(2)}, u32[]{:S(2)}) collective-permute-start(bf16[640,1024]{1,0:T(8,128)(2,1)} %collective-permute-done.44), channel_id=1, source_target_pairs={{16,24},{17,25},{18,26},{19,27},{20,28},{21,29},{22,30},{23,31}} | collective-permute-start | bytes 3932168 | tf_op jit(solution)/shard_map/ppermute | solution.py:618
  873.0 31.4 %collective-permute-start.21 = (bf16[128,1024]{1,0:T(8,128)(2,1)S(1)}, bf16[128,1024]{1,0:T(8,128)(2,1)S(1)}, u32[]{:S(2)}, u32[]{:S(2)}) collective-permute-start(bf16[128,1024]{1,0:T(8,128)(2,1)S(1)} %get-tuple-element.256), channel_id=1, source_target_pairs={{24,16},{25,17},{26,18},{27,19},{28,20},{29,21},{30,22},{31,23}} | collective-permute-start | bytes 786440 | tf_op jit(solution)/shard_map/ppermute | solution.py:657
  873.8 30.6 %collective-permute-start.19 = (bf16[128,1024]{1,0:T(8,128)(2,1)S(1)}, bf16[128,1024]{1,0:T(8,128)(2,1)S(1)}, u32[]{:S(2)}, u32[]{:S(2)}) collective-permute-start(bf16[128,1024]{1,0:T(8,128)(2,1)S(1)} %fusion.37), channel_id=1, source_target_pairs={{0,8},{8,16},{1,9},{9,17},{2,10},{10,18},{3,11},{11,19},{4,12},{12... | collective-permute-start | bytes 786440 | tf_op jit(solution)/shard_map/ppermute | solution.py:655
  882.2 28.5 %collective-permute-start.10 = (bf16[32,4096]{1,0:T(8,128)(2,1)S(1)}, bf16[32,4096]{1,0:T(8,128)(2,1)S(1)}, u32[]{:S(2)}, u32[]{:S(2)}) collective-permute-start(bf16[32,4096]{1,0:T(8,128)(2,1)S(1)} %get-tuple-element.258), channel_id=1, source_target_pairs={{16,8},{24,16},{17,9},{25,17},{18,10},{26,18},{19,11},{27,19},{20,... | collective-permute-start | bytes 786440 | tf_op jit(solution)/shard_map/ppermute | solution.py:657
  903.1 43.1 %collective-permute-start.47 = (bf16[640,1024]{1,0:T(8,128)(2,1)S(1)}, bf16[640,1024]{1,0:T(8,128)(2,1)S(1)}, u32[]{:S(2)}, u32[]{:S(2)}) collective-permute-start(bf16[640,1024]{1,0:T(8,128)(2,1)S(1)} %collective-permute-done.46), channel_id=1, source_target_pairs={{8,0},{9,1},{10,2},{11,3},{12,4},{13,5},{14,6},{15,7}} | collective-permute-start | bytes 3932168 | tf_op jit(solution)/shard_map/ppermute | solution.py:622
  904.7 14.4 %collective-permute-start.22 = (bf16[128,1024]{1,0:T(8,128)(2,1)S(1)}, bf16[128,1024]{1,0:T(8,128)(2,1)S(1)}, u32[]{:S(2)}, u32[]{:S(2)}) collective-permute-start(bf16[128,1024]{1,0:T(8,128)(2,1)S(1)} %get-tuple-element.254), channel_id=1, source_target_pairs={{16,8},{24,16},{17,9},{25,17},{18,10},{26,18},{19,11},{27,19},{20,... | collective-permute-start | bytes 786440 | tf_op jit(solution)/shard_map/ppermute | solution.py:657
  905.4 15.1 %collective-permute-start.8 = (bf16[32,4096]{1,0:T(8,128)(2,1)S(1)}, bf16[32,4096]{1,0:T(8,128)(2,1)S(1)}, u32[]{:S(2)}, u32[]{:S(2)}) collective-permute-start(bf16[32,4096]{1,0:T(8,128)(2,1)S(1)} %get-tuple-element.257), channel_id=1, source_target_pairs={{0,8},{8,16},{16,24},{1,9},{9,17},{17,25},{2,10},{10,18},{18,26},{... | collective-permute-start | bytes 786440 | tf_op jit(solution)/shard_map/ppermute | solution.py:655
  910.7 25.4 %collective-permute-start.11 = (bf16[32,4096]{1,0:T(8,128)(2,1)S(1)}, bf16[32,4096]{1,0:T(8,128)(2,1)S(1)}, u32[]{:S(2)}, u32[]{:S(2)}) collective-permute-start(bf16[32,4096]{1,0:T(8,128)(2,1)S(1)} %fusion.42), channel_id=1, source_target_pairs={{8,0},{16,8},{24,16},{9,1},{17,9},{25,17},{10,2},{18,10},{26,18},{... | collective-permute-start | bytes 786440 | tf_op jit(solution)/shard_map/ppermute | solution.py:657
  913.9 26.1 %collective-permute-start.20 = (bf16[128,1024]{1,0:T(8,128)(2,1)S(1)}, bf16[128,1024]{1,0:T(8,128)(2,1)S(1)}, u32[]{:S(2)}, u32[]{:S(2)}) collective-permute-start(bf16[128,1024]{1,0:T(8,128)(2,1)S(1)} %get-tuple-element.253), channel_id=1, source_target_pairs={{0,8},{8,16},{16,24},{1,9},{9,17},{17,25},{2,10},{10,18},{18,26},{... | collective-permute-start | bytes 786440 | tf_op jit(solution)/shard_map/ppermute | solution.py:655
  919.2 22.1 %collective-permute-start.23 = (bf16[128,1024]{1,0:T(8,128)(2,1)S(1)}, bf16[128,1024]{1,0:T(8,128)(2,1)S(1)}, u32[]{:S(2)}, u32[]{:S(2)}) collective-permute-start(bf16[128,1024]{1,0:T(8,128)(2,1)S(1)} %fusion.36), channel_id=1, source_target_pairs={{8,0},{16,8},{24,16},{9,1},{17,9},{25,17},{10,2},{18,10},{26,18},{... | collective-permute-start | bytes 786440 | tf_op jit(solution)/shard_map/ppermute | solution.py:657
  946.9 14.5 %collective-permute-start.26 = (bf16[128,1024]{1,0:T(8,128)(2,1)S(1)}, bf16[128,1024]{1,0:T(8,128)(2,1)S(1)}, u32[]{:S(2)}, u32[]{:S(2)}) collective-permute-start(bf16[128,1024]{1,0:T(8,128)(2,1)S(1)} %collective-permute-done.25), channel_id=1, source_target_pairs={{8,16},{16,24},{9,17},{17,25},{10,18},{18,26},{11,19},{19,27},{12,... | collective-permute-start | bytes 786440 | tf_op jit(solution)/shard_map/ppermute | solution.py:618
  (147 other events, 1569.6 us)
Sparse Core Ops, SparseCore 0:
  109.5 46.4 all-gather.4
  304.4 63.9 reduce-scatter.6
  371.1 33.9 all-gather.8
  407.0 72.1 all-gather.6
  482.9 71.3 reduce-scatter.8
  632.4 78.5 reduce-scatter.10
  793.2 73.7 reduce-scatter.12
  978.9 52.5 all-reduce.9

commit v2 on v1

--- a/solution.py
+++ b/solution.py
@@ -361,7 +361,7 @@
     )(scalars, table, *[value for pair in lists for value in pair])
 
 
-def band_grad_kernel(chunk, most, plan_ref, table_ref, rows_ref, fact_ref, out_ref, sum_ref):
+def band_grad_kernel(chunk, most, across, plan_ref, table_ref, rows_ref, fact_ref, out_ref, sum_ref):
     words = table_ref.shape[0]
     step_id = pl.program_id(0)
     base = plan_ref[most + 1] + step_id * words
@@ -406,7 +406,10 @@
         return unused
 
     lax.fori_loop(0, plan_ref[line], hits, 0)
-    out_ref[...] = sum_ref[:, : out_ref.shape[1]].astype(out_ref.dtype)
+    if across:
+        out_ref[...] = sum_ref[...].T[: out_ref.shape[0], :].astype(out_ref.dtype)
+    else:
+        out_ref[...] = sum_ref[...].astype(out_ref.dtype)
 
 
 def listed(flags):
@@ -417,7 +420,9 @@
     return jnp.concatenate([order[..., -1:], places], -1).astype(jnp.int32)
 
 
-def band_grad(table, rows, facts, active, lowest, highest, part, part_words, first_word, width, chunk):
+def band_grad(
+    table, rows, facts, active, lowest, highest, part, part_words, first_word, chunk, result, across
+):
     count, full = rows.shape[0], table.shape[1]
     word_block = chunk
     steps = part_words // word_block
@@ -435,7 +440,7 @@
     )
     last = plan.shape[0] - 1
     return pl.pallas_call(
-        functools.partial(band_grad_kernel, chunk // 2 if chunk > 832 else chunk, most),
+        functools.partial(band_grad_kernel, chunk // 2 if chunk > 832 else chunk, most, across),
         grid_spec=pltpu.PrefetchScalarGridSpec(
             num_scalar_prefetch=1,
             grid=(steps,),
@@ -444,10 +449,14 @@
                 pl.BlockSpec((count, full), lambda i, s: (0, 0), **ONCE),
                 pl.BlockSpec(facts.shape, lambda i, s: (0, 0), **ONCE),
             ],
-            out_specs=pl.BlockSpec((word_block, width), lambda i, s: (i, 0)),
+            out_specs=(
+                pl.BlockSpec((result.shape[0], word_block), lambda i, s: (0, i))
+                if across
+                else pl.BlockSpec((word_block, full), lambda i, s: (i, 0))
+            ),
             scratch_shapes=[pltpu.VMEM((word_block, full), jnp.float32)],
         ),
-        out_shape=jax.ShapeDtypeStruct((part_words, width), jnp.bfloat16),
+        out_shape=result,
         compiler_params=pltpu.CompilerParams(vmem_limit_bytes=VMEM_BYTES),
         cost_estimate=pl.CostEstimate(
             flops=2 * count * part_words * 256,
@@ -610,26 +619,35 @@
     )(member.reshape(1).astype(jnp.int32), everyone, facts, head_mix, middle_mix, tail_mix, *hits)
 
 
-def line_pieces(value, both=True):
-    size = lax.axis_size("seq")
+def line_gather(value, direct):
+    size, place = lax.axis_size("seq"), lax.axis_index("seq")
+    if direct:
+        return [value] + [
+            lax.ppermute(value, "seq", [(d, (d - k) % size) for d in range(size)])
+            for k in range(1, size)
+        ]
     before, behind = [value], [value]
     for step in range(1, size):
         before.append(
             lax.ppermute(before[-1], "seq", [(d, d + 1) for d in range(step - 1, size - 1)])
         )
-        if both:
-            behind.append(
-                lax.ppermute(behind[-1], "seq", [(d, d - 1) for d in range(1, size - step + 1)])
-            )
-    return before, behind
-
-
-def line_gather(value):
-    size, place = lax.axis_size("seq"), lax.axis_index("seq")
-    before, behind = line_pieces(value)
+        behind.append(
+            lax.ppermute(behind[-1], "seq", [(d, d - 1) for d in range(1, size - step + 1)])
+        )
     return [value] + [
         jnp.where(place + k < size, behind[k], before[size - k]) for k in range(1, size)
     ]
+
+
+def earlier_joined(value):
+    size, place = lax.axis_size("seq"), lax.axis_index("seq")
+    joined = jnp.zeros((size,) + value.shape, value.dtype)
+    for step in range(size - 1, -1, -1):
+        piece = value
+        if step:
+            piece = lax.ppermute(value, "seq", [(d, d + step) for d in range(size - step)])
+        joined = lax.dynamic_update_index_in_dim(joined, piece, jnp.maximum(place - step, 0), 0)
+    return joined.reshape((-1,) + value.shape[1:])
 
 
 def in_order(pieces):
@@ -640,28 +658,32 @@
     return joined.reshape((-1,) + pieces[0].shape[1:])
 
 
-def line_scatter(values, forward=True):
+def line_scatter(values, behind=True):
     size, place = lax.axis_size("seq"), lax.axis_index("seq")
     parts = values.reshape((size, -1) + values.shape[1:])
 
     def part(index):
-        index = jnp.clip(index, 0, size - 1)
-        return lax.dynamic_index_in_dim(parts, index, 0, False).astype(jnp.float32)
-
-    ahead, back = 0.0, 0.0
-    for step in range(1, size):
-        if forward:
-            sent = lowered(part(place + size - step) + ahead)
-            ahead = lax.ppermute(sent, "seq", [(d, d + 1) for d in range(step)]).astype(jnp.float32)
-        sent = lowered(part(place - size + step) + back)
-        back = lax.ppermute(
-            sent, "seq", [(d, d - 1) for d in range(size - step, size)]
-        ).astype(jnp.float32)
-    return part(place) + ahead + back
+        return lax.dynamic_index_in_dim(parts, lax.rem(index, size), 0, False)
+
+    total = part(place).astype(jnp.float32)
+    for k in range(1, size):
+        pairs = [(d, (d - k) % size) for d in range(0 if behind else k, size)]
+        total = total + lax.ppermute(part(place + size - k), "seq", pairs).astype(jnp.float32)
+    return total
 
 
 def line_sum(values):
-    return in_order(line_gather(lowered(line_scatter(values)))).astype(jnp.float32)
+    return in_order(line_gather(lowered(line_scatter(values)), True)).astype(jnp.float32)
+
+
+def turn_kernel(rows_ref, out_ref):
+    out_ref[...] = rows_ref[...].astype(jnp.float32).T.astype(out_ref.dtype)
+
+
+def turned(rows, kind):
+    return pl.pallas_call(
+        turn_kernel, out_shape=jax.ShapeDtypeStruct(rows.shape[::-1], kind), name="turned"
+    )(rows)
 
 
 def word_pad(rows, biggest, splits):
@@ -714,13 +736,7 @@
     query_start = (place * token_count).reshape(1)
 
     normed_low = lowered(layer_norm(tokens, first_gain, first_shift))
-    earlier, unused = line_pieces(normed_low, False)
-    normed_parts = jnp.zeros((nz,) + normed_low.shape, jnp.bfloat16)
-    for step in range(nz - 1, -1, -1):
-        normed_parts = lax.dynamic_update_index_in_dim(
-            normed_parts, earlier[step], jnp.maximum(place - step, 0), 0
-        )
-    normed_all = normed_parts.reshape(-1, feature_count)
+    normed_all = earlier_joined(normed_low)
     top_score = jnp.max(neighbour_scores[0], -1, keepdims=True)
     exponent = jnp.exp(neighbour_scores[0] - top_score)
     knn_prob = jnp.sum(jnp.where(neighbours[0] == 0, exponent, 0.0), -1) / jnp.sum(exponent, -1)
@@ -770,13 +786,13 @@
     tail_bias = jnp.where(tail_word < jnp.minimum(TAIL_WORDS - member * sizes[2], sizes[2]), 0.0, NEG_FILL)
     tail_pad = jnp.concatenate(
         [
-            jnp.pad(tail_table, ((0, tail_padded - sizes[2]), (0, 0))),
-            jnp.ones((tail_padded, 1), jnp.bfloat16),
-            lowered(tail_bias)[:, None],
-            jnp.zeros((tail_padded, 126 - tail_width), jnp.bfloat16),
+            jnp.pad(tail_table.T, ((0, 0), (0, tail_padded - sizes[2]))),
+            jnp.ones((1, tail_padded), jnp.bfloat16),
+            lowered(tail_bias)[None, :],
+            jnp.zeros((126 - tail_width, tail_padded), jnp.bfloat16),
         ],
-        1,
-    )
+        0,
+    ).T
     locals_ = (
         all_ids - member * sizes[0],
         all_ids - HEAD_WORDS - member * sizes[1],
@@ -806,6 +822,11 @@
     final = mixed + product(hidden_low, outer_weight) + outer_bias
     state_low = lowered(layer_norm(final, final_gain, final_shift))
     all_states = lax.all_gather(state_low, "batch", axis=0, tiled=True)
+    split = 2 * nz * group_count * feature_count <= 24 << 20
+    if split:
+        other_states = jnp.concatenate(line_gather(state_low, True)[1:], 0)
+        all_states, other_states = lax.optimization_barrier((all_states, other_states))
+        other_states = lax.all_gather(other_states, "batch", axis=0, tiled=True)
 
     middle_width = middle_map.shape[1]
     maps = jnp.pad(jnp.concatenate([middle_map, tail_map], 1), ((0, 0), (0, 128 - tail_width)))
@@ -823,12 +844,21 @@
         jnp.pad(slot_full[:, middle_width:], ((0, 0), (0, middle_width - 128))),
         slot_full[:, :middle_width],
     )
+    if split:
+        piece = slot_count // nb
+        slot_piece = lax.dynamic_slice_in_dim(slot_low, member * piece, piece, 0)
+        other_slots = jnp.concatenate(line_gather(slot_piece, True)[1:], 0)
     tail_stats, tail_mix = band_forward(
         tail_span, slot_low, tail_pad, tail_padded, tail_chunk, tail_width, 0.5
     )
     middle_stats, middle_mix = band_forward(
         middle_span, slot_low, middle_pad, sizes[1], middle_chunk, None, 0.25
     )
+    if split:
+        all_states, other_states, other_slots, tail_stats, middle_stats = lax.optimization_barrier(
+            (all_states, other_states, other_slots, tail_stats, middle_stats)
+        )
+        other_slots = lax.all_gather(other_slots, "batch", axis=0, tiled=True)
     head_stats, head_mix = band_forward(
         head_span, all_states, head_pad, sizes[0], head_chunk, None, 1.0
     )
@@ -852,6 +882,10 @@
         ],
         0,
     )
+    if split:
+        stats, other_states, other_slots = lax.optimization_barrier(
+            (stats, other_states, other_slots)
+        )
     everyone = lax.all_gather(stats, "batch")
 
     token_facts = jnp.concatenate(
@@ -875,7 +909,6 @@
 
     loglik = own_part(lines[0])
 
-    split = 2 * nz * group_count * feature_count <= 24 << 20
     kind = jnp.where(slot_middle, 1.0, jnp.where(slot_tail, 2.0, 0.0))
     slot_facts = jnp.stack(
         [
@@ -887,19 +920,13 @@
     )
     head_facts = jnp.concatenate([lines[1:4], jnp.zeros((1, group_count), jnp.float32)], 0)
     if split:
-        piece = slot_count // nb
-        slot_piece = lax.dynamic_slice_in_dim(slot_low, member * piece, piece, 0)
-        other_states = jnp.concatenate(line_gather(state_low)[1:], 0)
-        other_states = lax.all_gather(other_states, "batch", axis=0, tiled=True)
-        other_slots = jnp.concatenate(line_gather(slot_piece)[1:], 0)
-        other_slots = lax.all_gather(other_slots, "batch", axis=0, tiled=True)
         other_slots = (
             other_slots.reshape(nb, nz - 1, piece, middle_width)
             .transpose(1, 0, 2, 3)
             .reshape(-1, middle_width)
         )
         rows_all = jnp.concatenate([slot_low, other_slots], 0)
-        fact_pieces = line_gather(jnp.concatenate([slot_facts, head_facts], 1))
+        fact_pieces = line_gather(jnp.concatenate([slot_facts, head_facts], 1), True)
         facts = jnp.concatenate([value[:, :slot_count] for value in fact_pieces], 1)
         other_facts = (
             jnp.stack([value[:, slot_count:] for value in fact_pieces[1:]], 1)
@@ -921,34 +948,28 @@
     facts = jnp.concatenate(
         [facts[:2], jnp.where(facts[3:4] > 0, facts[2:3], -1e9), jnp.zeros_like(facts[:1])], 0
     )
-    table_parts = [head_part]
-    for band, table, padded, start, width, chunk in (
-        (1, middle_pad, middle_padded, HEAD_WORDS, middle_width, middle_chunk),
-        (2, tail_pad, tail_padded, HEAD_WORDS + MID_WORDS, tail_width, tail_chunk),
-    ):
-        part_words = padded // parts
-        table_parts.append(
-            band_grad(
-                table,
-                rows_all,
-                facts,
-                block_kind == band,
-                lowest,
-                highest,
-                part,
-                part_words,
-                start + member * sizes[band],
-                width,
-                math.gcd(part_words, chunk),
-            )
+    tail_part = band_grad(
+        tail_pad,
+        rows_all,
+        facts,
+        block_kind == 2,
+        lowest,
+        highest,
+        part,
+        tail_padded // parts,
+        HEAD_WORDS + MID_WORDS + member * sizes[2],
+        math.gcd(tail_padded // parts, tail_chunk),
+        jax.ShapeDtypeStruct((tail_width, tail_padded // parts), jnp.bfloat16),
+        True,
+    )
+    if split:
+        head_pieces = line_gather(head_part, True)
+        own_terms, tail_part, head_pieces[1] = lax.optimization_barrier(
+            (own_terms, tail_part, head_pieces[1])
         )
-    if split:
-        table_sums = [in_order(line_gather(value)) for value in table_parts]
+        tail_pieces = line_gather(tail_part[None], True)
     else:
-        table_sums = [lax.psum(value, "seq") for value in table_parts]
-    head_table_grad, middle_table_grad, tail_table_grad = (
-        value[:size].astype(jnp.float32) for value, size in zip(table_sums, sizes)
-    )
+        own_terms, tail_part = lax.optimization_barrier((own_terms, tail_part))
 
     own_middle = own_part(in_middle)
     own_tail = own_part(in_tail)
@@ -994,9 +1015,13 @@
     out_weight_grad = product_tn(attended_low, mixed_low)
     out_bias_grad = jnp.sum(mixed_grad, 0)
     attended_grad = lowered(product_nt(mixed_low, out_weight))
+    if split:
+        attended_grad, head_pieces[-1] = lax.optimization_barrier((attended_grad, head_pieces[-1]))
     query_low, key_low, value_low = attend_back(
         query_start, queries, key_rows, value_rows, attended_grad
     )
+    if split:
+        query_low, *head_pieces = lax.optimization_barrier((query_low, *head_pieces))
     query_weight_grad = product_tn(normed_low, query_low)
     key_weight_grad = product_tn(normed_all, key_low)
     value_weight_grad = product_tn(normed_all, value_low)
@@ -1042,20 +1067,51 @@
         value_weight_grad,
         out_weight_grad,
         middle_map_grad,
-        jnp.concatenate(rows, 0).T,
+        turned(jnp.concatenate(rows, 0), jnp.bfloat16),
     ]
-    rest_part = lax.psum_scatter(
-        jnp.concatenate([lowered(column) for column in columns], 1),
-        "batch",
-        scatter_dimension=0,
-        tiled=True,
-    )
+    rest = jnp.concatenate([lowered(column) for column in columns], 1)
+    rest, facts = lax.optimization_barrier((rest, facts))
+    if split:
+        rest, tail_pieces[1], tail_pieces[-1] = lax.optimization_barrier(
+            (rest, tail_pieces[1], tail_pieces[-1])
+        )
+    rest_part = lax.psum_scatter(rest, "batch", scatter_dimension=0, tiled=True)
+    middle_result = jax.ShapeDtypeStruct(
+        (sizes[1], middle_width) if split else (middle_padded, middle_width),
+        jnp.float32 if split else jnp.bfloat16,
+    )
+    middle_part = band_grad(
+        middle_pad,
+        rows_all,
+        facts,
+        block_kind == 1,
+        lowest,
+        highest,
+        0 * place,
+        middle_padded,
+        HEAD_WORDS + member * sizes[1],
+        middle_chunk,
+        middle_result,
+        False,
+    )
+    if split:
+        middle_table_grad = middle_part
+        head_table_grad = in_order(head_pieces)
+        tail_sum = in_order(tail_pieces)
+        tail_sum = tail_sum.transpose(1, 0, 2).reshape(tail_width, -1)
+    else:
+        middle_table_grad = lax.psum(middle_part, "seq")[: sizes[1]].astype(jnp.float32)
+        head_table_grad = lax.psum(head_part, "seq")
+        tail_sum = lax.psum(tail_part, "seq")
+    head_table_grad = head_table_grad[: sizes[0]].astype(jnp.float32)
+    tail_table_grad = tail_sum[:, : sizes[2]].astype(jnp.float32).T
     outer_sum = line_sum(outer_part)
     inner_sum = line_sum(inner_part)
-    rest_sum = lax.psum(rest_part, "seq").astype(jnp.float32)
+    rest_low = lax.psum(rest_part, "seq")
+    rest_sum = rest_low[:, : 4 * feature_count + middle_width].astype(jnp.float32)
     cut = [rest_sum[:, i * feature_count : (i + 1) * feature_count] for i in range(4)]
     middle_map_sum = rest_sum[:, 4 * feature_count : 4 * feature_count + middle_width]
-    row_sum = rest_sum[:, 4 * feature_count + middle_width :].T
+    row_sum = turned(rest_low[:, 4 * feature_count + middle_width :], jnp.float32)
     tail_map_sum, cluster_sum, inner_bias_sum = (
         row_sum[low:high] for low, high in zip(edges[:3], edges[1:4])
     )

time: 1070 us -> 1010 us (0.944)
  starting transfers between devices: 128 us -> 79.5 us
  waiting for transfers between devices: 182 us -> 224 us
  other arithmetic: 127 us -> 85.8 us
  local copies, waits for them, and re-layouts: 230 us -> 206 us
  Pallas kernels: 255 us -> 274 us
    ppermute x66 -> x33, starting transfers between devices: 128 us -> 79.2 us  [the longest x21 52.7 us: line_gather(): lax.ppermute(value, 'seq', [(d, (d - k) % size) for d in range(size)])]
    ppermute x66 -> x33, waiting for transfers between devices: 134 us -> 176 us  [the longest x21 142 us: line_gather(): lax.ppermute(value, 'seq', [(d, (d - k) % size) for d in range(size)])]
    unnamed x252 -> x163, local copies, waits for them, and re-layouts: 41 us -> 20.7 us
    pallas_call x2, Pallas kernels: 65.7 us -> 82.4 us  [band_grad(): pl.pallas_call(functools.partial(band_grad_kernel, chunk // 2 if chunk >...]
    broadcast_in_dim x10 -> x3, local copies, waits for them, and re-layouts: 14.7 us -> 2.75 us  [the longest x1 2.5 us: on_device(): tail_pieces = line_gather(tail_part[None], True)]
    transpose x0 -> x2, other arithmetic: none -> 11.9 us  [the longest x1 8.65 us: on_device(): tail_pad = jnp.concatenate([jnp.pad(tail_table.T, ((0, 0), (0, tail_padde...]
    concatenate x4 -> x3, other arithmetic: 13.3 us -> 2.12 us  [the longest x1 1.28 us: on_device(): other_states = jnp.concatenate(line_gather(state_low, True)[1:], 0)]
    dynamic_update_slice x6 -> x14, local copies, waits for them, and re-layouts: 83.2 us -> 88.2 us  [in_order(): lax.dynamic_update_index_in_dim(joined, piece, lax.rem(place + k, size), 0)]
  transfers between devices with their start and end apart: 74 -> 41, of which waited for: 22 -> 10; matrix products, arithmetic and copies ran while one was open for 36% -> 32% of each run, Pallas kernels for 12% -> 24%
where the time goes in v2:
time: 1010 us; the launch traced here: 995 us
  Pallas kernels  274 us (27%)
  waiting for transfers between devices  224 us (22%)
  local copies, waits for them, and re-layouts  206 us (20%)
  matrix products  87.1 us (9%)
  other arithmetic  85.8 us (8%)
  starting transfers between devices  79.5 us (8%)
  blocking collectives  20.1 us (2%)
  between operations  18.6 us (2%)
    ppermute x21, waiting for transfers between devices, line_gather(): lax.ppermute(value, 'seq', [(d, (d - k) % size) for d in range(size)])  142 us
    pallas_call x3, Pallas kernels, band_forward(): pl.pallas_call(functools.partial(band_kernel, chunk, per, words, sum_colu...  89.9 us
    dynamic_update_slice x14, local copies, waits for them, and re-layouts, in_order(): lax.dynamic_update_index_in_dim(joined, piece, lax.rem(place + k, size), 0)  88.2 us
    pallas_call x2, Pallas kernels, band_grad(): pl.pallas_call(functools.partial(band_grad_kernel, chunk // 2 if chunk >...  82.4 us
    ppermute x21, starting transfers between devices, line_gather(): lax.ppermute(value, 'seq', [(d, (d - k) % size) for d in range(size)])  52.7 us
    psum x1, waiting for transfers between devices, on_device(): rest_low = lax.psum(rest_part, 'seq')  47.3 us
    gather x3, local copies, waits for them, and re-layouts, on_device(): jnp.take(table, jnp.clip(local, 0, size - 1), axis=0, mode='clip')  34.8 us
    pallas_call x1, Pallas kernels, head_grad(): pl.pallas_call(functools.partial(head_grad_kernel, chunk, len(lists)), gr...  33.7 us
  transfers between devices with their start and end apart: 41, of which 10 were waited for; matrix products, arithmetic and copies ran while one was open for 32% of the time, Pallas kernels for 24%

profile of v2, /device:TPU:0, one launch (start us, length us, event | category | flops | bytes accessed | tf_op | source)
XLA Modules:
  0.0 995.3 jit_solution(1347197925062903780)
XLA Ops:
  13.1 7.9 collective-permute-start
  34.3 9.9 collective-permute-done.1
  45.2 9.0 collective-permute-done.2
  63.0 14.9 %attend.1 = bf16[256,1024]{1,0:T(8,128)(2,1)} custom-call(s32[1]{0:T(128)} %bitcast.2.start_ref, bf16[256,1024]{1,0:T(8,128)(2,1)} %fusion.19.query_ref, bf16[1024,1024]{1,0:T(8,128)(2,1)} %convolution_convert_fusion.2.key_ref, bf16[1024,1024]{1,0:T(8,128)(2,1)} %add_convert_fusion.value_ref), custom_call_target="tpu_custom_call" | custom-call | flops 1073741824 | bytes 5242880 | tf_op jit(solution)/shard_map/attend/pallas_call | solution.py:92
  81.3 6.0 convolution_add_fusion
  93.1 5.5 collective-permute-start.3
  98.6 9.2 collective-permute-start.4
  110.0 8.2 collective-permute-done.3
  118.1 35.6 %collective-permute-done.4 = bf16[256,1024]{1,0:T(8,128)(2,1)S(1)} collective-permute-done((bf16[256,1024]{1,0:T(8,128)(2,1)}, bf16[256,1024]{1,0:T(8,128)(2,1)S(1)}, u32[]{:S(2)}, u32[]{:S(2)}) %collective-permute-start.4) | collective-permute-done | bytes 524320 | tf_op jit(solution)/shard_map/ppermute | solution.py:626
  157.0 9.1 all_gather.20
  170.2 7.4 copy.132
  182.9 5.2 convert_reduce_fusion
  191.4 8.7 fusion.6.table_ref
  203.7 8.6 pick_rows.1
  218.2 47.8 %band_forward.3 = (f32[8,2304]{1,0:T(8,128)}, bf16[2304,128]{1,0:T(8,128)(2,1)}) custom-call(s32[2]{0:T(128)} %pad_add_fusion.2.span_ref, bf16[2304,256]{1,0:T(8,128)(2,1)} %copy-done.18, bf16[26624,128]{1,0:T(8,128)(2,1)} %fusion.6.table_ref), custom_call_target="tpu_custom_call" | custom-call | flops 31406948352 | bytes 8585216 | tf_op jit(solution)/shard_map/band_forward/pallas_call | solution.py:279
  266.0 11.7 %band_forward.4 = (f32[8,2304]{1,0:T(8,128)}, bf16[2304,256]{1,0:T(8,128)(2,1)}) custom-call(s32[2]{0:T(128)} %pad_add_fusion.3.span_ref, bf16[2304,256]{1,0:T(8,128)(2,1)} %copy-done.18, bf16[5120,256]{1,0:T(8,128)(2,1)} %pad.32.table_ref), custom_call_target="tpu_custom_call" | custom-call | flops 3019898880 | bytes 6160384 | tf_op jit(solution)/shard_map/band_forward/pallas_call | solution.py:279
  278.6 5.4 pad.33.table_ref
  284.0 11.9 %gather_fusion.2 = bf16[2048,128]{1,0:T(8,128)(2,1)} fusion(bf16[26624,128]{1,0:T(8,128)(2,1)} %fusion.6.table_ref, s32[2048]{0:T(1024)S(1)} %broadcast_clamp_fusion), kind=kCustom, calls=%fused_computation.2 | custom fusion | bytes 1056768 | tf_op jit(solution)/shard_map/jit(_take)/gather | solution.py:808
  296.0 8.7 gather_fusion.1
  305.0 14.2 %gather_fusion = bf16[2048,1024]{1,0:T(8,128)(2,1)} fusion(bf16[2560,1024]{1,0:T(8,128)(2,1)} %pad.33.table_ref, s32[2048]{0:T(1024)S(1)} %broadcast_clamp_fusion.2), kind=kCustom, calls=%fused_computation | custom fusion | bytes 8396800 | tf_op jit(solution)/shard_map/jit(_take)/gather | solution.py:808
  329.5 30.3 %band_forward.5 = (f32[8,2048]{1,0:T(8,128)}, bf16[2048,1024]{1,0:T(8,128)(2,1)}) custom-call(s32[2]{0:T(128)} %iota_multiply_fusion.span_ref, bf16[2048,1024]{1,0:T(8,128)(2,1)} %all-gather.5.cloned.1.call-done.rows_ref.refs_0_, bf16[2560,1024]{1,0:T(8,128)(2,1)} %pad.33.table_ref), custom_call_target="tpu_custom_call" | custom-call | flops 21474836480 | bytes 17825792 | tf_op jit(solution)/shard_map/band_forward/pallas_call | solution.py:279
  360.7 4.9 multiply_reduce_fusion
  366.6 11.0 %all-gather = f32[64,2304]{1,0:T(8,128)} all-gather(f32[8,2304]{1,0:T(8,128)S(1)} %maximum_maximum_fusion), channel_id=2, replica_groups=mesh['seq'=4,'batch'=8] {'batch'}, dimensions={0}, use_global_device_ids=true | all-gather | bytes 663552 | tf_op jit(solution)/shard_map/all_gather | solution.py:889
  377.6 17.6 %settle.1 = (bf16[2048,1280]{1,0:T(8,128)(2,1)}, f32[8,2048]{1,0:T(8,128)}, f32[16,2304]{1,0:T(8,128)}) custom-call(s32[1]{0:T(128)} %bitcast.member_ref, f32[8,8,2304]{2,1,0:T(8,128)} %bitcast.243, f32[8,2048]{1,0:T(8,128)} %concatenate.61.fact_ref, bf16[2048,1024]{1,0:T(8,128)(2,1)} %get-tuple-element.73.head_mix_ref, ...), custom_call_target="tpu_custom_call" | custom-call | flops 9663676416 | bytes 28114944 | tf_op jit(solution)/shard_map/settle/pallas_call | solution.py:594
  402.5 8.2 pad_maximum_fusion.rows_ref
  415.5 33.7 %head_grad.1 = bf16[640,1024]{1,0:T(8,128)(2,1)} custom-call(s32[2]{0:T(128)} %pad_add_fusion.4.base_ref, bf16[2560,1024]{1,0:T(8,128)(2,1)} %pad.33.table_ref, bf16[2048,1024]{1,0:T(8,128)(2,1)} %all-gather.5.cloned.1.call-done.rows_ref.refs_0_, f32[4,2048]{1,0:T(4,128)} %copy-done.36, bf16[6144,1024]{1,0:T(8,128)(2,1)} %all-gather.7.cloned.1.call-done.refs_2_, ...), custom_call_target="tpu_custom_call" | custom-call | flops 21474836480 | bytes 18087936 | tf_op jit(solution)/shard_map/head_grad/pallas_call | solution.py:344
  456.8 52.7 %band_grad.2 = bf16[64,6656]{1,0:T(8,128)(2,1)} custom-call(s32[187]{0:T(256)} %concatenate.66.plan_ref, bf16[26624,128]{1,0:T(8,128)(2,1)} %fusion.6.table_ref, bf16[9216,256]{1,0:T(8,128)(2,1)} %pad_maximum_fusion.rows_ref, f32[4,9216]{1,0:T(4,128)} %fusion.46.fact_ref), custom_call_target="tpu_custom_call" | custom-call | flops 31406948352 | bytes 5767168 | tf_op jit(solution)/shard_map/band_grad/pallas_call | solution.py:442
  515.3 7.1 convert_reduce_fusion.2
  523.8 5.8 convolution_convert_fusion.1
  529.6 10.2 %convolution_convert_fusion = bf16[4096,1024]{1,0:T(8,128)(2,1)} fusion(f32[256,1024]{1,0:T(8,128)} %copy-done.21, f32[256]{0:T(256)S(1)} %negate_multiply_fusion.2, f32[256,4096]{1,0:T(8,128)} %copy-done.75), kind=kOutput, calls=%fused_computation.12 | convolution fusion | flops 2161639424 | bytes 13632512 | tf_op jit(solution)/shard_map/dot_general | solution.py:47
  549.1 7.2 multiply_reduce_fusion.4
  559.5 17.1 %collective-permute-done.13 = bf16[640,1024]{1,0:T(8,128)(2,1)} collective-permute-done((bf16[640,1024]{1,0:T(8,128)(2,1)}, bf16[640,1024]{1,0:T(8,128)(2,1)}, u32[]{:S(2)}, u32[]{:S(2)}) %collective-permute-start.13) | collective-permute-done | bytes 1310752 | tf_op jit(solution)/shard_map/ppermute | solution.py:626
  576.6 23.9 %attend_back.1 = (bf16[256,1024]{1,0:T(8,128)(2,1)}, bf16[1024,1024]{1,0:T(8,128)(2,1)}, bf16[1024,1024]{1,0:T(8,128)(2,1)}) custom-call(s32[1]{0:T(128)} %bitcast.2.start_ref, bf16[256,1024]{1,0:T(8,128)(2,1)} %fusion.19.query_ref, bf16[1024,1024]{1,0:T(8,128)(2,1)} %convolution_convert_fusion.2.key_ref, bf16[1024,1024]{1,0:T(8,128)(2,1)} %add_convert_fusion.value_ref, ...), custom_call_target="tpu_custom_call" | custom-call | flops 2684354560 | bytes 7864320 | tf_op jit(solution)/shard_map/attend_back/pallas_call | solution.py:141
  600.4 49.3 %collective-permute-done.14 = bf16[640,1024]{1,0:T(8,128)(2,1)} collective-permute-done((bf16[640,1024]{1,0:T(8,128)(2,1)}, bf16[640,1024]{1,0:T(8,128)(2,1)}, u32[]{:S(2)}, u32[]{:S(2)}) %collective-permute-start.14) | collective-permute-done | bytes 1310752 | tf_op jit(solution)/shard_map/ppermute | solution.py:626
  649.7 4.2 fusion.77
  677.0 5.8 slice_convert_fusion
  688.9 20.4 %dynamic_update_slice.85 = bf16[4,64,6656]{2,0,1:T(4,128)(2,1)} dynamic-update-slice(bf16[4,64,6656]{2,0,1:T(4,128)(2,1)} %reshape.719, bf16[1,64,6656]{2,0,1:T(2,128)(2,1)} %copy.146, s32[]{:T(128)S(6)} %select_n.214, s32[]{:T(128)} %constant.242.clone.1, s32[]{:T(128)} %constant.242.clone.1) | dynamic-update-slice | bytes 1703940 | tf_op jit(solution)/shard_map/jit(dynamic_update_index_in_dim)/dynamic_update_slice | solution.py:657
  713.1 4.6 collective-permute-start.32
  717.7 4.4 multiply_reduce_fusion.5
  732.6 29.6 %band_grad.3 = f32[5000,256]{1,0:T(8,128)} custom-call(s32[187]{0:T(256)} %concatenate.72.plan_ref, bf16[5120,256]{1,0:T(8,128)(2,1)} %pad.32.table_ref, bf16[9216,256]{1,0:T(8,128)(2,1)} %pad_maximum_fusion.rows_ref, f32[4,9216]{1,0:T(4,128)} %fusion.46.fact_ref), custom_call_target="tpu_custom_call" | custom-call | flops 24159191040 | bytes 9961472 | tf_op jit(solution)/shard_map/band_grad/pallas_call | solution.py:442
  778.7 20.3 %dynamic_update_slice.86 = bf16[4,64,6656]{2,0,1:T(4,128)(2,1)} dynamic-update-slice(bf16[4,64,6656]{2,0,1:T(4,128)(2,1)} %dynamic_update_slice.85, bf16[1,64,6656]{2,0,1:T(2,128)(2,1)} %copy.147, s32[]{:T(128)S(6)} %select_n.217, s32[]{:T(128)} %constant.242.clone.1, s32[]{:T(128)} %constant.242.clone.1) | dynamic-update-slice | bytes 1703940 | tf_op jit(solution)/shard_map/jit(dynamic_update_index_in_dim)/dynamic_update_slice | solution.py:657
  802.7 20.3 %dynamic_update_slice.87 = bf16[4,64,6656]{2,0,1:T(4,128)(2,1)} dynamic-update-slice(bf16[4,64,6656]{2,0,1:T(4,128)(2,1)} %dynamic_update_slice.86, bf16[1,64,6656]{2,0,1:T(2,128)(2,1)} %copy.148, s32[]{:T(128)S(6)} %select_n.216, s32[]{:T(128)} %constant.242.clone.1, s32[]{:T(128)} %constant.242.clone.1) | dynamic-update-slice | bytes 1703940 | tf_op jit(solution)/shard_map/jit(dynamic_update_index_in_dim)/dynamic_update_slice | solution.py:657
  822.9 20.3 %dynamic_update_slice.88 = bf16[4,64,6656]{2,0,1:T(4,128)(2,1)} dynamic-update-slice(bf16[4,64,6656]{2,0,1:T(4,128)(2,1)} %dynamic_update_slice.87, bf16[1,64,6656]{2,0,1:T(2,128)(2,1)} %copy.149, s32[]{:T(128)S(6)} %select_n.215, s32[]{:T(128)} %constant.242.clone.1, s32[]{:T(128)} %constant.242.clone.1) | dynamic-update-slice | bytes 1703940 | tf_op jit(solution)/shard_map/jit(dynamic_update_index_in_dim)/dynamic_update_slice | solution.py:657
  843.2 4.3 copy.156
  863.1 11.4 %collective-permute-done.27 = bf16[128,1024]{1,0:T(8,128)(2,1)S(1)} collective-permute-done((bf16[128,1024]{1,0:T(8,128)(2,1)S(1)}, bf16[128,1024]{1,0:T(8,128)(2,1)S(1)}, u32[]{:S(2)}, u32[]{:S(2)}) %collective-permute-start.27) | collective-permute-done | bytes 262176 | tf_op jit(solution)/shard_map/ppermute | solution.py:671
  877.3 9.4 collective-permute-start.30
  891.8 31.3 %collective-permute-done.24 = bf16[32,4096]{1,0:T(8,128)(2,1)S(1)} collective-permute-done((bf16[32,4096]{1,0:T(8,128)(2,1)S(1)}, bf16[32,4096]{1,0:T(8,128)(2,1)S(1)}, u32[]{:S(2)}, u32[]{:S(2)}) %collective-permute-start.24) | collective-permute-done | bytes 262176 | tf_op jit(solution)/shard_map/ppermute | solution.py:626
  929.3 47.3 %all-reduce.10.cloned.1.call-done = bf16[128,4480]{1,0:T(8,128)(2,1)} async-done(((bf16[128,4480]{1,0:T(8,128)(2,1)}), bf16[128,4480]{1,0:T(8,128)(2,1)}) %all-reduce.10.cloned.1.call-update) | async-done | bytes 1146896 | tf_op jit(solution)/shard_map/psum | solution.py:1110
  (440 shorter events, 219.2 us)
Async XLA Ops:
  7.2 147.8 %all-gather.5.cloned.1.call-start = ((), (), s32[]{:S(2)}) async-start(), calls=%async_computation.4 | async-start | bytes 4718592 | tf_op jit(solution)/shard_map/all_gather | solution.py:824
  13.1 19.8 %collective-permute-start = (bf16[256,1024]{1,0:T(8,128)(2,1)}, bf16[256,1024]{1,0:T(8,128)(2,1)}, u32[]{:S(2)}, u32[]{:S(2)}) collective-permute-start(bf16[256,1024]{1,0:T(8,128)(2,1)} %add_convert_fusion.5), channel_id=1, source_target_pairs={{0,24},{1,25},{2,26},{3,27},{4,28},{5,29},{6,30},{7,31}} | collective-permute-start | bytes 1572872 | tf_op jit(solution)/shard_map/ppermute | solution.py:648
  21.0 23.2 %collective-permute-start.1 = (bf16[256,1024]{1,0:T(8,128)(2,1)}, bf16[256,1024]{1,0:T(8,128)(2,1)}, u32[]{:S(2)}, u32[]{:S(2)}) collective-permute-start(bf16[256,1024]{1,0:T(8,128)(2,1)} %add_convert_fusion.5), channel_id=1, source_target_pairs={{0,16},{8,24},{1,17},{9,25},{2,18},{10,26},{3,19},{11,27},{4,20},{... | collective-permute-start | bytes 1572872 | tf_op jit(solution)/shard_map/ppermute | solution.py:648
  23.1 31.2 %collective-permute-start.2 = (bf16[256,1024]{1,0:T(8,128)(2,1)}, bf16[256,1024]{1,0:T(8,128)(2,1)}, u32[]{:S(2)}, u32[]{:S(2)}) collective-permute-start(bf16[256,1024]{1,0:T(8,128)(2,1)} %add_convert_fusion.5), channel_id=1, source_target_pairs={{0,8},{8,16},{16,24},{1,9},{9,17},{17,25},{2,10},{10,18},{18,26},{... | collective-permute-start | bytes 1572872 | tf_op jit(solution)/shard_map/ppermute | solution.py:648
  90.4 64.7 %copy-start.69 = (s32[1,256]{1,0:T(1,128)S(1)}, s32[1,256]{1,0:T(1,128)}, u32[]{:S(2)}) copy-start(s32[1,256]{1,0:T(1,128)} %param.30) | copy-start | bytes 3076
  90.4 64.7 %copy-start.20 = (f32[1,256,1024]{2,1,0:T(8,128)S(1)}, f32[1,256,1024]{2,1,0:T(8,128)}, u32[]{:S(2)}) copy-start(f32[1,256,1024]{2,1,0:T(8,128)} %param.32) | copy-start | bytes 3145732
  93.0 63.9 %copy-start.68 = (f32[1,256]{1,0:T(1,128)S(1)}, f32[1,256]{1,0:T(1,128)}, u32[]{:S(2)}) copy-start(f32[1,256]{1,0:T(1,128)} %param.33) | copy-start | bytes 3076
  93.0 76.3 %copy-start.32 = (bf16[1024,64]{0,1:T(8,128)(2,1)S(1)}, bf16[1024,64]{0,1:T(8,128)(2,1)}, u32[]{:S(2)}) copy-start(bf16[1024,64]{0,1:T(8,128)(2,1)} %param.55) | copy-start | bytes 393220
  93.1 185.4 %all-gather.7.cloned.1.call-start = ((), (), s32[]{:S(2)}) async-start(), calls=%async_computation.5 | async-start | bytes 14155776 | tf_op jit(solution)/shard_map/all_gather | solution.py:829
  93.1 25.0 %collective-permute-start.3 = (bf16[256,1024]{1,0:T(8,128)(2,1)}, bf16[256,1024]{1,0:T(8,128)(2,1)S(1)}, u32[]{:S(2)}, u32[]{:S(2)}) collective-permute-start(bf16[256,1024]{1,0:T(8,128)(2,1)} %add_convert_fusion.2), channel_id=1, source_target_pairs={{0,24},{8,0},{16,8},{24,16},{1,25},{9,1},{17,9},{25,17},{2,26},{10... | collective-permute-start | bytes 1572872 | tf_op jit(solution)/shard_map/ppermute | solution.py:626
  98.6 55.2 %collective-permute-start.4 = (bf16[256,1024]{1,0:T(8,128)(2,1)}, bf16[256,1024]{1,0:T(8,128)(2,1)S(1)}, u32[]{:S(2)}, u32[]{:S(2)}) collective-permute-start(bf16[256,1024]{1,0:T(8,128)(2,1)} %add_convert_fusion.2), channel_id=1, source_target_pairs={{0,16},{8,24},{16,0},{24,8},{1,17},{9,25},{17,1},{25,9},{2,18},{10... | collective-permute-start | bytes 1572872 | tf_op jit(solution)/shard_map/ppermute | solution.py:626
  107.8 46.0 %collective-permute-start.5 = (bf16[256,1024]{1,0:T(8,128)(2,1)}, bf16[256,1024]{1,0:T(8,128)(2,1)S(1)}, u32[]{:S(2)}, u32[]{:S(2)}) collective-permute-start(bf16[256,1024]{1,0:T(8,128)(2,1)} %add_convert_fusion.2), channel_id=1, source_target_pairs={{0,8},{8,16},{16,24},{24,0},{1,9},{9,17},{17,25},{25,1},{2,10},{10... | collective-permute-start | bytes 1572872 | tf_op jit(solution)/shard_map/ppermute | solution.py:626
  155.1 211.5 %all-gather.9.cloned.1.call-start = ((), (), s32[]{:S(2)}) async-start(), calls=%async_computation.6 | async-start | bytes 3981312 | tf_op jit(solution)/shard_map/all_gather | solution.py:861
  215.7 62.0 %collective-permute-start.6 = (bf16[288,256]{1,0:T(8,128)(2,1)S(1)}, bf16[288,256]{1,0:T(8,128)(2,1)S(1)}, u32[]{:S(2)}, u32[]{:S(2)}) collective-permute-start(bf16[288,256]{1,0:T(8,128)(2,1)S(1)} %constant_dynamic-slice_fusion.1), channel_id=1, source_target_pairs={{0,24},{8,0},{16,8},{24,16},{1,25},{9,1},{17,9},{25,17},{2,26},{10... | collective-permute-start | bytes 442376 | tf_op jit(solution)/shard_map/ppermute | solution.py:626
  215.7 61.9 %collective-permute-start.7 = (bf16[288,256]{1,0:T(8,128)(2,1)S(1)}, bf16[288,256]{1,0:T(8,128)(2,1)S(1)}, u32[]{:S(2)}, u32[]{:S(2)}) collective-permute-start(bf16[288,256]{1,0:T(8,128)(2,1)S(1)} %constant_dynamic-slice_fusion.1), channel_id=1, source_target_pairs={{0,16},{8,24},{16,0},{24,8},{1,17},{9,25},{17,1},{25,9},{2,18},{10... | collective-permute-start | bytes 442376 | tf_op jit(solution)/shard_map/ppermute | solution.py:626
  215.8 61.9 %collective-permute-start.8 = (bf16[288,256]{1,0:T(8,128)(2,1)S(1)}, bf16[288,256]{1,0:T(8,128)(2,1)S(1)}, u32[]{:S(2)}, u32[]{:S(2)}) collective-permute-start(bf16[288,256]{1,0:T(8,128)(2,1)S(1)} %constant_dynamic-slice_fusion.1), channel_id=1, source_target_pairs={{0,8},{8,16},{16,24},{24,0},{1,9},{9,17},{17,25},{25,1},{2,10},{10... | collective-permute-start | bytes 442376 | tf_op jit(solution)/shard_map/ppermute | solution.py:626
  278.5 231.0 %reduce-scatter.5.cloned.1.call-start = ((), (), s32[]{:S(2)}) async-start(), calls=%async_computation.7 | async-start | bytes 5898240 | tf_op jit(solution)/shard_map/reduce_scatter | solution.py:905
  398.2 13.8 %collective-permute-start.9 = (f32[4,4352]{1,0:T(4,128)S(1)}, f32[4,4352]{1,0:T(4,128)S(1)}, u32[]{:S(2)}, u32[]{:S(2)}) collective-permute-start(f32[4,4352]{1,0:T(4,128)S(1)} %pad_maximum_fusion.4), channel_id=1, source_target_pairs={{0,24},{8,0},{16,8},{24,16},{1,25},{9,1},{17,9},{25,17},{2,26},{10... | collective-permute-start | bytes 208904 | tf_op jit(solution)/shard_map/ppermute | solution.py:626
  398.2 13.8 %collective-permute-start.10 = (f32[4,4352]{1,0:T(4,128)S(1)}, f32[4,4352]{1,0:T(4,128)S(1)}, u32[]{:S(2)}, u32[]{:S(2)}) collective-permute-start(f32[4,4352]{1,0:T(4,128)S(1)} %pad_maximum_fusion.4), channel_id=1, source_target_pairs={{0,16},{8,24},{16,0},{24,8},{1,17},{9,25},{17,1},{25,9},{2,18},{10... | collective-permute-start | bytes 208904 | tf_op jit(solution)/shard_map/ppermute | solution.py:626
  400.3 11.8 %collective-permute-start.11 = (f32[4,4352]{1,0:T(4,128)S(1)}, f32[4,4352]{1,0:T(4,128)S(1)}, u32[]{:S(2)}, u32[]{:S(2)}) collective-permute-start(f32[4,4352]{1,0:T(4,128)S(1)} %pad_maximum_fusion.4), channel_id=1, source_target_pairs={{0,8},{8,16},{16,24},{24,0},{1,9},{9,17},{17,25},{25,1},{2,10},{10... | collective-permute-start | bytes 208904 | tf_op jit(solution)/shard_map/ppermute | solution.py:626
  410.7 351.5 %reduce-scatter.9.cloned.1.call-start = ((), (), s32[]{:S(2)}) async-start(), calls=%async_computation.10 | async-start | bytes 9437184 | tf_op jit(solution)/shard_map/reduce_scatter | solution.py:1007
  449.2 61.7 %collective-permute-start.12 = (bf16[640,1024]{1,0:T(8,128)(2,1)}, bf16[640,1024]{1,0:T(8,128)(2,1)}, u32[]{:S(2)}, u32[]{:S(2)}) collective-permute-start(bf16[640,1024]{1,0:T(8,128)(2,1)} %head_grad.1), channel_id=1, source_target_pairs={{0,24},{8,0},{16,8},{24,16},{1,25},{9,1},{17,9},{25,17},{2,26},{10... | collective-permute-start | bytes 3932168 | tf_op jit(solution)/shard_map/ppermute | solution.py:626
  456.8 55.8 %copy-start.33 = (bf16[1024,64]{0,1:T(8,128)(2,1)S(1)}, bf16[1024,64]{0,1:T(8,128)(2,1)}, u32[]{:S(2)}) copy-start(bf16[1024,64]{0,1:T(8,128)(2,1)} %param.55) | copy-start | bytes 393220
  529.6 317.9 %reduce-scatter.11.cloned.1.call-start = ((), (), s32[]{:S(2)}) async-start(), calls=%async_computation.11 | async-start | bytes 9437184 | tf_op jit(solution)/shard_map/reduce_scatter | solution.py:1001
  539.8 384.9 %reduce-scatter.7.cloned.1.call-start = ((), (), s32[]{:S(2)}) async-start(), calls=%async_computation.8 | async-start | bytes 10321920 | tf_op jit(solution)/shard_map/reduce_scatter | solution.py:1078
  542.7 33.9 %collective-permute-start.13 = (bf16[640,1024]{1,0:T(8,128)(2,1)}, bf16[640,1024]{1,0:T(8,128)(2,1)}, u32[]{:S(2)}, u32[]{:S(2)}) collective-permute-start(bf16[640,1024]{1,0:T(8,128)(2,1)} %head_grad.1), channel_id=1, source_target_pairs={{0,8},{8,16},{16,24},{24,0},{1,9},{9,17},{17,25},{25,1},{2,10},{10... | collective-permute-start | bytes 3932168 | tf_op jit(solution)/shard_map/ppermute | solution.py:626
  542.8 106.9 %collective-permute-start.14 = (bf16[640,1024]{1,0:T(8,128)(2,1)}, bf16[640,1024]{1,0:T(8,128)(2,1)}, u32[]{:S(2)}, u32[]{:S(2)}) collective-permute-start(bf16[640,1024]{1,0:T(8,128)(2,1)} %head_grad.1), channel_id=1, source_target_pairs={{0,16},{8,24},{16,0},{24,8},{1,17},{9,25},{17,1},{25,9},{2,18},{10... | collective-permute-start | bytes 3932168 | tf_op jit(solution)/shard_map/ppermute | solution.py:626
  545.3 187.2 %collective-permute-start.18 = (bf16[1,64,6656]{2,1,0:T(8,128)(2,1)}, bf16[1,64,6656]{2,1,0:T(8,128)(2,1)}, u32[]{:S(2)}, u32[]{:S(2)}) collective-permute-start(bf16[1,64,6656]{2,1,0:T(8,128)(2,1)} %bitcast.239), channel_id=1, source_target_pairs={{0,24},{8,0},{16,8},{24,16},{1,25},{9,1},{17,9},{25,17},{2,26},{10... | collective-permute-start | bytes 2555912 | tf_op jit(solution)/shard_map/ppermute | solution.py:626
  548.4 184.1 %collective-permute-start.19 = (bf16[1,64,6656]{2,1,0:T(8,128)(2,1)}, bf16[1,64,6656]{2,1,0:T(8,128)(2,1)}, u32[]{:S(2)}, u32[]{:S(2)}) collective-permute-start(bf16[1,64,6656]{2,1,0:T(8,128)(2,1)} %bitcast.240), channel_id=1, source_target_pairs={{0,8},{8,16},{16,24},{24,0},{1,9},{9,17},{17,25},{25,1},{2,10},{10... | collective-permute-start | bytes 2555912 | tf_op jit(solution)/shard_map/ppermute | solution.py:626
  557.1 119.2 %copy-start.8 = (f32[256,1024]{1,0:T(8,128)}, f32[256,1024]{1,0:T(8,128)S(1)}, u32[]{:S(2)}) copy-start(f32[256,1024]{1,0:T(8,128)S(1)} %get-tuple-element.125) | copy-start | bytes 3145732
  559.5 90.2 %copy-start.71 = (bf16[1024,1024]{1,0:T(8,128)(2,1)S(1)}, bf16[1024,1024]{1,0:T(8,128)(2,1)}, u32[]{:S(2)}) copy-start(bf16[1024,1024]{1,0:T(8,128)(2,1)} %param.38) | copy-start | bytes 6291460
  659.4 53.7 %collective-permute-start.15 = (bf16[256,1024]{1,0:T(8,128)(2,1)}, bf16[256,1024]{1,0:T(8,128)(2,1)}, u32[]{:S(2)}, u32[]{:S(2)}) collective-permute-start(bf16[256,1024]{1,0:T(8,128)(2,1)} %get-tuple-element.155), channel_id=1, source_target_pairs={{8,0},{16,8},{24,16},{9,1},{17,9},{25,17},{10,2},{18,10},{26,18},{... | collective-permute-start | bytes 1572872 | tf_op jit(solution)/shard_map/ppermute | solution.py:671
  660.8 56.8 %collective-permute-start.16 = (bf16[256,1024]{1,0:T(8,128)(2,1)}, bf16[256,1024]{1,0:T(8,128)(2,1)}, u32[]{:S(2)}, u32[]{:S(2)}) collective-permute-start(bf16[256,1024]{1,0:T(8,128)(2,1)} %get-tuple-element.157), channel_id=1, source_target_pairs={{16,0},{24,8},{17,1},{25,9},{18,2},{26,10},{19,3},{27,11},{20,4},{... | collective-permute-start | bytes 1572872 | tf_op jit(solution)/shard_map/ppermute | solution.py:671
  662.1 55.6 %collective-permute-start.17 = (bf16[256,1024]{1,0:T(8,128)(2,1)}, bf16[256,1024]{1,0:T(8,128)(2,1)}, u32[]{:S(2)}, u32[]{:S(2)}) collective-permute-start(bf16[256,1024]{1,0:T(8,128)(2,1)} %get-tuple-element.156), channel_id=1, source_target_pairs={{24,0},{25,1},{26,2},{27,3},{28,4},{29,5},{30,6},{31,7}} | collective-permute-start | bytes 1572872 | tf_op jit(solution)/shard_map/ppermute | solution.py:671
  713.1 86.0 %collective-permute-start.32 = (bf16[1,64,6656]{2,1,0:T(8,128)(2,1)}, bf16[1,64,6656]{2,1,0:T(8,128)(2,1)}, u32[]{:S(2)}, u32[]{:S(2)}) collective-permute-start(bf16[1,64,6656]{2,1,0:T(8,128)(2,1)} %bitcast.241), channel_id=1, source_target_pairs={{0,16},{8,24},{16,0},{24,8},{1,17},{9,25},{17,1},{25,9},{2,18},{10... | collective-permute-start | bytes 2555912 | tf_op jit(solution)/shard_map/ppermute | solution.py:626
  732.5 244.1 %all-reduce.10.cloned.1.call-start = ((), (), s32[]{:S(2)}) async-start(), calls=%async_computation.9 | async-start | bytes 2293760 | tf_op jit(solution)/shard_map/psum | solution.py:1110
  764.2 88.7 %collective-permute-start.20 = (bf16[32,4096]{1,0:T(8,128)(2,1)}, bf16[32,4096]{1,0:T(8,128)(2,1)}, u32[]{:S(2)}, u32[]{:S(2)}) collective-permute-start(bf16[32,4096]{1,0:T(8,128)(2,1)} %get-tuple-element.162), channel_id=1, source_target_pairs={{0,24},{8,0},{16,8},{24,16},{1,25},{9,1},{17,9},{25,17},{2,26},{10... | collective-permute-start | bytes 786440 | tf_op jit(solution)/shard_map/ppermute | solution.py:671
  766.8 86.7 %collective-permute-start.21 = (bf16[32,4096]{1,0:T(8,128)(2,1)}, bf16[32,4096]{1,0:T(8,128)(2,1)}, u32[]{:S(2)}, u32[]{:S(2)}) collective-permute-start(bf16[32,4096]{1,0:T(8,128)(2,1)} %get-tuple-element.164), channel_id=1, source_target_pairs={{0,16},{8,24},{16,0},{24,8},{1,17},{9,25},{17,1},{25,9},{2,18},{10... | collective-permute-start | bytes 786440 | tf_op jit(solution)/shard_map/ppermute | solution.py:671
  769.0 84.5 %collective-permute-start.22 = (bf16[32,4096]{1,0:T(8,128)(2,1)S(1)}, bf16[32,4096]{1,0:T(8,128)(2,1)}, u32[]{:S(2)}, u32[]{:S(2)}) collective-permute-start(bf16[32,4096]{1,0:T(8,128)(2,1)S(1)} %get-tuple-element.163), channel_id=1, source_target_pairs={{0,8},{8,16},{16,24},{24,0},{1,9},{9,17},{17,25},{25,1},{2,10},{10... | collective-permute-start | bytes 786440 | tf_op jit(solution)/shard_map/ppermute | solution.py:671
  848.8 14.3 %collective-permute-start.26 = (bf16[128,1024]{1,0:T(8,128)(2,1)S(1)}, bf16[128,1024]{1,0:T(8,128)(2,1)S(1)}, u32[]{:S(2)}, u32[]{:S(2)}) collective-permute-start(bf16[128,1024]{1,0:T(8,128)(2,1)S(1)} %get-tuple-element.159), channel_id=1, source_target_pairs={{0,24},{8,0},{16,8},{24,16},{1,25},{9,1},{17,9},{25,17},{2,26},{10... | collective-permute-start | bytes 786440 | tf_op jit(solution)/shard_map/ppermute | solution.py:671
  852.9 21.6 %collective-permute-start.27 = (bf16[128,1024]{1,0:T(8,128)(2,1)S(1)}, bf16[128,1024]{1,0:T(8,128)(2,1)S(1)}, u32[]{:S(2)}, u32[]{:S(2)}) collective-permute-start(bf16[128,1024]{1,0:T(8,128)(2,1)S(1)} %get-tuple-element.161), channel_id=1, source_target_pairs={{0,16},{8,24},{16,0},{24,8},{1,17},{9,25},{17,1},{25,9},{2,18},{10... | collective-permute-start | bytes 786440 | tf_op jit(solution)/shard_map/ppermute | solution.py:671
  852.9 21.6 %collective-permute-start.28 = (bf16[128,1024]{1,0:T(8,128)(2,1)S(1)}, bf16[128,1024]{1,0:T(8,128)(2,1)S(1)}, u32[]{:S(2)}, u32[]{:S(2)}) collective-permute-start(bf16[128,1024]{1,0:T(8,128)(2,1)S(1)} %get-tuple-element.160), channel_id=1, source_target_pairs={{0,8},{8,16},{16,24},{24,0},{1,9},{9,17},{17,25},{25,1},{2,10},{10... | collective-permute-start | bytes 786440 | tf_op jit(solution)/shard_map/ppermute | solution.py:671
  856.7 32.0 %collective-permute-start.23 = (bf16[32,4096]{1,0:T(8,128)(2,1)S(1)}, bf16[32,4096]{1,0:T(8,128)(2,1)S(1)}, u32[]{:S(2)}, u32[]{:S(2)}) collective-permute-start(bf16[32,4096]{1,0:T(8,128)(2,1)S(1)} %get-tuple-element.123), channel_id=1, source_target_pairs={{0,24},{8,0},{16,8},{24,16},{1,25},{9,1},{17,9},{25,17},{2,26},{10... | collective-permute-start | bytes 786440 | tf_op jit(solution)/shard_map/ppermute | solution.py:626
  875.8 48.1 %collective-permute-start.29 = (bf16[128,1024]{1,0:T(8,128)(2,1)S(1)}, bf16[128,1024]{1,0:T(8,128)(2,1)S(1)}, u32[]{:S(2)}, u32[]{:S(2)}) collective-permute-start(bf16[128,1024]{1,0:T(8,128)(2,1)S(1)} %get-tuple-element.121), channel_id=1, source_target_pairs={{0,24},{8,0},{16,8},{24,16},{1,25},{9,1},{17,9},{25,17},{2,26},{10... | collective-permute-start | bytes 786440 | tf_op jit(solution)/shard_map/ppermute | solution.py:626
  877.3 46.6 %collective-permute-start.30 = (bf16[128,1024]{1,0:T(8,128)(2,1)S(1)}, bf16[128,1024]{1,0:T(8,128)(2,1)S(1)}, u32[]{:S(2)}, u32[]{:S(2)}) collective-permute-start(bf16[128,1024]{1,0:T(8,128)(2,1)S(1)} %get-tuple-element.121), channel_id=1, source_target_pairs={{0,16},{8,24},{16,0},{24,8},{1,17},{9,25},{17,1},{25,9},{2,18},{10... | collective-permute-start | bytes 786440 | tf_op jit(solution)/shard_map/ppermute | solution.py:626
  886.7 37.3 %collective-permute-start.31 = (bf16[128,1024]{1,0:T(8,128)(2,1)S(1)}, bf16[128,1024]{1,0:T(8,128)(2,1)S(1)}, u32[]{:S(2)}, u32[]{:S(2)}) collective-permute-start(bf16[128,1024]{1,0:T(8,128)(2,1)S(1)} %get-tuple-element.121), channel_id=1, source_target_pairs={{0,8},{8,16},{16,24},{24,0},{1,9},{9,17},{17,25},{25,1},{2,10},{10... | collective-permute-start | bytes 786440 | tf_op jit(solution)/shard_map/ppermute | solution.py:626
  888.7 34.5 %collective-permute-start.24 = (bf16[32,4096]{1,0:T(8,128)(2,1)S(1)}, bf16[32,4096]{1,0:T(8,128)(2,1)S(1)}, u32[]{:S(2)}, u32[]{:S(2)}) collective-permute-start(bf16[32,4096]{1,0:T(8,128)(2,1)S(1)} %get-tuple-element.123), channel_id=1, source_target_pairs={{0,16},{8,24},{16,0},{24,8},{1,17},{9,25},{17,1},{25,9},{2,18},{10... | collective-permute-start | bytes 786440 | tf_op jit(solution)/shard_map/ppermute | solution.py:626
  888.7 35.3 %collective-permute-start.25 = (bf16[32,4096]{1,0:T(8,128)(2,1)S(1)}, bf16[32,4096]{1,0:T(8,128)(2,1)S(1)}, u32[]{:S(2)}, u32[]{:S(2)}) collective-permute-start(bf16[32,4096]{1,0:T(8,128)(2,1)S(1)} %get-tuple-element.123), channel_id=1, source_target_pairs={{0,8},{8,16},{16,24},{24,0},{1,9},{9,17},{17,25},{25,1},{2,10},{10... | collective-permute-start | bytes 786440 | tf_op jit(solution)/shard_map/ppermute | solution.py:626
  (73 other events, 817.9 us)
Sparse Core Ops, SparseCore 0:
  93.2 48.9 all-gather.4
  155.2 70.3 all-gather.6
  278.6 32.5 all-gather.8
  410.8 55.2 reduce-scatter.4
  529.7 68.9 reduce-scatter.8
  602.1 71.2 reduce-scatter.10
  732.6 74.1 reduce-scatter.6
  924.9 51.6 all-reduce.9

commit v3 on v2

--- a/solution.py
+++ b/solution.py
@@ -619,24 +619,49 @@
     )(member.reshape(1).astype(jnp.int32), everyone, facts, head_mix, middle_mix, tail_mix, *hits)
 
 
-def line_gather(value, direct):
+def line_turns(value):
+    size = lax.axis_size("seq")
+    return [value] + [
+        lax.ppermute(value, "seq", [(d, (d - k) % size) for d in range(size)])
+        for k in range(1, size)
+    ]
+
+
+def line_step(before, behind, step):
+    size = lax.axis_size("seq")
+    return (
+        lax.ppermute(before, "seq", [(d, d + 1) for d in range(step - 1, size - 1)]),
+        lax.ppermute(behind, "seq", [(d, d - 1) for d in range(1, size - step + 1)]),
+    )
+
+
+def line_steps(value):
+    found = [(value, value)]
+
+    def advance(*others):
+        step = len(found)
+        if step == lax.axis_size("seq"):
+            return others
+        moved = line_step(*found[-1], step)
+        moved, others = lax.optimization_barrier((moved, others))
+        found.append(moved)
+        return others
+
+    return found, advance
+
+
+def line_ordered(found, axis):
     size, place = lax.axis_size("seq"), lax.axis_index("seq")
-    if direct:
-        return [value] + [
-            lax.ppermute(value, "seq", [(d, (d - k) % size) for d in range(size)])
-            for k in range(1, size)
-        ]
-    before, behind = [value], [value]
-    for step in range(1, size):
-        before.append(
-            lax.ppermute(before[-1], "seq", [(d, d + 1) for d in range(step - 1, size - 1)])
-        )
-        behind.append(
-            lax.ppermute(behind[-1], "seq", [(d, d - 1) for d in range(1, size - step + 1)])
-        )
-    return [value] + [
-        jnp.where(place + k < size, behind[k], before[size - k]) for k in range(1, size)
-    ]
+    ordered = []
+    for source in range(size):
+        value = found[0][0]
+        for step in range(1, size):
+            if source + step < size:
+                value = jnp.where(place == source + step, found[step][0], value)
+            if source - step >= 0:
+                value = jnp.where(place == source - step, found[step][1], value)
+        ordered.append(value)
+    return jnp.concatenate(ordered, axis)
 
 
 def earlier_joined(value):
@@ -670,10 +695,6 @@
         pairs = [(d, (d - k) % size) for d in range(0 if behind else k, size)]
         total = total + lax.ppermute(part(place + size - k), "seq", pairs).astype(jnp.float32)
     return total
-
-
-def line_sum(values):
-    return in_order(line_gather(lowered(line_scatter(values)), True)).astype(jnp.float32)
 
 
 def turn_kernel(rows_ref, out_ref):
@@ -824,8 +845,12 @@
     all_states = lax.all_gather(state_low, "batch", axis=0, tiled=True)
     split = 2 * nz * group_count * feature_count <= 24 << 20
     if split:
-        other_states = jnp.concatenate(line_gather(state_low, True)[1:], 0)
-        all_states, other_states = lax.optimization_barrier((all_states, other_states))
+        other_states = jnp.concatenate(line_turns(state_low)[1:], 0)
+        all_states, other_states, head_pad, middle_pad, tail_pad, hit_rows, slot, early = (
+            lax.optimization_barrier(
+                (all_states, other_states, head_pad, middle_pad, tail_pad, hit_rows, slot, early)
+            )
+        )
         other_states = lax.all_gather(other_states, "batch", axis=0, tiled=True)
 
     middle_width = middle_map.shape[1]
@@ -847,7 +872,7 @@
     if split:
         piece = slot_count // nb
         slot_piece = lax.dynamic_slice_in_dim(slot_low, member * piece, piece, 0)
-        other_slots = jnp.concatenate(line_gather(slot_piece, True)[1:], 0)
+        other_slots = jnp.concatenate(line_turns(slot_piece)[1:], 0)
     tail_stats, tail_mix = band_forward(
         tail_span, slot_low, tail_pad, tail_padded, tail_chunk, tail_width, 0.5
     )
@@ -926,7 +951,7 @@
             .reshape(-1, middle_width)
         )
         rows_all = jnp.concatenate([slot_low, other_slots], 0)
-        fact_pieces = line_gather(jnp.concatenate([slot_facts, head_facts], 1), True)
+        fact_pieces = line_turns(jnp.concatenate([slot_facts, head_facts], 1))
         facts = jnp.concatenate([value[:, :slot_count] for value in fact_pieces], 1)
         other_facts = (
             jnp.stack([value[:, slot_count:] for value in fact_pieces[1:]], 1)
@@ -963,11 +988,9 @@
         True,
     )
     if split:
-        head_pieces = line_gather(head_part, True)
-        own_terms, tail_part, head_pieces[1] = lax.optimization_barrier(
-            (own_terms, tail_part, head_pieces[1])
-        )
-        tail_pieces = line_gather(tail_part[None], True)
+        head_found, head_advance = line_steps(head_part)
+        own_terms, tail_part = head_advance(own_terms, tail_part)
+        tail_found, tail_advance = line_steps(tail_part)
     else:
         own_terms, tail_part = lax.optimization_barrier((own_terms, tail_part))
 
@@ -1016,12 +1039,14 @@
     out_bias_grad = jnp.sum(mixed_grad, 0)
     attended_grad = lowered(product_nt(mixed_low, out_weight))
     if split:
-        attended_grad, head_pieces[-1] = lax.optimization_barrier((attended_grad, head_pieces[-1]))
+        (attended_grad,) = head_advance(attended_grad)
     query_low, key_low, value_low = attend_back(
         query_start, queries, key_rows, value_rows, attended_grad
     )
     if split:
-        query_low, *head_pieces = lax.optimization_barrier((query_low, *head_pieces))
+        for unused in range(nz - 3):
+            (query_low,) = head_advance(query_low)
+        (query_low,) = tail_advance(query_low)
     query_weight_grad = product_tn(normed_low, query_low)
     key_weight_grad = product_tn(normed_all, key_low)
     value_weight_grad = product_tn(normed_all, value_low)
@@ -1070,11 +1095,9 @@
         turned(jnp.concatenate(rows, 0), jnp.bfloat16),
     ]
     rest = jnp.concatenate([lowered(column) for column in columns], 1)
-    rest, facts = lax.optimization_barrier((rest, facts))
+    rest, facts, inner_part = lax.optimization_barrier((rest, facts, inner_part))
     if split:
-        rest, tail_pieces[1], tail_pieces[-1] = lax.optimization_barrier(
-            (rest, tail_pieces[1], tail_pieces[-1])
-        )
+        rest, facts = tail_advance(rest, facts)
     rest_part = lax.psum_scatter(rest, "batch", scatter_dimension=0, tiled=True)
     middle_result = jax.ShapeDtypeStruct(
         (sizes[1], middle_width) if split else (middle_padded, middle_width),
@@ -1096,17 +1119,27 @@
     )
     if split:
         middle_table_grad = middle_part
-        head_table_grad = in_order(head_pieces)
-        tail_sum = in_order(tail_pieces)
-        tail_sum = tail_sum.transpose(1, 0, 2).reshape(tail_width, -1)
+        for unused in range(nz - 3):
+            (middle_table_grad,) = tail_advance(middle_table_grad)
+        head_table_grad = line_ordered(head_found, 0)
+        tail_sum = line_ordered(tail_found, 1)
     else:
         middle_table_grad = lax.psum(middle_part, "seq")[: sizes[1]].astype(jnp.float32)
         head_table_grad = lax.psum(head_part, "seq")
         tail_sum = lax.psum(tail_part, "seq")
     head_table_grad = head_table_grad[: sizes[0]].astype(jnp.float32)
     tail_table_grad = tail_sum[:, : sizes[2]].astype(jnp.float32).T
-    outer_sum = line_sum(outer_part)
-    inner_sum = line_sum(inner_part)
+    inner_low = lowered(line_scatter(inner_part))
+    inner_low, outer_part, middle_table_grad = lax.optimization_barrier(
+        (inner_low, outer_part, middle_table_grad)
+    )
+    inner_pieces = line_turns(inner_low)
+    outer_low = lowered(line_scatter(outer_part))
+    rest_part, outer_low, inner_pieces = lax.optimization_barrier(
+        (rest_part, outer_low, inner_pieces)
+    )
+    inner_sum = in_order(inner_pieces).astype(jnp.float32)
+    outer_sum = in_order(line_turns(outer_low)).astype(jnp.float32)
     rest_low = lax.psum(rest_part, "seq")
     rest_sum = rest_low[:, : 4 * feature_count + middle_width].astype(jnp.float32)
     cut = [rest_sum[:, i * feature_count : (i + 1) * feature_count] for i in range(4)]

time: 1010 us -> 871 us (0.86)
  local copies, waits for them, and re-layouts: 206 us -> 91.2 us
  waiting for transfers between devices: 224 us -> 172 us
  starting transfers between devices: 79.5 us -> 92.3 us
  other arithmetic: 85.8 us -> 97.4 us
    dynamic_update_slice x14 -> x8, local copies, waits for them, and re-layouts: 88.2 us -> 3.03 us  [in_order(): lax.dynamic_update_index_in_dim(joined, piece, lax.rem(place + k, size), 0)]
    ppermute x21 -> x27, waiting for transfers between devices: 142 us -> 94.3 us  [the longest x15 59.8 us: line_turns(): lax.ppermute(value, 'seq', [(d, (d - k) % size) for d in range(size)])]
    ppermute x9, waiting for transfers between devices: 11.4 us -> 48.9 us  [line_scatter(): lax.ppermute(part(place + size - k), 'seq', pairs).astype(jnp.float32)]
    ppermute x3, waiting for transfers between devices: 23 us -> 0.01 us  [earlier_joined(): lax.ppermute(value, 'seq', [(d, d + step) for d in range(size - step)])]
    psum x1, waiting for transfers between devices: 47.3 us -> 28.7 us  [on_device(): rest_low = lax.psum(rest_part, 'seq')]
    ppermute x9, starting transfers between devices: 14 us -> 31 us  [line_scatter(): lax.ppermute(part(place + size - k), 'seq', pairs).astype(jnp.float32)]
    select_n x0 -> x7, other arithmetic: none -> 13.7 us  [the longest x3 6.68 us: on_device(): jnp.where(own[:, None], jnp.take(table, jnp.clip(local, 0, size - 1), axi...]
    unnamed x163 -> x190, local copies, waits for them, and re-layouts: 20.7 us -> 12.7 us
  transfers between devices with their start and end apart: 41 -> 47, of which waited for: 10 -> 9; matrix products, arithmetic and copies ran while one was open for 32% -> 26% of each run, Pallas kernels for 24% -> 28%
where the time goes in v3:
time: 871 us; the launch traced here: 863 us
  Pallas kernels  277 us (32%)
  waiting for transfers between devices  172 us (20%)
  other arithmetic  97.4 us (11%)
  matrix products  93.6 us (11%)
  starting transfers between devices  92.3 us (11%)
  local copies, waits for them, and re-layouts  91.2 us (10%)
  blocking collectives  20.2 us (2%)
  between operations  19.3 us (2%)
    pallas_call x3, Pallas kernels, band_forward(): pl.pallas_call(functools.partial(band_kernel, chunk, per, words, sum_colu...  88.8 us
    pallas_call x2, Pallas kernels, band_grad(): pl.pallas_call(functools.partial(band_grad_kernel, chunk // 2 if chunk >...  86.3 us
    ppermute x15, waiting for transfers between devices, line_turns(): lax.ppermute(value, 'seq', [(d, (d - k) % size) for d in range(size)])  59.8 us
    ppermute x9, waiting for transfers between devices, line_scatter(): lax.ppermute(part(place + size - k), 'seq', pairs).astype(jnp.float32)  48.9 us
    dot_general x9, matrix products, product_tn(): lax.dot_general(former, latter, (((0,), (0,)), ((), ())), preferred_eleme...  34.8 us
    gather x3, local copies, waits for them, and re-layouts, on_device(): jnp.take(table, jnp.clip(local, 0, size - 1), axis=0, mode='clip')  34.5 us
    ppermute x6, waiting for transfers between devices, line_step(): lax.ppermute(behind, 'seq', [(d, d - 1) for d in range(1, size - step + 1)])  34.5 us
    pallas_call x1, Pallas kernels, head_grad(): pl.pallas_call(functools.partial(head_grad_kernel, chunk, len(lists)), gr...  33.6 us
  transfers between devices with their start and end apart: 47, of which 9 were waited for; matrix products, arithmetic and copies ran while one was open for 26% of the time, Pallas kernels for 28%

profile of v3, /device:TPU:0, one launch (start us, length us, event | category | flops | bytes accessed | tf_op | source)
XLA Modules:
  0.0 862.9 jit_solution(6400951296784566295)
XLA Ops:
  12.6 7.8 collective-permute-start
  27.4 9.1 %all_gather.19 = f32[3,2048]{1,0:T(4,128)S(1)} all-gather(f32[3,256]{1,0:T(4,128)S(1)} %pad_maximum_fusion.13), channel_id=1, replica_groups=mesh['seq'=4,'batch'=8] {'batch'}, dimensions={1}, use_global_device_ids=true | all-gather | bytes 27648 | tf_op jit(solution)/shard_map/all_gather | solution.py:765
  36.6 3.9 select_convert_fusion
  45.1 7.4 copy.114
  52.6 5.4 pad.29.table_ref
  62.0 3.7 convolution_convert_fusion.2.key_ref
  65.7 3.7 add_convert_fusion.value_ref
  69.4 15.1 %attend.1 = bf16[256,1024]{1,0:T(8,128)(2,1)} custom-call(s32[1]{0:T(128)} %bitcast.2.start_ref, bf16[256,1024]{1,0:T(8,128)(2,1)} %fusion.20.query_ref, bf16[1024,1024]{1,0:T(8,128)(2,1)} %convolution_convert_fusion.2.key_ref, bf16[1024,1024]{1,0:T(8,128)(2,1)} %add_convert_fusion.value_ref), custom_call_target="tpu_custom_call" | custom-call | flops 1073741824 | bytes 5242880 | tf_op jit(solution)/shard_map/attend/pallas_call | solution.py:92
  86.9 6.0 convolution_add_fusion
  98.0 11.1 %fusion.6.table_ref = bf16[26624,128]{1,0:T(8,128)(2,1)} fusion(bf16[64,25967]{0,1:T(8,128)(2,1)} %bitcast.209, bf16[1,26624]{0,1:T(8,128)(2,1)} %select_convert_fusion, bf16[128]{0:T(256)(128)(2,1)S(1)} %pad.92.clone, bf16[128]{0:T(256)(128)(2,1)S(1)} %pad.90.clone), kind=kLoop, calls=%fused_computation.17 | loop fusion | flops 34078720 | bytes 10193280 | tf_op jit(solution)/shard_map/transpose | solution.py:816
  109.1 9.9 %gather_fusion.2 = bf16[2048,128]{1,0:T(8,128)(2,1)S(1)} fusion(bf16[26624,128]{1,0:T(8,128)(2,1)} %fusion.6.table_ref, s32[2048]{0:T(1024)S(1)} %broadcast_clamp_fusion), kind=kCustom, calls=%fused_computation.2 | custom fusion | bytes 1056768 | tf_op jit(solution)/shard_map/jit(_take)/gather | solution.py:829
  119.0 14.1 %gather_fusion = bf16[2048,1024]{1,0:T(8,128)(2,1)} fusion(bf16[2560,1024]{1,0:T(8,128)(2,1)} %pad.29.table_ref, s32[2048]{0:T(1024)S(1)} %broadcast_clamp_fusion.2), kind=kCustom, calls=%fused_computation | custom fusion | bytes 8396800 | tf_op jit(solution)/shard_map/jit(_take)/gather | solution.py:829
  133.1 5.2 convert_reduce_fusion
  140.0 4.0 broadcast_select_fusion.head_hit_ref
  144.0 8.0 collective-permute-start.4
  155.9 10.6 %gather_fusion.1 = bf16[2048,256]{1,0:T(8,128)(2,1)} fusion(bf16[5120,256]{1,0:T(8,128)(2,1)} %pad.30.table_ref, s32[2048]{0:T(1024)S(1)} %broadcast_clamp_fusion.1), kind=kCustom, calls=%fused_computation.1 | custom fusion | bytes 2105344 | tf_op jit(solution)/shard_map/jit(_take)/gather | solution.py:829
  168.8 29.1 %collective-permute-done.4 = bf16[256,1024]{1,0:T(8,128)(2,1)} collective-permute-done((bf16[256,1024]{1,0:T(8,128)(2,1)S(1)}, bf16[256,1024]{1,0:T(8,128)(2,1)}, u32[]{:S(2)}, u32[]{:S(2)}) %collective-permute-start.4) | collective-permute-done | bytes 524320 | tf_op jit(solution)/shard_map/ppermute | solution.py:625
  206.3 6.3 add_convert_fusion.1.rows_ref
  212.6 8.6 pick_rows.1
  227.2 48.0 %band_forward.3 = (f32[8,2304]{1,0:T(8,128)}, bf16[2304,128]{1,0:T(8,128)(2,1)}) custom-call(s32[2]{0:T(128)} %pad_add_fusion.2.span_ref, bf16[2304,256]{1,0:T(8,128)(2,1)} %copy-done.14, bf16[26624,128]{1,0:T(8,128)(2,1)} %fusion.6.table_ref), custom_call_target="tpu_custom_call" | custom-call | flops 31406948352 | bytes 8585216 | tf_op jit(solution)/shard_map/band_forward/pallas_call | solution.py:279
  275.2 10.6 %band_forward.4 = (f32[8,2304]{1,0:T(8,128)}, bf16[2304,256]{1,0:T(8,128)(2,1)}) custom-call(s32[2]{0:T(128)} %pad_add_fusion.3.span_ref, bf16[2304,256]{1,0:T(8,128)(2,1)} %copy-done.14, bf16[5120,256]{1,0:T(8,128)(2,1)} %pad.30.table_ref), custom_call_target="tpu_custom_call" | custom-call | flops 3019898880 | bytes 6160384 | tf_op jit(solution)/shard_map/band_forward/pallas_call | solution.py:279
  295.7 30.3 %band_forward.5 = (f32[8,2048]{1,0:T(8,128)}, bf16[2048,1024]{1,0:T(8,128)(2,1)}) custom-call(s32[2]{0:T(128)} %iota_multiply_fusion.span_ref, bf16[2048,1024]{1,0:T(8,128)(2,1)} %all-gather.5.cloned.1.call-done.rows_ref.refs_0_, bf16[2560,1024]{1,0:T(8,128)(2,1)} %pad.29.table_ref), custom_call_target="tpu_custom_call" | custom-call | flops 21474836480 | bytes 17825792 | tf_op jit(solution)/shard_map/band_forward/pallas_call | solution.py:279
  331.2 11.1 %all-gather = f32[64,2304]{1,0:T(8,128)} all-gather(f32[8,2304]{1,0:T(8,128)S(1)} %maximum_maximum_fusion), channel_id=2, replica_groups=mesh['seq'=4,'batch'=8] {'batch'}, dimensions={0}, use_global_device_ids=true | all-gather | bytes 663552 | tf_op jit(solution)/shard_map/all_gather | solution.py:914
  342.3 17.2 %settle.1 = (bf16[2048,1280]{1,0:T(8,128)(2,1)}, f32[8,2048]{1,0:T(8,128)}, f32[16,2304]{1,0:T(8,128)}) custom-call(s32[1]{0:T(128)} %bitcast.member_ref, f32[8,8,2304]{2,1,0:T(8,128)} %bitcast.222, f32[8,2048]{1,0:T(8,128)} %concatenate.67.fact_ref, bf16[2048,1024]{1,0:T(8,128)(2,1)} %get-tuple-element.106.head_mix_ref, ...), custom_call_target="tpu_custom_call" | custom-call | flops 9663676416 | bytes 28114944 | tf_op jit(solution)/shard_map/settle/pallas_call | solution.py:594
  362.5 4.1 collective-permute-start.10
  367.1 8.1 pad_maximum_fusion.3.rows_ref
  379.8 33.6 %head_grad.1 = bf16[640,1024]{1,0:T(8,128)(2,1)} custom-call(s32[2]{0:T(128)} %pad_add_fusion.4.base_ref, bf16[2560,1024]{1,0:T(8,128)(2,1)} %pad.29.table_ref, bf16[2048,1024]{1,0:T(8,128)(2,1)} %all-gather.5.cloned.1.call-done.rows_ref.refs_0_, f32[4,2048]{1,0:T(4,128)} %copy-done.42, bf16[6144,1024]{1,0:T(8,128)(2,1)} %all-gather.7.cloned.1.call-done.refs_2_, ...), custom_call_target="tpu_custom_call" | custom-call | flops 21474836480 | bytes 18087936 | tf_op jit(solution)/shard_map/head_grad/pallas_call | solution.py:344
  424.2 52.7 %band_grad.2 = bf16[64,6656]{1,0:T(8,128)(2,1)} custom-call(s32[187]{0:T(256)} %concatenate.72.plan_ref, bf16[26624,128]{1,0:T(8,128)(2,1)} %fusion.6.table_ref, bf16[9216,256]{1,0:T(8,128)(2,1)} %pad_maximum_fusion.3.rows_ref, f32[4,9216]{1,0:T(4,128)} %fusion.47.fact_ref), custom_call_target="tpu_custom_call" | custom-call | flops 31406948352 | bytes 5767168 | tf_op jit(solution)/shard_map/band_grad/pallas_call | solution.py:442
  482.7 7.1 convert_reduce_fusion.2
  491.2 5.9 convolution_convert_fusion.1
  497.3 9.0 %convolution_convert_fusion = bf16[4096,1024]{1,0:T(8,128)(2,1)} fusion(f32[256,1024]{1,0:T(8,128)} %copy-done.17, f32[256]{0:T(256)S(1)} %negate_multiply_fusion.2, f32[256,4096]{1,0:T(8,128)} %copy-done.89), kind=kOutput, calls=%fused_computation.12 | convolution fusion | flops 2161639424 | bytes 13632512 | tf_op jit(solution)/shard_map/dot_general | solution.py:47
  507.7 6.0 collective-permute-start.14
  517.0 6.7 multiply_reduce_fusion.4
  528.7 34.5 %collective-permute-done.17 = bf16[640,1024]{1,0:T(8,128)(2,1)S(1)} collective-permute-done((bf16[640,1024]{1,0:T(8,128)(2,1)}, bf16[640,1024]{1,0:T(8,128)(2,1)S(1)}, u32[]{:S(2)}, u32[]{:S(2)}) %collective-permute-start.17) | collective-permute-done | bytes 1310752 | tf_op jit(solution)/shard_map/ppermute | solution.py:634
  565.4 24.0 %attend_back.1 = (bf16[256,1024]{1,0:T(8,128)(2,1)}, bf16[1024,1024]{1,0:T(8,128)(2,1)}, bf16[1024,1024]{1,0:T(8,128)(2,1)}) custom-call(s32[1]{0:T(128)} %bitcast.2.start_ref, bf16[256,1024]{1,0:T(8,128)(2,1)} %fusion.20.query_ref, bf16[1024,1024]{1,0:T(8,128)(2,1)} %convolution_convert_fusion.2.key_ref, bf16[1024,1024]{1,0:T(8,128)(2,1)} %add_convert_fusion.value_ref, ...), custom_call_target="tpu_custom_call" | custom-call | flops 2684354560 | bytes 7864320 | tf_op jit(solution)/shard_map/attend_back/pallas_call | solution.py:141
  589.4 5.0 fusion.73
  608.2 3.9 convert_dynamic-update-slice_fusion.2
  612.1 4.0 convert_dynamic-update-slice_fusion.1
  616.6 34.4 %collective-permute-done.21 = bf16[256,1024]{1,0:T(8,128)(2,1)S(1)} collective-permute-done((bf16[256,1024]{1,0:T(8,128)(2,1)S(1)}, bf16[256,1024]{1,0:T(8,128)(2,1)S(1)}, u32[]{:S(2)}, u32[]{:S(2)}) %collective-permute-start.21) | collective-permute-done | bytes 524320 | tf_op jit(solution)/shard_map/ppermute | solution.py:696
  654.0 3.6 concatenate.75.rows_ref
  678.0 4.8 fusion.7
  685.9 5.0 collective-permute-start.26
  690.8 33.6 %band_grad.3 = f32[5000,256]{1,0:T(8,128)} custom-call(s32[187]{0:T(256)} %concatenate.78.plan_ref, bf16[5120,256]{1,0:T(8,128)(2,1)} %pad.30.table_ref, bf16[9216,256]{1,0:T(8,128)(2,1)} %pad_maximum_fusion.3.rows_ref, f32[4,9216]{1,0:T(4,128)} %fusion.47.fact_ref), custom_call_target="tpu_custom_call" | custom-call | flops 24159191040 | bytes 9961472 | tf_op jit(solution)/shard_map/band_grad/pallas_call | solution.py:442
  724.7 4.0 collective-permute-start.33
  737.4 13.1 %collective-permute-done.30 = bf16[128,1024]{1,0:T(8,128)(2,1)S(1)} collective-permute-done((bf16[128,1024]{1,0:T(8,128)(2,1)S(1)}, bf16[128,1024]{1,0:T(8,128)(2,1)S(1)}, u32[]{:S(2)}, u32[]{:S(2)}) %collective-permute-start.30) | collective-permute-done | bytes 262176 | tf_op jit(solution)/shard_map/ppermute | solution.py:696
  750.6 17.6 %collective-permute-start.32 = (bf16[128,1024]{1,0:T(8,128)(2,1)S(1)}, bf16[128,1024]{1,0:T(8,128)(2,1)S(1)}, u32[]{:S(2)}, u32[]{:S(2)}) collective-permute-start(bf16[128,1024]{1,0:T(8,128)(2,1)S(1)} %get-tuple-element.208), channel_id=1, source_target_pairs={{0,8},{8,16},{16,24},{24,0},{1,9},{9,17},{17,25},{25,1},{2,10},{10... | collective-permute-start | bytes 786440 | tf_op jit(solution)/shard_map/ppermute | solution.py:696
  783.5 30.0 %collective-permute-done.37 = bf16[128,1024]{1,0:T(8,128)(2,1)S(1)} collective-permute-done((bf16[128,1024]{1,0:T(8,128)(2,1)S(1)}, bf16[128,1024]{1,0:T(8,128)(2,1)S(1)}, u32[]{:S(2)}, u32[]{:S(2)}) %collective-permute-start.37) | collective-permute-done | bytes 262176 | tf_op jit(solution)/shard_map/ppermute | solution.py:625
  815.1 28.7 %all-reduce.10.cloned.1.call-done = bf16[128,4480]{1,0:T(8,128)(2,1)} async-done(((bf16[128,4480]{1,0:T(8,128)(2,1)}), bf16[128,4480]{1,0:T(8,128)(2,1)}) %all-reduce.10.cloned.1.call-update) | async-done | bytes 1146896 | tf_op jit(solution)/shard_map/psum | solution.py:1143
  (474 shorter events, 178.3 us)
Async XLA Ops:
  7.2 193.3 %all-gather.5.cloned.1.call-start = ((), (), s32[]{:S(2)}) async-start(), calls=%async_computation.4 | async-start | bytes 4718592 | tf_op jit(solution)/shard_map/all_gather | solution.py:845
  12.6 45.4 %collective-permute-start = (bf16[256,1024]{1,0:T(8,128)(2,1)}, bf16[256,1024]{1,0:T(8,128)(2,1)}, u32[]{:S(2)}, u32[]{:S(2)}) collective-permute-start(bf16[256,1024]{1,0:T(8,128)(2,1)} %add_convert_fusion.5), channel_id=1, source_target_pairs={{0,24},{1,25},{2,26},{3,27},{4,28},{5,29},{6,30},{7,31}} | collective-permute-start | bytes 1572872 | tf_op jit(solution)/shard_map/ppermute | solution.py:673
  20.4 39.1 %collective-permute-start.1 = (bf16[256,1024]{1,0:T(8,128)(2,1)}, bf16[256,1024]{1,0:T(8,128)(2,1)}, u32[]{:S(2)}, u32[]{:S(2)}) collective-permute-start(bf16[256,1024]{1,0:T(8,128)(2,1)} %add_convert_fusion.5), channel_id=1, source_target_pairs={{0,16},{8,24},{1,17},{9,25},{2,18},{10,26},{3,19},{11,27},{4,20},{... | collective-permute-start | bytes 1572872 | tf_op jit(solution)/shard_map/ppermute | solution.py:673
  22.5 38.1 %collective-permute-start.2 = (bf16[256,1024]{1,0:T(8,128)(2,1)}, bf16[256,1024]{1,0:T(8,128)(2,1)}, u32[]{:S(2)}, u32[]{:S(2)}) collective-permute-start(bf16[256,1024]{1,0:T(8,128)(2,1)} %add_convert_fusion.5), channel_id=1, source_target_pairs={{0,8},{8,16},{16,24},{1,9},{9,17},{17,25},{2,10},{10,18},{18,26},{... | collective-permute-start | bytes 1572872 | tf_op jit(solution)/shard_map/ppermute | solution.py:673
  97.9 188.6 %all-gather.7.cloned.1.call-start = ((), (), s32[]{:S(2)}) async-start(), calls=%async_computation.5 | async-start | bytes 14155776 | tf_op jit(solution)/shard_map/all_gather | solution.py:854
  139.9 152.3 %copy-start.25 = (bf16[2048,128]{1,0:T(8,128)(2,1)}, bf16[2048,128]{1,0:T(8,128)(2,1)S(1)}, u32[]{:S(2)}) copy-start(bf16[2048,128]{1,0:T(8,128)(2,1)S(1)} %broadcast_select_fusion.2.tail_hit_ref) | copy-start | bytes 1572868
  144.0 24.7 %collective-permute-start.3 = (bf16[256,1024]{1,0:T(8,128)(2,1)S(1)}, bf16[256,1024]{1,0:T(8,128)(2,1)}, u32[]{:S(2)}, u32[]{:S(2)}) collective-permute-start(bf16[256,1024]{1,0:T(8,128)(2,1)S(1)} %copy-done.9), channel_id=1, source_target_pairs={{0,24},{8,0},{16,8},{24,16},{1,25},{9,1},{17,9},{25,17},{2,26},{10... | collective-permute-start | bytes 1572872 | tf_op jit(solution)/shard_map/ppermute | solution.py:625
  144.0 53.8 %collective-permute-start.4 = (bf16[256,1024]{1,0:T(8,128)(2,1)S(1)}, bf16[256,1024]{1,0:T(8,128)(2,1)}, u32[]{:S(2)}, u32[]{:S(2)}) collective-permute-start(bf16[256,1024]{1,0:T(8,128)(2,1)S(1)} %copy-done.9), channel_id=1, source_target_pairs={{0,16},{8,24},{16,0},{24,8},{1,17},{9,25},{17,1},{25,9},{2,18},{10... | collective-permute-start | bytes 1572872 | tf_op jit(solution)/shard_map/ppermute | solution.py:625
  152.0 45.9 %collective-permute-start.5 = (bf16[256,1024]{1,0:T(8,128)(2,1)S(1)}, bf16[256,1024]{1,0:T(8,128)(2,1)}, u32[]{:S(2)}, u32[]{:S(2)}) collective-permute-start(bf16[256,1024]{1,0:T(8,128)(2,1)S(1)} %copy-done.9), channel_id=1, source_target_pairs={{0,8},{8,16},{16,24},{24,0},{1,9},{9,17},{17,25},{25,1},{2,10},{10... | collective-permute-start | bytes 1572872 | tf_op jit(solution)/shard_map/ppermute | solution.py:625
  200.6 130.6 %all-gather.9.cloned.1.call-start = ((), (), s32[]{:S(2)}) async-start(), calls=%async_computation.6 | async-start | bytes 3981312 | tf_op jit(solution)/shard_map/all_gather | solution.py:886
  224.6 61.1 %collective-permute-start.6 = (bf16[288,256]{1,0:T(8,128)(2,1)S(1)}, bf16[288,256]{1,0:T(8,128)(2,1)S(1)}, u32[]{:S(2)}, u32[]{:S(2)}) collective-permute-start(bf16[288,256]{1,0:T(8,128)(2,1)S(1)} %constant_dynamic-slice_fusion.1), channel_id=1, source_target_pairs={{0,24},{8,0},{16,8},{24,16},{1,25},{9,1},{17,9},{25,17},{2,26},{10... | collective-permute-start | bytes 442376 | tf_op jit(solution)/shard_map/ppermute | solution.py:625
  224.7 61.0 %collective-permute-start.7 = (bf16[288,256]{1,0:T(8,128)(2,1)S(1)}, bf16[288,256]{1,0:T(8,128)(2,1)S(1)}, u32[]{:S(2)}, u32[]{:S(2)}) collective-permute-start(bf16[288,256]{1,0:T(8,128)(2,1)S(1)} %constant_dynamic-slice_fusion.1), channel_id=1, source_target_pairs={{0,16},{8,24},{16,0},{24,8},{1,17},{9,25},{17,1},{25,9},{2,18},{10... | collective-permute-start | bytes 442376 | tf_op jit(solution)/shard_map/ppermute | solution.py:625
  224.8 61.0 %collective-permute-start.8 = (bf16[288,256]{1,0:T(8,128)(2,1)S(1)}, bf16[288,256]{1,0:T(8,128)(2,1)S(1)}, u32[]{:S(2)}, u32[]{:S(2)}) collective-permute-start(bf16[288,256]{1,0:T(8,128)(2,1)S(1)} %constant_dynamic-slice_fusion.1), channel_id=1, source_target_pairs={{0,8},{8,16},{16,24},{24,0},{1,9},{9,17},{17,25},{25,1},{2,10},{10... | collective-permute-start | bytes 442376 | tf_op jit(solution)/shard_map/ppermute | solution.py:625
  286.6 190.4 %reduce-scatter.5.cloned.1.call-start = ((), (), s32[]{:S(2)}) async-start(), calls=%async_computation.7 | async-start | bytes 5898240 | tf_op jit(solution)/shard_map/reduce_scatter | solution.py:930
  362.4 14.0 %collective-permute-start.9 = (f32[4,4352]{1,0:T(4,128)S(1)}, f32[4,4352]{1,0:T(4,128)S(1)}, u32[]{:S(2)}, u32[]{:S(2)}) collective-permute-start(f32[4,4352]{1,0:T(4,128)S(1)} %pad_maximum_fusion.10), channel_id=1, source_target_pairs={{0,24},{8,0},{16,8},{24,16},{1,25},{9,1},{17,9},{25,17},{2,26},{10... | collective-permute-start | bytes 208904 | tf_op jit(solution)/shard_map/ppermute | solution.py:625
  362.5 13.9 %collective-permute-start.10 = (f32[4,4352]{1,0:T(4,128)S(1)}, f32[4,4352]{1,0:T(4,128)S(1)}, u32[]{:S(2)}, u32[]{:S(2)}) collective-permute-start(f32[4,4352]{1,0:T(4,128)S(1)} %pad_maximum_fusion.10), channel_id=1, source_target_pairs={{0,16},{8,24},{16,0},{24,8},{1,17},{9,25},{17,1},{25,9},{2,18},{10... | collective-permute-start | bytes 208904 | tf_op jit(solution)/shard_map/ppermute | solution.py:625
  366.6 9.8 %collective-permute-start.11 = (f32[4,4352]{1,0:T(4,128)S(1)}, f32[4,4352]{1,0:T(4,128)S(1)}, u32[]{:S(2)}, u32[]{:S(2)}) collective-permute-start(f32[4,4352]{1,0:T(4,128)S(1)} %pad_maximum_fusion.10), channel_id=1, source_target_pairs={{0,8},{8,16},{16,24},{24,0},{1,9},{9,17},{17,25},{25,1},{2,10},{10... | collective-permute-start | bytes 208904 | tf_op jit(solution)/shard_map/ppermute | solution.py:625
  375.2 291.0 %reduce-scatter.7.cloned.1.call-start = ((), (), s32[]{:S(2)}) async-start(), calls=%async_computation.8 | async-start | bytes 9437184 | tf_op jit(solution)/shard_map/reduce_scatter | solution.py:1030
  413.4 64.9 %collective-permute-start.12 = (bf16[640,1024]{1,0:T(8,128)(2,1)}, bf16[640,1024]{1,0:T(8,128)(2,1)}, u32[]{:S(2)}, u32[]{:S(2)}) collective-permute-start(bf16[640,1024]{1,0:T(8,128)(2,1)} %head_grad.1), channel_id=1, source_target_pairs={{0,8},{8,16},{16,24},{1,9},{9,17},{17,25},{2,10},{10,18},{18,26},{... | collective-permute-start | bytes 3932168 | tf_op jit(solution)/shard_map/ppermute | solution.py:633
  416.7 61.6 %collective-permute-start.13 = (bf16[640,1024]{1,0:T(8,128)(2,1)}, bf16[640,1024]{1,0:T(8,128)(2,1)}, u32[]{:S(2)}, u32[]{:S(2)}) collective-permute-start(bf16[640,1024]{1,0:T(8,128)(2,1)} %head_grad.1), channel_id=1, source_target_pairs={{8,0},{16,8},{24,16},{9,1},{17,9},{25,17},{10,2},{18,10},{26,18},{... | collective-permute-start | bytes 3932168 | tf_op jit(solution)/shard_map/ppermute | solution.py:634
  497.1 227.6 %reduce-scatter.11.cloned.1.call-start = ((), (), s32[]{:S(2)}) async-start(), calls=%async_computation.10 | async-start | bytes 9437184 | tf_op jit(solution)/shard_map/reduce_scatter | solution.py:1024
  506.4 267.6 %reduce-scatter.9.cloned.1.call-start = ((), (), s32[]{:S(2)}) async-start(), calls=%async_computation.9 | async-start | bytes 10321920 | tf_op jit(solution)/shard_map/reduce_scatter | solution.py:1101
  507.7 94.2 %collective-permute-start.14 = (bf16[64,6656]{1,0:T(8,128)(2,1)}, bf16[64,6656]{1,0:T(8,128)(2,1)}, u32[]{:S(2)}, u32[]{:S(2)}) collective-permute-start(bf16[64,6656]{1,0:T(8,128)(2,1)} %band_grad.2), channel_id=1, source_target_pairs={{0,8},{8,16},{16,24},{1,9},{9,17},{17,25},{2,10},{10,18},{18,26},{... | collective-permute-start | bytes 2555912 | tf_op jit(solution)/shard_map/ppermute | solution.py:633
  513.7 88.2 %collective-permute-start.15 = (bf16[64,6656]{1,0:T(8,128)(2,1)}, bf16[64,6656]{1,0:T(8,128)(2,1)}, u32[]{:S(2)}, u32[]{:S(2)}) collective-permute-start(bf16[64,6656]{1,0:T(8,128)(2,1)} %band_grad.2), channel_id=1, source_target_pairs={{8,0},{16,8},{24,16},{9,1},{17,9},{25,17},{10,2},{18,10},{26,18},{... | collective-permute-start | bytes 2555912 | tf_op jit(solution)/shard_map/ppermute | solution.py:634
  515.0 13.7 %collective-permute-start.16 = (bf16[640,1024]{1,0:T(8,128)(2,1)}, bf16[640,1024]{1,0:T(8,128)(2,1)S(1)}, u32[]{:S(2)}, u32[]{:S(2)}) collective-permute-start(bf16[640,1024]{1,0:T(8,128)(2,1)} %collective-permute-done.12), channel_id=1, source_target_pairs={{8,16},{16,24},{9,17},{17,25},{10,18},{18,26},{11,19},{19,27},{12,... | collective-permute-start | bytes 3932168 | tf_op jit(solution)/shard_map/ppermute | solution.py:633
  515.7 47.4 %collective-permute-start.17 = (bf16[640,1024]{1,0:T(8,128)(2,1)}, bf16[640,1024]{1,0:T(8,128)(2,1)S(1)}, u32[]{:S(2)}, u32[]{:S(2)}) collective-permute-start(bf16[640,1024]{1,0:T(8,128)(2,1)} %collective-permute-done.13), channel_id=1, source_target_pairs={{8,0},{16,8},{9,1},{17,9},{10,2},{18,10},{11,3},{19,11},{12,4},{20... | collective-permute-start | bytes 3932168 | tf_op jit(solution)/shard_map/ppermute | solution.py:634
  563.1 36.1 %collective-permute-start.18 = (bf16[640,1024]{1,0:T(8,128)(2,1)S(1)}, bf16[640,1024]{1,0:T(8,128)(2,1)S(1)}, u32[]{:S(2)}, u32[]{:S(2)}) collective-permute-start(bf16[640,1024]{1,0:T(8,128)(2,1)S(1)} %collective-permute-done.16), channel_id=1, source_target_pairs={{16,24},{17,25},{18,26},{19,27},{20,28},{21,29},{22,30},{23,31}} | collective-permute-start | bytes 3932168 | tf_op jit(solution)/shard_map/ppermute | solution.py:633
  563.9 36.7 %collective-permute-start.19 = (bf16[640,1024]{1,0:T(8,128)(2,1)S(1)}, bf16[640,1024]{1,0:T(8,128)(2,1)S(1)}, u32[]{:S(2)}, u32[]{:S(2)}) collective-permute-start(bf16[640,1024]{1,0:T(8,128)(2,1)S(1)} %collective-permute-done.17), channel_id=1, source_target_pairs={{8,0},{9,1},{10,2},{11,3},{12,4},{13,5},{14,6},{15,7}} | collective-permute-start | bytes 3932168 | tf_op jit(solution)/shard_map/ppermute | solution.py:634
  597.4 19.2 %collective-permute-start.20 = (bf16[256,1024]{1,0:T(8,128)(2,1)S(1)}, bf16[256,1024]{1,0:T(8,128)(2,1)S(1)}, u32[]{:S(2)}, u32[]{:S(2)}) collective-permute-start(bf16[256,1024]{1,0:T(8,128)(2,1)S(1)} %get-tuple-element.203), channel_id=1, source_target_pairs={{8,0},{16,8},{24,16},{9,1},{17,9},{25,17},{10,2},{18,10},{26,18},{... | collective-permute-start | bytes 1572872 | tf_op jit(solution)/shard_map/ppermute | solution.py:696
  599.3 51.7 %collective-permute-start.21 = (bf16[256,1024]{1,0:T(8,128)(2,1)S(1)}, bf16[256,1024]{1,0:T(8,128)(2,1)S(1)}, u32[]{:S(2)}, u32[]{:S(2)}) collective-permute-start(bf16[256,1024]{1,0:T(8,128)(2,1)S(1)} %get-tuple-element.205), channel_id=1, source_target_pairs={{16,0},{24,8},{17,1},{25,9},{18,2},{26,10},{19,3},{27,11},{20,4},{... | collective-permute-start | bytes 1572872 | tf_op jit(solution)/shard_map/ppermute | solution.py:696
  600.6 50.4 %collective-permute-start.22 = (bf16[256,1024]{1,0:T(8,128)(2,1)S(1)}, bf16[256,1024]{1,0:T(8,128)(2,1)S(1)}, u32[]{:S(2)}, u32[]{:S(2)}) collective-permute-start(bf16[256,1024]{1,0:T(8,128)(2,1)S(1)} %get-tuple-element.204), channel_id=1, source_target_pairs={{24,0},{25,1},{26,2},{27,3},{28,4},{29,5},{30,6},{31,7}} | collective-permute-start | bytes 1572872 | tf_op jit(solution)/shard_map/ppermute | solution.py:696
  601.9 64.3 %collective-permute-start.23 = (bf16[64,6656]{1,0:T(8,128)(2,1)}, bf16[64,6656]{1,0:T(8,128)(2,1)}, u32[]{:S(2)}, u32[]{:S(2)}) collective-permute-start(bf16[64,6656]{1,0:T(8,128)(2,1)} %collective-permute-done.14), channel_id=1, source_target_pairs={{8,16},{16,24},{9,17},{17,25},{10,18},{18,26},{11,19},{19,27},{12,... | collective-permute-start | bytes 2555912 | tf_op jit(solution)/shard_map/ppermute | solution.py:633
  603.5 62.7 %collective-permute-start.24 = (bf16[64,6656]{1,0:T(8,128)(2,1)}, bf16[64,6656]{1,0:T(8,128)(2,1)}, u32[]{:S(2)}, u32[]{:S(2)}) collective-permute-start(bf16[64,6656]{1,0:T(8,128)(2,1)} %collective-permute-done.15), channel_id=1, source_target_pairs={{8,0},{16,8},{9,1},{17,9},{10,2},{18,10},{11,3},{19,11},{12,4},{20... | collective-permute-start | bytes 2555912 | tf_op jit(solution)/shard_map/ppermute | solution.py:634
  666.2 177.7 %all-reduce.10.cloned.1.call-start = ((), (), s32[]{:S(2)}) async-start(), calls=%async_computation.11 | async-start | bytes 2293760 | tf_op jit(solution)/shard_map/psum | solution.py:1143
  682.8 41.8 %collective-permute-start.28 = (bf16[64,6656]{1,0:T(8,128)(2,1)}, bf16[64,6656]{1,0:T(8,128)(2,1)}, u32[]{:S(2)}, u32[]{:S(2)}) collective-permute-start(bf16[64,6656]{1,0:T(8,128)(2,1)} %collective-permute-done.23), channel_id=1, source_target_pairs={{16,24},{17,25},{18,26},{19,27},{20,28},{21,29},{22,30},{23,31}} | collective-permute-start | bytes 2555912 | tf_op jit(solution)/shard_map/ppermute | solution.py:633
  684.4 40.2 %collective-permute-start.29 = (bf16[64,6656]{1,0:T(8,128)(2,1)}, bf16[64,6656]{1,0:T(8,128)(2,1)}, u32[]{:S(2)}, u32[]{:S(2)}) collective-permute-start(bf16[64,6656]{1,0:T(8,128)(2,1)} %collective-permute-done.24), channel_id=1, source_target_pairs={{8,0},{9,1},{10,2},{11,3},{12,4},{13,5},{14,6},{15,7}} | collective-permute-start | bytes 2555912 | tf_op jit(solution)/shard_map/ppermute | solution.py:634
  685.8 38.7 %collective-permute-start.25 = (bf16[32,4096]{1,0:T(8,128)(2,1)S(1)}, bf16[32,4096]{1,0:T(8,128)(2,1)S(1)}, u32[]{:S(2)}, u32[]{:S(2)}) collective-permute-start(bf16[32,4096]{1,0:T(8,128)(2,1)S(1)} %get-tuple-element.210), channel_id=1, source_target_pairs={{0,24},{8,0},{16,8},{24,16},{1,25},{9,1},{17,9},{25,17},{2,26},{10... | collective-permute-start | bytes 786440 | tf_op jit(solution)/shard_map/ppermute | solution.py:696
  685.9 38.6 %collective-permute-start.26 = (bf16[32,4096]{1,0:T(8,128)(2,1)S(1)}, bf16[32,4096]{1,0:T(8,128)(2,1)S(1)}, u32[]{:S(2)}, u32[]{:S(2)}) collective-permute-start(bf16[32,4096]{1,0:T(8,128)(2,1)S(1)} %get-tuple-element.212), channel_id=1, source_target_pairs={{0,16},{8,24},{16,0},{24,8},{1,17},{9,25},{17,1},{25,9},{2,18},{10... | collective-permute-start | bytes 786440 | tf_op jit(solution)/shard_map/ppermute | solution.py:696
  690.8 33.6 %collective-permute-start.27 = (bf16[32,4096]{1,0:T(8,128)(2,1)S(1)}, bf16[32,4096]{1,0:T(8,128)(2,1)S(1)}, u32[]{:S(2)}, u32[]{:S(2)}) collective-permute-start(bf16[32,4096]{1,0:T(8,128)(2,1)S(1)} %get-tuple-element.211), channel_id=1, source_target_pairs={{0,8},{8,16},{16,24},{24,0},{1,9},{9,17},{17,25},{25,1},{2,10},{10... | collective-permute-start | bytes 786440 | tf_op jit(solution)/shard_map/ppermute | solution.py:696
  724.7 48.6 %collective-permute-start.33 = (bf16[32,4096]{1,0:T(8,128)(2,1)S(1)}, bf16[32,4096]{1,0:T(8,128)(2,1)S(1)}, u32[]{:S(2)}, u32[]{:S(2)}) collective-permute-start(bf16[32,4096]{1,0:T(8,128)(2,1)S(1)} %fusion.42), channel_id=1, source_target_pairs={{0,24},{8,0},{16,8},{24,16},{1,25},{9,1},{17,9},{25,17},{2,26},{10... | collective-permute-start | bytes 786440 | tf_op jit(solution)/shard_map/ppermute | solution.py:625
  728.7 44.5 %collective-permute-start.34 = (bf16[32,4096]{1,0:T(8,128)(2,1)S(1)}, bf16[32,4096]{1,0:T(8,128)(2,1)S(1)}, u32[]{:S(2)}, u32[]{:S(2)}) collective-permute-start(bf16[32,4096]{1,0:T(8,128)(2,1)S(1)} %fusion.42), channel_id=1, source_target_pairs={{0,16},{8,24},{16,0},{24,8},{1,17},{9,25},{17,1},{25,9},{2,18},{10... | collective-permute-start | bytes 786440 | tf_op jit(solution)/shard_map/ppermute | solution.py:625
  728.7 45.2 %collective-permute-start.35 = (bf16[32,4096]{1,0:T(8,128)(2,1)S(1)}, bf16[32,4096]{1,0:T(8,128)(2,1)}, u32[]{:S(2)}, u32[]{:S(2)}) collective-permute-start(bf16[32,4096]{1,0:T(8,128)(2,1)S(1)} %fusion.42), channel_id=1, source_target_pairs={{0,8},{8,16},{16,24},{24,0},{1,9},{9,17},{17,25},{25,1},{2,10},{10... | collective-permute-start | bytes 786440 | tf_op jit(solution)/shard_map/ppermute | solution.py:625
  730.5 20.1 %collective-permute-start.30 = (bf16[128,1024]{1,0:T(8,128)(2,1)S(1)}, bf16[128,1024]{1,0:T(8,128)(2,1)S(1)}, u32[]{:S(2)}, u32[]{:S(2)}) collective-permute-start(bf16[128,1024]{1,0:T(8,128)(2,1)S(1)} %get-tuple-element.207), channel_id=1, source_target_pairs={{0,24},{8,0},{16,8},{24,16},{1,25},{9,1},{17,9},{25,17},{2,26},{10... | collective-permute-start | bytes 786440 | tf_op jit(solution)/shard_map/ppermute | solution.py:696
  733.7 37.5 %collective-permute-start.31 = (bf16[128,1024]{1,0:T(8,128)(2,1)S(1)}, bf16[128,1024]{1,0:T(8,128)(2,1)S(1)}, u32[]{:S(2)}, u32[]{:S(2)}) collective-permute-start(bf16[128,1024]{1,0:T(8,128)(2,1)S(1)} %get-tuple-element.209), channel_id=1, source_target_pairs={{0,16},{8,24},{16,0},{24,8},{1,17},{9,25},{17,1},{25,9},{2,18},{10... | collective-permute-start | bytes 786440 | tf_op jit(solution)/shard_map/ppermute | solution.py:696
  750.6 21.5 %collective-permute-start.32 = (bf16[128,1024]{1,0:T(8,128)(2,1)S(1)}, bf16[128,1024]{1,0:T(8,128)(2,1)S(1)}, u32[]{:S(2)}, u32[]{:S(2)}) collective-permute-start(bf16[128,1024]{1,0:T(8,128)(2,1)S(1)} %get-tuple-element.208), channel_id=1, source_target_pairs={{0,8},{8,16},{16,24},{24,0},{1,9},{9,17},{17,25},{25,1},{2,10},{10... | collective-permute-start | bytes 786440 | tf_op jit(solution)/shard_map/ppermute | solution.py:696
  773.9 8.5 collective-permute-start.36
  775.6 37.9 %collective-permute-start.37 = (bf16[128,1024]{1,0:T(8,128)(2,1)S(1)}, bf16[128,1024]{1,0:T(8,128)(2,1)S(1)}, u32[]{:S(2)}, u32[]{:S(2)}) collective-permute-start(bf16[128,1024]{1,0:T(8,128)(2,1)S(1)} %fusion.39), channel_id=1, source_target_pairs={{0,16},{8,24},{16,0},{24,8},{1,17},{9,25},{17,1},{25,9},{2,18},{10... | collective-permute-start | bytes 786440 | tf_op jit(solution)/shard_map/ppermute | solution.py:625
  777.9 35.6 %collective-permute-start.38 = (bf16[128,1024]{1,0:T(8,128)(2,1)S(1)}, bf16[128,1024]{1,0:T(8,128)(2,1)S(1)}, u32[]{:S(2)}, u32[]{:S(2)}) collective-permute-start(bf16[128,1024]{1,0:T(8,128)(2,1)S(1)} %fusion.39), channel_id=1, source_target_pairs={{0,8},{8,16},{16,24},{24,0},{1,9},{9,17},{17,25},{25,1},{2,10},{10... | collective-permute-start | bytes 786440 | tf_op jit(solution)/shard_map/ppermute | solution.py:625
  (94 other events, 1153.8 us)
Sparse Core Ops, SparseCore 0:
  98.1 41.9 all-gather.4
  200.7 70.3 all-gather.6
  286.7 34.2 all-gather.8
  375.3 57.0 reduce-scatter.4
  497.2 74.1 reduce-scatter.6
  574.7 71.2 reduce-scatter.10
  666.3 73.5 reduce-scatter.8
  781.8 62.0 all-reduce.9

commit v4 on v3

--- a/solution.py
+++ b/solution.py
@@ -845,13 +845,10 @@
     all_states = lax.all_gather(state_low, "batch", axis=0, tiled=True)
     split = 2 * nz * group_count * feature_count <= 24 << 20
     if split:
-        other_states = jnp.concatenate(line_turns(state_low)[1:], 0)
-        all_states, other_states, head_pad, middle_pad, tail_pad, hit_rows, slot, early = (
-            lax.optimization_barrier(
-                (all_states, other_states, head_pad, middle_pad, tail_pad, hit_rows, slot, early)
-            )
-        )
-        other_states = lax.all_gather(other_states, "batch", axis=0, tiled=True)
+        block_states = lax.all_gather(state_low, "seq", axis=0, tiled=True)
+    all_states, head_pad, middle_pad, tail_pad, hit_rows, slot, early = lax.optimization_barrier(
+        (all_states, head_pad, middle_pad, tail_pad, hit_rows, slot, early)
+    )
 
     middle_width = middle_map.shape[1]
     maps = jnp.pad(jnp.concatenate([middle_map, tail_map], 1), ((0, 0), (0, 128 - tail_width)))
@@ -873,17 +870,20 @@
         piece = slot_count // nb
         slot_piece = lax.dynamic_slice_in_dim(slot_low, member * piece, piece, 0)
         other_slots = jnp.concatenate(line_turns(slot_piece)[1:], 0)
+        slot_low, block_states = lax.optimization_barrier((slot_low, block_states))
+        other_states = lax.dynamic_slice_in_dim(
+            jnp.concatenate([block_states, block_states], 0),
+            (place + 1) * token_count,
+            (nz - 1) * token_count,
+            0,
+        )
+        other_states = lax.all_gather(other_states, "batch", axis=0, tiled=True)
     tail_stats, tail_mix = band_forward(
         tail_span, slot_low, tail_pad, tail_padded, tail_chunk, tail_width, 0.5
     )
     middle_stats, middle_mix = band_forward(
         middle_span, slot_low, middle_pad, sizes[1], middle_chunk, None, 0.25
     )
-    if split:
-        all_states, other_states, other_slots, tail_stats, middle_stats = lax.optimization_barrier(
-            (all_states, other_states, other_slots, tail_stats, middle_stats)
-        )
-        other_slots = lax.all_gather(other_slots, "batch", axis=0, tiled=True)
     head_stats, head_mix = band_forward(
         head_span, all_states, head_pad, sizes[0], head_chunk, None, 1.0
     )
@@ -911,6 +911,7 @@
         stats, other_states, other_slots = lax.optimization_barrier(
             (stats, other_states, other_slots)
         )
+        other_slots = lax.all_gather(other_slots, "batch", axis=0, tiled=True)
     everyone = lax.all_gather(stats, "batch")
 
     token_facts = jnp.concatenate(
@@ -973,26 +974,29 @@
     facts = jnp.concatenate(
         [facts[:2], jnp.where(facts[3:4] > 0, facts[2:3], -1e9), jnp.zeros_like(facts[:1])], 0
     )
-    tail_part = band_grad(
-        tail_pad,
+    middle_result = jax.ShapeDtypeStruct(
+        (sizes[1], middle_width) if split else (middle_padded, middle_width),
+        jnp.float32 if split else jnp.bfloat16,
+    )
+    middle_part = band_grad(
+        middle_pad,
         rows_all,
         facts,
-        block_kind == 2,
+        block_kind == 1,
         lowest,
         highest,
-        part,
-        tail_padded // parts,
-        HEAD_WORDS + MID_WORDS + member * sizes[2],
-        math.gcd(tail_padded // parts, tail_chunk),
-        jax.ShapeDtypeStruct((tail_width, tail_padded // parts), jnp.bfloat16),
-        True,
+        0 * place,
+        middle_padded,
+        HEAD_WORDS + member * sizes[1],
+        middle_chunk,
+        middle_result,
+        False,
     )
     if split:
         head_found, head_advance = line_steps(head_part)
-        own_terms, tail_part = head_advance(own_terms, tail_part)
-        tail_found, tail_advance = line_steps(tail_part)
+        own_terms, middle_part = head_advance(own_terms, middle_part)
     else:
-        own_terms, tail_part = lax.optimization_barrier((own_terms, tail_part))
+        own_terms, middle_part = lax.optimization_barrier((own_terms, middle_part))
 
     own_middle = own_part(in_middle)
     own_tail = own_part(in_tail)
@@ -1045,8 +1049,7 @@
     )
     if split:
         for unused in range(nz - 3):
-            (query_low,) = head_advance(query_low)
-        (query_low,) = tail_advance(query_low)
+            query_low, key_low, value_low = head_advance(query_low, key_low, value_low)
     query_weight_grad = product_tn(normed_low, query_low)
     key_weight_grad = product_tn(normed_all, key_low)
     value_weight_grad = product_tn(normed_all, value_low)
@@ -1060,10 +1063,6 @@
     own_spread = jnp.mean((tokens - own_average) ** 2, -1, keepdims=True)
     own_centred = (tokens - own_average) * lax.rsqrt(own_spread + EPSILON)
     first_gain_grad = jnp.sum(all_centred * spread, 0) + jnp.sum(own_centred * query_spread, 0)
-    normed_grad = query_spread + line_scatter(lowered(spread), False)
-    first_in_grad, unused, unused = norm_back(tokens, first_gain, first_shift, normed_grad)
-    input_grad = mixed_grad + first_in_grad
-
     bias_rows = inner_bias_grad.shape[0] // feature_count
     inner_bias_rows = (
         inner_bias_grad.reshape(nb, bias_rows, -1).transpose(1, 0, 2).reshape(bias_rows, -1)
@@ -1095,49 +1094,61 @@
         turned(jnp.concatenate(rows, 0), jnp.bfloat16),
     ]
     rest = jnp.concatenate([lowered(column) for column in columns], 1)
-    rest, facts, inner_part = lax.optimization_barrier((rest, facts, inner_part))
-    if split:
-        rest, facts = tail_advance(rest, facts)
+    inner_low = lowered(line_scatter(inner_part))
+    spread_low = lowered(spread)
+    rest, facts, inner_low, spread_low = lax.optimization_barrier(
+        (rest, facts, inner_low, spread_low)
+    )
     rest_part = lax.psum_scatter(rest, "batch", scatter_dimension=0, tiled=True)
-    middle_result = jax.ShapeDtypeStruct(
-        (sizes[1], middle_width) if split else (middle_padded, middle_width),
-        jnp.float32 if split else jnp.bfloat16,
-    )
-    middle_part = band_grad(
-        middle_pad,
-        rows_all,
-        facts,
-        block_kind == 1,
-        lowest,
-        highest,
-        0 * place,
-        middle_padded,
-        HEAD_WORDS + member * sizes[1],
-        middle_chunk,
-        middle_result,
-        False,
-    )
+    inner_pieces = line_turns(inner_low)
+
+    def tail_gradient(part, parts):
+        return band_grad(
+            tail_pad,
+            rows_all,
+            facts,
+            block_kind == 2,
+            lowest,
+            highest,
+            part,
+            tail_padded // parts,
+            HEAD_WORDS + MID_WORDS + member * sizes[2],
+            math.gcd(tail_padded // parts, tail_chunk),
+            jax.ShapeDtypeStruct((tail_width, tail_padded // parts), jnp.bfloat16),
+            True,
+        )
+
     if split:
         middle_table_grad = middle_part
-        for unused in range(nz - 3):
-            (middle_table_grad,) = tail_advance(middle_table_grad)
         head_table_grad = line_ordered(head_found, 0)
-        tail_sum = line_ordered(tail_found, 1)
+        first_tail = tail_gradient(2 * place, 2 * nz)
+        first_tail, facts, inner_pieces, outer_part = lax.optimization_barrier(
+            (first_tail, facts, inner_pieces, outer_part)
+        )
+        first_found, first_advance = line_steps(first_tail)
+        second_tail = tail_gradient(2 * place + 1, 2 * nz)
+        outer_low = lowered(line_scatter(outer_part))
+        second_tail, outer_low = first_advance(second_tail, outer_low)
+        second_found, second_advance = line_steps(second_tail)
+        for unused in range(nz - 1):
+            first_advance()
+            second_advance()
+        halves = [
+            line_ordered(found, 0).reshape(nz, tail_width, -1)
+            for found in (first_found, second_found)
+        ]
+        tail_sum = jnp.stack(halves, 1).transpose(2, 0, 1, 3).reshape(tail_width, -1)
     else:
+        outer_low = lowered(line_scatter(outer_part))
         middle_table_grad = lax.psum(middle_part, "seq")[: sizes[1]].astype(jnp.float32)
         head_table_grad = lax.psum(head_part, "seq")
-        tail_sum = lax.psum(tail_part, "seq")
+        tail_sum = lax.psum(tail_gradient(part, parts), "seq")
     head_table_grad = head_table_grad[: sizes[0]].astype(jnp.float32)
     tail_table_grad = tail_sum[:, : sizes[2]].astype(jnp.float32).T
-    inner_low = lowered(line_scatter(inner_part))
-    inner_low, outer_part, middle_table_grad = lax.optimization_barrier(
-        (inner_low, outer_part, middle_table_grad)
-    )
-    inner_pieces = line_turns(inner_low)
-    outer_low = lowered(line_scatter(outer_part))
-    rest_part, outer_low, inner_pieces = lax.optimization_barrier(
-        (rest_part, outer_low, inner_pieces)
-    )
+    normed_grad = query_spread + line_scatter(spread_low, False)
+    first_in_grad, unused, unused = norm_back(tokens, first_gain, first_shift, normed_grad)
+    input_grad = mixed_grad + first_in_grad
+
     inner_sum = in_order(inner_pieces).astype(jnp.float32)
     outer_sum = in_order(line_turns(outer_low)).astype(jnp.float32)
     rest_low = lax.psum(rest_part, "seq")

time: 871 us -> 907 us (1.041)
  local copies, waits for them, and re-layouts: 91.2 us -> 112 us
    ppermute x15 -> x12, waiting for transfers between devices: 59.8 us -> 16.9 us  [line_turns(): lax.ppermute(value, 'seq', [(d, (d - k) % size) for d in range(size)])]
    psum x1, waiting for transfers between devices: 28.7 us -> 49.2 us  [on_device(): rest_low = lax.psum(rest_part, 'seq')]
    all_gather x0 -> x1, waiting for transfers between devices: none -> 20.3 us  [on_device(): block_states = lax.all_gather(state_low, 'seq', axis=0, tiled=True)]
    ppermute x6 -> x9, waiting for transfers between devices: 34.5 us -> 54.3 us  [line_step(): lax.ppermute(behind, 'seq', [(d, d - 1) for d in range(1, size - step + 1)])]
    ppermute x9, starting transfers between devices: 31 us -> 16.1 us  [line_scatter(): lax.ppermute(part(place + size - k), 'seq', pairs).astype(jnp.float32)]
    ppermute x9, waiting for transfers between devices: 48.9 us -> 35.3 us  [line_scatter(): lax.ppermute(part(place + size - k), 'seq', pairs).astype(jnp.float32)]
    ppermute x6 -> x9, starting transfers between devices: 13.9 us -> 20.6 us  [line_step(): lax.ppermute(before, 'seq', [(d, d + 1) for d in range(step - 1, size - 1)])]
    pallas_call x2 -> x3, Pallas kernels: 86.3 us -> 89.1 us  [band_grad(): pl.pallas_call(functools.partial(band_grad_kernel, chunk // 2 if chunk >...]
  transfers between devices with their start and end apart: 47 -> 51, of which waited for: 9 -> 14; matrix products, arithmetic and copies ran while one was open for 26% -> 27% of each run, Pallas kernels for 28% -> 30%
where the time goes in v4:
time: 907 us; the launch traced here: 891 us
  Pallas kernels  280 us (31%)
  waiting for transfers between devices  176 us (19%)
  local copies, waits for them, and re-layouts  112 us (12%)
  other arithmetic  104 us (11%)
  matrix products  91.8 us (10%)
  starting transfers between devices  85.3 us (9%)
  blocking collectives  22.3 us (2%)
  between operations  18.8 us (2%)
    pallas_call x3, Pallas kernels, band_forward(): pl.pallas_call(functools.partial(band_kernel, chunk, per, words, sum_colu...  90 us
    pallas_call x3, Pallas kernels, band_grad(): pl.pallas_call(functools.partial(band_grad_kernel, chunk // 2 if chunk >...  89.1 us
    ppermute x9, waiting for transfers between devices, line_step(): lax.ppermute(behind, 'seq', [(d, d - 1) for d in range(1, size - step + 1)])  54.3 us
    psum x1, waiting for transfers between devices, on_device(): rest_low = lax.psum(rest_part, 'seq')  49.2 us
    ppermute x9, waiting for transfers between devices, line_scatter(): lax.ppermute(part(place + size - k), 'seq', pairs).astype(jnp.float32)  35.3 us
    gather x3, local copies, waits for them, and re-layouts, on_device(): jnp.take(table, jnp.clip(local, 0, size - 1), axis=0, mode='clip')  34.4 us
    dot_general x9, matrix products, product_tn(): lax.dot_general(former, latter, (((0,), (0,)), ((), ())), preferred_eleme...  33.4 us
    pallas_call x1, Pallas kernels, head_grad(): pl.pallas_call(functools.partial(head_grad_kernel, chunk, len(lists)), gr...  32.7 us
  transfers between devices with their start and end apart: 51, of which 14 were waited for; matrix products, arithmetic and copies ran while one was open for 27% of the time, Pallas kernels for 30%

profile of v4, /device:TPU:0, one launch (start us, length us, event | category | flops | bytes accessed | tf_op | source)
XLA Modules:
  0.0 890.5 jit_solution(9052413033978949892)
XLA Ops:
  12.6 7.8 collective-permute-start
  26.8 9.1 %all_gather.22 = f32[3,2048]{1,0:T(4,128)S(1)} all-gather(f32[3,256]{1,0:T(4,128)S(1)} %pad_maximum_fusion.11), channel_id=1, replica_groups=mesh['seq'=4,'batch'=8] {'batch'}, dimensions={1}, use_global_device_ids=true | all-gather | bytes 27648 | tf_op jit(solution)/shard_map/all_gather | solution.py:765
  47.3 7.4 copy.123
  55.9 5.6 pad.29.table_ref
  74.6 15.2 %attend.1 = bf16[256,1024]{1,0:T(8,128)(2,1)} custom-call(s32[1]{0:T(128)} %bitcast.2.start_ref, bf16[256,1024]{1,0:T(8,128)(2,1)} %fusion.21.query_ref, bf16[1024,1024]{1,0:T(8,128)(2,1)} %convolution_convert_fusion.2.key_ref, bf16[1024,1024]{1,0:T(8,128)(2,1)} %add_convert_fusion.value_ref), custom_call_target="tpu_custom_call" | custom-call | flops 1073741824 | bytes 5242880 | tf_op jit(solution)/shard_map/attend/pallas_call | solution.py:92
  92.2 6.0 convolution_add_fusion
  104.0 11.7 %fusion.6.table_ref = bf16[26624,128]{1,0:T(8,128)(2,1)} fusion(bf16[64,25967]{0,1:T(8,128)(2,1)} %bitcast.215, bf16[1,26624]{0,1:T(8,128)(2,1)} %select_convert_fusion, bf16[128]{0:T(256)(128)(2,1)S(1)} %copy-done.86, bf16[128]{0:T(256)(128)(2,1)S(1)} %copy-done.87), kind=kLoop, calls=%fused_computation.17 | loop fusion | flops 34078720 | bytes 10193280 | tf_op jit(solution)/shard_map/transpose | solution.py:816
  115.7 11.5 %gather_fusion.2 = bf16[2048,128]{1,0:T(8,128)(2,1)} fusion(bf16[26624,128]{1,0:T(8,128)(2,1)} %fusion.6.table_ref, s32[2048]{0:T(1024)S(1)} %copy-done.56), kind=kCustom, calls=%fused_computation.2 | custom fusion | bytes 1056768 | tf_op jit(solution)/shard_map/jit(_take)/gather | solution.py:829
  127.2 14.1 %gather_fusion = bf16[2048,1024]{1,0:T(8,128)(2,1)} fusion(bf16[2560,1024]{1,0:T(8,128)(2,1)} %pad.29.table_ref, s32[2048]{0:T(1024)S(1)} %broadcast_clamp_fusion.2), kind=kCustom, calls=%fused_computation | custom fusion | bytes 8396800 | tf_op jit(solution)/shard_map/jit(_take)/gather | solution.py:829
  141.3 8.7 gather_fusion.1
  150.7 5.2 convert_reduce_fusion
  165.2 5.9 add_convert_fusion.1.rows_ref
  171.0 8.6 pick_rows.1
  183.0 20.3 %all-gather.8.cloned.1.call-done = bf16[1024,1024]{1,0:T(8,128)(2,1)} async-done(((bf16[256,1024]{1,0:T(8,128)(2,1)}), bf16[1024,1024]{1,0:T(8,128)(2,1)}) %all-gather.8.cloned.1.call-update) | async-done | bytes 2097168 | tf_op jit(solution)/shard_map/all_gather | solution.py:848
  214.1 31.0 %band_forward.3 = (f32[8,2048]{1,0:T(8,128)}, bf16[2048,1024]{1,0:T(8,128)(2,1)}) custom-call(s32[2]{0:T(128)} %iota_multiply_fusion.1.span_ref, bf16[2048,1024]{1,0:T(8,128)(2,1)} %all-gather.6.cloned.1.call-done.rows_ref.refs_0_, bf16[2560,1024]{1,0:T(8,128)(2,1)} %pad.29.table_ref), custom_call_target="tpu_custom_call" | custom-call | flops 21474836480 | bytes 17825792 | tf_op jit(solution)/shard_map/band_forward/pallas_call | solution.py:279
  252.6 10.4 %band_forward.5 = (f32[8,2304]{1,0:T(8,128)}, bf16[2304,256]{1,0:T(8,128)(2,1)}) custom-call(s32[2]{0:T(128)} %pad_add_fusion.4.span_ref, bf16[2304,256]{1,0:T(8,128)(2,1)} %copy-done.16, bf16[5120,256]{1,0:T(8,128)(2,1)} %pad.30.table_ref), custom_call_target="tpu_custom_call" | custom-call | flops 3019898880 | bytes 6160384 | tf_op jit(solution)/shard_map/band_forward/pallas_call | solution.py:279
  263.1 48.5 %band_forward.4 = (f32[8,2304]{1,0:T(8,128)}, bf16[2304,128]{1,0:T(8,128)(2,1)}) custom-call(s32[2]{0:T(128)} %pad_add_fusion.3.span_ref, bf16[2304,256]{1,0:T(8,128)(2,1)} %copy-done.16, bf16[26624,128]{1,0:T(8,128)(2,1)} %fusion.6.table_ref), custom_call_target="tpu_custom_call" | custom-call | flops 31406948352 | bytes 8585216 | tf_op jit(solution)/shard_map/band_forward/pallas_call | solution.py:279
  320.9 13.2 %all-gather = f32[64,2304]{1,0:T(8,128)} all-gather(f32[8,2304]{1,0:T(8,128)S(1)} %maximum_maximum_fusion), channel_id=2, replica_groups=mesh['seq'=4,'batch'=8] {'batch'}, dimensions={0}, use_global_device_ids=true | all-gather | bytes 663552 | tf_op jit(solution)/shard_map/all_gather | solution.py:915
  334.1 17.0 %settle.1 = (bf16[2048,1280]{1,0:T(8,128)(2,1)}, f32[8,2048]{1,0:T(8,128)}, f32[16,2304]{1,0:T(8,128)}) custom-call(s32[1]{0:T(128)} %bitcast.member_ref, f32[8,8,2304]{2,1,0:T(8,128)} %bitcast.230, f32[8,2048]{1,0:T(8,128)} %concatenate.76.fact_ref, bf16[2048,1024]{1,0:T(8,128)(2,1)} %get-tuple-element.103.head_mix_ref, ...), custom_call_target="tpu_custom_call" | custom-call | flops 9663676416 | bytes 28114944 | tf_op jit(solution)/shard_map/settle/pallas_call | solution.py:594
  359.2 4.9 collective-permute-done.7
  367.6 32.7 %head_grad.1 = bf16[640,1024]{1,0:T(8,128)(2,1)} custom-call(s32[2]{0:T(128)} %pad_add_fusion.5.base_ref, bf16[2560,1024]{1,0:T(8,128)(2,1)} %pad.29.table_ref, bf16[2048,1024]{1,0:T(8,128)(2,1)} %all-gather.6.cloned.1.call-done.rows_ref.refs_0_, f32[4,2048]{1,0:T(4,128)} %copy-done.44, bf16[6144,1024]{1,0:T(8,128)(2,1)} %all-gather.10.cloned.1.call-done.refs_2_, ...), custom_call_target="tpu_custom_call" | custom-call | flops 21474836480 | bytes 18087936 | tf_op jit(solution)/shard_map/head_grad/pallas_call | solution.py:344
  401.6 5.7 collective-permute-start.9
  414.5 8.3 pad_maximum_fusion.3.rows_ref
  422.8 30.4 %band_grad.3 = f32[5000,256]{1,0:T(8,128)} custom-call(s32[187]{0:T(256)} %concatenate.81.plan_ref, bf16[5120,256]{1,0:T(8,128)(2,1)} %pad.30.table_ref, bf16[9216,256]{1,0:T(8,128)(2,1)} %pad_maximum_fusion.3.rows_ref, f32[4,9216]{1,0:T(4,128)} %fusion.48.fact_ref), custom_call_target="tpu_custom_call" | custom-call | flops 24159191040 | bytes 9961472 | tf_op jit(solution)/shard_map/band_grad/pallas_call | solution.py:442
  459.0 7.1 convert_reduce_fusion.2
  467.5 5.8 convolution_convert_fusion.1
  473.6 10.2 %convolution_convert_fusion = bf16[4096,1024]{1,0:T(8,128)(2,1)} fusion(f32[256,1024]{1,0:T(8,128)} %copy-done.19, f32[256]{0:T(256)S(1)} %negate_multiply_fusion.2, f32[256,4096]{1,0:T(8,128)} %copy-done.94), kind=kOutput, calls=%fused_computation.12 | convolution fusion | flops 2161639424 | bytes 13632512 | tf_op jit(solution)/shard_map/dot_general | solution.py:47
  487.0 7.0 multiply_reduce_fusion.5
  498.0 20.5 %collective-permute-done.12 = bf16[640,1024]{1,0:T(8,128)(2,1)} collective-permute-done((bf16[640,1024]{1,0:T(8,128)(2,1)}, bf16[640,1024]{1,0:T(8,128)(2,1)}, u32[]{:S(2)}, u32[]{:S(2)}) %collective-permute-start.12) | collective-permute-done | bytes 1310752 | tf_op jit(solution)/shard_map/ppermute | solution.py:634
  529.9 24.5 %attend_back.1 = (bf16[256,1024]{1,0:T(8,128)(2,1)}, bf16[1024,1024]{1,0:T(8,128)(2,1)}, bf16[1024,1024]{1,0:T(8,128)(2,1)}) custom-call(s32[1]{0:T(128)} %bitcast.2.start_ref, bf16[256,1024]{1,0:T(8,128)(2,1)} %fusion.21.query_ref, bf16[1024,1024]{1,0:T(8,128)(2,1)} %convolution_convert_fusion.2.key_ref, bf16[1024,1024]{1,0:T(8,128)(2,1)} %add_convert_fusion.value_ref, ...), custom_call_target="tpu_custom_call" | custom-call | flops 2684354560 | bytes 7864320 | tf_op jit(solution)/shard_map/attend_back/pallas_call | solution.py:141
  589.1 4.8 fusion.7
  595.9 4.4 collective-permute-start.16
  604.0 18.0 %collective-permute-done.16 = bf16[32,4096]{1,0:T(8,128)(2,1)} collective-permute-done((bf16[32,4096]{1,0:T(8,128)(2,1)}, bf16[32,4096]{1,0:T(8,128)(2,1)}, u32[]{:S(2)}, u32[]{:S(2)}) %collective-permute-start.16) | collective-permute-done | bytes 262176 | tf_op jit(solution)/shard_map/ppermute | solution.py:696
  630.6 29.3 %band_grad.4 = bf16[64,3328]{1,0:T(8,128)(2,1)} custom-call(s32[113]{0:T(128)} %concatenate.87.plan_ref, bf16[26624,128]{1,0:T(8,128)(2,1)} %fusion.6.table_ref, bf16[9216,256]{1,0:T(8,128)(2,1)} %pad_maximum_fusion.3.rows_ref, f32[4,9216]{1,0:T(4,128)} %fusion.48.fact_ref), custom_call_target="tpu_custom_call" | custom-call | flops 15703474176 | bytes 4063232 | tf_op jit(solution)/shard_map/band_grad/pallas_call | solution.py:442
  661.2 4.7 collective-permute-start.24
  670.3 29.4 %band_grad.5 = bf16[64,3328]{1,0:T(8,128)(2,1)} custom-call(s32[113]{0:T(128)} %concatenate.89.plan_ref, bf16[26624,128]{1,0:T(8,128)(2,1)} %fusion.6.table_ref, bf16[9216,256]{1,0:T(8,128)(2,1)} %pad_maximum_fusion.3.rows_ref, f32[4,9216]{1,0:T(4,128)} %fusion.48.fact_ref), custom_call_target="tpu_custom_call" | custom-call | flops 15703474176 | bytes 4063232 | tf_op jit(solution)/shard_map/band_grad/pallas_call | solution.py:442
  701.5 7.2 collective-permute-start.26
  715.5 13.0 %collective-permute-done.27 = bf16[128,1024]{1,0:T(8,128)(2,1)S(1)} collective-permute-done((bf16[128,1024]{1,0:T(8,128)(2,1)S(1)}, bf16[128,1024]{1,0:T(8,128)(2,1)S(1)}, u32[]{:S(2)}, u32[]{:S(2)}) %collective-permute-start.27) | collective-permute-done | bytes 262176 | tf_op jit(solution)/shard_map/ppermute | solution.py:696
  728.7 12.8 %collective-permute-start.30 = (bf16[128,1024]{1,0:T(8,128)(2,1)S(1)}, bf16[128,1024]{1,0:T(8,128)(2,1)S(1)}, u32[]{:S(2)}, u32[]{:S(2)}) collective-permute-start(bf16[128,1024]{1,0:T(8,128)(2,1)S(1)} %fusion.40), channel_id=1, source_target_pairs={{0,16},{8,24},{16,0},{24,8},{1,17},{9,25},{17,1},{25,9},{2,18},{10... | collective-permute-start | bytes 786440 | tf_op jit(solution)/shard_map/ppermute | solution.py:625
  751.6 11.2 %collective-permute-done.30 = bf16[128,1024]{1,0:T(8,128)(2,1)S(1)} collective-permute-done((bf16[128,1024]{1,0:T(8,128)(2,1)S(1)}, bf16[128,1024]{1,0:T(8,128)(2,1)S(1)}, u32[]{:S(2)}, u32[]{:S(2)}) %collective-permute-start.30) | collective-permute-done | bytes 262176 | tf_op jit(solution)/shard_map/ppermute | solution.py:625
  764.1 11.8 %collective-permute-done.33 = bf16[64,3328]{1,0:T(8,128)(2,1)S(1)} collective-permute-done((bf16[64,3328]{1,0:T(8,128)(2,1)S(1)}, bf16[64,3328]{1,0:T(8,128)(2,1)S(1)}, u32[]{:S(2)}, u32[]{:S(2)}) %collective-permute-start.33) | collective-permute-done | bytes 426016 | tf_op jit(solution)/shard_map/ppermute | solution.py:634
  781.6 5.0 collective-permute-done.35
  786.7 8.8 collective-permute-done.39
  798.0 8.2 collective-permute-done.41
  806.9 5.3 copy.140
  812.1 5.5 reshape.770
  817.7 5.2 convert_bitcast_fusion
  822.9 49.2 %all-reduce.10.cloned.1.call-done = bf16[128,4480]{1,0:T(8,128)(2,1)} async-done(((bf16[128,4480]{1,0:T(8,128)(2,1)}), bf16[128,4480]{1,0:T(8,128)(2,1)}) %all-reduce.10.cloned.1.call-update) | async-done | bytes 1146896 | tf_op jit(solution)/shard_map/psum | solution.py:1154
  (514 shorter events, 223.5 us)
Async XLA Ops:
  7.2 157.9 %all-gather.6.cloned.1.call-start = ((), (), s32[]{:S(2)}) async-start(), calls=%async_computation.4 | async-start | bytes 4718592 | tf_op jit(solution)/shard_map/all_gather | solution.py:845
  12.6 50.8 %collective-permute-start = (bf16[256,1024]{1,0:T(8,128)(2,1)}, bf16[256,1024]{1,0:T(8,128)(2,1)}, u32[]{:S(2)}, u32[]{:S(2)}) collective-permute-start(bf16[256,1024]{1,0:T(8,128)(2,1)} %add_convert_fusion.5), channel_id=1, source_target_pairs={{0,24},{1,25},{2,26},{3,27},{4,28},{5,29},{6,30},{7,31}} | collective-permute-start | bytes 1572872 | tf_op jit(solution)/shard_map/ppermute | solution.py:673
  20.4 44.4 %collective-permute-start.1 = (bf16[256,1024]{1,0:T(8,128)(2,1)}, bf16[256,1024]{1,0:T(8,128)(2,1)}, u32[]{:S(2)}, u32[]{:S(2)}) collective-permute-start(bf16[256,1024]{1,0:T(8,128)(2,1)} %add_convert_fusion.5), channel_id=1, source_target_pairs={{0,16},{8,24},{1,17},{9,25},{2,18},{10,26},{3,19},{11,27},{4,20},{... | collective-permute-start | bytes 1572872 | tf_op jit(solution)/shard_map/ppermute | solution.py:673
  22.5 43.4 %collective-permute-start.2 = (bf16[256,1024]{1,0:T(8,128)(2,1)}, bf16[256,1024]{1,0:T(8,128)(2,1)}, u32[]{:S(2)}, u32[]{:S(2)}) collective-permute-start(bf16[256,1024]{1,0:T(8,128)(2,1)} %add_convert_fusion.5), channel_id=1, source_target_pairs={{0,8},{8,16},{16,24},{1,9},{9,17},{17,25},{2,10},{10,18},{18,26},{... | collective-permute-start | bytes 1572872 | tf_op jit(solution)/shard_map/ppermute | solution.py:673
  103.9 99.4 %all-gather.8.cloned.1.call-start = ((), (), s32[]{:S(2)}) async-start(), calls=%async_computation.5 | async-start | bytes 2621440 | tf_op jit(solution)/shard_map/all_gather | solution.py:848
  157.2 157.3 %all-gather.10.cloned.1.call-start = ((), (), s32[]{:S(2)}) async-start(), calls=%async_computation.6 | async-start | bytes 14155776 | tf_op jit(solution)/shard_map/all_gather | solution.py:880
  207.2 204.9 %all-gather.12.cloned.1.call-start = ((), (), s32[]{:S(2)}) async-start(), calls=%async_computation.8 | async-start | bytes 3981312 | tf_op jit(solution)/shard_map/all_gather | solution.py:914
  211.0 101.7 %collective-permute-start.3 = (bf16[288,256]{1,0:T(8,128)(2,1)}, bf16[288,256]{1,0:T(8,128)(2,1)S(1)}, u32[]{:S(2)}, u32[]{:S(2)}) collective-permute-start(bf16[288,256]{1,0:T(8,128)(2,1)} %constant_dynamic-slice_fusion.1), channel_id=1, source_target_pairs={{0,24},{8,0},{16,8},{24,16},{1,25},{9,1},{17,9},{25,17},{2,26},{10... | collective-permute-start | bytes 442376 | tf_op jit(solution)/shard_map/ppermute | solution.py:625
  212.2 100.5 %collective-permute-start.4 = (bf16[288,256]{1,0:T(8,128)(2,1)}, bf16[288,256]{1,0:T(8,128)(2,1)}, u32[]{:S(2)}, u32[]{:S(2)}) collective-permute-start(bf16[288,256]{1,0:T(8,128)(2,1)} %constant_dynamic-slice_fusion.1), channel_id=1, source_target_pairs={{0,16},{8,24},{16,0},{24,8},{1,17},{9,25},{17,1},{25,9},{2,18},{10... | collective-permute-start | bytes 442376 | tf_op jit(solution)/shard_map/ppermute | solution.py:625
  212.3 100.4 %collective-permute-start.5 = (bf16[288,256]{1,0:T(8,128)(2,1)}, bf16[288,256]{1,0:T(8,128)(2,1)}, u32[]{:S(2)}, u32[]{:S(2)}) collective-permute-start(bf16[288,256]{1,0:T(8,128)(2,1)} %constant_dynamic-slice_fusion.1), channel_id=1, source_target_pairs={{0,8},{8,16},{16,24},{24,0},{1,9},{9,17},{17,25},{25,1},{2,10},{10... | collective-permute-start | bytes 442376 | tf_op jit(solution)/shard_map/ppermute | solution.py:625
  314.5 138.7 %reduce-scatter.5.cloned.1.call-start = ((), (), s32[]{:S(2)}) async-start(), calls=%async_computation.7 | async-start | bytes 5898240 | tf_op jit(solution)/shard_map/reduce_scatter | solution.py:931
  356.6 7.5 collective-permute-start.7
  357.3 6.9 collective-permute-start.8
  357.3 236.6 %reduce-scatter.7.cloned.1.call-start = ((), (), s32[]{:S(2)}) async-start(), calls=%async_computation.9 | async-start | bytes 9437184 | tf_op jit(solution)/shard_map/reduce_scatter | solution.py:1034
  400.3 54.3 %collective-permute-start.10 = (bf16[640,1024]{1,0:T(8,128)(2,1)}, bf16[640,1024]{1,0:T(8,128)(2,1)}, u32[]{:S(2)}, u32[]{:S(2)}) collective-permute-start(bf16[640,1024]{1,0:T(8,128)(2,1)} %head_grad.1), channel_id=1, source_target_pairs={{8,0},{16,8},{24,16},{9,1},{17,9},{25,17},{10,2},{18,10},{26,18},{... | collective-permute-start | bytes 3932168 | tf_op jit(solution)/shard_map/ppermute | solution.py:634
  401.6 53.0 %collective-permute-start.9 = (bf16[640,1024]{1,0:T(8,128)(2,1)}, bf16[640,1024]{1,0:T(8,128)(2,1)}, u32[]{:S(2)}, u32[]{:S(2)}) collective-permute-start(bf16[640,1024]{1,0:T(8,128)(2,1)} %head_grad.1), channel_id=1, source_target_pairs={{0,8},{8,16},{16,24},{1,9},{9,17},{17,25},{2,10},{10,18},{18,26},{... | collective-permute-start | bytes 3932168 | tf_op jit(solution)/shard_map/ppermute | solution.py:633
  473.3 187.9 %reduce-scatter.11.cloned.1.call-start = ((), (), s32[]{:S(2)}) async-start(), calls=%async_computation.12 | async-start | bytes 9437184 | tf_op jit(solution)/shard_map/reduce_scatter | solution.py:1028
  483.8 333.9 %reduce-scatter.9.cloned.1.call-start = ((), (), s32[]{:S(2)}) async-start(), calls=%async_computation.10 | async-start | bytes 10321920 | tf_op jit(solution)/shard_map/reduce_scatter | solution.py:1102
  483.9 14.1 %collective-permute-start.11 = (bf16[640,1024]{1,0:T(8,128)(2,1)}, bf16[640,1024]{1,0:T(8,128)(2,1)}, u32[]{:S(2)}, u32[]{:S(2)}) collective-permute-start(bf16[640,1024]{1,0:T(8,128)(2,1)} %collective-permute-done.9), channel_id=1, source_target_pairs={{8,16},{16,24},{9,17},{17,25},{10,18},{18,26},{11,19},{19,27},{12,... | collective-permute-start | bytes 3932168 | tf_op jit(solution)/shard_map/ppermute | solution.py:633
  485.7 32.9 %collective-permute-start.12 = (bf16[640,1024]{1,0:T(8,128)(2,1)}, bf16[640,1024]{1,0:T(8,128)(2,1)}, u32[]{:S(2)}, u32[]{:S(2)}) collective-permute-start(bf16[640,1024]{1,0:T(8,128)(2,1)} %collective-permute-done.10), channel_id=1, source_target_pairs={{8,0},{16,8},{9,1},{17,9},{10,2},{18,10},{11,3},{19,11},{12,4},{20... | collective-permute-start | bytes 3932168 | tf_op jit(solution)/shard_map/ppermute | solution.py:634
  518.5 35.9 %collective-permute-start.13 = (bf16[640,1024]{1,0:T(8,128)(2,1)}, bf16[640,1024]{1,0:T(8,128)(2,1)}, u32[]{:S(2)}, u32[]{:S(2)}) collective-permute-start(bf16[640,1024]{1,0:T(8,128)(2,1)} %collective-permute-done.11), channel_id=1, source_target_pairs={{16,24},{17,25},{18,26},{19,27},{20,28},{21,29},{22,30},{23,31}} | collective-permute-start | bytes 3932168 | tf_op jit(solution)/shard_map/ppermute | solution.py:633
  520.3 34.2 %collective-permute-start.14 = (bf16[640,1024]{1,0:T(8,128)(2,1)}, bf16[640,1024]{1,0:T(8,128)(2,1)}, u32[]{:S(2)}, u32[]{:S(2)}) collective-permute-start(bf16[640,1024]{1,0:T(8,128)(2,1)} %collective-permute-done.12), channel_id=1, source_target_pairs={{8,0},{9,1},{10,2},{11,3},{12,4},{13,5},{14,6},{15,7}} | collective-permute-start | bytes 3932168 | tf_op jit(solution)/shard_map/ppermute | solution.py:634
  595.9 8.1 collective-permute-start.15
  595.9 26.1 %collective-permute-start.16 = (bf16[32,4096]{1,0:T(8,128)(2,1)}, bf16[32,4096]{1,0:T(8,128)(2,1)}, u32[]{:S(2)}, u32[]{:S(2)}) collective-permute-start(bf16[32,4096]{1,0:T(8,128)(2,1)} %get-tuple-element.220), channel_id=1, source_target_pairs={{0,16},{8,24},{16,0},{24,8},{1,17},{9,25},{17,1},{25,9},{2,18},{10... | collective-permute-start | bytes 786440 | tf_op jit(solution)/shard_map/ppermute | solution.py:696
  600.3 21.7 %collective-permute-start.17 = (bf16[32,4096]{1,0:T(8,128)(2,1)}, bf16[32,4096]{1,0:T(8,128)(2,1)}, u32[]{:S(2)}, u32[]{:S(2)}) collective-permute-start(bf16[32,4096]{1,0:T(8,128)(2,1)} %get-tuple-element.219), channel_id=1, source_target_pairs={{0,8},{8,16},{16,24},{24,0},{1,9},{9,17},{17,25},{25,1},{2,10},{10... | collective-permute-start | bytes 786440 | tf_op jit(solution)/shard_map/ppermute | solution.py:696
  623.3 36.6 %collective-permute-start.21 = (bf16[32,4096]{1,0:T(8,128)(2,1)S(1)}, bf16[32,4096]{1,0:T(8,128)(2,1)}, u32[]{:S(2)}, u32[]{:S(2)}) collective-permute-start(bf16[32,4096]{1,0:T(8,128)(2,1)S(1)} %fusion.43), channel_id=1, source_target_pairs={{0,24},{8,0},{16,8},{24,16},{1,25},{9,1},{17,9},{25,17},{2,26},{10... | collective-permute-start | bytes 786440 | tf_op jit(solution)/shard_map/ppermute | solution.py:625
  623.4 37.8 %collective-permute-start.22 = (bf16[32,4096]{1,0:T(8,128)(2,1)S(1)}, bf16[32,4096]{1,0:T(8,128)(2,1)}, u32[]{:S(2)}, u32[]{:S(2)}) collective-permute-start(bf16[32,4096]{1,0:T(8,128)(2,1)S(1)} %fusion.43), channel_id=1, source_target_pairs={{0,16},{8,24},{16,0},{24,8},{1,17},{9,25},{17,1},{25,9},{2,18},{10... | collective-permute-start | bytes 786440 | tf_op jit(solution)/shard_map/ppermute | solution.py:625
  623.5 37.7 %collective-permute-start.23 = (bf16[32,4096]{1,0:T(8,128)(2,1)S(1)}, bf16[32,4096]{1,0:T(8,128)(2,1)}, u32[]{:S(2)}, u32[]{:S(2)}) collective-permute-start(bf16[32,4096]{1,0:T(8,128)(2,1)S(1)} %fusion.43), channel_id=1, source_target_pairs={{0,8},{8,16},{16,24},{24,0},{1,9},{9,17},{17,25},{25,1},{2,10},{10... | collective-permute-start | bytes 786440 | tf_op jit(solution)/shard_map/ppermute | solution.py:625
  627.9 73.5 %collective-permute-start.18 = (bf16[256,1024]{1,0:T(8,128)(2,1)}, bf16[256,1024]{1,0:T(8,128)(2,1)}, u32[]{:S(2)}, u32[]{:S(2)}) collective-permute-start(bf16[256,1024]{1,0:T(8,128)(2,1)} %get-tuple-element.203), channel_id=1, source_target_pairs={{8,0},{16,8},{24,16},{9,1},{17,9},{25,17},{10,2},{18,10},{26,18},{... | collective-permute-start | bytes 1572872 | tf_op jit(solution)/shard_map/ppermute | solution.py:696
  629.2 79.5 %collective-permute-start.19 = (bf16[256,1024]{1,0:T(8,128)(2,1)}, bf16[256,1024]{1,0:T(8,128)(2,1)}, u32[]{:S(2)}, u32[]{:S(2)}) collective-permute-start(bf16[256,1024]{1,0:T(8,128)(2,1)} %get-tuple-element.205), channel_id=1, source_target_pairs={{16,0},{24,8},{17,1},{25,9},{18,2},{26,10},{19,3},{27,11},{20,4},{... | collective-permute-start | bytes 1572872 | tf_op jit(solution)/shard_map/ppermute | solution.py:696
  630.5 241.5 %all-reduce.10.cloned.1.call-start = ((), (), s32[]{:S(2)}) async-start(), calls=%async_computation.11 | async-start | bytes 2293760 | tf_op jit(solution)/shard_map/psum | solution.py:1154
  659.9 48.8 %collective-permute-start.20 = (bf16[256,1024]{1,0:T(8,128)(2,1)}, bf16[256,1024]{1,0:T(8,128)(2,1)}, u32[]{:S(2)}, u32[]{:S(2)}) collective-permute-start(bf16[256,1024]{1,0:T(8,128)(2,1)} %get-tuple-element.204), channel_id=1, source_target_pairs={{24,0},{25,1},{26,2},{27,3},{28,4},{29,5},{30,6},{31,7}} | collective-permute-start | bytes 1572872 | tf_op jit(solution)/shard_map/ppermute | solution.py:696
  661.2 67.4 %collective-permute-start.24 = (bf16[64,3328]{1,0:T(8,128)(2,1)}, bf16[64,3328]{1,0:T(8,128)(2,1)S(1)}, u32[]{:S(2)}, u32[]{:S(2)}) collective-permute-start(bf16[64,3328]{1,0:T(8,128)(2,1)} %band_grad.4), channel_id=1, source_target_pairs={{0,8},{8,16},{16,24},{1,9},{9,17},{17,25},{2,10},{10,18},{18,26},{... | collective-permute-start | bytes 1277960 | tf_op jit(solution)/shard_map/ppermute | solution.py:633
  666.0 62.7 %collective-permute-start.25 = (bf16[64,3328]{1,0:T(8,128)(2,1)}, bf16[64,3328]{1,0:T(8,128)(2,1)S(1)}, u32[]{:S(2)}, u32[]{:S(2)}) collective-permute-start(bf16[64,3328]{1,0:T(8,128)(2,1)} %band_grad.4), channel_id=1, source_target_pairs={{8,0},{16,8},{24,16},{9,1},{17,9},{25,17},{10,2},{18,10},{26,18},{... | collective-permute-start | bytes 1277960 | tf_op jit(solution)/shard_map/ppermute | solution.py:634
  701.5 14.0 %collective-permute-start.26 = (bf16[128,1024]{1,0:T(8,128)(2,1)S(1)}, bf16[128,1024]{1,0:T(8,128)(2,1)S(1)}, u32[]{:S(2)}, u32[]{:S(2)}) collective-permute-start(bf16[128,1024]{1,0:T(8,128)(2,1)S(1)} %get-tuple-element.215), channel_id=1, source_target_pairs={{0,24},{8,0},{16,8},{24,16},{1,25},{9,1},{17,9},{25,17},{2,26},{10... | collective-permute-start | bytes 786440 | tf_op jit(solution)/shard_map/ppermute | solution.py:696
  708.7 19.8 %collective-permute-start.27 = (bf16[128,1024]{1,0:T(8,128)(2,1)S(1)}, bf16[128,1024]{1,0:T(8,128)(2,1)S(1)}, u32[]{:S(2)}, u32[]{:S(2)}) collective-permute-start(bf16[128,1024]{1,0:T(8,128)(2,1)S(1)} %get-tuple-element.217), channel_id=1, source_target_pairs={{0,16},{8,24},{16,0},{24,8},{1,17},{9,25},{17,1},{25,9},{2,18},{10... | collective-permute-start | bytes 786440 | tf_op jit(solution)/shard_map/ppermute | solution.py:696
  708.7 19.8 %collective-permute-start.28 = (bf16[128,1024]{1,0:T(8,128)(2,1)S(1)}, bf16[128,1024]{1,0:T(8,128)(2,1)S(1)}, u32[]{:S(2)}, u32[]{:S(2)}) collective-permute-start(bf16[128,1024]{1,0:T(8,128)(2,1)S(1)} %get-tuple-element.216), channel_id=1, source_target_pairs={{0,8},{8,16},{16,24},{24,0},{1,9},{9,17},{17,25},{25,1},{2,10},{10... | collective-permute-start | bytes 786440 | tf_op jit(solution)/shard_map/ppermute | solution.py:696
  728.7 22.2 %collective-permute-start.29 = (bf16[128,1024]{1,0:T(8,128)(2,1)S(1)}, bf16[128,1024]{1,0:T(8,128)(2,1)S(1)}, u32[]{:S(2)}, u32[]{:S(2)}) collective-permute-start(bf16[128,1024]{1,0:T(8,128)(2,1)S(1)} %fusion.40), channel_id=1, source_target_pairs={{0,24},{8,0},{16,8},{24,16},{1,25},{9,1},{17,9},{25,17},{2,26},{10... | collective-permute-start | bytes 786440 | tf_op jit(solution)/shard_map/ppermute | solution.py:625
  728.7 34.0 %collective-permute-start.30 = (bf16[128,1024]{1,0:T(8,128)(2,1)S(1)}, bf16[128,1024]{1,0:T(8,128)(2,1)S(1)}, u32[]{:S(2)}, u32[]{:S(2)}) collective-permute-start(bf16[128,1024]{1,0:T(8,128)(2,1)S(1)} %fusion.40), channel_id=1, source_target_pairs={{0,16},{8,24},{16,0},{24,8},{1,17},{9,25},{17,1},{25,9},{2,18},{10... | collective-permute-start | bytes 786440 | tf_op jit(solution)/shard_map/ppermute | solution.py:625
  742.7 35.2 %collective-permute-start.36 = (bf16[64,3328]{1,0:T(8,128)(2,1)S(1)}, bf16[64,3328]{1,0:T(8,128)(2,1)S(1)}, u32[]{:S(2)}, u32[]{:S(2)}) collective-permute-start(bf16[64,3328]{1,0:T(8,128)(2,1)S(1)} %copy-done.41), channel_id=1, source_target_pairs={{0,8},{8,16},{16,24},{1,9},{9,17},{17,25},{2,10},{10,18},{18,26},{... | collective-permute-start | bytes 1277960 | tf_op jit(solution)/shard_map/ppermute | solution.py:633
  746.7 31.2 %collective-permute-start.37 = (bf16[64,3328]{1,0:T(8,128)(2,1)S(1)}, bf16[64,3328]{1,0:T(8,128)(2,1)S(1)}, u32[]{:S(2)}, u32[]{:S(2)}) collective-permute-start(bf16[64,3328]{1,0:T(8,128)(2,1)S(1)} %copy-done.41), channel_id=1, source_target_pairs={{8,0},{16,8},{24,16},{9,1},{17,9},{25,17},{10,2},{18,10},{26,18},{... | collective-permute-start | bytes 1277960 | tf_op jit(solution)/shard_map/ppermute | solution.py:634
  748.0 31.9 %collective-permute-start.31 = (bf16[128,1024]{1,0:T(8,128)(2,1)S(1)}, bf16[128,1024]{1,0:T(8,128)(2,1)S(1)}, u32[]{:S(2)}, u32[]{:S(2)}) collective-permute-start(bf16[128,1024]{1,0:T(8,128)(2,1)S(1)} %fusion.40), channel_id=1, source_target_pairs={{0,8},{8,16},{16,24},{24,0},{1,9},{9,17},{17,25},{25,1},{2,10},{10... | collective-permute-start | bytes 786440 | tf_op jit(solution)/shard_map/ppermute | solution.py:625
  750.9 13.2 %collective-permute-start.32 = (bf16[64,3328]{1,0:T(8,128)(2,1)S(1)}, bf16[64,3328]{1,0:T(8,128)(2,1)S(1)}, u32[]{:S(2)}, u32[]{:S(2)}) collective-permute-start(bf16[64,3328]{1,0:T(8,128)(2,1)S(1)} %collective-permute-done.24), channel_id=1, source_target_pairs={{8,16},{16,24},{9,17},{17,25},{10,18},{18,26},{11,19},{19,27},{12,... | collective-permute-start | bytes 1277960 | tf_op jit(solution)/shard_map/ppermute | solution.py:633
  762.8 13.2 %collective-permute-start.33 = (bf16[64,3328]{1,0:T(8,128)(2,1)S(1)}, bf16[64,3328]{1,0:T(8,128)(2,1)S(1)}, u32[]{:S(2)}, u32[]{:S(2)}) collective-permute-start(bf16[64,3328]{1,0:T(8,128)(2,1)S(1)} %collective-permute-done.25), channel_id=1, source_target_pairs={{8,0},{16,8},{9,1},{17,9},{10,2},{18,10},{11,3},{19,11},{12,4},{20... | collective-permute-start | bytes 1277960 | tf_op jit(solution)/shard_map/ppermute | solution.py:634
  776.6 10.0 %collective-permute-start.35 = (bf16[64,3328]{1,0:T(8,128)(2,1)S(1)}, bf16[64,3328]{1,0:T(8,128)(2,1)S(1)}, u32[]{:S(2)}, u32[]{:S(2)}) collective-permute-start(bf16[64,3328]{1,0:T(8,128)(2,1)S(1)} %collective-permute-done.33), channel_id=1, source_target_pairs={{8,0},{9,1},{10,2},{11,3},{12,4},{13,5},{14,6},{15,7}} | collective-permute-start | bytes 1277960 | tf_op jit(solution)/shard_map/ppermute | solution.py:634
  778.0 8.7 collective-permute-start.38
  778.7 16.8 %collective-permute-start.39 = (bf16[64,3328]{1,0:T(8,128)(2,1)S(1)}, bf16[64,3328]{1,0:T(8,128)(2,1)S(1)}, u32[]{:S(2)}, u32[]{:S(2)}) collective-permute-start(bf16[64,3328]{1,0:T(8,128)(2,1)S(1)} %collective-permute-done.37), channel_id=1, source_target_pairs={{8,0},{16,8},{9,1},{17,9},{10,2},{18,10},{11,3},{19,11},{12,4},{20... | collective-permute-start | bytes 1277960 | tf_op jit(solution)/shard_map/ppermute | solution.py:634
  796.2 10.0 %collective-permute-start.41 = (bf16[64,3328]{1,0:T(8,128)(2,1)S(1)}, bf16[64,3328]{1,0:T(8,128)(2,1)S(1)}, u32[]{:S(2)}, u32[]{:S(2)}) collective-permute-start(bf16[64,3328]{1,0:T(8,128)(2,1)S(1)} %collective-permute-done.39), channel_id=1, source_target_pairs={{8,0},{9,1},{10,2},{11,3},{12,4},{13,5},{14,6},{15,7}} | collective-permute-start | bytes 1277960 | tf_op jit(solution)/shard_map/ppermute | solution.py:634
  (104 other events, 1193.0 us)
Sparse Core Ops, SparseCore 0:
  104.0 36.6 all-gather.5
  157.4 45.9 all-gather.7
  207.3 70.8 all-gather.9
  314.6 36.6 all-gather.11
  357.4 56.9 reduce-scatter.4
  473.4 70.0 reduce-scatter.6
  547.0 71.2 reduce-scatter.10
  630.7 80.3 reduce-scatter.8
  817.8 54.2 all-reduce.9

commit v5 on v4

--- a/solution.py
+++ b/solution.py
@@ -650,7 +650,7 @@
     return found, advance
 
 
-def line_ordered(found, axis):
+def line_ordered(found):
     size, place = lax.axis_size("seq"), lax.axis_index("seq")
     ordered = []
     for source in range(size):
@@ -661,7 +661,7 @@
             if source - step >= 0:
                 value = jnp.where(place == source - step, found[step][1], value)
         ordered.append(value)
-    return jnp.concatenate(ordered, axis)
+    return ordered
 
 
 def earlier_joined(value):
@@ -695,6 +695,28 @@
         pairs = [(d, (d - k) % size) for d in range(0 if behind else k, size)]
         total = total + lax.ppermute(part(place + size - k), "seq", pairs).astype(jnp.float32)
     return total
+
+
+def batch_halves(values, bit):
+    member, size = lax.axis_index("batch"), lax.axis_size("batch")
+    blocks, bits_left = values
+    axis = bits_left.index(bit)
+    mine = (member >> bit) & 1
+    got = lax.ppermute(
+        lax.dynamic_index_in_dim(blocks, 1 - mine, axis, False),
+        "batch",
+        [(d, d ^ (1 << bit)) for d in range(size)],
+    )
+    kept = lax.dynamic_index_in_dim(blocks, mine, axis, False)
+    total = lowered(kept.astype(jnp.float32) + got.astype(jnp.float32))
+    return total, bits_left[:axis] + bits_left[axis + 1 :]
+
+
+def batch_blocks(values):
+    size = lax.axis_size("batch")
+    bits = size.bit_length() - 1
+    assert size == 1 << bits
+    return values.reshape((2,) * bits + (-1,) + values.shape[1:]), list(range(bits - 1, -1, -1))
 
 
 def turn_kernel(rows_ref, out_ref):
@@ -846,9 +868,10 @@
     split = 2 * nz * group_count * feature_count <= 24 << 20
     if split:
         block_states = lax.all_gather(state_low, "seq", axis=0, tiled=True)
-    all_states, head_pad, middle_pad, tail_pad, hit_rows, slot, early = lax.optimization_barrier(
-        (all_states, head_pad, middle_pad, tail_pad, hit_rows, slot, early)
-    )
+    all_states, head_pad, middle_pad, tail_pad, tail_hits, slot, early = lax.optimization_barrier(
+        (all_states, head_pad, middle_pad, tail_pad, hit_rows[2], slot, early)
+    )
+    hit_rows = hit_rows[:2] + (tail_hits,)
 
     middle_width = middle_map.shape[1]
     maps = jnp.pad(jnp.concatenate([middle_map, tail_map], 1), ((0, 0), (0, 128 - tail_width)))
@@ -870,7 +893,9 @@
         piece = slot_count // nb
         slot_piece = lax.dynamic_slice_in_dim(slot_low, member * piece, piece, 0)
         other_slots = jnp.concatenate(line_turns(slot_piece)[1:], 0)
-        slot_low, block_states = lax.optimization_barrier((slot_low, block_states))
+        slot_low, block_states, hit_rows = lax.optimization_barrier(
+            (slot_low, block_states, hit_rows)
+        )
         other_states = lax.dynamic_slice_in_dim(
             jnp.concatenate([block_states, block_states], 0),
             (place + 1) * token_count,
@@ -974,29 +999,9 @@
     facts = jnp.concatenate(
         [facts[:2], jnp.where(facts[3:4] > 0, facts[2:3], -1e9), jnp.zeros_like(facts[:1])], 0
     )
-    middle_result = jax.ShapeDtypeStruct(
-        (sizes[1], middle_width) if split else (middle_padded, middle_width),
-        jnp.float32 if split else jnp.bfloat16,
-    )
-    middle_part = band_grad(
-        middle_pad,
-        rows_all,
-        facts,
-        block_kind == 1,
-        lowest,
-        highest,
-        0 * place,
-        middle_padded,
-        HEAD_WORDS + member * sizes[1],
-        middle_chunk,
-        middle_result,
-        False,
-    )
+    own_terms, head_part = lax.optimization_barrier((own_terms, head_part))
     if split:
         head_found, head_advance = line_steps(head_part)
-        own_terms, middle_part = head_advance(own_terms, middle_part)
-    else:
-        own_terms, middle_part = lax.optimization_barrier((own_terms, middle_part))
 
     own_middle = own_part(in_middle)
     own_tail = own_part(in_tail)
@@ -1048,8 +1053,7 @@
         query_start, queries, key_rows, value_rows, attended_grad
     )
     if split:
-        for unused in range(nz - 3):
-            query_low, key_low, value_low = head_advance(query_low, key_low, value_low)
+        query_low, key_low, value_low = head_advance(query_low, key_low, value_low)
     query_weight_grad = product_tn(normed_low, query_low)
     key_weight_grad = product_tn(normed_all, key_low)
     value_weight_grad = product_tn(normed_all, value_low)
@@ -1093,14 +1097,18 @@
         middle_map_grad,
         turned(jnp.concatenate(rows, 0), jnp.bfloat16),
     ]
-    rest = jnp.concatenate([lowered(column) for column in columns], 1)
+    spread_low = lowered(spread)
+    rests = [
+        jnp.concatenate([lowered(column) for column in group], 1)
+        for group in (columns[:2], columns[2:])
+    ]
+    rests, facts, spread_low = lax.optimization_barrier((rests, facts, spread_low))
+    rests = [batch_halves(batch_blocks(value), 0) for value in rests]
+    bits = rests[0][1]
+    values, facts = lax.optimization_barrier(([value for value, left in rests], facts))
+    rests = [(value, bits) for value in values]
+    orders = (bits, bits[::-1])
     inner_low = lowered(line_scatter(inner_part))
-    spread_low = lowered(spread)
-    rest, facts, inner_low, spread_low = lax.optimization_barrier(
-        (rest, facts, inner_low, spread_low)
-    )
-    rest_part = lax.psum_scatter(rest, "batch", scatter_dimension=0, tiled=True)
-    inner_pieces = line_turns(inner_low)
 
     def tail_gradient(part, parts):
         return band_grad(
@@ -1118,31 +1126,64 @@
             True,
         )
 
+    first_tail = tail_gradient(2 * part, 2 * parts)
+    for step in range(len(bits)):
+        rests = [batch_halves(value, order[step]) for value, order in zip(rests, orders)]
+        if step == 0:
+            values = [value for value, left in rests]
+            if split:
+                for unused in range(nz - 3):
+                    (first_tail,) = head_advance(first_tail)
+            values, first_tail, facts = lax.optimization_barrier((values, first_tail, facts))
+            rests = [(value, left) for value, (unused, left) in zip(values, rests)]
+    rest_parts, facts = lax.optimization_barrier(([value for value, left in rests], facts))
+    rest_lows = [lax.psum(value, "seq") for value in rest_parts]
+    second_tail = tail_gradient(2 * part + 1, 2 * parts)
     if split:
-        middle_table_grad = middle_part
-        head_table_grad = line_ordered(head_found, 0)
-        first_tail = tail_gradient(2 * place, 2 * nz)
-        first_tail, facts, inner_pieces, outer_part = lax.optimization_barrier(
-            (first_tail, facts, inner_pieces, outer_part)
+        first_found, first_advance = line_steps(first_tail)
+        second_tail, inner_low, outer_part, facts, spread_low = first_advance(
+            second_tail, inner_low, outer_part, facts, spread_low
         )
-        first_found, first_advance = line_steps(first_tail)
-        second_tail = tail_gradient(2 * place + 1, 2 * nz)
-        outer_low = lowered(line_scatter(outer_part))
-        second_tail, outer_low = first_advance(second_tail, outer_low)
+    inner_pieces = line_turns(inner_low)
+    outer_low = lowered(line_scatter(outer_part))
+    middle_result = jax.ShapeDtypeStruct(
+        (sizes[1], middle_width) if split else (middle_padded, middle_width),
+        jnp.float32 if split else jnp.bfloat16,
+    )
+    middle_part = band_grad(
+        middle_pad,
+        rows_all,
+        facts,
+        block_kind == 1,
+        lowest,
+        highest,
+        0 * place,
+        middle_padded,
+        HEAD_WORDS + member * sizes[1],
+        middle_chunk,
+        middle_result,
+        False,
+    )
+    if split:
         second_found, second_advance = line_steps(second_tail)
+        middle_part, outer_low, inner_pieces, rest_lows = second_advance(
+            middle_part, outer_low, inner_pieces, rest_lows
+        )
         for unused in range(nz - 1):
             first_advance()
             second_advance()
-        halves = [
-            line_ordered(found, 0).reshape(nz, tail_width, -1)
-            for found in (first_found, second_found)
+        middle_table_grad = middle_part
+        head_table_grad = jnp.concatenate(line_ordered(head_found), 0)
+        tail_sum = [
+            value
+            for pair in zip(line_ordered(first_found), line_ordered(second_found))
+            for value in pair
         ]
-        tail_sum = jnp.stack(halves, 1).transpose(2, 0, 1, 3).reshape(tail_width, -1)
+        tail_sum = jnp.concatenate(tail_sum, 1)
     else:
-        outer_low = lowered(line_scatter(outer_part))
         middle_table_grad = lax.psum(middle_part, "seq")[: sizes[1]].astype(jnp.float32)
         head_table_grad = lax.psum(head_part, "seq")
-        tail_sum = lax.psum(tail_gradient(part, parts), "seq")
+        tail_sum = lax.psum(jnp.concatenate([first_tail, second_tail], 1), "seq")
     head_table_grad = head_table_grad[: sizes[0]].astype(jnp.float32)
     tail_table_grad = tail_sum[:, : sizes[2]].astype(jnp.float32).T
     normed_grad = query_spread + line_scatter(spread_low, False)
@@ -1151,11 +1192,14 @@
 
     inner_sum = in_order(inner_pieces).astype(jnp.float32)
     outer_sum = in_order(line_turns(outer_low)).astype(jnp.float32)
-    rest_low = lax.psum(rest_part, "seq")
-    rest_sum = rest_low[:, : 4 * feature_count + middle_width].astype(jnp.float32)
-    cut = [rest_sum[:, i * feature_count : (i + 1) * feature_count] for i in range(4)]
-    middle_map_sum = rest_sum[:, 4 * feature_count : 4 * feature_count + middle_width]
-    row_sum = turned(rest_low[:, 4 * feature_count + middle_width :], jnp.float32)
+    edge = 2 * feature_count
+    cut = [
+        low[:, start : start + feature_count].astype(jnp.float32)
+        for low in rest_lows
+        for start in (0, feature_count)
+    ]
+    middle_map_sum = rest_lows[1][:, edge : edge + middle_width].astype(jnp.float32)
+    row_sum = turned(rest_lows[1][:, edge + middle_width :], jnp.float32)
     tail_map_sum, cluster_sum, inner_bias_sum = (
         row_sum[low:high] for low, high in zip(edges[:3], edges[1:4])
     )

time: 907 us -> 977 us (1.077)
  starting transfers between devices: 85.3 us -> 151 us
  waiting for transfers between devices: 176 us -> 126 us
  local copies, waits for them, and re-layouts: 112 us -> 154 us
  other arithmetic: 104 us -> 137 us
    psum x1, waiting for transfers between devices: 49.2 us -> 0.02 us  [on_device(): rest_lows = [lax.psum(value, 'seq') for value in rest_parts]]
    ppermute x12, starting transfers between devices: 23.9 us -> 66.2 us  [line_turns(): lax.ppermute(value, 'seq', [(d, (d - k) % size) for d in range(size)])]
    dynamic_slice x0 -> x4, local copies, waits for them, and re-layouts: none -> 27.7 us  [the longest x2 15.5 us: batch_halves(): kept = lax.dynamic_index_in_dim(blocks, mine, axis, False)]
    ppermute x0 -> x6, waiting for transfers between devices: none -> 21.8 us  [batch_halves(): lax.ppermute(lax.dynamic_index_in_dim(blocks, 1 - mine, axis, False), 'ba...]
    ppermute x9, waiting for transfers between devices: 54.3 us -> 33.5 us  [line_step(): lax.ppermute(behind, 'seq', [(d, d - 1) for d in range(1, size - step + 1)])]
    concatenate x2 -> x4, other arithmetic: 0.23 us -> 18.8 us  [the longest x2 18.5 us: on_device(): jnp.concatenate([lowered(column) for column in group], 1)]
    all_gather x1, starting transfers between devices: 0.04 us -> 12.4 us  [on_device(): other_states = lax.all_gather(other_states, 'batch', axis=0, tiled=True)]
    unnamed x202 -> x231, local copies, waits for them, and re-layouts: 15.1 us -> 26.8 us
  transfers between devices with their start and end apart: 51 -> 56, of which waited for: 14 -> 14; matrix products, arithmetic and copies ran while one was open for 27% -> 34% of each run, Pallas kernels for 30% -> 25%
where the time goes in v5:
time: 977 us; the launch traced here: 963 us
  Pallas kernels  272 us (28%)
  local copies, waits for them, and re-layouts  154 us (16%)
  starting transfers between devices  151 us (15%)
  other arithmetic  137 us (14%)
  waiting for transfers between devices  126 us (13%)
  matrix products  83 us (8%)
  blocking collectives  20.6 us (2%)
  between operations  19.4 us (2%)
    pallas_call x3, Pallas kernels, band_grad(): pl.pallas_call(functools.partial(band_grad_kernel, chunk // 2 if chunk >...  87.6 us
    pallas_call x3, Pallas kernels, band_forward(): pl.pallas_call(functools.partial(band_kernel, chunk, per, words, sum_colu...  83.5 us
    ppermute x12, starting transfers between devices, line_turns(): lax.ppermute(value, 'seq', [(d, (d - k) % size) for d in range(size)])  66.2 us
    gather x3, local copies, waits for them, and re-layouts, on_device(): jnp.take(table, jnp.clip(local, 0, size - 1), axis=0, mode='clip')  34.4 us
    ppermute x9, waiting for transfers between devices, line_step(): lax.ppermute(behind, 'seq', [(d, d - 1) for d in range(1, size - step + 1)])  33.5 us
    pallas_call x1, Pallas kernels, head_grad(): pl.pallas_call(functools.partial(head_grad_kernel, chunk, len(lists)), gr...  32 us
    dot_general x9, matrix products, product_tn(): lax.dot_general(former, latter, (((0,), (0,)), ((), ())), preferred_eleme...  28.8 us
    dot_general x10, matrix products, product_nt(): lax.dot_general(former, latter, (((1,), (1,)), ((), ())), preferred_eleme...  27.5 us
  transfers between devices with their start and end apart: 56, of which 14 were waited for; matrix products, arithmetic and copies ran while one was open for 34% of the time, Pallas kernels for 25%

profile of v5, /device:TPU:0, one launch (start us, length us, event | category | flops | bytes accessed | tf_op | source)
XLA Modules:
  0.0 962.9 jit_solution(2308949707709179893)
XLA Ops:
  12.6 7.8 collective-permute-start
  26.7 9.1 all_gather.22
  47.3 7.4 copy.120
  55.8 5.5 pad.29.table_ref
  74.5 15.1 %attend.1 = bf16[256,1024]{1,0:T(8,128)(2,1)} custom-call(s32[1]{0:T(128)} %bitcast.2.start_ref, bf16[256,1024]{1,0:T(8,128)(2,1)} %fusion.24.query_ref, bf16[1024,1024]{1,0:T(8,128)(2,1)} %convolution_convert_fusion.6.key_ref, bf16[1024,1024]{1,0:T(8,128)(2,1)} %add_convert_fusion.value_ref), custom_call_target="tpu_custom_call" | custom-call | flops 1073741824 | bytes 5242880 | tf_op jit(solution)/shard_map/attend/pallas_call | solution.py:92
  92.1 6.0 convolution_add_fusion
  103.7 11.3 %fusion.6.table_ref = bf16[26624,128]{1,0:T(8,128)(2,1)} fusion(bf16[64,25967]{0,1:T(8,128)(2,1)} %bitcast.246, bf16[1,26624]{0,1:T(8,128)(2,1)} %select_convert_fusion, bf16[128]{0:T(256)(128)(2,1)S(1)} %copy-done.98, bf16[128]{0:T(256)(128)(2,1)S(1)} %copy-done.99), kind=kLoop, calls=%fused_computation.17 | loop fusion | flops 34078720 | bytes 10193280 | tf_op jit(solution)/shard_map/transpose | solution.py:838
  115.1 11.5 %gather_fusion = bf16[2048,128]{1,0:T(8,128)(2,1)} fusion(bf16[26624,128]{1,0:T(8,128)(2,1)} %fusion.6.table_ref, s32[2048]{0:T(1024)S(1)} %copy-done.59), kind=kCustom, calls=%fused_computation | custom fusion | bytes 1056768 | tf_op jit(solution)/shard_map/jit(_take)/gather | solution.py:851
  126.7 14.1 %gather_fusion.1 = bf16[2048,1024]{1,0:T(8,128)(2,1)} fusion(bf16[2560,1024]{1,0:T(8,128)(2,1)} %pad.29.table_ref, s32[2048]{0:T(1024)S(1)} %get-tuple-element.291), kind=kCustom, calls=%fused_computation.1 | custom fusion | bytes 8396800 | tf_op jit(solution)/shard_map/jit(_take)/gather | solution.py:851
  140.8 8.7 gather_fusion.2
  156.1 12.4 %all-gather.10.cloned.1.call-start = ((), (), s32[]{:S(2)}) async-start(), calls=%async_computation.5 | async-start | bytes 14155776 | tf_op jit(solution)/shard_map/all_gather | solution.py:905
  175.8 5.7 add_convert_fusion.1.rows_ref
  181.5 8.6 pick_rows.1
  193.5 8.7 all-gather.8.cloned.1.call-done
  213.0 31.0 %band_forward.3 = (f32[8,2048]{1,0:T(8,128)}, bf16[2048,1024]{1,0:T(8,128)(2,1)}) custom-call(s32[2]{0:T(128)} %iota_multiply_fusion.1.span_ref, bf16[2048,1024]{1,0:T(8,128)(2,1)} %all-gather.6.cloned.1.call-done.rows_ref.refs_0_, bf16[2560,1024]{1,0:T(8,128)(2,1)} %pad.29.table_ref), custom_call_target="tpu_custom_call" | custom-call | flops 21474836480 | bytes 17825792 | tf_op jit(solution)/shard_map/band_forward/pallas_call | solution.py:279
  251.5 11.7 %band_forward.5 = (f32[8,2304]{1,0:T(8,128)}, bf16[2304,256]{1,0:T(8,128)(2,1)}) custom-call(s32[2]{0:T(128)} %pad_add_fusion.4.span_ref, bf16[2304,256]{1,0:T(8,128)(2,1)} %copy-done.17, bf16[5120,256]{1,0:T(8,128)(2,1)} %pad.30.table_ref), custom_call_target="tpu_custom_call" | custom-call | flops 3019898880 | bytes 6160384 | tf_op jit(solution)/shard_map/band_forward/pallas_call | solution.py:279
  263.2 40.8 %band_forward.4 = (f32[8,2304]{1,0:T(8,128)}, bf16[2304,128]{1,0:T(8,128)(2,1)}) custom-call(s32[2]{0:T(128)} %pad_add_fusion.3.span_ref, bf16[2304,256]{1,0:T(8,128)(2,1)} %copy-done.17, bf16[26624,128]{1,0:T(8,128)(2,1)} %fusion.6.table_ref), custom_call_target="tpu_custom_call" | custom-call | flops 31406948352 | bytes 8585216 | tf_op jit(solution)/shard_map/band_forward/pallas_call | solution.py:279
  308.8 11.5 %all-gather = f32[64,2304]{1,0:T(8,128)} all-gather(f32[8,2304]{1,0:T(8,128)S(1)} %maximum_maximum_fusion), channel_id=2, replica_groups=mesh['seq'=4,'batch'=8] {'batch'}, dimensions={0}, use_global_device_ids=true | all-gather | bytes 663552 | tf_op jit(solution)/shard_map/all_gather | solution.py:940
  320.4 17.0 %settle.1 = (bf16[2048,1280]{1,0:T(8,128)(2,1)}, f32[8,2048]{1,0:T(8,128)}, f32[16,2304]{1,0:T(8,128)}) custom-call(s32[1]{0:T(128)} %bitcast.member_ref, f32[8,8,2304]{2,1,0:T(8,128)} %bitcast.261, f32[8,2048]{1,0:T(8,128)} %concatenate.76.fact_ref, bf16[2048,1024]{1,0:T(8,128)(2,1)} %get-tuple-element.120.head_mix_ref, ...), custom_call_target="tpu_custom_call" | custom-call | flops 9663676416 | bytes 28114944 | tf_op jit(solution)/shard_map/settle/pallas_call | solution.py:594
  340.7 9.7 %collective-permute-start.6 = (f32[4,4352]{1,0:T(4,128)S(1)}, f32[4,4352]{1,0:T(4,128)S(1)}, u32[]{:S(2)}, u32[]{:S(2)}) collective-permute-start(f32[4,4352]{1,0:T(4,128)S(1)} %pad_maximum_fusion.9), channel_id=1, source_target_pairs={{0,24},{8,0},{16,8},{24,16},{1,25},{9,1},{17,9},{25,17},{2,26},{10... | collective-permute-start | bytes 208904 | tf_op jit(solution)/shard_map/ppermute | solution.py:625
  359.1 32.0 %head_grad.1 = bf16[640,1024]{1,0:T(8,128)(2,1)} custom-call(s32[2]{0:T(128)} %pad_add_fusion.5.base_ref, bf16[2560,1024]{1,0:T(8,128)(2,1)} %pad.29.table_ref, bf16[2048,1024]{1,0:T(8,128)(2,1)} %all-gather.6.cloned.1.call-done.rows_ref.refs_0_, f32[4,2048]{1,0:T(4,128)} %copy-done.45, bf16[6144,1024]{1,0:T(8,128)(2,1)} %all-gather.10.cloned.1.call-done.refs_2_, ...), custom_call_target="tpu_custom_call" | custom-call | flops 21474836480 | bytes 18087936 | tf_op jit(solution)/shard_map/head_grad/pallas_call | solution.py:344
  391.1 9.4 reduce-scatter.4.cloned.1.call-done
  405.8 7.1 convert_reduce_fusion.2
  414.2 5.8 convolution_convert_fusion.1
  430.8 5.6 collective-permute-start.9
  436.4 6.8 multiply_reduce_fusion.5
  447.3 15.0 %collective-permute-done.10 = bf16[640,1024]{1,0:T(8,128)(2,1)} collective-permute-done((bf16[640,1024]{1,0:T(8,128)(2,1)}, bf16[640,1024]{1,0:T(8,128)(2,1)}, u32[]{:S(2)}, u32[]{:S(2)}) %collective-permute-start.10) | collective-permute-done | bytes 1310752 | tf_op jit(solution)/shard_map/ppermute | solution.py:634
  478.8 24.4 %attend_back.1 = (bf16[256,1024]{1,0:T(8,128)(2,1)}, bf16[1024,1024]{1,0:T(8,128)(2,1)}, bf16[1024,1024]{1,0:T(8,128)(2,1)}) custom-call(s32[1]{0:T(128)} %bitcast.2.start_ref, bf16[256,1024]{1,0:T(8,128)(2,1)} %fusion.24.query_ref, bf16[1024,1024]{1,0:T(8,128)(2,1)} %convolution_convert_fusion.6.key_ref, bf16[1024,1024]{1,0:T(8,128)(2,1)} %add_convert_fusion.value_ref, ...), custom_call_target="tpu_custom_call" | custom-call | flops 2684354560 | bytes 7864320 | tf_op jit(solution)/shard_map/attend_back/pallas_call | solution.py:141
  536.4 13.6 %pad_maximum_fusion.3 = bf16[1024,2432]{0,1:T(8,128)(2,1)} fusion(bf16[1024,128]{0,1:T(8,128)(2,1)S(1)} %copy.126, bf16[1024,256]{0,1:T(8,128)(2,1)S(1)} %copy-done.28, bf16[1024,1024]{0,1:T(8,128)(2,1)S(1)} %copy-done.13, bf16[1024,1024]{0,1:T(8,128)(2,1)S(1)} %copy-done.27), kind=kLoop, calls=%fused_computation.26 | loop fusion | flops 19922944 | bytes 9961472 | tf_op jit(solution)/shard_map/concatenate | solution.py:1102
  550.0 7.8 reshape.770
  557.7 11.2 %constant_dynamic-slice_fusion.3 = (bf16[2,2,1,128,2048]{3,2,1,0,4:T(2,128)(2,1)}, bf16[2,2,1,128,2048]{3,2,1,0,4:T(2,128)(2,1)}) fusion(bf16[2,2,2,128,2048]{3,2,1,0,4:T(2,128)(2,1)} %reshape.770, s32[]{:T(128)S(6)} %select_n.399, s32[]{:T(128)S(6)} %select_n.400), kind=kLoop, calls=%fused_computation.214 | loop fusion | bytes 8388616 | tf_op jit(solution)/shard_map/jit(dynamic_index_in_dim)/dynamic_slice | solution.py:710
  569.0 7.4 copy.129
  576.4 10.5 %copy.128 = bf16[2,2,1,128,2048]{4,3,1,0,2:T(8,128)(2,1)} copy(bf16[2,2,1,128,2048]{3,2,1,0,4:T(2,128)(2,1)} %get-tuple-element.232) | data formatting | bytes 4194304 | tf_op jit(solution)/shard_map/jit(dynamic_index_in_dim)/dynamic_slice | solution.py:706
  601.5 8.1 pad_maximum_fusion.4.rows_ref
  609.5 10.6 %copy.139 = bf16[2,2,1,128,2048]{4,3,1,0,2:T(8,128)(2,1)} copy(bf16[2,2,1,128,2048]{3,2,1,0,4:T(2,128)(2,1)} %get-tuple-element.231) | data formatting | bytes 4194304
  631.6 27.0 %band_grad.3 = bf16[64,3328]{1,0:T(8,128)(2,1)} custom-call(s32[113]{0:T(128)} %concatenate.85.plan_ref, bf16[26624,128]{1,0:T(8,128)(2,1)} %fusion.6.table_ref, bf16[9216,256]{1,0:T(8,128)(2,1)} %pad_maximum_fusion.4.rows_ref, f32[4,9216]{1,0:T(4,128)} %pad_maximum_fusion.8.fact_ref), custom_call_target="tpu_custom_call" | custom-call | flops 15703474176 | bytes 4063232 | tf_op jit(solution)/shard_map/band_grad/pallas_call | solution.py:442
  666.0 21.7 %collective-permute-done.16 = bf16[2,128,2432]{2,1,0:T(8,128)(2,1)S(1)} collective-permute-done((bf16[2,128,2432]{2,1,0:T(8,128)(2,1)S(1)}, bf16[2,128,2432]{2,1,0:T(8,128)(2,1)S(1)}, u32[]{:S(2)}, u32[]{:S(2)}) %collective-permute-start.16) | collective-permute-done | bytes 1245216 | tf_op jit(solution)/shard_map/ppermute | solution.py:705
  695.0 9.6 collective-permute-start.19
  717.1 27.0 %band_grad.4 = bf16[64,3328]{1,0:T(8,128)(2,1)} custom-call(s32[113]{0:T(128)} %concatenate.88.plan_ref, bf16[26624,128]{1,0:T(8,128)(2,1)} %fusion.6.table_ref, bf16[9216,256]{1,0:T(8,128)(2,1)} %pad_maximum_fusion.4.rows_ref, f32[4,9216]{1,0:T(4,128)} %pad_maximum_fusion.8.fact_ref), custom_call_target="tpu_custom_call" | custom-call | flops 15703474176 | bytes 4063232 | tf_op jit(solution)/shard_map/band_grad/pallas_call | solution.py:442
  756.5 33.6 %band_grad.5 = f32[5000,256]{1,0:T(8,128)} custom-call(s32[187]{0:T(256)} %concatenate.90.plan_ref, bf16[5120,256]{1,0:T(8,128)(2,1)} %pad.30.table_ref, bf16[9216,256]{1,0:T(8,128)(2,1)} %pad_maximum_fusion.4.rows_ref, f32[4,9216]{1,0:T(4,128)} %pad_maximum_fusion.8.fact_ref), custom_call_target="tpu_custom_call" | custom-call | flops 24159191040 | bytes 9961472 | tf_op jit(solution)/shard_map/band_grad/pallas_call | solution.py:442
  793.5 15.5 %collective-permute-done.32 = bf16[128,1024]{1,0:T(8,128)(2,1)S(1)} collective-permute-done((bf16[128,1024]{1,0:T(8,128)(2,1)S(1)}, bf16[128,1024]{1,0:T(8,128)(2,1)S(1)}, u32[]{:S(2)}, u32[]{:S(2)}) %collective-permute-start.32) | collective-permute-done | bytes 262176 | tf_op jit(solution)/shard_map/ppermute | solution.py:696
  808.9 15.3 %collective-permute-start.36 = (bf16[32,4096]{1,0:T(8,128)(2,1)}, bf16[32,4096]{1,0:T(8,128)(2,1)}, u32[]{:S(2)}, u32[]{:S(2)}) collective-permute-start(bf16[32,4096]{1,0:T(8,128)(2,1)} %fusion.48), channel_id=1, source_target_pairs={{0,8},{8,16},{16,24},{24,0},{1,9},{9,17},{17,25},{25,1},{2,10},{10... | collective-permute-start | bytes 786440 | tf_op jit(solution)/shard_map/ppermute | solution.py:625
  828.0 14.6 %collective-permute-done.35 = bf16[32,4096]{1,0:T(8,128)(2,1)} collective-permute-done((bf16[32,4096]{1,0:T(8,128)(2,1)}, bf16[32,4096]{1,0:T(8,128)(2,1)}, u32[]{:S(2)}, u32[]{:S(2)}) %collective-permute-start.35) | collective-permute-done | bytes 262176 | tf_op jit(solution)/shard_map/ppermute | solution.py:625
  863.5 7.8 collective-permute-start.37
  873.5 26.4 %collective-permute-start.39 = (bf16[128,1024]{1,0:T(8,128)(2,1)S(1)}, bf16[128,1024]{1,0:T(8,128)(2,1)S(1)}, u32[]{:S(2)}, u32[]{:S(2)}) collective-permute-start(bf16[128,1024]{1,0:T(8,128)(2,1)S(1)} %fusion.45), channel_id=1, source_target_pairs={{0,8},{8,16},{16,24},{24,0},{1,9},{9,17},{17,25},{25,1},{2,10},{10... | collective-permute-start | bytes 786440 | tf_op jit(solution)/shard_map/ppermute | solution.py:625
  899.9 10.7 %collective-permute-done.27 = bf16[256,1024]{1,0:T(8,128)(2,1)} collective-permute-done((bf16[256,1024]{1,0:T(8,128)(2,1)}, bf16[256,1024]{1,0:T(8,128)(2,1)}, u32[]{:S(2)}, u32[]{:S(2)}) %collective-permute-start.27) | collective-permute-done | bytes 524320 | tf_op jit(solution)/shard_map/ppermute | solution.py:696
  931.7 7.1 collective-permute-done.43
  940.1 6.4 collective-permute-done.47
  (569 shorter events, 291.8 us)
Async XLA Ops:
  7.2 168.5 %all-gather.6.cloned.1.call-start = ((), (), s32[]{:S(2)}) async-start(), calls=%async_computation.3 | async-start | bytes 4718592 | tf_op jit(solution)/shard_map/all_gather | solution.py:867
  12.6 50.6 %collective-permute-start = (bf16[256,1024]{1,0:T(8,128)(2,1)}, bf16[256,1024]{1,0:T(8,128)(2,1)}, u32[]{:S(2)}, u32[]{:S(2)}) collective-permute-start(bf16[256,1024]{1,0:T(8,128)(2,1)} %add_convert_fusion.5), channel_id=1, source_target_pairs={{0,24},{1,25},{2,26},{3,27},{4,28},{5,29},{6,30},{7,31}} | collective-permute-start | bytes 1572872 | tf_op jit(solution)/shard_map/ppermute | solution.py:673
  20.4 44.2 %collective-permute-start.1 = (bf16[256,1024]{1,0:T(8,128)(2,1)}, bf16[256,1024]{1,0:T(8,128)(2,1)}, u32[]{:S(2)}, u32[]{:S(2)}) collective-permute-start(bf16[256,1024]{1,0:T(8,128)(2,1)} %add_convert_fusion.5), channel_id=1, source_target_pairs={{0,16},{8,24},{1,17},{9,25},{2,18},{10,26},{3,19},{11,27},{4,20},{... | collective-permute-start | bytes 1572872 | tf_op jit(solution)/shard_map/ppermute | solution.py:673
  22.5 43.2 %collective-permute-start.2 = (bf16[256,1024]{1,0:T(8,128)(2,1)}, bf16[256,1024]{1,0:T(8,128)(2,1)}, u32[]{:S(2)}, u32[]{:S(2)}) collective-permute-start(bf16[256,1024]{1,0:T(8,128)(2,1)} %add_convert_fusion.5), channel_id=1, source_target_pairs={{0,8},{8,16},{16,24},{1,9},{9,17},{17,25},{2,10},{10,18},{18,26},{... | collective-permute-start | bytes 1572872 | tf_op jit(solution)/shard_map/ppermute | solution.py:673
  103.7 98.6 %all-gather.8.cloned.1.call-start = ((), (), s32[]{:S(2)}) async-start(), calls=%async_computation.4 | async-start | bytes 2621440 | tf_op jit(solution)/shard_map/all_gather | solution.py:870
  156.1 152.8 %all-gather.10.cloned.1.call-start = ((), (), s32[]{:S(2)}) async-start(), calls=%async_computation.5 | async-start | bytes 14155776 | tf_op jit(solution)/shard_map/all_gather | solution.py:905
  206.1 194.4 %reduce-scatter.4.cloned.1.call-start = ((), (), s32[]{:S(2)}) async-start(), calls=%async_computation.6 | async-start | bytes 5898240 | tf_op jit(solution)/shard_map/reduce_scatter | solution.py:956
  209.9 97.1 %collective-permute-start.3 = (bf16[288,256]{1,0:T(8,128)(2,1)}, bf16[288,256]{1,0:T(8,128)(2,1)S(1)}, u32[]{:S(2)}, u32[]{:S(2)}) collective-permute-start(bf16[288,256]{1,0:T(8,128)(2,1)} %constant_dynamic-slice_fusion.5), channel_id=1, source_target_pairs={{0,24},{8,0},{16,8},{24,16},{1,25},{9,1},{17,9},{25,17},{2,26},{10... | collective-permute-start | bytes 442376 | tf_op jit(solution)/shard_map/ppermute | solution.py:625
  211.1 96.0 %collective-permute-start.4 = (bf16[288,256]{1,0:T(8,128)(2,1)}, bf16[288,256]{1,0:T(8,128)(2,1)}, u32[]{:S(2)}, u32[]{:S(2)}) collective-permute-start(bf16[288,256]{1,0:T(8,128)(2,1)} %constant_dynamic-slice_fusion.5), channel_id=1, source_target_pairs={{0,16},{8,24},{16,0},{24,8},{1,17},{9,25},{17,1},{25,9},{2,18},{10... | collective-permute-start | bytes 442376 | tf_op jit(solution)/shard_map/ppermute | solution.py:625
  211.2 95.9 %collective-permute-start.5 = (bf16[288,256]{1,0:T(8,128)(2,1)}, bf16[288,256]{1,0:T(8,128)(2,1)}, u32[]{:S(2)}, u32[]{:S(2)}) collective-permute-start(bf16[288,256]{1,0:T(8,128)(2,1)} %constant_dynamic-slice_fusion.5), channel_id=1, source_target_pairs={{0,8},{8,16},{16,24},{24,0},{1,9},{9,17},{17,25},{25,1},{2,10},{10... | collective-permute-start | bytes 442376 | tf_op jit(solution)/shard_map/ppermute | solution.py:625
  337.4 261.7 %all-gather.12.cloned.1.call-start = ((), (), s32[]{:S(2)}) async-start(), calls=%async_computation.7 | async-start | bytes 3981312 | tf_op jit(solution)/shard_map/all_gather | solution.py:939
  340.6 367.2 %reduce-scatter.6.cloned.1.call-start = ((), (), s32[]{:S(2)}) async-start(), calls=%async_computation.8 | async-start | bytes 9437184 | tf_op jit(solution)/shard_map/reduce_scatter | solution.py:1039
  420.1 326.1 %reduce-scatter.8.cloned.1.call-start = ((), (), s32[]{:S(2)}) async-start(), calls=%async_computation.9 | async-start | bytes 9437184 | tf_op jit(solution)/shard_map/reduce_scatter | solution.py:1033
  429.4 32.9 %collective-permute-start.10 = (bf16[640,1024]{1,0:T(8,128)(2,1)}, bf16[640,1024]{1,0:T(8,128)(2,1)}, u32[]{:S(2)}, u32[]{:S(2)}) collective-permute-start(bf16[640,1024]{1,0:T(8,128)(2,1)} %head_grad.1), channel_id=1, source_target_pairs={{8,0},{16,8},{24,16},{9,1},{17,9},{25,17},{10,2},{18,10},{26,18},{... | collective-permute-start | bytes 3932168 | tf_op jit(solution)/shard_map/ppermute | solution.py:634
  430.8 32.7 %collective-permute-start.9 = (bf16[640,1024]{1,0:T(8,128)(2,1)}, bf16[640,1024]{1,0:T(8,128)(2,1)}, u32[]{:S(2)}, u32[]{:S(2)}) collective-permute-start(bf16[640,1024]{1,0:T(8,128)(2,1)} %head_grad.1), channel_id=1, source_target_pairs={{0,8},{8,16},{16,24},{1,9},{9,17},{17,25},{2,10},{10,18},{18,26},{... | collective-permute-start | bytes 3932168 | tf_op jit(solution)/shard_map/ppermute | solution.py:633
  463.5 39.7 %collective-permute-start.11 = (bf16[640,1024]{1,0:T(8,128)(2,1)}, bf16[640,1024]{1,0:T(8,128)(2,1)}, u32[]{:S(2)}, u32[]{:S(2)}) collective-permute-start(bf16[640,1024]{1,0:T(8,128)(2,1)} %collective-permute-done.9), channel_id=1, source_target_pairs={{8,16},{16,24},{9,17},{17,25},{10,18},{18,26},{11,19},{19,27},{12,... | collective-permute-start | bytes 3932168 | tf_op jit(solution)/shard_map/ppermute | solution.py:633
  465.2 38.0 %collective-permute-start.12 = (bf16[640,1024]{1,0:T(8,128)(2,1)}, bf16[640,1024]{1,0:T(8,128)(2,1)}, u32[]{:S(2)}, u32[]{:S(2)}) collective-permute-start(bf16[640,1024]{1,0:T(8,128)(2,1)} %collective-permute-done.10), channel_id=1, source_target_pairs={{8,0},{16,8},{9,1},{17,9},{10,2},{18,10},{11,3},{19,11},{12,4},{20... | collective-permute-start | bytes 3932168 | tf_op jit(solution)/shard_map/ppermute | solution.py:634
  471.9 375.9 %all-reduce.11.cloned.1.call-start = ((), (), s32[]{:S(2)}) async-start(), calls=%async_computation.10 | async-start | bytes 2293760 | tf_op jit(solution)/shard_map/psum | solution.py:1140
  586.9 36.6 %collective-permute-start.13 = (bf16[2,2,128,2048]{3,2,1,0:T(8,128)(2,1)}, bf16[2,2,128,2048]{3,2,1,0:T(8,128)(2,1)}, u32[]{:S(2)}, u32[]{:S(2)}) collective-permute-start(bf16[2,2,128,2048]{3,2,1,0:T(8,128)(2,1)} %bitcast.250), channel_id=1, source_target_pairs={{0,1},{1,0},{2,3},{3,2},{4,5},{5,4},{6,7},{7,6},{8,9},{9,8},{10,11... | collective-permute-start | bytes 6291464 | tf_op jit(solution)/shard_map/ppermute | solution.py:705
  592.8 33.8 %collective-permute-start.14 = (bf16[2,2,128,2432]{3,2,0,1:T(8,128)(2,1)}, bf16[2,2,128,2432]{3,2,0,1:T(8,128)(2,1)}, u32[]{:S(2)}, u32[]{:S(2)}) collective-permute-start(bf16[2,2,128,2432]{3,2,0,1:T(8,128)(2,1)} %bitcast.245), channel_id=1, source_target_pairs={{0,1},{1,0},{2,3},{3,2},{4,5},{5,4},{6,7},{7,6},{8,9},{9,8},{10,11... | collective-permute-start | bytes 7471112 | tf_op jit(solution)/shard_map/ppermute | solution.py:705
  620.1 38.5 %collective-permute-start.17 = (bf16[640,1024]{1,0:T(8,128)(2,1)}, bf16[640,1024]{1,0:T(8,128)(2,1)}, u32[]{:S(2)}, u32[]{:S(2)}) collective-permute-start(bf16[640,1024]{1,0:T(8,128)(2,1)} %collective-permute-done.11), channel_id=1, source_target_pairs={{16,24},{17,25},{18,26},{19,27},{20,28},{21,29},{22,30},{23,31}} | collective-permute-start | bytes 3932168 | tf_op jit(solution)/shard_map/ppermute | solution.py:633
  622.0 36.7 %collective-permute-start.18 = (bf16[640,1024]{1,0:T(8,128)(2,1)}, bf16[640,1024]{1,0:T(8,128)(2,1)}, u32[]{:S(2)}, u32[]{:S(2)}) collective-permute-start(bf16[640,1024]{1,0:T(8,128)(2,1)} %collective-permute-done.12), channel_id=1, source_target_pairs={{8,0},{9,1},{10,2},{11,3},{12,4},{13,5},{14,6},{15,7}} | collective-permute-start | bytes 3932168 | tf_op jit(solution)/shard_map/ppermute | solution.py:634
  630.1 34.3 %collective-permute-start.15 = (bf16[2,128,2048]{2,1,0:T(8,128)(2,1)}, bf16[2,128,2048]{2,1,0:T(8,128)(2,1)}, u32[]{:S(2)}, u32[]{:S(2)}) collective-permute-start(bf16[2,128,2048]{2,1,0:T(8,128)(2,1)} %dynamic-slice_bitcast_fusion.1), channel_id=1, source_target_pairs={{0,4},{1,5},{2,6},{3,7},{4,0},{5,1},{6,2},{7,3},{8,12},{9,13},{10,... | collective-permute-start | bytes 3145736 | tf_op jit(solution)/shard_map/ppermute | solution.py:705
  658.7 29.1 %collective-permute-start.16 = (bf16[2,128,2432]{2,1,0:T(8,128)(2,1)S(1)}, bf16[2,128,2432]{2,1,0:T(8,128)(2,1)S(1)}, u32[]{:S(2)}, u32[]{:S(2)}) collective-permute-start(bf16[2,128,2432]{2,1,0:T(8,128)(2,1)S(1)} %dynamic-slice_bitcast_fusion), channel_id=1, source_target_pairs={{0,2},{1,3},{2,0},{3,1},{4,6},{5,7},{6,4},{7,5},{8,10},{9,11},{10,... | collective-permute-start | bytes 3735560 | tf_op jit(solution)/shard_map/ppermute | solution.py:705
  688.2 18.6 %collective-permute-start.22 = (bf16[128,2432]{1,0:T(8,128)(2,1)S(1)}, bf16[128,2432]{1,0:T(8,128)(2,1)S(1)}, u32[]{:S(2)}, u32[]{:S(2)}) collective-permute-start(bf16[128,2432]{1,0:T(8,128)(2,1)S(1)} %dynamic-slice_bitcast_fusion.2), channel_id=1, source_target_pairs={{0,4},{1,5},{2,6},{3,7},{4,0},{5,1},{6,2},{7,3},{8,12},{9,13},{10,... | collective-permute-start | bytes 1867784 | tf_op jit(solution)/shard_map/ppermute | solution.py:705
  695.0 51.1 %collective-permute-start.19 = (bf16[64,3328]{1,0:T(8,128)(2,1)}, bf16[64,3328]{1,0:T(8,128)(2,1)}, u32[]{:S(2)}, u32[]{:S(2)}) collective-permute-start(bf16[64,3328]{1,0:T(8,128)(2,1)} %band_grad.3), channel_id=1, source_target_pairs={{0,8},{8,16},{16,24},{1,9},{9,17},{17,25},{2,10},{10,18},{18,26},{... | collective-permute-start | bytes 1277960 | tf_op jit(solution)/shard_map/ppermute | solution.py:633
  704.6 41.6 %collective-permute-start.20 = (bf16[64,3328]{1,0:T(8,128)(2,1)}, bf16[64,3328]{1,0:T(8,128)(2,1)}, u32[]{:S(2)}, u32[]{:S(2)}) collective-permute-start(bf16[64,3328]{1,0:T(8,128)(2,1)} %band_grad.3), channel_id=1, source_target_pairs={{8,0},{16,8},{24,16},{9,1},{17,9},{25,17},{10,2},{18,10},{26,18},{... | collective-permute-start | bytes 1277960 | tf_op jit(solution)/shard_map/ppermute | solution.py:634
  709.8 34.4 %collective-permute-start.23 = (bf16[32,4096]{1,0:T(8,128)(2,1)}, bf16[32,4096]{1,0:T(8,128)(2,1)S(1)}, u32[]{:S(2)}, u32[]{:S(2)}) collective-permute-start(bf16[32,4096]{1,0:T(8,128)(2,1)} %get-tuple-element.245), channel_id=1, source_target_pairs={{0,24},{8,0},{16,8},{24,16},{1,25},{9,1},{17,9},{25,17},{2,26},{10... | collective-permute-start | bytes 786440 | tf_op jit(solution)/shard_map/ppermute | solution.py:696
  714.1 30.1 %collective-permute-start.24 = (bf16[32,4096]{1,0:T(8,128)(2,1)}, bf16[32,4096]{1,0:T(8,128)(2,1)}, u32[]{:S(2)}, u32[]{:S(2)}) collective-permute-start(bf16[32,4096]{1,0:T(8,128)(2,1)} %get-tuple-element.247), channel_id=1, source_target_pairs={{0,16},{8,24},{16,0},{24,8},{1,17},{9,25},{17,1},{25,9},{2,18},{10... | collective-permute-start | bytes 786440 | tf_op jit(solution)/shard_map/ppermute | solution.py:696
  715.1 29.1 %collective-permute-start.25 = (bf16[32,4096]{1,0:T(8,128)(2,1)}, bf16[32,4096]{1,0:T(8,128)(2,1)}, u32[]{:S(2)}, u32[]{:S(2)}) collective-permute-start(bf16[32,4096]{1,0:T(8,128)(2,1)} %get-tuple-element.246), channel_id=1, source_target_pairs={{0,8},{8,16},{16,24},{24,0},{1,9},{9,17},{17,25},{25,1},{2,10},{10... | collective-permute-start | bytes 786440 | tf_op jit(solution)/shard_map/ppermute | solution.py:696
  746.2 99.0 %collective-permute-start.29 = (bf16[64,3328]{1,0:T(8,128)(2,1)}, bf16[64,3328]{1,0:T(8,128)(2,1)}, u32[]{:S(2)}, u32[]{:S(2)}) collective-permute-start(bf16[64,3328]{1,0:T(8,128)(2,1)} %band_grad.4), channel_id=1, source_target_pairs={{0,8},{8,16},{16,24},{1,9},{9,17},{17,25},{2,10},{10,18},{18,26},{... | collective-permute-start | bytes 1277960 | tf_op jit(solution)/shard_map/ppermute | solution.py:633
  749.3 97.2 %collective-permute-start.30 = (bf16[64,3328]{1,0:T(8,128)(2,1)}, bf16[64,3328]{1,0:T(8,128)(2,1)}, u32[]{:S(2)}, u32[]{:S(2)}) collective-permute-start(bf16[64,3328]{1,0:T(8,128)(2,1)} %band_grad.4), channel_id=1, source_target_pairs={{8,0},{16,8},{24,16},{9,1},{17,9},{25,17},{10,2},{18,10},{26,18},{... | collective-permute-start | bytes 1277960 | tf_op jit(solution)/shard_map/ppermute | solution.py:634
  751.8 38.3 %collective-permute-start.31 = (bf16[128,1024]{1,0:T(8,128)(2,1)S(1)}, bf16[128,1024]{1,0:T(8,128)(2,1)S(1)}, u32[]{:S(2)}, u32[]{:S(2)}) collective-permute-start(bf16[128,1024]{1,0:T(8,128)(2,1)S(1)} %get-tuple-element.242), channel_id=1, source_target_pairs={{0,24},{8,0},{16,8},{24,16},{1,25},{9,1},{17,9},{25,17},{2,26},{10... | collective-permute-start | bytes 786440 | tf_op jit(solution)/shard_map/ppermute | solution.py:696
  755.8 53.1 %collective-permute-start.32 = (bf16[128,1024]{1,0:T(8,128)(2,1)S(1)}, bf16[128,1024]{1,0:T(8,128)(2,1)S(1)}, u32[]{:S(2)}, u32[]{:S(2)}) collective-permute-start(bf16[128,1024]{1,0:T(8,128)(2,1)S(1)} %get-tuple-element.244), channel_id=1, source_target_pairs={{0,16},{8,24},{16,0},{24,8},{1,17},{9,25},{17,1},{25,9},{2,18},{10... | collective-permute-start | bytes 786440 | tf_op jit(solution)/shard_map/ppermute | solution.py:696
  755.9 53.0 %collective-permute-start.33 = (bf16[128,1024]{1,0:T(8,128)(2,1)S(1)}, bf16[128,1024]{1,0:T(8,128)(2,1)S(1)}, u32[]{:S(2)}, u32[]{:S(2)}) collective-permute-start(bf16[128,1024]{1,0:T(8,128)(2,1)S(1)} %get-tuple-element.243), channel_id=1, source_target_pairs={{0,8},{8,16},{16,24},{24,0},{1,9},{9,17},{17,25},{25,1},{2,10},{10... | collective-permute-start | bytes 786440 | tf_op jit(solution)/shard_map/ppermute | solution.py:696
  790.1 36.4 %collective-permute-start.34 = (bf16[32,4096]{1,0:T(8,128)(2,1)}, bf16[32,4096]{1,0:T(8,128)(2,1)}, u32[]{:S(2)}, u32[]{:S(2)}) collective-permute-start(bf16[32,4096]{1,0:T(8,128)(2,1)} %fusion.48), channel_id=1, source_target_pairs={{0,24},{8,0},{16,8},{24,16},{1,25},{9,1},{17,9},{25,17},{2,26},{10... | collective-permute-start | bytes 786440 | tf_op jit(solution)/shard_map/ppermute | solution.py:625
  808.9 33.6 %collective-permute-start.35 = (bf16[32,4096]{1,0:T(8,128)(2,1)}, bf16[32,4096]{1,0:T(8,128)(2,1)}, u32[]{:S(2)}, u32[]{:S(2)}) collective-permute-start(bf16[32,4096]{1,0:T(8,128)(2,1)} %fusion.48), channel_id=1, source_target_pairs={{0,16},{8,24},{16,0},{24,8},{1,17},{9,25},{17,1},{25,9},{2,18},{10... | collective-permute-start | bytes 786440 | tf_op jit(solution)/shard_map/ppermute | solution.py:625
  808.9 34.9 %collective-permute-start.36 = (bf16[32,4096]{1,0:T(8,128)(2,1)}, bf16[32,4096]{1,0:T(8,128)(2,1)}, u32[]{:S(2)}, u32[]{:S(2)}) collective-permute-start(bf16[32,4096]{1,0:T(8,128)(2,1)} %fusion.48), channel_id=1, source_target_pairs={{0,8},{8,16},{16,24},{24,0},{1,9},{9,17},{17,25},{25,1},{2,10},{10... | collective-permute-start | bytes 786440 | tf_op jit(solution)/shard_map/ppermute | solution.py:625
  826.5 37.0 %collective-permute-start.40 = (bf16[64,3328]{1,0:T(8,128)(2,1)}, bf16[64,3328]{1,0:T(8,128)(2,1)}, u32[]{:S(2)}, u32[]{:S(2)}) collective-permute-start(bf16[64,3328]{1,0:T(8,128)(2,1)} %collective-permute-done.19), channel_id=1, source_target_pairs={{8,16},{16,24},{9,17},{17,25},{10,18},{18,26},{11,19},{19,27},{12,... | collective-permute-start | bytes 1277960 | tf_op jit(solution)/shard_map/ppermute | solution.py:633
  842.6 28.8 %collective-permute-start.41 = (bf16[64,3328]{1,0:T(8,128)(2,1)}, bf16[64,3328]{1,0:T(8,128)(2,1)}, u32[]{:S(2)}, u32[]{:S(2)}) collective-permute-start(bf16[64,3328]{1,0:T(8,128)(2,1)} %collective-permute-done.20), channel_id=1, source_target_pairs={{8,0},{16,8},{9,1},{17,9},{10,2},{18,10},{11,3},{19,11},{12,4},{20... | collective-permute-start | bytes 1277960 | tf_op jit(solution)/shard_map/ppermute | solution.py:634
  843.9 29.6 %collective-permute-start.26 = (bf16[256,1024]{1,0:T(8,128)(2,1)}, bf16[256,1024]{1,0:T(8,128)(2,1)}, u32[]{:S(2)}, u32[]{:S(2)}) collective-permute-start(bf16[256,1024]{1,0:T(8,128)(2,1)} %get-tuple-element.238), channel_id=1, source_target_pairs={{8,0},{16,8},{24,16},{9,1},{17,9},{25,17},{10,2},{18,10},{26,18},{... | collective-permute-start | bytes 1572872 | tf_op jit(solution)/shard_map/ppermute | solution.py:696
  845.2 65.4 %collective-permute-start.27 = (bf16[256,1024]{1,0:T(8,128)(2,1)}, bf16[256,1024]{1,0:T(8,128)(2,1)}, u32[]{:S(2)}, u32[]{:S(2)}) collective-permute-start(bf16[256,1024]{1,0:T(8,128)(2,1)} %get-tuple-element.240), channel_id=1, source_target_pairs={{16,0},{24,8},{17,1},{25,9},{18,2},{26,10},{19,3},{27,11},{20,4},{... | collective-permute-start | bytes 1572872 | tf_op jit(solution)/shard_map/ppermute | solution.py:696
  846.5 64.8 %collective-permute-start.28 = (bf16[256,1024]{1,0:T(8,128)(2,1)}, bf16[256,1024]{1,0:T(8,128)(2,1)}, u32[]{:S(2)}, u32[]{:S(2)}) collective-permute-start(bf16[256,1024]{1,0:T(8,128)(2,1)} %get-tuple-element.239), channel_id=1, source_target_pairs={{24,0},{25,1},{26,2},{27,3},{28,4},{29,5},{30,6},{31,7}} | collective-permute-start | bytes 1572872 | tf_op jit(solution)/shard_map/ppermute | solution.py:696
  863.5 52.8 %collective-permute-start.37 = (bf16[128,1024]{1,0:T(8,128)(2,1)S(1)}, bf16[128,1024]{1,0:T(8,128)(2,1)S(1)}, u32[]{:S(2)}, u32[]{:S(2)}) collective-permute-start(bf16[128,1024]{1,0:T(8,128)(2,1)S(1)} %fusion.45), channel_id=1, source_target_pairs={{0,24},{8,0},{16,8},{24,16},{1,25},{9,1},{17,9},{25,17},{2,26},{10... | collective-permute-start | bytes 786440 | tf_op jit(solution)/shard_map/ppermute | solution.py:625
  871.3 50.4 %collective-permute-start.38 = (bf16[128,1024]{1,0:T(8,128)(2,1)S(1)}, bf16[128,1024]{1,0:T(8,128)(2,1)S(1)}, u32[]{:S(2)}, u32[]{:S(2)}) collective-permute-start(bf16[128,1024]{1,0:T(8,128)(2,1)S(1)} %fusion.45), channel_id=1, source_target_pairs={{0,16},{8,24},{16,0},{24,8},{1,17},{9,25},{17,1},{25,9},{2,18},{10... | collective-permute-start | bytes 786440 | tf_op jit(solution)/shard_map/ppermute | solution.py:625
  873.5 49.6 %collective-permute-start.39 = (bf16[128,1024]{1,0:T(8,128)(2,1)S(1)}, bf16[128,1024]{1,0:T(8,128)(2,1)S(1)}, u32[]{:S(2)}, u32[]{:S(2)}) collective-permute-start(bf16[128,1024]{1,0:T(8,128)(2,1)S(1)} %fusion.45), channel_id=1, source_target_pairs={{0,8},{8,16},{16,24},{24,0},{1,9},{9,17},{17,25},{25,1},{2,10},{10... | collective-permute-start | bytes 786440 | tf_op jit(solution)/shard_map/ppermute | solution.py:625
  911.3 18.4 %collective-permute-start.45 = (bf16[64,3328]{1,0:T(8,128)(2,1)}, bf16[64,3328]{1,0:T(8,128)(2,1)S(1)}, u32[]{:S(2)}, u32[]{:S(2)}) collective-permute-start(bf16[64,3328]{1,0:T(8,128)(2,1)} %collective-permute-done.30), channel_id=1, source_target_pairs={{8,0},{16,8},{9,1},{17,9},{10,2},{18,10},{11,3},{19,11},{12,4},{20... | collective-permute-start | bytes 1277960 | tf_op jit(solution)/shard_map/ppermute | solution.py:634
  921.8 17.1 %collective-permute-start.43 = (bf16[64,3328]{1,0:T(8,128)(2,1)}, bf16[64,3328]{1,0:T(8,128)(2,1)S(1)}, u32[]{:S(2)}, u32[]{:S(2)}) collective-permute-start(bf16[64,3328]{1,0:T(8,128)(2,1)} %collective-permute-done.41), channel_id=1, source_target_pairs={{8,0},{9,1},{10,2},{11,3},{12,4},{13,5},{14,6},{15,7}} | collective-permute-start | bytes 1277960 | tf_op jit(solution)/shard_map/ppermute | solution.py:634
  (123 other events, 1463.6 us)
Sparse Core Ops, SparseCore 0:
  103.8 36.8 all-gather.5
  156.2 46.0 all-gather.7
  206.2 70.8 all-gather.9
  337.6 62.8 reduce-scatter.3
  402.4 33.9 all-gather.11
  440.1 71.3 reduce-scatter.5
  514.9 71.2 reduce-scatter.7
  744.3 95.2 all-reduce.10

commit v6 on v3

--- a/solution.py
+++ b/solution.py
@@ -845,13 +845,11 @@
     all_states = lax.all_gather(state_low, "batch", axis=0, tiled=True)
     split = 2 * nz * group_count * feature_count <= 24 << 20
     if split:
-        other_states = jnp.concatenate(line_turns(state_low)[1:], 0)
-        all_states, other_states, head_pad, middle_pad, tail_pad, hit_rows, slot, early = (
-            lax.optimization_barrier(
-                (all_states, other_states, head_pad, middle_pad, tail_pad, hit_rows, slot, early)
-            )
-        )
-        other_states = lax.all_gather(other_states, "batch", axis=0, tiled=True)
+        block_states = lax.all_gather(state_low, "seq", axis=0, tiled=True)
+    all_states, head_pad, middle_pad, tail_pad, tail_hits, slot, early = lax.optimization_barrier(
+        (all_states, head_pad, middle_pad, tail_pad, hit_rows[2], slot, early)
+    )
+    hit_rows = hit_rows[:2] + (tail_hits,)
 
     middle_width = middle_map.shape[1]
     maps = jnp.pad(jnp.concatenate([middle_map, tail_map], 1), ((0, 0), (0, 128 - tail_width)))
@@ -873,17 +871,22 @@
         piece = slot_count // nb
         slot_piece = lax.dynamic_slice_in_dim(slot_low, member * piece, piece, 0)
         other_slots = jnp.concatenate(line_turns(slot_piece)[1:], 0)
+        slot_low, block_states, hit_rows = lax.optimization_barrier(
+            (slot_low, block_states, hit_rows)
+        )
+        other_states = lax.dynamic_slice_in_dim(
+            jnp.concatenate([block_states, block_states], 0),
+            (place + 1) * token_count,
+            (nz - 1) * token_count,
+            0,
+        )
+        other_states = lax.all_gather(other_states, "batch", axis=0, tiled=True)
     tail_stats, tail_mix = band_forward(
         tail_span, slot_low, tail_pad, tail_padded, tail_chunk, tail_width, 0.5
     )
     middle_stats, middle_mix = band_forward(
         middle_span, slot_low, middle_pad, sizes[1], middle_chunk, None, 0.25
     )
-    if split:
-        all_states, other_states, other_slots, tail_stats, middle_stats = lax.optimization_barrier(
-            (all_states, other_states, other_slots, tail_stats, middle_stats)
-        )
-        other_slots = lax.all_gather(other_slots, "batch", axis=0, tiled=True)
     head_stats, head_mix = band_forward(
         head_span, all_states, head_pad, sizes[0], head_chunk, None, 1.0
     )
@@ -911,6 +914,7 @@
         stats, other_states, other_slots = lax.optimization_barrier(
             (stats, other_states, other_slots)
         )
+        other_slots = lax.all_gather(other_slots, "batch", axis=0, tiled=True)
     everyone = lax.all_gather(stats, "batch")
 
     token_facts = jnp.concatenate(
@@ -1045,8 +1049,8 @@
     )
     if split:
         for unused in range(nz - 3):
-            (query_low,) = head_advance(query_low)
-        (query_low,) = tail_advance(query_low)
+            query_low, key_low, value_low = head_advance(query_low, key_low, value_low)
+        query_low, key_low, value_low = tail_advance(query_low, key_low, value_low)
     query_weight_grad = product_tn(normed_low, query_low)
     key_weight_grad = product_tn(normed_all, key_low)
     value_weight_grad = product_tn(normed_all, value_low)
@@ -1060,10 +1064,6 @@
     own_spread = jnp.mean((tokens - own_average) ** 2, -1, keepdims=True)
     own_centred = (tokens - own_average) * lax.rsqrt(own_spread + EPSILON)
     first_gain_grad = jnp.sum(all_centred * spread, 0) + jnp.sum(own_centred * query_spread, 0)
-    normed_grad = query_spread + line_scatter(lowered(spread), False)
-    first_in_grad, unused, unused = norm_back(tokens, first_gain, first_shift, normed_grad)
-    input_grad = mixed_grad + first_in_grad
-
     bias_rows = inner_bias_grad.shape[0] // feature_count
     inner_bias_rows = (
         inner_bias_grad.reshape(nb, bias_rows, -1).transpose(1, 0, 2).reshape(bias_rows, -1)
@@ -1095,10 +1095,13 @@
         turned(jnp.concatenate(rows, 0), jnp.bfloat16),
     ]
     rest = jnp.concatenate([lowered(column) for column in columns], 1)
-    rest, facts, inner_part = lax.optimization_barrier((rest, facts, inner_part))
+    spread_low = lowered(spread)
+    rest, facts, spread_low = lax.optimization_barrier((rest, facts, spread_low))
     if split:
-        rest, facts = tail_advance(rest, facts)
+        rest, facts, spread_low, inner_part = tail_advance(rest, facts, spread_low, inner_part)
     rest_part = lax.psum_scatter(rest, "batch", scatter_dimension=0, tiled=True)
+    inner_low = lowered(line_scatter(inner_part))
+    spread_sum = line_scatter(spread_low, False)
     middle_result = jax.ShapeDtypeStruct(
         (sizes[1], middle_width) if split else (middle_padded, middle_width),
         jnp.float32 if split else jnp.bfloat16,
@@ -1118,9 +1121,18 @@
         False,
     )
     if split:
+        for unused in range(nz - 3):
+            (middle_part,) = tail_advance(middle_part)
+    middle_part, inner_low, spread_sum, outer_part = lax.optimization_barrier(
+        (middle_part, inner_low, spread_sum, outer_part)
+    )
+    inner_pieces = line_turns(inner_low)
+    outer_low = lowered(line_scatter(outer_part))
+    rest_part, inner_pieces, outer_low = lax.optimization_barrier(
+        (rest_part, inner_pieces, outer_low)
+    )
+    if split:
         middle_table_grad = middle_part
-        for unused in range(nz - 3):
-            (middle_table_grad,) = tail_advance(middle_table_grad)
         head_table_grad = line_ordered(head_found, 0)
         tail_sum = line_ordered(tail_found, 1)
     else:
@@ -1129,15 +1141,9 @@
         tail_sum = lax.psum(tail_part, "seq")
     head_table_grad = head_table_grad[: sizes[0]].astype(jnp.float32)
     tail_table_grad = tail_sum[:, : sizes[2]].astype(jnp.float32).T
-    inner_low = lowered(line_scatter(inner_part))
-    inner_low, outer_part, middle_table_grad = lax.optimization_barrier(
-        (inner_low, outer_part, middle_table_grad)
-    )
-    inner_pieces = line_turns(inner_low)
-    outer_low = lowered(line_scatter(outer_part))
-    rest_part, outer_low, inner_pieces = lax.optimization_barrier(
-        (rest_part, outer_low, inner_pieces)
-    )
+    normed_grad = query_spread + spread_sum
+    first_in_grad, unused, unused = norm_back(tokens, first_gain, first_shift, normed_grad)
+    input_grad = mixed_grad + first_in_grad
     inner_sum = in_order(inner_pieces).astype(jnp.float32)
     outer_sum = in_order(line_turns(outer_low)).astype(jnp.float32)
     rest_low = lax.psum(rest_part, "seq")

time: 871 us -> 888 us (1.020)
  other arithmetic: 97.4 us -> 114 us
  starting transfers between devices: 92.3 us -> 80.4 us
    ppermute x15 -> x12, waiting for transfers between devices: 59.8 us -> 14 us  [line_turns(): lax.ppermute(value, 'seq', [(d, (d - k) % size) for d in range(size)])]
    psum x1, waiting for transfers between devices: 28.7 us -> 51.2 us  [on_device(): rest_low = lax.psum(rest_part, 'seq')]
    all_gather x0 -> x1, waiting for transfers between devices: none -> 20.7 us  [on_device(): block_states = lax.all_gather(state_low, 'seq', axis=0, tiled=True)]
    ppermute x15 -> x12, starting transfers between devices: 25.7 us -> 12.4 us  [line_turns(): lax.ppermute(value, 'seq', [(d, (d - k) % size) for d in range(size)])]
  transfers between devices with their start and end apart: 47 -> 45, of which waited for: 9 -> 13; matrix products, arithmetic and copies ran while one was open for 26% -> 28% of each run, Pallas kernels for 28% -> 29%
where the time goes in v6:
time: 888 us; the launch traced here: 879 us
  Pallas kernels  276 us (31%)
  waiting for transfers between devices  177 us (20%)
  other arithmetic  114 us (13%)
  local copies, waits for them, and re-layouts  99 us (11%)
  matrix products  93.2 us (10%)
  starting transfers between devices  80.4 us (9%)
  blocking collectives  21.3 us (2%)
  between operations  18.6 us (2%)
    pallas_call x3, Pallas kernels, band_forward(): pl.pallas_call(functools.partial(band_kernel, chunk, per, words, sum_colu...  89.9 us
    pallas_call x2, Pallas kernels, band_grad(): pl.pallas_call(functools.partial(band_grad_kernel, chunk // 2 if chunk >...  84.5 us
    ppermute x9, waiting for transfers between devices, line_scatter(): lax.ppermute(part(place + size - k), 'seq', pairs).astype(jnp.float32)  54.6 us
    psum x1, waiting for transfers between devices, on_device(): rest_low = lax.psum(rest_part, 'seq')  51.2 us
    ppermute x6, waiting for transfers between devices, line_step(): lax.ppermute(behind, 'seq', [(d, d - 1) for d in range(1, size - step + 1)])  35.8 us
    dot_general x9, matrix products, product_tn(): lax.dot_general(former, latter, (((0,), (0,)), ((), ())), preferred_eleme...  34.8 us
    gather x3, local copies, waits for them, and re-layouts, on_device(): jnp.take(table, jnp.clip(local, 0, size - 1), axis=0, mode='clip')  34.3 us
    pallas_call x1, Pallas kernels, head_grad(): pl.pallas_call(functools.partial(head_grad_kernel, chunk, len(lists)), gr...  32.7 us
  transfers between devices with their start and end apart: 45, of which 13 were waited for; matrix products, arithmetic and copies ran while one was open for 28% of the time, Pallas kernels for 29%

profile of v6, /device:TPU:0, one launch (start us, length us, event | category | flops | bytes accessed | tf_op | source)
XLA Modules:
  0.0 878.9 jit_solution(11057272329892186903)
XLA Ops:
  12.6 7.8 collective-permute-start
  27.4 9.1 %all_gather.22 = f32[3,2048]{1,0:T(4,128)S(1)} all-gather(f32[3,256]{1,0:T(4,128)S(1)} %pad_maximum_fusion.12), channel_id=1, replica_groups=mesh['seq'=4,'batch'=8] {'batch'}, dimensions={1}, use_global_device_ids=true | all-gather | bytes 27648 | tf_op jit(solution)/shard_map/all_gather | solution.py:765
  37.1 3.9 select_convert_fusion
  47.4 7.4 copy.114
  55.9 5.5 pad.29.table_ref
  71.6 3.7 add_convert_fusion.value_ref
  75.3 15.2 %attend.1 = bf16[256,1024]{1,0:T(8,128)(2,1)} custom-call(s32[1]{0:T(128)} %bitcast.2.start_ref, bf16[256,1024]{1,0:T(8,128)(2,1)} %fusion.21.query_ref, bf16[1024,1024]{1,0:T(8,128)(2,1)} %convolution_convert_fusion.2.key_ref, bf16[1024,1024]{1,0:T(8,128)(2,1)} %add_convert_fusion.value_ref), custom_call_target="tpu_custom_call" | custom-call | flops 1073741824 | bytes 5242880 | tf_op jit(solution)/shard_map/attend/pallas_call | solution.py:92
  92.9 6.0 convolution_add_fusion
  104.6 11.8 %fusion.6.table_ref = bf16[26624,128]{1,0:T(8,128)(2,1)} fusion(bf16[64,25967]{0,1:T(8,128)(2,1)} %bitcast.208, bf16[1,26624]{0,1:T(8,128)(2,1)} %select_convert_fusion, bf16[128]{0:T(256)(128)(2,1)S(1)} %copy-done.93, bf16[128]{0:T(256)(128)(2,1)S(1)} %copy-done.94), kind=kLoop, calls=%fused_computation.17 | loop fusion | flops 34078720 | bytes 10193280 | tf_op jit(solution)/shard_map/transpose | solution.py:816
  116.4 11.5 %gather_fusion = bf16[2048,128]{1,0:T(8,128)(2,1)} fusion(bf16[26624,128]{1,0:T(8,128)(2,1)} %fusion.6.table_ref, s32[2048]{0:T(1024)S(1)} %copy-done.59), kind=kCustom, calls=%fused_computation | custom fusion | bytes 1056768 | tf_op jit(solution)/shard_map/jit(_take)/gather | solution.py:829
  128.0 14.1 %gather_fusion.1 = bf16[2048,1024]{1,0:T(8,128)(2,1)} fusion(bf16[2560,1024]{1,0:T(8,128)(2,1)} %pad.29.table_ref, s32[2048]{0:T(1024)S(1)} %broadcast_clamp_fusion.1), kind=kCustom, calls=%fused_computation.1 | custom fusion | bytes 8396800 | tf_op jit(solution)/shard_map/jit(_take)/gather | solution.py:829
  142.1 8.7 gather_fusion.2
  151.5 5.2 convert_reduce_fusion
  161.6 3.9 broadcast_select_fusion.head_hit_ref
  165.5 5.9 add_convert_fusion.1.rows_ref
  171.4 8.6 pick_rows.1
  183.4 20.7 %all-gather.8.cloned.1.call-done = bf16[1024,1024]{1,0:T(8,128)(2,1)} async-done(((bf16[256,1024]{1,0:T(8,128)(2,1)}), bf16[1024,1024]{1,0:T(8,128)(2,1)}) %all-gather.8.cloned.1.call-update) | async-done | bytes 2097168 | tf_op jit(solution)/shard_map/all_gather | solution.py:848
  204.2 3.9 fusion.15
  214.9 31.1 %band_forward.3 = (f32[8,2048]{1,0:T(8,128)}, bf16[2048,1024]{1,0:T(8,128)(2,1)}) custom-call(s32[2]{0:T(128)} %iota_multiply_fusion.span_ref, bf16[2048,1024]{1,0:T(8,128)(2,1)} %all-gather.6.cloned.1.call-done.rows_ref.refs_0_, bf16[2560,1024]{1,0:T(8,128)(2,1)} %pad.29.table_ref), custom_call_target="tpu_custom_call" | custom-call | flops 21474836480 | bytes 17825792 | tf_op jit(solution)/shard_map/band_forward/pallas_call | solution.py:279
  253.5 10.4 %band_forward.5 = (f32[8,2304]{1,0:T(8,128)}, bf16[2304,256]{1,0:T(8,128)(2,1)}) custom-call(s32[2]{0:T(128)} %pad_add_fusion.3.span_ref, bf16[2304,256]{1,0:T(8,128)(2,1)} %copy-done.17, bf16[5120,256]{1,0:T(8,128)(2,1)} %pad.30.table_ref), custom_call_target="tpu_custom_call" | custom-call | flops 3019898880 | bytes 6160384 | tf_op jit(solution)/shard_map/band_forward/pallas_call | solution.py:279
  263.9 48.4 %band_forward.4 = (f32[8,2304]{1,0:T(8,128)}, bf16[2304,128]{1,0:T(8,128)(2,1)}) custom-call(s32[2]{0:T(128)} %pad_add_fusion.2.span_ref, bf16[2304,256]{1,0:T(8,128)(2,1)} %copy-done.17, bf16[26624,128]{1,0:T(8,128)(2,1)} %fusion.6.table_ref), custom_call_target="tpu_custom_call" | custom-call | flops 31406948352 | bytes 8585216 | tf_op jit(solution)/shard_map/band_forward/pallas_call | solution.py:279
  324.2 12.3 %all-gather = f32[64,2304]{1,0:T(8,128)} all-gather(f32[8,2304]{1,0:T(8,128)S(1)} %maximum_maximum_fusion), channel_id=2, replica_groups=mesh['seq'=4,'batch'=8] {'batch'}, dimensions={0}, use_global_device_ids=true | all-gather | bytes 663552 | tf_op jit(solution)/shard_map/all_gather | solution.py:918
  336.5 17.6 %settle.1 = (bf16[2048,1280]{1,0:T(8,128)(2,1)}, f32[8,2048]{1,0:T(8,128)}, f32[16,2304]{1,0:T(8,128)}) custom-call(s32[1]{0:T(128)} %bitcast.member_ref, f32[8,8,2304]{2,1,0:T(8,128)} %bitcast.221, f32[8,2048]{1,0:T(8,128)} %concatenate.67.fact_ref, bf16[2048,1024]{1,0:T(8,128)(2,1)} %get-tuple-element.107.head_mix_ref, ...), custom_call_target="tpu_custom_call" | custom-call | flops 9663676416 | bytes 28114944 | tf_op jit(solution)/shard_map/settle/pallas_call | solution.py:594
  362.1 4.9 collective-permute-done.7
  372.0 32.7 %head_grad.1 = bf16[640,1024]{1,0:T(8,128)(2,1)} custom-call(s32[2]{0:T(128)} %pad_add_fusion.4.base_ref, bf16[2560,1024]{1,0:T(8,128)(2,1)} %pad.29.table_ref, bf16[2048,1024]{1,0:T(8,128)(2,1)} %all-gather.6.cloned.1.call-done.rows_ref.refs_0_, f32[4,2048]{1,0:T(4,128)} %copy-done.46, bf16[6144,1024]{1,0:T(8,128)(2,1)} %all-gather.10.cloned.1.call-done.refs_2_, ...), custom_call_target="tpu_custom_call" | custom-call | flops 21474836480 | bytes 18087936 | tf_op jit(solution)/shard_map/head_grad/pallas_call | solution.py:344
  406.1 5.6 collective-permute-start.9
  427.3 8.2 pad_maximum_fusion.3.rows_ref
  435.5 57.3 %band_grad.2 = bf16[64,6656]{1,0:T(8,128)(2,1)} custom-call(s32[187]{0:T(256)} %concatenate.72.plan_ref, bf16[26624,128]{1,0:T(8,128)(2,1)} %fusion.6.table_ref, bf16[9216,256]{1,0:T(8,128)(2,1)} %pad_maximum_fusion.3.rows_ref, f32[4,9216]{1,0:T(4,128)} %fusion.46.fact_ref), custom_call_target="tpu_custom_call" | custom-call | flops 31406948352 | bytes 5767168 | tf_op jit(solution)/shard_map/band_grad/pallas_call | solution.py:442
  498.7 7.3 convert_reduce_fusion.2
  507.4 5.9 convolution_convert_fusion.1
  513.4 10.2 %convolution_convert_fusion = bf16[4096,1024]{1,0:T(8,128)(2,1)} fusion(f32[256,1024]{1,0:T(8,128)} %copy-done.20, f32[256]{0:T(256)S(1)} %negate_multiply_fusion.2, f32[256,4096]{1,0:T(8,128)} %copy-done.103), kind=kOutput, calls=%fused_computation.12 | convolution fusion | flops 2161639424 | bytes 13632512 | tf_op jit(solution)/shard_map/dot_general | solution.py:47
  525.8 7.5 multiply_reduce_fusion.5
  536.6 21.2 %collective-permute-done.14 = bf16[640,1024]{1,0:T(8,128)(2,1)S(1)} collective-permute-done((bf16[640,1024]{1,0:T(8,128)(2,1)}, bf16[640,1024]{1,0:T(8,128)(2,1)S(1)}, u32[]{:S(2)}, u32[]{:S(2)}) %collective-permute-start.14) | collective-permute-done | bytes 1310752 | tf_op jit(solution)/shard_map/ppermute | solution.py:634
  559.8 6.6 collective-permute-start.11
  569.2 24.0 %attend_back.1 = (bf16[256,1024]{1,0:T(8,128)(2,1)}, bf16[1024,1024]{1,0:T(8,128)(2,1)}, bf16[1024,1024]{1,0:T(8,128)(2,1)}) custom-call(s32[1]{0:T(128)} %bitcast.2.start_ref, bf16[256,1024]{1,0:T(8,128)(2,1)} %fusion.21.query_ref, bf16[1024,1024]{1,0:T(8,128)(2,1)} %convolution_convert_fusion.2.key_ref, bf16[1024,1024]{1,0:T(8,128)(2,1)} %add_convert_fusion.value_ref, ...), custom_call_target="tpu_custom_call" | custom-call | flops 2684354560 | bytes 7864320 | tf_op jit(solution)/shard_map/attend_back/pallas_call | solution.py:141
  593.3 14.5 %collective-permute-done.12 = bf16[64,6656]{1,0:T(8,128)(2,1)} collective-permute-done((bf16[64,6656]{1,0:T(8,128)(2,1)}, bf16[64,6656]{1,0:T(8,128)(2,1)}, u32[]{:S(2)}, u32[]{:S(2)}) %collective-permute-start.12) | collective-permute-done | bytes 852000 | tf_op jit(solution)/shard_map/ppermute | solution.py:634
  619.0 3.8 convert_dynamic-update-slice_fusion.2
  622.8 3.8 convert_dynamic-update-slice_fusion.1
  626.7 4.2 fusion.60
  651.6 4.7 fusion.7
  660.4 4.6 collective-permute-start.22
  666.0 27.1 %band_grad.3 = f32[5000,256]{1,0:T(8,128)} custom-call(s32[187]{0:T(256)} %concatenate.78.plan_ref, bf16[5120,256]{1,0:T(8,128)(2,1)} %pad.30.table_ref, bf16[9216,256]{1,0:T(8,128)(2,1)} %pad_maximum_fusion.3.rows_ref, f32[4,9216]{1,0:T(4,128)} %fusion.46.fact_ref), custom_call_target="tpu_custom_call" | custom-call | flops 24159191040 | bytes 9961472 | tf_op jit(solution)/shard_map/band_grad/pallas_call | solution.py:442
  699.8 8.7 collective-permute-done.24
  708.6 39.4 %collective-permute-done.25 = bf16[256,1024]{1,0:T(8,128)(2,1)S(1)} collective-permute-done((bf16[256,1024]{1,0:T(8,128)(2,1)S(1)}, bf16[256,1024]{1,0:T(8,128)(2,1)S(1)}, u32[]{:S(2)}, u32[]{:S(2)}) %collective-permute-start.25) | collective-permute-done | bytes 524320 | tf_op jit(solution)/shard_map/ppermute | solution.py:696
  765.0 17.0 %collective-permute-start.32 = (bf16[128,1024]{1,0:T(8,128)(2,1)S(1)}, bf16[128,1024]{1,0:T(8,128)(2,1)S(1)}, u32[]{:S(2)}, u32[]{:S(2)}) collective-permute-start(bf16[128,1024]{1,0:T(8,128)(2,1)S(1)} %get-tuple-element.214), channel_id=1, source_target_pairs={{0,8},{8,16},{16,24},{24,0},{1,9},{9,17},{17,25},{25,1},{2,10},{10... | collective-permute-start | bytes 786440 | tf_op jit(solution)/shard_map/ppermute | solution.py:696
  789.6 3.9 collective-permute-start.34
  799.1 8.4 collective-permute-done.34
  809.2 51.2 %all-reduce.10.cloned.1.call-done = bf16[128,4480]{1,0:T(8,128)(2,1)} async-done(((bf16[128,4480]{1,0:T(8,128)(2,1)}), bf16[128,4480]{1,0:T(8,128)(2,1)}) %all-reduce.10.cloned.1.call-update) | async-done | bytes 1146896 | tf_op jit(solution)/shard_map/psum | solution.py:1149
  (503 shorter events, 205.0 us)
Async XLA Ops:
  7.2 60.7 %copy-start = (bf16[1024,1024]{1,0:T(8,128)(2,1)S(1)}, bf16[1024,1024]{1,0:T(8,128)(2,1)}, u32[]{:S(2)}) copy-start(bf16[1024,1024]{1,0:T(8,128)(2,1)} %param.38) | copy-start | bytes 6291460
  7.2 158.3 %all-gather.6.cloned.1.call-start = ((), (), s32[]{:S(2)}) async-start(), calls=%async_computation.4 | async-start | bytes 4718592 | tf_op jit(solution)/shard_map/all_gather | solution.py:845
  12.6 50.7 %collective-permute-start = (bf16[256,1024]{1,0:T(8,128)(2,1)}, bf16[256,1024]{1,0:T(8,128)(2,1)}, u32[]{:S(2)}, u32[]{:S(2)}) collective-permute-start(bf16[256,1024]{1,0:T(8,128)(2,1)} %add_convert_fusion.5), channel_id=1, source_target_pairs={{0,24},{1,25},{2,26},{3,27},{4,28},{5,29},{6,30},{7,31}} | collective-permute-start | bytes 1572872 | tf_op jit(solution)/shard_map/ppermute | solution.py:673
  20.4 44.3 %collective-permute-start.1 = (bf16[256,1024]{1,0:T(8,128)(2,1)}, bf16[256,1024]{1,0:T(8,128)(2,1)}, u32[]{:S(2)}, u32[]{:S(2)}) collective-permute-start(bf16[256,1024]{1,0:T(8,128)(2,1)} %add_convert_fusion.5), channel_id=1, source_target_pairs={{0,16},{8,24},{1,17},{9,25},{2,18},{10,26},{3,19},{11,27},{4,20},{... | collective-permute-start | bytes 1572872 | tf_op jit(solution)/shard_map/ppermute | solution.py:673
  22.4 43.4 %collective-permute-start.2 = (bf16[256,1024]{1,0:T(8,128)(2,1)}, bf16[256,1024]{1,0:T(8,128)(2,1)}, u32[]{:S(2)}, u32[]{:S(2)}) collective-permute-start(bf16[256,1024]{1,0:T(8,128)(2,1)} %add_convert_fusion.5), channel_id=1, source_target_pairs={{0,8},{8,16},{16,24},{1,9},{9,17},{17,25},{2,10},{10,18},{18,26},{... | collective-permute-start | bytes 1572872 | tf_op jit(solution)/shard_map/ppermute | solution.py:673
  104.5 99.6 %all-gather.8.cloned.1.call-start = ((), (), s32[]{:S(2)}) async-start(), calls=%async_computation.5 | async-start | bytes 2621440 | tf_op jit(solution)/shard_map/all_gather | solution.py:848
  158.0 157.2 %all-gather.10.cloned.1.call-start = ((), (), s32[]{:S(2)}) async-start(), calls=%async_computation.6 | async-start | bytes 14155776 | tf_op jit(solution)/shard_map/all_gather | solution.py:883
  183.4 62.5 %copy-start.17 = (bf16[2304,256]{1,0:T(8,128)(2,1)}, bf16[2304,256]{1,0:T(8,128)(2,1)S(1)}, u32[]{:S(2)}) copy-start(bf16[2304,256]{1,0:T(8,128)(2,1)S(1)} %slice_select_fusion.rows_ref) | copy-start | bytes 3538948
  208.0 217.0 %all-gather.12.cloned.1.call-start = ((), (), s32[]{:S(2)}) async-start(), calls=%async_computation.8 | async-start | bytes 3981312 | tf_op jit(solution)/shard_map/all_gather | solution.py:917
  211.9 101.5 %collective-permute-start.3 = (bf16[288,256]{1,0:T(8,128)(2,1)}, bf16[288,256]{1,0:T(8,128)(2,1)S(1)}, u32[]{:S(2)}, u32[]{:S(2)}) collective-permute-start(bf16[288,256]{1,0:T(8,128)(2,1)} %constant_dynamic-slice_fusion.1), channel_id=1, source_target_pairs={{0,24},{8,0},{16,8},{24,16},{1,25},{9,1},{17,9},{25,17},{2,26},{10... | collective-permute-start | bytes 442376 | tf_op jit(solution)/shard_map/ppermute | solution.py:625
  213.0 100.4 %collective-permute-start.4 = (bf16[288,256]{1,0:T(8,128)(2,1)}, bf16[288,256]{1,0:T(8,128)(2,1)}, u32[]{:S(2)}, u32[]{:S(2)}) collective-permute-start(bf16[288,256]{1,0:T(8,128)(2,1)} %constant_dynamic-slice_fusion.1), channel_id=1, source_target_pairs={{0,16},{8,24},{16,0},{24,8},{1,17},{9,25},{17,1},{25,9},{2,18},{10... | collective-permute-start | bytes 442376 | tf_op jit(solution)/shard_map/ppermute | solution.py:625
  213.1 100.3 %collective-permute-start.5 = (bf16[288,256]{1,0:T(8,128)(2,1)}, bf16[288,256]{1,0:T(8,128)(2,1)}, u32[]{:S(2)}, u32[]{:S(2)}) collective-permute-start(bf16[288,256]{1,0:T(8,128)(2,1)} %constant_dynamic-slice_fusion.1), channel_id=1, source_target_pairs={{0,8},{8,16},{16,24},{24,0},{1,9},{9,17},{17,25},{25,1},{2,10},{10... | collective-permute-start | bytes 442376 | tf_op jit(solution)/shard_map/ppermute | solution.py:625
  315.2 177.7 %reduce-scatter.5.cloned.1.call-start = ((), (), s32[]{:S(2)}) async-start(), calls=%async_computation.7 | async-start | bytes 5898240 | tf_op jit(solution)/shard_map/reduce_scatter | solution.py:934
  357.1 5.1 collective-permute-start.6
  358.7 8.3 collective-permute-start.7
  360.1 6.9 collective-permute-start.8
  360.4 283.9 %reduce-scatter.7.cloned.1.call-start = ((), (), s32[]{:S(2)}) async-start(), calls=%async_computation.9 | async-start | bytes 9437184 | tf_op jit(solution)/shard_map/reduce_scatter | solution.py:1034
  404.7 89.5 %collective-permute-start.10 = (bf16[640,1024]{1,0:T(8,128)(2,1)}, bf16[640,1024]{1,0:T(8,128)(2,1)}, u32[]{:S(2)}, u32[]{:S(2)}) collective-permute-start(bf16[640,1024]{1,0:T(8,128)(2,1)} %head_grad.1), channel_id=1, source_target_pairs={{8,0},{16,8},{24,16},{9,1},{17,9},{25,17},{10,2},{18,10},{26,18},{... | collective-permute-start | bytes 3932168 | tf_op jit(solution)/shard_map/ppermute | solution.py:634
  406.1 88.1 %collective-permute-start.9 = (bf16[640,1024]{1,0:T(8,128)(2,1)}, bf16[640,1024]{1,0:T(8,128)(2,1)}, u32[]{:S(2)}, u32[]{:S(2)}) collective-permute-start(bf16[640,1024]{1,0:T(8,128)(2,1)} %head_grad.1), channel_id=1, source_target_pairs={{0,8},{8,16},{16,24},{1,9},{9,17},{17,25},{2,10},{10,18},{18,26},{... | collective-permute-start | bytes 3932168 | tf_op jit(solution)/shard_map/ppermute | solution.py:633
  435.5 60.5 %copy-start.90 = (pred[256]{0:T(512)(128)(4,1)S(1)}, pred[256]{0:T(512)(128)(4,1)}, u32[]{:S(2)}) copy-start(pred[256]{0:T(512)(128)(4,1)} %copy-done.89) | copy-start | bytes 772
  513.3 235.9 %reduce-scatter.9.cloned.1.call-start = ((), (), s32[]{:S(2)}) async-start(), calls=%async_computation.10 | async-start | bytes 9437184 | tf_op jit(solution)/shard_map/reduce_scatter | solution.py:1028
  523.6 266.0 %reduce-scatter.11.cloned.1.call-start = ((), (), s32[]{:S(2)}) async-start(), calls=%async_computation.11 | async-start | bytes 10321920 | tf_op jit(solution)/shard_map/reduce_scatter | solution.py:1102
  523.7 12.9 %collective-permute-start.13 = (bf16[640,1024]{1,0:T(8,128)(2,1)}, bf16[640,1024]{1,0:T(8,128)(2,1)S(1)}, u32[]{:S(2)}, u32[]{:S(2)}) collective-permute-start(bf16[640,1024]{1,0:T(8,128)(2,1)} %collective-permute-done.9), channel_id=1, source_target_pairs={{8,16},{16,24},{9,17},{17,25},{10,18},{18,26},{11,19},{19,27},{12,... | collective-permute-start | bytes 3932168 | tf_op jit(solution)/shard_map/ppermute | solution.py:633
  524.5 33.2 %collective-permute-start.14 = (bf16[640,1024]{1,0:T(8,128)(2,1)}, bf16[640,1024]{1,0:T(8,128)(2,1)S(1)}, u32[]{:S(2)}, u32[]{:S(2)}) collective-permute-start(bf16[640,1024]{1,0:T(8,128)(2,1)} %collective-permute-done.10), channel_id=1, source_target_pairs={{8,0},{16,8},{9,1},{17,9},{10,2},{18,10},{11,3},{19,11},{12,4},{20... | collective-permute-start | bytes 3932168 | tf_op jit(solution)/shard_map/ppermute | solution.py:634
  557.8 35.4 %collective-permute-start.15 = (bf16[640,1024]{1,0:T(8,128)(2,1)S(1)}, bf16[640,1024]{1,0:T(8,128)(2,1)S(1)}, u32[]{:S(2)}, u32[]{:S(2)}) collective-permute-start(bf16[640,1024]{1,0:T(8,128)(2,1)S(1)} %collective-permute-done.13), channel_id=1, source_target_pairs={{16,24},{17,25},{18,26},{19,27},{20,28},{21,29},{22,30},{23,31}} | collective-permute-start | bytes 3932168 | tf_op jit(solution)/shard_map/ppermute | solution.py:633
  558.5 34.7 %collective-permute-start.16 = (bf16[640,1024]{1,0:T(8,128)(2,1)S(1)}, bf16[640,1024]{1,0:T(8,128)(2,1)}, u32[]{:S(2)}, u32[]{:S(2)}) collective-permute-start(bf16[640,1024]{1,0:T(8,128)(2,1)S(1)} %collective-permute-done.14), channel_id=1, source_target_pairs={{8,0},{9,1},{10,2},{11,3},{12,4},{13,5},{14,6},{15,7}} | collective-permute-start | bytes 3932168 | tf_op jit(solution)/shard_map/ppermute | solution.py:634
  559.8 33.4 %collective-permute-start.11 = (bf16[64,6656]{1,0:T(8,128)(2,1)}, bf16[64,6656]{1,0:T(8,128)(2,1)}, u32[]{:S(2)}, u32[]{:S(2)}) collective-permute-start(bf16[64,6656]{1,0:T(8,128)(2,1)} %band_grad.2), channel_id=1, source_target_pairs={{0,8},{8,16},{16,24},{1,9},{9,17},{17,25},{2,10},{10,18},{18,26},{... | collective-permute-start | bytes 2555912 | tf_op jit(solution)/shard_map/ppermute | solution.py:633
  566.4 41.4 %collective-permute-start.12 = (bf16[64,6656]{1,0:T(8,128)(2,1)}, bf16[64,6656]{1,0:T(8,128)(2,1)}, u32[]{:S(2)}, u32[]{:S(2)}) collective-permute-start(bf16[64,6656]{1,0:T(8,128)(2,1)} %band_grad.2), channel_id=1, source_target_pairs={{8,0},{16,8},{24,16},{9,1},{17,9},{25,17},{10,2},{18,10},{26,18},{... | collective-permute-start | bytes 2555912 | tf_op jit(solution)/shard_map/ppermute | solution.py:634
  607.8 36.5 %collective-permute-start.17 = (bf16[64,6656]{1,0:T(8,128)(2,1)}, bf16[64,6656]{1,0:T(8,128)(2,1)}, u32[]{:S(2)}, u32[]{:S(2)}) collective-permute-start(bf16[64,6656]{1,0:T(8,128)(2,1)} %collective-permute-done.11), channel_id=1, source_target_pairs={{8,16},{16,24},{9,17},{17,25},{10,18},{18,26},{11,19},{19,27},{12,... | collective-permute-start | bytes 2555912 | tf_op jit(solution)/shard_map/ppermute | solution.py:633
  609.4 34.9 %collective-permute-start.18 = (bf16[64,6656]{1,0:T(8,128)(2,1)}, bf16[64,6656]{1,0:T(8,128)(2,1)}, u32[]{:S(2)}, u32[]{:S(2)}) collective-permute-start(bf16[64,6656]{1,0:T(8,128)(2,1)} %collective-permute-done.12), channel_id=1, source_target_pairs={{8,0},{16,8},{9,1},{17,9},{10,2},{18,10},{11,3},{19,11},{12,4},{20... | collective-permute-start | bytes 2555912 | tf_op jit(solution)/shard_map/ppermute | solution.py:634
  644.4 216.1 %all-reduce.10.cloned.1.call-start = ((), (), s32[]{:S(2)}) async-start(), calls=%async_computation.12 | async-start | bytes 2293760 | tf_op jit(solution)/shard_map/psum | solution.py:1149
  656.2 93.0 %collective-permute-start.19 = (bf16[64,6656]{1,0:T(8,128)(2,1)}, bf16[64,6656]{1,0:T(8,128)(2,1)}, u32[]{:S(2)}, u32[]{:S(2)}) collective-permute-start(bf16[64,6656]{1,0:T(8,128)(2,1)} %collective-permute-done.17), channel_id=1, source_target_pairs={{16,24},{17,25},{18,26},{19,27},{20,28},{21,29},{22,30},{23,31}} | collective-permute-start | bytes 2555912 | tf_op jit(solution)/shard_map/ppermute | solution.py:633
  657.8 91.4 %collective-permute-start.20 = (bf16[64,6656]{1,0:T(8,128)(2,1)}, bf16[64,6656]{1,0:T(8,128)(2,1)}, u32[]{:S(2)}, u32[]{:S(2)}) collective-permute-start(bf16[64,6656]{1,0:T(8,128)(2,1)} %collective-permute-done.18), channel_id=1, source_target_pairs={{8,0},{9,1},{10,2},{11,3},{12,4},{13,5},{14,6},{15,7}} | collective-permute-start | bytes 2555912 | tf_op jit(solution)/shard_map/ppermute | solution.py:634
  660.0 34.6 %collective-permute-start.21 = (bf16[32,4096]{1,0:T(8,128)(2,1)}, bf16[32,4096]{1,0:T(8,128)(2,1)S(1)}, u32[]{:S(2)}, u32[]{:S(2)}) collective-permute-start(bf16[32,4096]{1,0:T(8,128)(2,1)} %get-tuple-element.216), channel_id=1, source_target_pairs={{0,24},{8,0},{16,8},{24,16},{1,25},{9,1},{17,9},{25,17},{2,26},{10... | collective-permute-start | bytes 786440 | tf_op jit(solution)/shard_map/ppermute | solution.py:696
  660.4 35.6 %collective-permute-start.22 = (bf16[32,4096]{1,0:T(8,128)(2,1)}, bf16[32,4096]{1,0:T(8,128)(2,1)}, u32[]{:S(2)}, u32[]{:S(2)}) collective-permute-start(bf16[32,4096]{1,0:T(8,128)(2,1)} %get-tuple-element.218), channel_id=1, source_target_pairs={{0,16},{8,24},{16,0},{24,8},{1,17},{9,25},{17,1},{25,9},{2,18},{10... | collective-permute-start | bytes 786440 | tf_op jit(solution)/shard_map/ppermute | solution.py:696
  665.0 32.3 %collective-permute-start.23 = (bf16[32,4096]{1,0:T(8,128)(2,1)}, bf16[32,4096]{1,0:T(8,128)(2,1)}, u32[]{:S(2)}, u32[]{:S(2)}) collective-permute-start(bf16[32,4096]{1,0:T(8,128)(2,1)} %get-tuple-element.217), channel_id=1, source_target_pairs={{0,8},{8,16},{16,24},{24,0},{1,9},{9,17},{17,25},{25,1},{2,10},{10... | collective-permute-start | bytes 786440 | tf_op jit(solution)/shard_map/ppermute | solution.py:696
  694.7 13.9 %collective-permute-start.24 = (bf16[256,1024]{1,0:T(8,128)(2,1)S(1)}, bf16[256,1024]{1,0:T(8,128)(2,1)S(1)}, u32[]{:S(2)}, u32[]{:S(2)}) collective-permute-start(bf16[256,1024]{1,0:T(8,128)(2,1)S(1)} %get-tuple-element.209), channel_id=1, source_target_pairs={{8,0},{16,8},{24,16},{9,1},{17,9},{25,17},{10,2},{18,10},{26,18},{... | collective-permute-start | bytes 1572872 | tf_op jit(solution)/shard_map/ppermute | solution.py:696
  696.0 52.0 %collective-permute-start.25 = (bf16[256,1024]{1,0:T(8,128)(2,1)S(1)}, bf16[256,1024]{1,0:T(8,128)(2,1)S(1)}, u32[]{:S(2)}, u32[]{:S(2)}) collective-permute-start(bf16[256,1024]{1,0:T(8,128)(2,1)S(1)} %get-tuple-element.211), channel_id=1, source_target_pairs={{16,0},{24,8},{17,1},{25,9},{18,2},{26,10},{19,3},{27,11},{20,4},{... | collective-permute-start | bytes 1572872 | tf_op jit(solution)/shard_map/ppermute | solution.py:696
  697.3 50.7 %collective-permute-start.26 = (bf16[256,1024]{1,0:T(8,128)(2,1)S(1)}, bf16[256,1024]{1,0:T(8,128)(2,1)S(1)}, u32[]{:S(2)}, u32[]{:S(2)}) collective-permute-start(bf16[256,1024]{1,0:T(8,128)(2,1)S(1)} %get-tuple-element.210), channel_id=1, source_target_pairs={{24,0},{25,1},{26,2},{27,3},{28,4},{29,5},{30,6},{31,7}} | collective-permute-start | bytes 1572872 | tf_op jit(solution)/shard_map/ppermute | solution.py:696
  749.3 38.9 %collective-permute-start.27 = (bf16[32,4096]{1,0:T(8,128)(2,1)S(1)}, bf16[32,4096]{1,0:T(8,128)(2,1)S(1)}, u32[]{:S(2)}, u32[]{:S(2)}) collective-permute-start(bf16[32,4096]{1,0:T(8,128)(2,1)S(1)} %fusion.41), channel_id=1, source_target_pairs={{0,24},{8,0},{16,8},{24,16},{1,25},{9,1},{17,9},{25,17},{2,26},{10... | collective-permute-start | bytes 786440 | tf_op jit(solution)/shard_map/ppermute | solution.py:625
  749.3 38.9 %collective-permute-start.28 = (bf16[32,4096]{1,0:T(8,128)(2,1)S(1)}, bf16[32,4096]{1,0:T(8,128)(2,1)S(1)}, u32[]{:S(2)}, u32[]{:S(2)}) collective-permute-start(bf16[32,4096]{1,0:T(8,128)(2,1)S(1)} %fusion.41), channel_id=1, source_target_pairs={{0,16},{8,24},{16,0},{24,8},{1,17},{9,25},{17,1},{25,9},{2,18},{10... | collective-permute-start | bytes 786440 | tf_op jit(solution)/shard_map/ppermute | solution.py:625
  749.4 40.2 %collective-permute-start.29 = (bf16[32,4096]{1,0:T(8,128)(2,1)S(1)}, bf16[32,4096]{1,0:T(8,128)(2,1)}, u32[]{:S(2)}, u32[]{:S(2)}) collective-permute-start(bf16[32,4096]{1,0:T(8,128)(2,1)S(1)} %fusion.41), channel_id=1, source_target_pairs={{0,8},{8,16},{16,24},{24,0},{1,9},{9,17},{17,25},{25,1},{2,10},{10... | collective-permute-start | bytes 786440 | tf_op jit(solution)/shard_map/ppermute | solution.py:625
  752.5 12.5 %collective-permute-start.30 = (bf16[128,1024]{1,0:T(8,128)(2,1)S(1)}, bf16[128,1024]{1,0:T(8,128)(2,1)S(1)}, u32[]{:S(2)}, u32[]{:S(2)}) collective-permute-start(bf16[128,1024]{1,0:T(8,128)(2,1)S(1)} %get-tuple-element.213), channel_id=1, source_target_pairs={{0,24},{8,0},{16,8},{24,16},{1,25},{9,1},{17,9},{25,17},{2,26},{10... | collective-permute-start | bytes 786440 | tf_op jit(solution)/shard_map/ppermute | solution.py:696
  754.9 29.4 %collective-permute-start.31 = (bf16[128,1024]{1,0:T(8,128)(2,1)S(1)}, bf16[128,1024]{1,0:T(8,128)(2,1)S(1)}, u32[]{:S(2)}, u32[]{:S(2)}) collective-permute-start(bf16[128,1024]{1,0:T(8,128)(2,1)S(1)} %get-tuple-element.215), channel_id=1, source_target_pairs={{0,16},{8,24},{16,0},{24,8},{1,17},{9,25},{17,1},{25,9},{2,18},{10... | collective-permute-start | bytes 786440 | tf_op jit(solution)/shard_map/ppermute | solution.py:696
  765.0 22.0 %collective-permute-start.32 = (bf16[128,1024]{1,0:T(8,128)(2,1)S(1)}, bf16[128,1024]{1,0:T(8,128)(2,1)S(1)}, u32[]{:S(2)}, u32[]{:S(2)}) collective-permute-start(bf16[128,1024]{1,0:T(8,128)(2,1)S(1)} %get-tuple-element.214), channel_id=1, source_target_pairs={{0,8},{8,16},{16,24},{24,0},{1,9},{9,17},{17,25},{25,1},{2,10},{10... | collective-permute-start | bytes 786440 | tf_op jit(solution)/shard_map/ppermute | solution.py:696
  789.6 9.5 %collective-permute-start.33 = (bf16[128,1024]{1,0:T(8,128)(2,1)S(1)}, bf16[128,1024]{1,0:T(8,128)(2,1)S(1)}, u32[]{:S(2)}, u32[]{:S(2)}) collective-permute-start(bf16[128,1024]{1,0:T(8,128)(2,1)S(1)} %fusion.38), channel_id=1, source_target_pairs={{0,24},{8,0},{16,8},{24,16},{1,25},{9,1},{17,9},{25,17},{2,26},{10... | collective-permute-start | bytes 786440 | tf_op jit(solution)/shard_map/ppermute | solution.py:625
  789.6 17.9 %collective-permute-start.34 = (bf16[128,1024]{1,0:T(8,128)(2,1)S(1)}, bf16[128,1024]{1,0:T(8,128)(2,1)S(1)}, u32[]{:S(2)}, u32[]{:S(2)}) collective-permute-start(bf16[128,1024]{1,0:T(8,128)(2,1)S(1)} %fusion.38), channel_id=1, source_target_pairs={{0,16},{8,24},{16,0},{24,8},{1,17},{9,25},{17,1},{25,9},{2,18},{10... | collective-permute-start | bytes 786440 | tf_op jit(solution)/shard_map/ppermute | solution.py:625
  793.6 14.0 %collective-permute-start.35 = (bf16[128,1024]{1,0:T(8,128)(2,1)S(1)}, bf16[128,1024]{1,0:T(8,128)(2,1)S(1)}, u32[]{:S(2)}, u32[]{:S(2)}) collective-permute-start(bf16[128,1024]{1,0:T(8,128)(2,1)S(1)} %fusion.38), channel_id=1, source_target_pairs={{0,8},{8,16},{16,24},{24,0},{1,9},{9,17},{17,25},{25,1},{2,10},{10... | collective-permute-start | bytes 786440 | tf_op jit(solution)/shard_map/ppermute | solution.py:625
  (106 other events, 1428.0 us)
Sparse Core Ops, SparseCore 0:
  104.6 36.7 all-gather.5
  158.1 46.0 all-gather.7
  208.2 70.8 all-gather.9
  315.3 35.3 all-gather.11
  360.5 56.2 reduce-scatter.4
  513.4 70.0 reduce-scatter.6
  587.0 71.2 reduce-scatter.8
  662.4 75.0 reduce-scatter.10
  798.4 62.0 all-reduce.9

commit v7 on v6

--- a/solution.py
+++ b/solution.py
@@ -650,7 +650,7 @@
     return found, advance
 
 
-def line_ordered(found, axis):
+def line_ordered(found):
     size, place = lax.axis_size("seq"), lax.axis_index("seq")
     ordered = []
     for source in range(size):
@@ -661,7 +661,7 @@
             if source - step >= 0:
                 value = jnp.where(place == source - step, found[step][1], value)
         ordered.append(value)
-    return jnp.concatenate(ordered, axis)
+    return ordered
 
 
 def earlier_joined(value):
@@ -871,8 +871,12 @@
         piece = slot_count // nb
         slot_piece = lax.dynamic_slice_in_dim(slot_low, member * piece, piece, 0)
         other_slots = jnp.concatenate(line_turns(slot_piece)[1:], 0)
-        slot_low, block_states, hit_rows = lax.optimization_barrier(
-            (slot_low, block_states, hit_rows)
+    head_stats, head_mix = band_forward(
+        head_span, all_states, head_pad, sizes[0], head_chunk, None, 1.0
+    )
+    if split:
+        slot_low, block_states, hit_rows, head_stats = lax.optimization_barrier(
+            (slot_low, block_states, hit_rows, head_stats)
         )
         other_states = lax.dynamic_slice_in_dim(
             jnp.concatenate([block_states, block_states], 0),
@@ -886,9 +890,6 @@
     )
     middle_stats, middle_mix = band_forward(
         middle_span, slot_low, middle_pad, sizes[1], middle_chunk, None, 0.25
-    )
-    head_stats, head_mix = band_forward(
-        head_span, all_states, head_pad, sizes[0], head_chunk, None, 1.0
     )
     inner_lane = jnp.arange(128) < tail_width
     target_part = (
@@ -977,26 +978,36 @@
     facts = jnp.concatenate(
         [facts[:2], jnp.where(facts[3:4] > 0, facts[2:3], -1e9), jnp.zeros_like(facts[:1])], 0
     )
-    tail_part = band_grad(
-        tail_pad,
-        rows_all,
-        facts,
-        block_kind == 2,
-        lowest,
-        highest,
-        part,
-        tail_padded // parts,
-        HEAD_WORDS + MID_WORDS + member * sizes[2],
-        math.gcd(tail_padded // parts, tail_chunk),
-        jax.ShapeDtypeStruct((tail_width, tail_padded // parts), jnp.bfloat16),
-        True,
-    )
+    def tail_gradient(part, parts):
+        return band_grad(
+            tail_pad,
+            rows_all,
+            facts,
+            block_kind == 2,
+            lowest,
+            highest,
+            part,
+            tail_padded // parts,
+            HEAD_WORDS + MID_WORDS + member * sizes[2],
+            math.gcd(tail_padded // parts, tail_chunk),
+            jax.ShapeDtypeStruct((tail_width, tail_padded // parts), jnp.bfloat16),
+            True,
+        )
+
+    first_tail = tail_gradient(2 * part, 2 * parts)
     if split:
         head_found, head_advance = line_steps(head_part)
-        own_terms, tail_part = head_advance(own_terms, tail_part)
-        tail_found, tail_advance = line_steps(tail_part)
+        first_tail, facts = head_advance(first_tail, facts)
+        first_found, first_advance = line_steps(first_tail)
+        second_tail = tail_gradient(2 * part + 1, 2 * parts)
+        second_tail, own_terms = head_advance(second_tail, own_terms)
+        second_tail, own_terms = first_advance(second_tail, own_terms)
+        second_found, second_advance = line_steps(second_tail)
     else:
-        own_terms, tail_part = lax.optimization_barrier((own_terms, tail_part))
+        second_tail = tail_gradient(2 * part + 1, 2 * parts)
+        own_terms, first_tail, second_tail = lax.optimization_barrier(
+            (own_terms, first_tail, second_tail)
+        )
 
     own_middle = own_part(in_middle)
     own_tail = own_part(in_tail)
@@ -1043,14 +1054,15 @@
     out_bias_grad = jnp.sum(mixed_grad, 0)
     attended_grad = lowered(product_nt(mixed_low, out_weight))
     if split:
-        (attended_grad,) = head_advance(attended_grad)
+        for unused in range(nz - 3):
+            (attended_grad,) = head_advance(attended_grad)
+        (attended_grad,) = second_advance(attended_grad)
     query_low, key_low, value_low = attend_back(
         query_start, queries, key_rows, value_rows, attended_grad
     )
     if split:
-        for unused in range(nz - 3):
-            query_low, key_low, value_low = head_advance(query_low, key_low, value_low)
-        query_low, key_low, value_low = tail_advance(query_low, key_low, value_low)
+        query_low, key_low, value_low = first_advance(query_low, key_low, value_low)
+        query_low, key_low, value_low = second_advance(query_low, key_low, value_low)
     query_weight_grad = product_tn(normed_low, query_low)
     key_weight_grad = product_tn(normed_all, key_low)
     value_weight_grad = product_tn(normed_all, value_low)
@@ -1096,11 +1108,16 @@
     ]
     rest = jnp.concatenate([lowered(column) for column in columns], 1)
     spread_low = lowered(spread)
-    rest, facts, spread_low = lax.optimization_barrier((rest, facts, spread_low))
+    inner_low = lowered(line_scatter(inner_part))
+    rest, facts, spread_low, inner_low = lax.optimization_barrier(
+        (rest, facts, spread_low, inner_low)
+    )
     if split:
-        rest, facts, spread_low, inner_part = tail_advance(rest, facts, spread_low, inner_part)
+        for unused in range(nz - 3):
+            rest, facts, spread_low = first_advance(rest, facts, spread_low)
+            rest, facts, spread_low = second_advance(rest, facts, spread_low)
     rest_part = lax.psum_scatter(rest, "batch", scatter_dimension=0, tiled=True)
-    inner_low = lowered(line_scatter(inner_part))
+    inner_pieces = line_turns(inner_low)
     spread_sum = line_scatter(spread_low, False)
     middle_result = jax.ShapeDtypeStruct(
         (sizes[1], middle_width) if split else (middle_padded, middle_width),
@@ -1120,25 +1137,20 @@
         middle_result,
         False,
     )
-    if split:
-        for unused in range(nz - 3):
-            (middle_part,) = tail_advance(middle_part)
-    middle_part, inner_low, spread_sum, outer_part = lax.optimization_barrier(
-        (middle_part, inner_low, spread_sum, outer_part)
-    )
-    inner_pieces = line_turns(inner_low)
+    middle_part, inner_pieces, spread_sum, outer_part = lax.optimization_barrier(
+        (middle_part, inner_pieces, spread_sum, outer_part)
+    )
     outer_low = lowered(line_scatter(outer_part))
-    rest_part, inner_pieces, outer_low = lax.optimization_barrier(
-        (rest_part, inner_pieces, outer_low)
-    )
+    rest_part, outer_low = lax.optimization_barrier((rest_part, outer_low))
     if split:
         middle_table_grad = middle_part
-        head_table_grad = line_ordered(head_found, 0)
-        tail_sum = line_ordered(tail_found, 1)
+        head_table_grad = jnp.concatenate(line_ordered(head_found), 0)
+        pairs = zip(line_ordered(first_found), line_ordered(second_found))
+        tail_sum = jnp.concatenate([value for pair in pairs for value in pair], 1)
     else:
         middle_table_grad = lax.psum(middle_part, "seq")[: sizes[1]].astype(jnp.float32)
         head_table_grad = lax.psum(head_part, "seq")
-        tail_sum = lax.psum(tail_part, "seq")
+        tail_sum = lax.psum(jnp.concatenate([first_tail, second_tail], 1), "seq")
     head_table_grad = head_table_grad[: sizes[0]].astype(jnp.float32)
     tail_table_grad = tail_sum[:, : sizes[2]].astype(jnp.float32).T
     normed_grad = query_spread + spread_sum

time: 888 us -> 855 us (0.963)
  waiting for transfers between devices: 177 us -> 136 us
  other arithmetic: 114 us -> 125 us
    ppermute x9, waiting for transfers between devices: 54.6 us -> 15.9 us  [line_scatter(): lax.ppermute(part(place + size - k), 'seq', pairs).astype(jnp.float32)]
    ppermute x12, waiting for transfers between devices: 14 us -> 46.4 us  [line_turns(): lax.ppermute(value, 'seq', [(d, (d - k) % size) for d in range(size)])]
    all_gather x1, waiting for transfers between devices: 20.7 us -> 0.01 us  [on_device(): block_states = lax.all_gather(state_low, 'seq', axis=0, tiled=True)]
    psum x1, waiting for transfers between devices: 51.2 us -> 30.9 us  [on_device(): rest_low = lax.psum(rest_part, 'seq')]
    ppermute x9, starting transfers between devices: 30 us -> 14.7 us  [line_scatter(): lax.ppermute(part(place + size - k), 'seq', pairs).astype(jnp.float32)]
    ppermute x12, starting transfers between devices: 12.4 us -> 23.8 us  [line_turns(): lax.ppermute(value, 'seq', [(d, (d - k) % size) for d in range(size)])]
    unnamed x1 -> x8, other arithmetic: 0.01 us -> 11 us
    reduce_scatter x1, waiting for transfers between devices: 0.01 us -> 9.74 us  [on_device(): rest_part = lax.psum_scatter(rest, 'batch', scatter_dimension=0, tiled=True)]
  transfers between devices with their start and end apart: 45 -> 51, of which waited for: 13 -> 13; matrix products, arithmetic and copies ran while one was open for 28% -> 30% of each run, Pallas kernels for 29% -> 30%
where the time goes in v7:
time: 855 us; the launch traced here: 841 us
  Pallas kernels  268 us (31%)
  waiting for transfers between devices  136 us (16%)
  other arithmetic  125 us (15%)
  local copies, waits for them, and re-layouts  99.5 us (12%)
  matrix products  90.1 us (11%)
  starting transfers between devices  82.5 us (10%)
  blocking collectives  21.7 us (3%)
  between operations  18.7 us (2%)
    pallas_call x3, Pallas kernels, band_grad(): pl.pallas_call(functools.partial(band_grad_kernel, chunk // 2 if chunk >...  84.6 us
    pallas_call x3, Pallas kernels, band_forward(): pl.pallas_call(functools.partial(band_kernel, chunk, per, words, sum_colu...  82.1 us
    ppermute x12, waiting for transfers between devices, line_turns(): lax.ppermute(value, 'seq', [(d, (d - k) % size) for d in range(size)])  46.4 us
    gather x3, local copies, waits for them, and re-layouts, on_device(): jnp.take(table, jnp.clip(local, 0, size - 1), axis=0, mode='clip')  34.3 us
    dot_general x9, matrix products, product_tn(): lax.dot_general(former, latter, (((0,), (0,)), ((), ())), preferred_eleme...  33 us
    pallas_call x1, Pallas kernels, head_grad(): pl.pallas_call(functools.partial(head_grad_kernel, chunk, len(lists)), gr...  32.7 us
    ppermute x9, waiting for transfers between devices, line_step(): lax.ppermute(behind, 'seq', [(d, d - 1) for d in range(1, size - step + 1)])  31 us
    psum x1, waiting for transfers between devices, on_device(): rest_low = lax.psum(rest_part, 'seq')  30.9 us
  transfers between devices with their start and end apart: 51, of which 13 were waited for; matrix products, arithmetic and copies ran while one was open for 30% of the time, Pallas kernels for 30%

profile of v7, /device:TPU:0, one launch (start us, length us, event | category | flops | bytes accessed | tf_op | source)
XLA Modules:
  0.0 840.8 jit_solution(15930966321542100050)
XLA Ops:
  12.6 7.8 collective-permute-start
  26.8 9.1 %all_gather.21 = f32[3,2048]{1,0:T(4,128)S(1)} all-gather(f32[3,256]{1,0:T(4,128)S(1)} %pad_maximum_fusion.9), channel_id=1, replica_groups=mesh['seq'=4,'batch'=8] {'batch'}, dimensions={1}, use_global_device_ids=true | all-gather | bytes 27648 | tf_op jit(solution)/shard_map/all_gather | solution.py:765
  46.7 7.4 copy.119
  55.3 5.5 pad.29.table_ref
  73.9 15.2 %attend.1 = bf16[256,1024]{1,0:T(8,128)(2,1)} custom-call(s32[1]{0:T(128)} %bitcast.6.start_ref, bf16[256,1024]{1,0:T(8,128)(2,1)} %fusion.21.query_ref, bf16[1024,1024]{1,0:T(8,128)(2,1)} %convolution_convert_fusion.2.key_ref, bf16[1024,1024]{1,0:T(8,128)(2,1)} %add_convert_fusion.value_ref), custom_call_target="tpu_custom_call" | custom-call | flops 1073741824 | bytes 5242880 | tf_op jit(solution)/shard_map/attend/pallas_call | solution.py:92
  91.5 6.0 convolution_add_fusion
  103.2 11.9 %fusion.6.table_ref = bf16[26624,128]{1,0:T(8,128)(2,1)} fusion(bf16[64,25967]{0,1:T(8,128)(2,1)} %bitcast.210, bf16[1,26624]{0,1:T(8,128)(2,1)} %select_convert_fusion, bf16[128]{0:T(256)(128)(2,1)S(1)} %copy-done.87, bf16[128]{0:T(256)(128)(2,1)S(1)} %copy-done.88), kind=kLoop, calls=%fused_computation.17 | loop fusion | flops 34078720 | bytes 10193280 | tf_op jit(solution)/shard_map/transpose | solution.py:816
  115.1 11.5 %gather_fusion = bf16[2048,128]{1,0:T(8,128)(2,1)} fusion(bf16[26624,128]{1,0:T(8,128)(2,1)} %fusion.6.table_ref, s32[2048]{0:T(1024)S(1)} %copy-done.57), kind=kCustom, calls=%fused_computation | custom fusion | bytes 1056768 | tf_op jit(solution)/shard_map/jit(_take)/gather | solution.py:829
  126.7 14.1 %gather_fusion.1 = bf16[2048,1024]{1,0:T(8,128)(2,1)} fusion(bf16[2560,1024]{1,0:T(8,128)(2,1)} %pad.29.table_ref, s32[2048]{0:T(1024)S(1)} %broadcast_clamp_fusion.1), kind=kCustom, calls=%fused_computation.1 | custom fusion | bytes 8396800 | tf_op jit(solution)/shard_map/jit(_take)/gather | solution.py:829
  140.8 8.7 %gather_fusion.2 = bf16[2048,256]{1,0:T(8,128)(2,1)S(1)} fusion(bf16[5120,256]{1,0:T(8,128)(2,1)} %pad.30.table_ref, s32[2048]{0:T(1024)S(1)} %broadcast_clamp_fusion), kind=kCustom, calls=%fused_computation.2 | custom fusion | bytes 2105344 | tf_op jit(solution)/shard_map/jit(_take)/gather | solution.py:829
  150.7 5.2 convert_reduce_fusion
  160.6 3.9 broadcast_select_fusion.head_hit_ref
  164.6 5.7 add_convert_fusion.1.rows_ref
  170.3 8.8 %pick_rows.1 = bf16[2304,384]{1,0:T(8,128)(2,1)} custom-call(s32[1,2048]{1,0:T(1,128)} %bitcast.229, bf16[2048,384]{1,0:T(8,128)(2,1)} %add_convert_fusion.1.rows_ref), custom_call_target="tpu_custom_call" | custom-call | flops 3623878656 | bytes 5111808 | tf_op jit(solution)/shard_map/pick_rows/pallas_call | solution.py:188
  182.5 29.8 %band_forward.3 = (f32[8,2048]{1,0:T(8,128)}, bf16[2048,1024]{1,0:T(8,128)(2,1)}) custom-call(s32[2]{0:T(128)} %iota_multiply_fusion.1.span_ref, bf16[2048,1024]{1,0:T(8,128)(2,1)} %all-gather.6.cloned.1.call-done.rows_ref.refs_0_, bf16[2560,1024]{1,0:T(8,128)(2,1)} %pad.29.table_ref), custom_call_target="tpu_custom_call" | custom-call | flops 21474836480 | bytes 17825792 | tf_op jit(solution)/shard_map/band_forward/pallas_call | solution.py:279
  228.8 4.6 multiply_reduce_fusion
  233.5 11.9 %band_forward.5 = (f32[8,2304]{1,0:T(8,128)}, bf16[2304,256]{1,0:T(8,128)(2,1)}) custom-call(s32[2]{0:T(128)} %pad_add_fusion.4.span_ref, bf16[2304,256]{1,0:T(8,128)(2,1)} %copy-done.18, bf16[5120,256]{1,0:T(8,128)(2,1)} %pad.30.table_ref), custom_call_target="tpu_custom_call" | custom-call | flops 3019898880 | bytes 6160384 | tf_op jit(solution)/shard_map/band_forward/pallas_call | solution.py:279
  245.5 40.3 %band_forward.4 = (f32[8,2304]{1,0:T(8,128)}, bf16[2304,128]{1,0:T(8,128)(2,1)}) custom-call(s32[2]{0:T(128)} %pad_add_fusion.3.span_ref, bf16[2304,256]{1,0:T(8,128)(2,1)} %copy-done.18, bf16[26624,128]{1,0:T(8,128)(2,1)} %fusion.6.table_ref), custom_call_target="tpu_custom_call" | custom-call | flops 31406948352 | bytes 8585216 | tf_op jit(solution)/shard_map/band_forward/pallas_call | solution.py:279
  295.7 12.7 %all-gather = f32[64,2304]{1,0:T(8,128)} all-gather(f32[8,2304]{1,0:T(8,128)S(1)} %maximum_maximum_fusion), channel_id=2, replica_groups=mesh['seq'=4,'batch'=8] {'batch'}, dimensions={0}, use_global_device_ids=true | all-gather | bytes 663552 | tf_op jit(solution)/shard_map/all_gather | solution.py:919
  308.3 17.4 %settle.1 = (bf16[2048,1280]{1,0:T(8,128)(2,1)}, f32[8,2048]{1,0:T(8,128)}, f32[16,2304]{1,0:T(8,128)}) custom-call(s32[1]{0:T(128)} %bitcast.member_ref, f32[8,8,2304]{2,1,0:T(8,128)} %bitcast.223, f32[8,2048]{1,0:T(8,128)} %concatenate.73.fact_ref, bf16[2048,1024]{1,0:T(8,128)(2,1)} %get-tuple-element.121.head_mix_ref, ...), custom_call_target="tpu_custom_call" | custom-call | flops 9663676416 | bytes 28114944 | tf_op jit(solution)/shard_map/settle/pallas_call | solution.py:594
  335.6 5.6 collective-permute-done.7
  344.7 32.7 %head_grad.1 = bf16[640,1024]{1,0:T(8,128)(2,1)} custom-call(s32[2]{0:T(128)} %pad_add_fusion.5.base_ref, bf16[2560,1024]{1,0:T(8,128)(2,1)} %pad.29.table_ref, bf16[2048,1024]{1,0:T(8,128)(2,1)} %all-gather.6.cloned.1.call-done.rows_ref.refs_0_, f32[4,2048]{1,0:T(4,128)} %copy-done.45, bf16[6144,1024]{1,0:T(8,128)(2,1)} %all-gather.10.cloned.1.call-done.refs_2_, ...), custom_call_target="tpu_custom_call" | custom-call | flops 21474836480 | bytes 18087936 | tf_op jit(solution)/shard_map/head_grad/pallas_call | solution.py:344
  378.7 5.6 collective-permute-start.9
  393.8 8.3 pad_maximum_fusion.3.rows_ref
  402.1 27.0 %band_grad.3 = bf16[64,3328]{1,0:T(8,128)(2,1)} custom-call(s32[113]{0:T(128)} %concatenate.78.plan_ref, bf16[26624,128]{1,0:T(8,128)(2,1)} %fusion.6.table_ref, bf16[9216,256]{1,0:T(8,128)(2,1)} %pad_maximum_fusion.3.rows_ref, f32[4,9216]{1,0:T(4,128)} %fusion.46.fact_ref), custom_call_target="tpu_custom_call" | custom-call | flops 15703474176 | bytes 4063232 | tf_op jit(solution)/shard_map/band_grad/pallas_call | solution.py:442
  435.5 27.2 %band_grad.4 = bf16[64,3328]{1,0:T(8,128)(2,1)} custom-call(s32[113]{0:T(128)} %concatenate.82.plan_ref, bf16[26624,128]{1,0:T(8,128)(2,1)} %fusion.6.table_ref, bf16[9216,256]{1,0:T(8,128)(2,1)} %pad_maximum_fusion.3.rows_ref, f32[4,9216]{1,0:T(4,128)} %fusion.46.fact_ref), custom_call_target="tpu_custom_call" | custom-call | flops 15703474176 | bytes 4063232 | tf_op jit(solution)/shard_map/band_grad/pallas_call | solution.py:442
  464.0 8.3 collective-permute-done.14
  476.5 7.1 convert_reduce_fusion.2
  484.9 5.9 convolution_convert_fusion.1
  496.7 3.9 collective-permute-start.15
  506.7 9.0 %convolution_convert_fusion = bf16[4096,1024]{1,0:T(8,128)(2,1)} fusion(f32[256,1024]{1,0:T(8,128)} %copy-done.21, f32[256]{0:T(256)S(1)} %negate_multiply_fusion.2, f32[256,4096]{1,0:T(8,128)} %copy-done.95), kind=kOutput, calls=%fused_computation.12 | convolution fusion | flops 2161639424 | bytes 13632512 | tf_op jit(solution)/shard_map/dot_general | solution.py:47
  515.8 7.5 multiply_reduce_fusion.5
  530.5 13.2 %collective-permute-done.18 = bf16[640,1024]{1,0:T(8,128)(2,1)} collective-permute-done((bf16[640,1024]{1,0:T(8,128)(2,1)}, bf16[640,1024]{1,0:T(8,128)(2,1)}, u32[]{:S(2)}, u32[]{:S(2)}) %collective-permute-start.18) | collective-permute-done | bytes 1310752 | tf_op jit(solution)/shard_map/ppermute | solution.py:634
  543.7 23.9 %attend_back.1 = (bf16[256,1024]{1,0:T(8,128)(2,1)}, bf16[1024,1024]{1,0:T(8,128)(2,1)}, bf16[1024,1024]{1,0:T(8,128)(2,1)}) custom-call(s32[1]{0:T(128)} %bitcast.6.start_ref, bf16[256,1024]{1,0:T(8,128)(2,1)} %fusion.21.query_ref, bf16[1024,1024]{1,0:T(8,128)(2,1)} %convolution_convert_fusion.2.key_ref, bf16[1024,1024]{1,0:T(8,128)(2,1)} %add_convert_fusion.value_ref, ...), custom_call_target="tpu_custom_call" | custom-call | flops 2684354560 | bytes 7864320 | tf_op jit(solution)/shard_map/attend_back/pallas_call | solution.py:141
  572.3 4.5 select_select_fusion.3
  576.8 5.3 fusion.7
  587.3 4.2 fusion.64
  613.6 3.9 collective-permute-start.28
  625.6 9.6 %collective-permute-done.28 = bf16[32,4096]{1,0:T(8,128)(2,1)} collective-permute-done((bf16[32,4096]{1,0:T(8,128)(2,1)}, bf16[32,4096]{1,0:T(8,128)(2,1)}, u32[]{:S(2)}, u32[]{:S(2)}) %collective-permute-start.28) | collective-permute-done | bytes 262176 | tf_op jit(solution)/shard_map/ppermute | solution.py:696
  638.0 4.1 collective-permute-start.31
  642.1 9.4 %collective-permute-done.24 = bf16[64,3328]{1,0:T(8,128)(2,1)S(1)} collective-permute-done((bf16[64,3328]{1,0:T(8,128)(2,1)}, bf16[64,3328]{1,0:T(8,128)(2,1)S(1)}, u32[]{:S(2)}, u32[]{:S(2)}) %collective-permute-start.24) | collective-permute-done | bytes 426016 | tf_op jit(solution)/shard_map/ppermute | solution.py:634
  670.0 5.2 convert_bitcast_fusion
  675.2 30.4 %band_grad.5 = f32[5000,256]{1,0:T(8,128)} custom-call(s32[187]{0:T(256)} %concatenate.84.plan_ref, bf16[5120,256]{1,0:T(8,128)(2,1)} %pad.30.table_ref, bf16[9216,256]{1,0:T(8,128)(2,1)} %pad_maximum_fusion.3.rows_ref, f32[4,9216]{1,0:T(4,128)} %fusion.46.fact_ref), custom_call_target="tpu_custom_call" | custom-call | flops 24159191040 | bytes 9961472 | tf_op jit(solution)/shard_map/band_grad/pallas_call | solution.py:442
  705.6 4.4 collective-permute-start.32
  712.8 7.6 collective-permute-done.32
  739.7 9.7 %reduce-scatter.11.cloned.1.call-done = bf16[128,4480]{1,0:T(8,128)(2,1)} async-done(((bf16[1024,4480]{1,0:T(8,128)(2,1)}), bf16[128,4480]{1,0:T(8,128)(2,1)}) %reduce-scatter.11.cloned.1.call-update) | async-done | bytes 1146896 | tf_op jit(solution)/shard_map/reduce_scatter | solution.py:1119
  759.5 30.2 %collective-permute-done.40 = bf16[128,1024]{1,0:T(8,128)(2,1)S(1)} collective-permute-done((bf16[128,1024]{1,0:T(8,128)(2,1)S(1)}, bf16[128,1024]{1,0:T(8,128)(2,1)S(1)}, u32[]{:S(2)}, u32[]{:S(2)}) %collective-permute-start.40) | collective-permute-done | bytes 262176 | tf_op jit(solution)/shard_map/ppermute | solution.py:625
  791.5 30.9 %all-reduce.10.cloned.1.call-done = bf16[128,4480]{1,0:T(8,128)(2,1)} async-done(((bf16[128,4480]{1,0:T(8,128)(2,1)}), bf16[128,4480]{1,0:T(8,128)(2,1)}) %all-reduce.10.cloned.1.call-update) | async-done | bytes 1146896 | tf_op jit(solution)/shard_map/psum | solution.py:1161
  (518 shorter events, 239.8 us)
Async XLA Ops:
  7.2 157.3 %all-gather.6.cloned.1.call-start = ((), (), s32[]{:S(2)}) async-start(), calls=%async_computation.4 | async-start | bytes 4718592 | tf_op jit(solution)/shard_map/all_gather | solution.py:845
  12.6 50.0 %collective-permute-start = (bf16[256,1024]{1,0:T(8,128)(2,1)}, bf16[256,1024]{1,0:T(8,128)(2,1)}, u32[]{:S(2)}, u32[]{:S(2)}) collective-permute-start(bf16[256,1024]{1,0:T(8,128)(2,1)} %add_convert_fusion.5), channel_id=1, source_target_pairs={{0,24},{1,25},{2,26},{3,27},{4,28},{5,29},{6,30},{7,31}} | collective-permute-start | bytes 1572872 | tf_op jit(solution)/shard_map/ppermute | solution.py:673
  20.4 43.6 %collective-permute-start.1 = (bf16[256,1024]{1,0:T(8,128)(2,1)}, bf16[256,1024]{1,0:T(8,128)(2,1)}, u32[]{:S(2)}, u32[]{:S(2)}) collective-permute-start(bf16[256,1024]{1,0:T(8,128)(2,1)} %add_convert_fusion.5), channel_id=1, source_target_pairs={{0,16},{8,24},{1,17},{9,25},{2,18},{10,26},{3,19},{11,27},{4,20},{... | collective-permute-start | bytes 1572872 | tf_op jit(solution)/shard_map/ppermute | solution.py:673
  22.5 42.6 %collective-permute-start.2 = (bf16[256,1024]{1,0:T(8,128)(2,1)}, bf16[256,1024]{1,0:T(8,128)(2,1)}, u32[]{:S(2)}, u32[]{:S(2)}) collective-permute-start(bf16[256,1024]{1,0:T(8,128)(2,1)} %add_convert_fusion.5), channel_id=1, source_target_pairs={{0,8},{8,16},{16,24},{1,9},{9,17},{17,25},{2,10},{10,18},{18,26},{... | collective-permute-start | bytes 1572872 | tf_op jit(solution)/shard_map/ppermute | solution.py:673
  103.1 109.2 %all-gather.8.cloned.1.call-start = ((), (), s32[]{:S(2)}) async-start(), calls=%async_computation.5 | async-start | bytes 2621440 | tf_op jit(solution)/shard_map/all_gather | solution.py:848
  164.5 124.8 %all-gather.10.cloned.1.call-start = ((), (), s32[]{:S(2)}) async-start(), calls=%async_computation.6 | async-start | bytes 14155776 | tf_op jit(solution)/shard_map/all_gather | solution.py:887
  216.2 175.3 %all-gather.12.cloned.1.call-start = ((), (), s32[]{:S(2)}) async-start(), calls=%async_computation.7 | async-start | bytes 3981312 | tf_op jit(solution)/shard_map/all_gather | solution.py:918
  218.8 68.0 %collective-permute-start.3 = (bf16[288,256]{1,0:T(8,128)(2,1)S(1)}, bf16[288,256]{1,0:T(8,128)(2,1)S(1)}, u32[]{:S(2)}, u32[]{:S(2)}) collective-permute-start(bf16[288,256]{1,0:T(8,128)(2,1)S(1)} %constant_dynamic-slice_fusion.1), channel_id=1, source_target_pairs={{0,24},{8,0},{16,8},{24,16},{1,25},{9,1},{17,9},{25,17},{2,26},{10... | collective-permute-start | bytes 442376 | tf_op jit(solution)/shard_map/ppermute | solution.py:625
  219.0 67.9 %collective-permute-start.4 = (bf16[288,256]{1,0:T(8,128)(2,1)S(1)}, bf16[288,256]{1,0:T(8,128)(2,1)S(1)}, u32[]{:S(2)}, u32[]{:S(2)}) collective-permute-start(bf16[288,256]{1,0:T(8,128)(2,1)S(1)} %constant_dynamic-slice_fusion.1), channel_id=1, source_target_pairs={{0,16},{8,24},{16,0},{24,8},{1,17},{9,25},{17,1},{25,9},{2,18},{10... | collective-permute-start | bytes 442376 | tf_op jit(solution)/shard_map/ppermute | solution.py:625
  222.0 64.8 %collective-permute-start.5 = (bf16[288,256]{1,0:T(8,128)(2,1)S(1)}, bf16[288,256]{1,0:T(8,128)(2,1)S(1)}, u32[]{:S(2)}, u32[]{:S(2)}) collective-permute-start(bf16[288,256]{1,0:T(8,128)(2,1)S(1)} %constant_dynamic-slice_fusion.1), channel_id=1, source_target_pairs={{0,8},{8,16},{16,24},{24,0},{1,9},{9,17},{17,25},{25,1},{2,10},{10... | collective-permute-start | bytes 442376 | tf_op jit(solution)/shard_map/ppermute | solution.py:625
  289.3 173.4 %reduce-scatter.5.cloned.1.call-start = ((), (), s32[]{:S(2)}) async-start(), calls=%async_computation.8 | async-start | bytes 5898240 | tf_op jit(solution)/shard_map/reduce_scatter | solution.py:935
  334.4 277.2 %reduce-scatter.7.cloned.1.call-start = ((), (), s32[]{:S(2)}) async-start(), calls=%async_computation.9 | async-start | bytes 9437184 | tf_op jit(solution)/shard_map/reduce_scatter | solution.py:1045
  377.4 51.7 %collective-permute-start.10 = (bf16[640,1024]{1,0:T(8,128)(2,1)}, bf16[640,1024]{1,0:T(8,128)(2,1)}, u32[]{:S(2)}, u32[]{:S(2)}) collective-permute-start(bf16[640,1024]{1,0:T(8,128)(2,1)} %head_grad.1), channel_id=1, source_target_pairs={{8,0},{16,8},{24,16},{9,1},{17,9},{25,17},{10,2},{18,10},{26,18},{... | collective-permute-start | bytes 3932168 | tf_op jit(solution)/shard_map/ppermute | solution.py:634
  378.7 50.4 %collective-permute-start.9 = (bf16[640,1024]{1,0:T(8,128)(2,1)}, bf16[640,1024]{1,0:T(8,128)(2,1)}, u32[]{:S(2)}, u32[]{:S(2)}) collective-permute-start(bf16[640,1024]{1,0:T(8,128)(2,1)} %head_grad.1), channel_id=1, source_target_pairs={{0,8},{8,16},{16,24},{1,9},{9,17},{17,25},{2,10},{10,18},{18,26},{... | collective-permute-start | bytes 3932168 | tf_op jit(solution)/shard_map/ppermute | solution.py:633
  429.1 43.3 %collective-permute-start.11 = (bf16[64,3328]{1,0:T(8,128)(2,1)}, bf16[64,3328]{1,0:T(8,128)(2,1)}, u32[]{:S(2)}, u32[]{:S(2)}) collective-permute-start(bf16[64,3328]{1,0:T(8,128)(2,1)} %band_grad.3), channel_id=1, source_target_pairs={{0,8},{8,16},{16,24},{1,9},{9,17},{17,25},{2,10},{10,18},{18,26},{... | collective-permute-start | bytes 1277960 | tf_op jit(solution)/shard_map/ppermute | solution.py:633
  431.1 41.2 %collective-permute-start.12 = (bf16[64,3328]{1,0:T(8,128)(2,1)}, bf16[64,3328]{1,0:T(8,128)(2,1)}, u32[]{:S(2)}, u32[]{:S(2)}) collective-permute-start(bf16[64,3328]{1,0:T(8,128)(2,1)} %band_grad.3), channel_id=1, source_target_pairs={{8,0},{16,8},{24,16},{9,1},{17,9},{25,17},{10,2},{18,10},{26,18},{... | collective-permute-start | bytes 1277960 | tf_op jit(solution)/shard_map/ppermute | solution.py:634
  432.4 31.6 %collective-permute-start.13 = (bf16[640,1024]{1,0:T(8,128)(2,1)}, bf16[640,1024]{1,0:T(8,128)(2,1)}, u32[]{:S(2)}, u32[]{:S(2)}) collective-permute-start(bf16[640,1024]{1,0:T(8,128)(2,1)} %collective-permute-done.9), channel_id=1, source_target_pairs={{8,16},{16,24},{9,17},{17,25},{10,18},{18,26},{11,19},{19,27},{12,... | collective-permute-start | bytes 3932168 | tf_op jit(solution)/shard_map/ppermute | solution.py:633
  434.2 38.2 %collective-permute-start.14 = (bf16[640,1024]{1,0:T(8,128)(2,1)}, bf16[640,1024]{1,0:T(8,128)(2,1)}, u32[]{:S(2)}, u32[]{:S(2)}) collective-permute-start(bf16[640,1024]{1,0:T(8,128)(2,1)} %collective-permute-done.10), channel_id=1, source_target_pairs={{8,0},{16,8},{9,1},{17,9},{10,2},{18,10},{11,3},{19,11},{12,4},{20... | collective-permute-start | bytes 3932168 | tf_op jit(solution)/shard_map/ppermute | solution.py:634
  490.8 222.0 %reduce-scatter.9.cloned.1.call-start = ((), (), s32[]{:S(2)}) async-start(), calls=%async_computation.10 | async-start | bytes 9437184 | tf_op jit(solution)/shard_map/reduce_scatter | solution.py:1039
  496.7 46.9 %collective-permute-start.15 = (bf16[64,3328]{1,0:T(8,128)(2,1)}, bf16[64,3328]{1,0:T(8,128)(2,1)}, u32[]{:S(2)}, u32[]{:S(2)}) collective-permute-start(bf16[64,3328]{1,0:T(8,128)(2,1)} %band_grad.4), channel_id=1, source_target_pairs={{0,8},{8,16},{16,24},{1,9},{9,17},{17,25},{2,10},{10,18},{18,26},{... | collective-permute-start | bytes 1277960 | tf_op jit(solution)/shard_map/ppermute | solution.py:633
  500.6 43.0 %collective-permute-start.16 = (bf16[64,3328]{1,0:T(8,128)(2,1)}, bf16[64,3328]{1,0:T(8,128)(2,1)}, u32[]{:S(2)}, u32[]{:S(2)}) collective-permute-start(bf16[64,3328]{1,0:T(8,128)(2,1)} %band_grad.4), channel_id=1, source_target_pairs={{8,0},{16,8},{24,16},{9,1},{17,9},{25,17},{10,2},{18,10},{26,18},{... | collective-permute-start | bytes 1277960 | tf_op jit(solution)/shard_map/ppermute | solution.py:634
  501.9 26.0 %collective-permute-start.17 = (bf16[640,1024]{1,0:T(8,128)(2,1)}, bf16[640,1024]{1,0:T(8,128)(2,1)}, u32[]{:S(2)}, u32[]{:S(2)}) collective-permute-start(bf16[640,1024]{1,0:T(8,128)(2,1)} %collective-permute-done.13), channel_id=1, source_target_pairs={{16,24},{17,25},{18,26},{19,27},{20,28},{21,29},{22,30},{23,31}} | collective-permute-start | bytes 3932168 | tf_op jit(solution)/shard_map/ppermute | solution.py:633
  503.7 40.0 %collective-permute-start.18 = (bf16[640,1024]{1,0:T(8,128)(2,1)}, bf16[640,1024]{1,0:T(8,128)(2,1)}, u32[]{:S(2)}, u32[]{:S(2)}) collective-permute-start(bf16[640,1024]{1,0:T(8,128)(2,1)} %collective-permute-done.14), channel_id=1, source_target_pairs={{8,0},{9,1},{10,2},{11,3},{12,4},{13,5},{14,6},{15,7}} | collective-permute-start | bytes 3932168 | tf_op jit(solution)/shard_map/ppermute | solution.py:634
  504.9 62.6 %collective-permute-start.21 = (bf16[64,3328]{1,0:T(8,128)(2,1)}, bf16[64,3328]{1,0:T(8,128)(2,1)}, u32[]{:S(2)}, u32[]{:S(2)}) collective-permute-start(bf16[64,3328]{1,0:T(8,128)(2,1)} %collective-permute-done.11), channel_id=1, source_target_pairs={{8,16},{16,24},{9,17},{17,25},{10,18},{18,26},{11,19},{19,27},{12,... | collective-permute-start | bytes 1277960 | tf_op jit(solution)/shard_map/ppermute | solution.py:633
  523.4 226.1 %reduce-scatter.11.cloned.1.call-start = ((), (), s32[]{:S(2)}) async-start(), calls=%async_computation.11 | async-start | bytes 10321920 | tf_op jit(solution)/shard_map/reduce_scatter | solution.py:1119
  527.9 39.6 %collective-permute-start.22 = (bf16[64,3328]{1,0:T(8,128)(2,1)}, bf16[64,3328]{1,0:T(8,128)(2,1)}, u32[]{:S(2)}, u32[]{:S(2)}) collective-permute-start(bf16[64,3328]{1,0:T(8,128)(2,1)} %collective-permute-done.12), channel_id=1, source_target_pairs={{8,0},{16,8},{9,1},{17,9},{10,2},{18,10},{11,3},{19,11},{12,4},{20... | collective-permute-start | bytes 1277960 | tf_op jit(solution)/shard_map/ppermute | solution.py:634
  567.5 14.6 %collective-permute-start.19 = (bf16[64,3328]{1,0:T(8,128)(2,1)}, bf16[64,3328]{1,0:T(8,128)(2,1)S(1)}, u32[]{:S(2)}, u32[]{:S(2)}) collective-permute-start(bf16[64,3328]{1,0:T(8,128)(2,1)} %collective-permute-done.15), channel_id=1, source_target_pairs={{8,16},{16,24},{9,17},{17,25},{10,18},{18,26},{11,19},{19,27},{12,... | collective-permute-start | bytes 1277960 | tf_op jit(solution)/shard_map/ppermute | solution.py:633
  568.2 14.0 %collective-permute-start.20 = (bf16[64,3328]{1,0:T(8,128)(2,1)}, bf16[64,3328]{1,0:T(8,128)(2,1)S(1)}, u32[]{:S(2)}, u32[]{:S(2)}) collective-permute-start(bf16[64,3328]{1,0:T(8,128)(2,1)} %collective-permute-done.16), channel_id=1, source_target_pairs={{8,0},{16,8},{9,1},{17,9},{10,2},{18,10},{11,3},{19,11},{12,4},{20... | collective-permute-start | bytes 1277960 | tf_op jit(solution)/shard_map/ppermute | solution.py:634
  569.5 68.4 %collective-permute-start.25 = (bf16[64,3328]{1,0:T(8,128)(2,1)}, bf16[64,3328]{1,0:T(8,128)(2,1)}, u32[]{:S(2)}, u32[]{:S(2)}) collective-permute-start(bf16[64,3328]{1,0:T(8,128)(2,1)} %collective-permute-done.21), channel_id=1, source_target_pairs={{16,24},{17,25},{18,26},{19,27},{20,28},{21,29},{22,30},{23,31}} | collective-permute-start | bytes 1277960 | tf_op jit(solution)/shard_map/ppermute | solution.py:633
  571.0 71.1 %collective-permute-start.26 = (bf16[64,3328]{1,0:T(8,128)(2,1)}, bf16[64,3328]{1,0:T(8,128)(2,1)}, u32[]{:S(2)}, u32[]{:S(2)}) collective-permute-start(bf16[64,3328]{1,0:T(8,128)(2,1)} %collective-permute-done.22), channel_id=1, source_target_pairs={{8,0},{9,1},{10,2},{11,3},{12,4},{13,5},{14,6},{15,7}} | collective-permute-start | bytes 1277960 | tf_op jit(solution)/shard_map/ppermute | solution.py:634
  613.6 11.3 %collective-permute-start.27 = (bf16[32,4096]{1,0:T(8,128)(2,1)}, bf16[32,4096]{1,0:T(8,128)(2,1)}, u32[]{:S(2)}, u32[]{:S(2)}) collective-permute-start(bf16[32,4096]{1,0:T(8,128)(2,1)} %get-tuple-element.240), channel_id=1, source_target_pairs={{0,24},{8,0},{16,8},{24,16},{1,25},{9,1},{17,9},{25,17},{2,26},{10... | collective-permute-start | bytes 786440 | tf_op jit(solution)/shard_map/ppermute | solution.py:696
  613.6 21.6 %collective-permute-start.28 = (bf16[32,4096]{1,0:T(8,128)(2,1)}, bf16[32,4096]{1,0:T(8,128)(2,1)}, u32[]{:S(2)}, u32[]{:S(2)}) collective-permute-start(bf16[32,4096]{1,0:T(8,128)(2,1)} %get-tuple-element.242), channel_id=1, source_target_pairs={{0,16},{8,24},{16,0},{24,8},{1,17},{9,25},{17,1},{25,9},{2,18},{10... | collective-permute-start | bytes 786440 | tf_op jit(solution)/shard_map/ppermute | solution.py:696
  617.5 19.0 %collective-permute-start.29 = (bf16[32,4096]{1,0:T(8,128)(2,1)}, bf16[32,4096]{1,0:T(8,128)(2,1)}, u32[]{:S(2)}, u32[]{:S(2)}) collective-permute-start(bf16[32,4096]{1,0:T(8,128)(2,1)} %get-tuple-element.241), channel_id=1, source_target_pairs={{0,8},{8,16},{16,24},{24,0},{1,9},{9,17},{17,25},{25,1},{2,10},{10... | collective-permute-start | bytes 786440 | tf_op jit(solution)/shard_map/ppermute | solution.py:696
  625.0 17.1 %collective-permute-start.23 = (bf16[64,3328]{1,0:T(8,128)(2,1)}, bf16[64,3328]{1,0:T(8,128)(2,1)S(1)}, u32[]{:S(2)}, u32[]{:S(2)}) collective-permute-start(bf16[64,3328]{1,0:T(8,128)(2,1)} %copy-done.36), channel_id=1, source_target_pairs={{16,24},{17,25},{18,26},{19,27},{20,28},{21,29},{22,30},{23,31}} | collective-permute-start | bytes 1277960 | tf_op jit(solution)/shard_map/ppermute | solution.py:633
  635.3 16.2 %collective-permute-start.24 = (bf16[64,3328]{1,0:T(8,128)(2,1)}, bf16[64,3328]{1,0:T(8,128)(2,1)S(1)}, u32[]{:S(2)}, u32[]{:S(2)}) collective-permute-start(bf16[64,3328]{1,0:T(8,128)(2,1)} %copy-done.34), channel_id=1, source_target_pairs={{8,0},{9,1},{10,2},{11,3},{12,4},{13,5},{14,6},{15,7}} | collective-permute-start | bytes 1277960 | tf_op jit(solution)/shard_map/ppermute | solution.py:634
  637.9 74.9 %collective-permute-start.30 = (bf16[32,4096]{1,0:T(8,128)(2,1)S(1)}, bf16[32,4096]{1,0:T(8,128)(2,1)}, u32[]{:S(2)}, u32[]{:S(2)}) collective-permute-start(bf16[32,4096]{1,0:T(8,128)(2,1)S(1)} %fusion.41), channel_id=1, source_target_pairs={{0,24},{8,0},{16,8},{24,16},{1,25},{9,1},{17,9},{25,17},{2,26},{10... | collective-permute-start | bytes 786440 | tf_op jit(solution)/shard_map/ppermute | solution.py:625
  638.0 74.8 %collective-permute-start.31 = (bf16[32,4096]{1,0:T(8,128)(2,1)S(1)}, bf16[32,4096]{1,0:T(8,128)(2,1)}, u32[]{:S(2)}, u32[]{:S(2)}) collective-permute-start(bf16[32,4096]{1,0:T(8,128)(2,1)S(1)} %fusion.41), channel_id=1, source_target_pairs={{0,16},{8,24},{16,0},{24,8},{1,17},{9,25},{17,1},{25,9},{2,18},{10... | collective-permute-start | bytes 786440 | tf_op jit(solution)/shard_map/ppermute | solution.py:625
  654.0 51.6 %collective-permute-start.33 = (bf16[256,1024]{1,0:T(8,128)(2,1)}, bf16[256,1024]{1,0:T(8,128)(2,1)}, u32[]{:S(2)}, u32[]{:S(2)}) collective-permute-start(bf16[256,1024]{1,0:T(8,128)(2,1)} %get-tuple-element.233), channel_id=1, source_target_pairs={{8,0},{16,8},{24,16},{9,1},{17,9},{25,17},{10,2},{18,10},{26,18},{... | collective-permute-start | bytes 1572872 | tf_op jit(solution)/shard_map/ppermute | solution.py:696
  655.3 54.6 %collective-permute-start.34 = (bf16[256,1024]{1,0:T(8,128)(2,1)}, bf16[256,1024]{1,0:T(8,128)(2,1)}, u32[]{:S(2)}, u32[]{:S(2)}) collective-permute-start(bf16[256,1024]{1,0:T(8,128)(2,1)} %get-tuple-element.235), channel_id=1, source_target_pairs={{16,0},{24,8},{17,1},{25,9},{18,2},{26,10},{19,3},{27,11},{20,4},{... | collective-permute-start | bytes 1572872 | tf_op jit(solution)/shard_map/ppermute | solution.py:696
  656.6 53.4 %collective-permute-start.35 = (bf16[256,1024]{1,0:T(8,128)(2,1)}, bf16[256,1024]{1,0:T(8,128)(2,1)}, u32[]{:S(2)}, u32[]{:S(2)}) collective-permute-start(bf16[256,1024]{1,0:T(8,128)(2,1)} %get-tuple-element.234), channel_id=1, source_target_pairs={{24,0},{25,1},{26,2},{27,3},{28,4},{29,5},{30,6},{31,7}} | collective-permute-start | bytes 1572872 | tf_op jit(solution)/shard_map/ppermute | solution.py:696
  670.0 152.4 %all-reduce.10.cloned.1.call-start = ((), (), s32[]{:S(2)}) async-start(), calls=%async_computation.12 | async-start | bytes 2293760 | tf_op jit(solution)/shard_map/psum | solution.py:1161
  705.6 14.9 %collective-permute-start.32 = (bf16[32,4096]{1,0:T(8,128)(2,1)S(1)}, bf16[32,4096]{1,0:T(8,128)(2,1)}, u32[]{:S(2)}, u32[]{:S(2)}) collective-permute-start(bf16[32,4096]{1,0:T(8,128)(2,1)S(1)} %fusion.41), channel_id=1, source_target_pairs={{0,8},{8,16},{16,24},{24,0},{1,9},{9,17},{17,25},{25,1},{2,10},{10... | collective-permute-start | bytes 786440 | tf_op jit(solution)/shard_map/ppermute | solution.py:625
  721.6 14.2 %collective-permute-start.36 = (bf16[128,1024]{1,0:T(8,128)(2,1)S(1)}, bf16[128,1024]{1,0:T(8,128)(2,1)S(1)}, u32[]{:S(2)}, u32[]{:S(2)}) collective-permute-start(bf16[128,1024]{1,0:T(8,128)(2,1)S(1)} %get-tuple-element.237), channel_id=1, source_target_pairs={{0,24},{8,0},{16,8},{24,16},{1,25},{9,1},{17,9},{25,17},{2,26},{10... | collective-permute-start | bytes 786440 | tf_op jit(solution)/shard_map/ppermute | solution.py:696
  725.2 13.3 %collective-permute-start.37 = (bf16[128,1024]{1,0:T(8,128)(2,1)S(1)}, bf16[128,1024]{1,0:T(8,128)(2,1)S(1)}, u32[]{:S(2)}, u32[]{:S(2)}) collective-permute-start(bf16[128,1024]{1,0:T(8,128)(2,1)S(1)} %get-tuple-element.239), channel_id=1, source_target_pairs={{0,16},{8,24},{16,0},{24,8},{1,17},{9,25},{17,1},{25,9},{2,18},{10... | collective-permute-start | bytes 786440 | tf_op jit(solution)/shard_map/ppermute | solution.py:696
  725.8 12.7 %collective-permute-start.38 = (bf16[128,1024]{1,0:T(8,128)(2,1)S(1)}, bf16[128,1024]{1,0:T(8,128)(2,1)S(1)}, u32[]{:S(2)}, u32[]{:S(2)}) collective-permute-start(bf16[128,1024]{1,0:T(8,128)(2,1)S(1)} %get-tuple-element.238), channel_id=1, source_target_pairs={{0,8},{8,16},{16,24},{24,0},{1,9},{9,17},{17,25},{25,1},{2,10},{10... | collective-permute-start | bytes 786440 | tf_op jit(solution)/shard_map/ppermute | solution.py:696
  749.4 10.1 %collective-permute-start.39 = (bf16[128,1024]{1,0:T(8,128)(2,1)S(1)}, bf16[128,1024]{1,0:T(8,128)(2,1)S(1)}, u32[]{:S(2)}, u32[]{:S(2)}) collective-permute-start(bf16[128,1024]{1,0:T(8,128)(2,1)S(1)} %fusion.38), channel_id=1, source_target_pairs={{0,24},{8,0},{16,8},{24,16},{1,25},{9,1},{17,9},{25,17},{2,26},{10... | collective-permute-start | bytes 786440 | tf_op jit(solution)/shard_map/ppermute | solution.py:625
  755.4 34.4 %collective-permute-start.40 = (bf16[128,1024]{1,0:T(8,128)(2,1)S(1)}, bf16[128,1024]{1,0:T(8,128)(2,1)S(1)}, u32[]{:S(2)}, u32[]{:S(2)}) collective-permute-start(bf16[128,1024]{1,0:T(8,128)(2,1)S(1)} %fusion.38), channel_id=1, source_target_pairs={{0,16},{8,24},{16,0},{24,8},{1,17},{9,25},{17,1},{25,9},{2,18},{10... | collective-permute-start | bytes 786440 | tf_op jit(solution)/shard_map/ppermute | solution.py:625
  755.4 34.4 %collective-permute-start.41 = (bf16[128,1024]{1,0:T(8,128)(2,1)S(1)}, bf16[128,1024]{1,0:T(8,128)(2,1)S(1)}, u32[]{:S(2)}, u32[]{:S(2)}) collective-permute-start(bf16[128,1024]{1,0:T(8,128)(2,1)S(1)} %fusion.38), channel_id=1, source_target_pairs={{0,8},{8,16},{16,24},{24,0},{1,9},{9,17},{17,25},{25,1},{2,10},{10... | collective-permute-start | bytes 786440 | tf_op jit(solution)/shard_map/ppermute | solution.py:625
  (105 other events, 1084.3 us)
Sparse Core Ops, SparseCore 0:
  103.3 37.4 all-gather.5
  164.6 46.6 all-gather.7
  216.3 72.9 all-gather.9
  291.0 36.6 all-gather.11
  334.5 57.0 reduce-scatter.4
  490.9 69.4 reduce-scatter.6
  563.9 71.2 reduce-scatter.8
  670.1 79.2 reduce-scatter.10
  756.7 65.6 all-reduce.9

commit v8 on v7

--- a/solution.py
+++ b/solution.py
@@ -833,6 +833,9 @@
     )
 
     queries = lowered(product(normed_low, query_weight) + query_bias)
+    normed_all, head_pad, middle_pad, tail_pad, slot = lax.optimization_barrier(
+        (normed_all, head_pad, middle_pad, tail_pad, slot)
+    )
     key_rows = lowered(product(normed_all, key_weight))
     value_rows = lowered(product(normed_all, value_weight) + value_bias)
     attended_low = attend(query_start, queries, key_rows, value_rows)
@@ -846,9 +849,7 @@
     split = 2 * nz * group_count * feature_count <= 24 << 20
     if split:
         block_states = lax.all_gather(state_low, "seq", axis=0, tiled=True)
-    all_states, head_pad, middle_pad, tail_pad, tail_hits, slot, early = lax.optimization_barrier(
-        (all_states, head_pad, middle_pad, tail_pad, hit_rows[2], slot, early)
-    )
+    all_states, tail_hits, early = lax.optimization_barrier((all_states, hit_rows[2], early))
     hit_rows = hit_rows[:2] + (tail_hits,)
 
     middle_width = middle_map.shape[1]
@@ -1108,16 +1109,11 @@
     ]
     rest = jnp.concatenate([lowered(column) for column in columns], 1)
     spread_low = lowered(spread)
+    rest, facts, spread_low, inner_part = lax.optimization_barrier(
+        (rest, facts, spread_low, inner_part)
+    )
+    rest_part = lax.psum_scatter(rest, "batch", scatter_dimension=0, tiled=True)
     inner_low = lowered(line_scatter(inner_part))
-    rest, facts, spread_low, inner_low = lax.optimization_barrier(
-        (rest, facts, spread_low, inner_low)
-    )
-    if split:
-        for unused in range(nz - 3):
-            rest, facts, spread_low = first_advance(rest, facts, spread_low)
-            rest, facts, spread_low = second_advance(rest, facts, spread_low)
-    rest_part = lax.psum_scatter(rest, "batch", scatter_dimension=0, tiled=True)
-    inner_pieces = line_turns(inner_low)
     spread_sum = line_scatter(spread_low, False)
     middle_result = jax.ShapeDtypeStruct(
         (sizes[1], middle_width) if split else (middle_padded, middle_width),
@@ -1137,11 +1133,15 @@
         middle_result,
         False,
     )
-    middle_part, inner_pieces, spread_sum, outer_part = lax.optimization_barrier(
-        (middle_part, inner_pieces, spread_sum, outer_part)
-    )
+    if split:
+        for unused in range(nz - 3):
+            (rest_part,) = first_advance(rest_part)
+            (rest_part,) = second_advance(rest_part)
+    rest_part, middle_part, inner_low, spread_sum, outer_part = lax.optimization_barrier(
+        (rest_part, middle_part, inner_low, spread_sum, outer_part)
+    )
+    inner_pieces = line_turns(inner_low)
     outer_low = lowered(line_scatter(outer_part))
-    rest_part, outer_low = lax.optimization_barrier((rest_part, outer_low))
     if split:
         middle_table_grad = middle_part
         head_table_grad = jnp.concatenate(line_ordered(head_found), 0)

time: 855 us -> 890 us (1.041)
  starting transfers between devices: 82.5 us -> 106 us
  waiting for transfers between devices: 136 us -> 152 us
  other arithmetic: 125 us -> 112 us
    reduce_scatter x1, waiting for transfers between devices: 0.01 us -> 38.9 us  [on_device(): lax.psum_scatter(lowered(outer_weight_grad), 'batch', scatter_dimension=0...]
    psum x1, waiting for transfers between devices: 30.9 us -> 0.01 us  [on_device(): rest_low = lax.psum(rest_part, 'seq')]
    ppermute x12, starting transfers between devices: 23.8 us -> 47.2 us  [line_turns(): lax.ppermute(value, 'seq', [(d, (d - k) % size) for d in range(size)])]
    ppermute x9, waiting for transfers between devices: 15.9 us -> 37.4 us  [line_scatter(): lax.ppermute(part(place + size - k), 'seq', pairs).astype(jnp.float32)]
    ppermute x12, waiting for transfers between devices: 46.4 us -> 34.4 us  [line_turns(): lax.ppermute(value, 'seq', [(d, (d - k) % size) for d in range(size)])]
    reduce_scatter x1, waiting for transfers between devices: 9.74 us -> 0.01 us  [on_device(): rest_part = lax.psum_scatter(rest, 'batch', scatter_dimension=0, tiled=True)]
    ppermute x9, waiting for transfers between devices: 31 us -> 39.9 us  [line_step(): lax.ppermute(behind, 'seq', [(d, d - 1) for d in range(1, size - step + 1)])]
  transfers between devices with their start and end apart: 51 -> 51, of which waited for: 13 -> 13; matrix products, arithmetic and copies ran while one was open for 30% -> 27% of each run, Pallas kernels for 30% -> 30%
where the time goes in v8:
time: 890 us; the launch traced here: 879 us
  Pallas kernels  276 us (31%)
  waiting for transfers between devices  152 us (17%)
  other arithmetic  112 us (13%)
  starting transfers between devices  106 us (12%)
  local copies, waits for them, and re-layouts  99.7 us (11%)
  matrix products  93.7 us (11%)
  blocking collectives  20 us (2%)
  between operations  19 us (2%)
    pallas_call x3, Pallas kernels, band_grad(): pl.pallas_call(functools.partial(band_grad_kernel, chunk // 2 if chunk >...  92.6 us
    pallas_call x3, Pallas kernels, band_forward(): pl.pallas_call(functools.partial(band_kernel, chunk, per, words, sum_colu...  82 us
    ppermute x12, starting transfers between devices, line_turns(): lax.ppermute(value, 'seq', [(d, (d - k) % size) for d in range(size)])  47.2 us
    ppermute x9, waiting for transfers between devices, line_step(): lax.ppermute(behind, 'seq', [(d, d - 1) for d in range(1, size - step + 1)])  39.9 us
    reduce_scatter x1, waiting for transfers between devices, on_device(): lax.psum_scatter(lowered(outer_weight_grad), 'batch', scatter_dimension=0...  38.9 us
    ppermute x9, waiting for transfers between devices, line_scatter(): lax.ppermute(part(place + size - k), 'seq', pairs).astype(jnp.float32)  37.4 us
    ppermute x12, waiting for transfers between devices, line_turns(): lax.ppermute(value, 'seq', [(d, (d - k) % size) for d in range(size)])  34.4 us
    gather x3, local copies, waits for them, and re-layouts, on_device(): jnp.take(table, jnp.clip(local, 0, size - 1), axis=0, mode='clip')  34.4 us
  transfers between devices with their start and end apart: 51, of which 13 were waited for; matrix products, arithmetic and copies ran while one was open for 27% of the time, Pallas kernels for 30%

profile of v8, /device:TPU:0, one launch (start us, length us, event | category | flops | bytes accessed | tf_op | source)
XLA Modules:
  0.0 878.5 jit_solution(15733129607895507704)
XLA Ops:
  13.2 7.8 collective-permute-start
  27.3 9.1 %all_gather.21 = f32[3,2048]{1,0:T(4,128)S(1)} all-gather(f32[3,256]{1,0:T(4,128)S(1)} %pad_maximum_fusion.9), channel_id=1, replica_groups=mesh['seq'=4,'batch'=8] {'batch'}, dimensions={1}, use_global_device_ids=true | all-gather | bytes 27648 | tf_op jit(solution)/shard_map/all_gather | solution.py:765
  37.0 5.2 convert_reduce_fusion
  46.1 7.4 copy.119
  57.0 11.1 %fusion.6.table_ref = bf16[26624,128]{1,0:T(8,128)(2,1)} fusion(bf16[64,25967]{0,1:T(8,128)(2,1)} %bitcast.210, bf16[1,26624]{0,1:T(8,128)(2,1)} %select_convert_fusion, bf16[128]{0:T(256)(128)(2,1)S(1)} %pad.89.clone, bf16[128]{0:T(256)(128)(2,1)S(1)} %pad.87.clone), kind=kLoop, calls=%fused_computation.17 | loop fusion | flops 34078720 | bytes 10193280 | tf_op jit(solution)/shard_map/transpose | solution.py:816
  71.3 5.6 pad.29.table_ref
  89.9 15.1 %attend.1 = bf16[256,1024]{1,0:T(8,128)(2,1)} custom-call(s32[1]{0:T(128)} %bitcast.13.start_ref, bf16[256,1024]{1,0:T(8,128)(2,1)} %fusion.21.query_ref, bf16[1024,1024]{1,0:T(8,128)(2,1)} %convolution_convert_fusion.2.key_ref, bf16[1024,1024]{1,0:T(8,128)(2,1)} %add_convert_fusion.value_ref), custom_call_target="tpu_custom_call" | custom-call | flops 1073741824 | bytes 5242880 | tf_op jit(solution)/shard_map/attend/pallas_call | solution.py:92
  108.6 6.0 convolution_add_fusion
  119.7 11.5 %gather_fusion = bf16[2048,128]{1,0:T(8,128)(2,1)} fusion(bf16[26624,128]{1,0:T(8,128)(2,1)} %fusion.6.table_ref, s32[2048]{0:T(1024)S(1)} %broadcast_clamp_fusion.2), kind=kCustom, calls=%fused_computation | custom fusion | bytes 1056768 | tf_op jit(solution)/shard_map/jit(_take)/gather | solution.py:829
  131.4 14.1 %gather_fusion.1 = bf16[2048,1024]{1,0:T(8,128)(2,1)} fusion(bf16[2560,1024]{1,0:T(8,128)(2,1)} %pad.29.table_ref, s32[2048]{0:T(1024)S(1)} %broadcast_clamp_fusion.1), kind=kCustom, calls=%fused_computation.1 | custom fusion | bytes 8396800 | tf_op jit(solution)/shard_map/jit(_take)/gather | solution.py:829
  145.5 8.7 gather_fusion.2
  158.2 3.9 broadcast_select_fusion.head_hit_ref
  162.2 5.8 add_convert_fusion.1.rows_ref
  167.9 9.0 %pick_rows.1 = bf16[2304,384]{1,0:T(8,128)(2,1)} custom-call(s32[1,2048]{1,0:T(1,128)} %bitcast.229, bf16[2048,384]{1,0:T(8,128)(2,1)} %add_convert_fusion.1.rows_ref), custom_call_target="tpu_custom_call" | custom-call | flops 3623878656 | bytes 5111808 | tf_op jit(solution)/shard_map/pick_rows/pallas_call | solution.py:188
  180.4 29.7 %band_forward.3 = (f32[8,2048]{1,0:T(8,128)}, bf16[2048,1024]{1,0:T(8,128)(2,1)}) custom-call(s32[2]{0:T(128)} %iota_multiply_fusion.1.span_ref, bf16[2048,1024]{1,0:T(8,128)(2,1)} %all-gather.6.cloned.1.call-done.rows_ref.refs_0_, bf16[2560,1024]{1,0:T(8,128)(2,1)} %pad.29.table_ref), custom_call_target="tpu_custom_call" | custom-call | flops 21474836480 | bytes 17825792 | tf_op jit(solution)/shard_map/band_forward/pallas_call | solution.py:279
  223.4 4.6 multiply_reduce_fusion
  228.0 11.9 %band_forward.5 = (f32[8,2304]{1,0:T(8,128)}, bf16[2304,256]{1,0:T(8,128)(2,1)}) custom-call(s32[2]{0:T(128)} %pad_add_fusion.4.span_ref, bf16[2304,256]{1,0:T(8,128)(2,1)} %copy-done.20, bf16[5120,256]{1,0:T(8,128)(2,1)} %pad.30.table_ref), custom_call_target="tpu_custom_call" | custom-call | flops 3019898880 | bytes 6160384 | tf_op jit(solution)/shard_map/band_forward/pallas_call | solution.py:279
  240.0 40.4 %band_forward.4 = (f32[8,2304]{1,0:T(8,128)}, bf16[2304,128]{1,0:T(8,128)(2,1)}) custom-call(s32[2]{0:T(128)} %pad_add_fusion.3.span_ref, bf16[2304,256]{1,0:T(8,128)(2,1)} %copy-done.20, bf16[26624,128]{1,0:T(8,128)(2,1)} %fusion.6.table_ref), custom_call_target="tpu_custom_call" | custom-call | flops 31406948352 | bytes 8585216 | tf_op jit(solution)/shard_map/band_forward/pallas_call | solution.py:279
  289.4 10.9 %all-gather = f32[64,2304]{1,0:T(8,128)} all-gather(f32[8,2304]{1,0:T(8,128)S(1)} %maximum_maximum_fusion), channel_id=2, replica_groups=mesh['seq'=4,'batch'=8] {'batch'}, dimensions={0}, use_global_device_ids=true | all-gather | bytes 663552 | tf_op jit(solution)/shard_map/all_gather | solution.py:920
  300.3 17.2 %settle.1 = (bf16[2048,1280]{1,0:T(8,128)(2,1)}, f32[8,2048]{1,0:T(8,128)}, f32[16,2304]{1,0:T(8,128)}) custom-call(s32[1]{0:T(128)} %bitcast.member_ref, f32[8,8,2304]{2,1,0:T(8,128)} %bitcast.224, f32[8,2048]{1,0:T(8,128)} %concatenate.73.fact_ref, bf16[2048,1024]{1,0:T(8,128)(2,1)} %get-tuple-element.115.head_mix_ref, ...), custom_call_target="tpu_custom_call" | custom-call | flops 9663676416 | bytes 28114944 | tf_op jit(solution)/shard_map/settle/pallas_call | solution.py:594
  320.5 9.3 %collective-permute-start.6 = (f32[4,4352]{1,0:T(4,128)S(1)}, f32[4,4352]{1,0:T(4,128)S(1)}, u32[]{:S(2)}, u32[]{:S(2)}) collective-permute-start(f32[4,4352]{1,0:T(4,128)S(1)} %pad_maximum_fusion.6), channel_id=1, source_target_pairs={{0,24},{8,0},{16,8},{24,16},{1,25},{9,1},{17,9},{25,17},{2,26},{10... | collective-permute-start | bytes 208904 | tf_op jit(solution)/shard_map/ppermute | solution.py:625
  334.5 4.1 collective-permute-done.7
  341.9 32.7 %head_grad.1 = bf16[640,1024]{1,0:T(8,128)(2,1)} custom-call(s32[2]{0:T(128)} %pad_add_fusion.5.base_ref, bf16[2560,1024]{1,0:T(8,128)(2,1)} %pad.29.table_ref, bf16[2048,1024]{1,0:T(8,128)(2,1)} %all-gather.6.cloned.1.call-done.rows_ref.refs_0_, f32[4,2048]{1,0:T(4,128)} %copy-done.56, bf16[6144,1024]{1,0:T(8,128)(2,1)} %all-gather.10.cloned.1.call-done.refs_2_, ...), custom_call_target="tpu_custom_call" | custom-call | flops 21474836480 | bytes 18087936 | tf_op jit(solution)/shard_map/head_grad/pallas_call | solution.py:344
  376.0 5.6 collective-permute-start.9
  391.1 8.3 pad_maximum_fusion.3.rows_ref
  399.4 29.3 %band_grad.3 = bf16[64,3328]{1,0:T(8,128)(2,1)} custom-call(s32[113]{0:T(128)} %concatenate.78.plan_ref, bf16[26624,128]{1,0:T(8,128)(2,1)} %fusion.6.table_ref, bf16[9216,256]{1,0:T(8,128)(2,1)} %pad_maximum_fusion.3.rows_ref, f32[4,9216]{1,0:T(4,128)} %fusion.46.fact_ref), custom_call_target="tpu_custom_call" | custom-call | flops 15703474176 | bytes 4063232 | tf_op jit(solution)/shard_map/band_grad/pallas_call | solution.py:442
  435.1 29.7 %band_grad.4 = bf16[64,3328]{1,0:T(8,128)(2,1)} custom-call(s32[113]{0:T(128)} %concatenate.82.plan_ref, bf16[26624,128]{1,0:T(8,128)(2,1)} %fusion.6.table_ref, bf16[9216,256]{1,0:T(8,128)(2,1)} %pad_maximum_fusion.3.rows_ref, f32[4,9216]{1,0:T(4,128)} %fusion.46.fact_ref), custom_call_target="tpu_custom_call" | custom-call | flops 15703474176 | bytes 4063232 | tf_op jit(solution)/shard_map/band_grad/pallas_call | solution.py:442
  466.2 6.1 collective-permute-done.14
  476.4 7.1 convert_reduce_fusion.2
  484.8 5.9 convolution_convert_fusion.1
  501.0 8.5 multiply_reduce_fusion.5
  514.3 24.6 %collective-permute-done.18 = bf16[640,1024]{1,0:T(8,128)(2,1)S(1)} collective-permute-done((bf16[640,1024]{1,0:T(8,128)(2,1)}, bf16[640,1024]{1,0:T(8,128)(2,1)S(1)}, u32[]{:S(2)}, u32[]{:S(2)}) %collective-permute-start.18) | collective-permute-done | bytes 1310752 | tf_op jit(solution)/shard_map/ppermute | solution.py:634
  543.1 24.3 %attend_back.1 = (bf16[256,1024]{1,0:T(8,128)(2,1)}, bf16[1024,1024]{1,0:T(8,128)(2,1)}, bf16[1024,1024]{1,0:T(8,128)(2,1)}) custom-call(s32[1]{0:T(128)} %bitcast.13.start_ref, bf16[256,1024]{1,0:T(8,128)(2,1)} %fusion.21.query_ref, bf16[1024,1024]{1,0:T(8,128)(2,1)} %convolution_convert_fusion.2.key_ref, bf16[1024,1024]{1,0:T(8,128)(2,1)} %add_convert_fusion.value_ref, ...), custom_call_target="tpu_custom_call" | custom-call | flops 2684354560 | bytes 7864320 | tf_op jit(solution)/shard_map/attend_back/pallas_call | solution.py:141
  573.2 4.1 fusion.64
  600.7 9.7 %convolution_convert_fusion = bf16[4096,1024]{1,0:T(8,128)(2,1)} fusion(f32[256,1024]{1,0:T(8,128)} %copy-done.23, f32[256]{0:T(256)S(1)} %negate_multiply_fusion.2, f32[256,4096]{1,0:T(8,128)} %copy-done.97), kind=kOutput, calls=%fused_computation.12 | convolution fusion | flops 2161639424 | bytes 13632512 | tf_op jit(solution)/shard_map/dot_general | solution.py:47
  615.1 4.1 select_select_fusion.3
  619.3 4.7 fusion.7
  628.5 6.9 collective-permute-start.27
  636.0 33.5 %band_grad.5 = f32[5000,256]{1,0:T(8,128)} custom-call(s32[187]{0:T(256)} %concatenate.86.plan_ref, bf16[5120,256]{1,0:T(8,128)(2,1)} %pad.30.table_ref, bf16[9216,256]{1,0:T(8,128)(2,1)} %pad_maximum_fusion.3.rows_ref, f32[4,9216]{1,0:T(4,128)} %fusion.46.fact_ref), custom_call_target="tpu_custom_call" | custom-call | flops 24159191040 | bytes 9961472 | tf_op jit(solution)/shard_map/band_grad/pallas_call | solution.py:442
  670.2 12.1 %collective-permute-done.28 = bf16[32,4096]{1,0:T(8,128)(2,1)} collective-permute-done((bf16[32,4096]{1,0:T(8,128)(2,1)}, bf16[32,4096]{1,0:T(8,128)(2,1)}, u32[]{:S(2)}, u32[]{:S(2)}) %collective-permute-start.28) | collective-permute-done | bytes 262176 | tf_op jit(solution)/shard_map/ppermute | solution.py:696
  689.2 10.2 %collective-permute-done.32 = bf16[256,1024]{1,0:T(8,128)(2,1)S(1)} collective-permute-done((bf16[256,1024]{1,0:T(8,128)(2,1)S(1)}, bf16[256,1024]{1,0:T(8,128)(2,1)S(1)}, u32[]{:S(2)}, u32[]{:S(2)}) %collective-permute-start.32) | collective-permute-done | bytes 524320 | tf_op jit(solution)/shard_map/ppermute | solution.py:696
  702.6 4.1 collective-permute-done.26
  706.8 4.9 collective-permute-done.24
  711.7 38.9 %reduce-scatter.11.cloned.1.call-done = bf16[512,1024]{1,0:T(8,128)(2,1)} async-done(((bf16[4096,1024]{1,0:T(8,128)(2,1)}), bf16[512,1024]{1,0:T(8,128)(2,1)}) %reduce-scatter.11.cloned.1.call-update) | async-done | bytes 1048592 | tf_op jit(solution)/shard_map/reduce_scatter | solution.py:1040
  776.7 27.0 %collective-permute-start.35 = (bf16[32,4096]{1,0:T(8,128)(2,1)S(1)}, bf16[32,4096]{1,0:T(8,128)(2,1)S(1)}, u32[]{:S(2)}, u32[]{:S(2)}) collective-permute-start(bf16[32,4096]{1,0:T(8,128)(2,1)S(1)} %fusion.41), channel_id=1, source_target_pairs={{0,8},{8,16},{16,24},{24,0},{1,9},{9,17},{17,25},{25,1},{2,10},{10... | collective-permute-start | bytes 786440 | tf_op jit(solution)/shard_map/ppermute | solution.py:625
  803.6 13.7 %collective-permute-done.37 = bf16[128,1024]{1,0:T(8,128)(2,1)} collective-permute-done((bf16[128,1024]{1,0:T(8,128)(2,1)}, bf16[128,1024]{1,0:T(8,128)(2,1)}, u32[]{:S(2)}, u32[]{:S(2)}) %collective-permute-start.37) | collective-permute-done | bytes 262176 | tf_op jit(solution)/shard_map/ppermute | solution.py:696
  827.8 5.1 collective-permute-done.39
  832.9 25.2 %collective-permute-done.40 = bf16[128,1024]{1,0:T(8,128)(2,1)S(1)} collective-permute-done((bf16[128,1024]{1,0:T(8,128)(2,1)S(1)}, bf16[128,1024]{1,0:T(8,128)(2,1)S(1)}, u32[]{:S(2)}, u32[]{:S(2)}) %collective-permute-start.40) | collective-permute-done | bytes 262176 | tf_op jit(solution)/shard_map/ppermute | solution.py:625
  (520 shorter events, 224.6 us)
Async XLA Ops:
  7.2 154.9 %all-gather.6.cloned.1.call-start = ((), (), s32[]{:S(2)}) async-start(), calls=%async_computation.4 | async-start | bytes 4718592 | tf_op jit(solution)/shard_map/all_gather | solution.py:848
  13.2 65.5 %collective-permute-start = (bf16[256,1024]{1,0:T(8,128)(2,1)}, bf16[256,1024]{1,0:T(8,128)(2,1)}, u32[]{:S(2)}, u32[]{:S(2)}) collective-permute-start(bf16[256,1024]{1,0:T(8,128)(2,1)} %add_convert_fusion.5), channel_id=1, source_target_pairs={{0,24},{1,25},{2,26},{3,27},{4,28},{5,29},{6,30},{7,31}} | collective-permute-start | bytes 1572872 | tf_op jit(solution)/shard_map/ppermute | solution.py:673
  20.9 59.1 %collective-permute-start.1 = (bf16[256,1024]{1,0:T(8,128)(2,1)}, bf16[256,1024]{1,0:T(8,128)(2,1)}, u32[]{:S(2)}, u32[]{:S(2)}) collective-permute-start(bf16[256,1024]{1,0:T(8,128)(2,1)} %add_convert_fusion.5), channel_id=1, source_target_pairs={{0,16},{8,24},{1,17},{9,25},{2,18},{10,26},{3,19},{11,27},{4,20},{... | collective-permute-start | bytes 1572872 | tf_op jit(solution)/shard_map/ppermute | solution.py:673
  23.0 58.1 %collective-permute-start.2 = (bf16[256,1024]{1,0:T(8,128)(2,1)}, bf16[256,1024]{1,0:T(8,128)(2,1)}, u32[]{:S(2)}, u32[]{:S(2)}) collective-permute-start(bf16[256,1024]{1,0:T(8,128)(2,1)} %add_convert_fusion.5), channel_id=1, source_target_pairs={{0,8},{8,16},{16,24},{1,9},{9,17},{17,25},{2,10},{10,18},{18,26},{... | collective-permute-start | bytes 1572872 | tf_op jit(solution)/shard_map/ppermute | solution.py:673
  119.6 90.5 %all-gather.8.cloned.1.call-start = ((), (), s32[]{:S(2)}) async-start(), calls=%async_computation.5 | async-start | bytes 2621440 | tf_op jit(solution)/shard_map/all_gather | solution.py:851
  162.1 121.6 %all-gather.10.cloned.1.call-start = ((), (), s32[]{:S(2)}) async-start(), calls=%async_computation.6 | async-start | bytes 14155776 | tf_op jit(solution)/shard_map/all_gather | solution.py:888
  214.0 174.7 %all-gather.12.cloned.1.call-start = ((), (), s32[]{:S(2)}) async-start(), calls=%async_computation.7 | async-start | bytes 3981312 | tf_op jit(solution)/shard_map/all_gather | solution.py:919
  216.6 64.8 %collective-permute-start.3 = (bf16[288,256]{1,0:T(8,128)(2,1)S(1)}, bf16[288,256]{1,0:T(8,128)(2,1)S(1)}, u32[]{:S(2)}, u32[]{:S(2)}) collective-permute-start(bf16[288,256]{1,0:T(8,128)(2,1)S(1)} %constant_dynamic-slice_fusion.1), channel_id=1, source_target_pairs={{0,24},{8,0},{16,8},{24,16},{1,25},{9,1},{17,9},{25,17},{2,26},{10... | collective-permute-start | bytes 442376 | tf_op jit(solution)/shard_map/ppermute | solution.py:625
  216.7 64.7 %collective-permute-start.4 = (bf16[288,256]{1,0:T(8,128)(2,1)S(1)}, bf16[288,256]{1,0:T(8,128)(2,1)S(1)}, u32[]{:S(2)}, u32[]{:S(2)}) collective-permute-start(bf16[288,256]{1,0:T(8,128)(2,1)S(1)} %constant_dynamic-slice_fusion.1), channel_id=1, source_target_pairs={{0,16},{8,24},{16,0},{24,8},{1,17},{9,25},{17,1},{25,9},{2,18},{10... | collective-permute-start | bytes 442376 | tf_op jit(solution)/shard_map/ppermute | solution.py:625
  217.5 63.9 %collective-permute-start.5 = (bf16[288,256]{1,0:T(8,128)(2,1)S(1)}, bf16[288,256]{1,0:T(8,128)(2,1)S(1)}, u32[]{:S(2)}, u32[]{:S(2)}) collective-permute-start(bf16[288,256]{1,0:T(8,128)(2,1)S(1)} %constant_dynamic-slice_fusion.1), channel_id=1, source_target_pairs={{0,8},{8,16},{16,24},{24,0},{1,9},{9,17},{17,25},{25,1},{2,10},{10... | collective-permute-start | bytes 442376 | tf_op jit(solution)/shard_map/ppermute | solution.py:625
  283.7 181.2 %reduce-scatter.5.cloned.1.call-start = ((), (), s32[]{:S(2)}) async-start(), calls=%async_computation.8 | async-start | bytes 5898240 | tf_op jit(solution)/shard_map/reduce_scatter | solution.py:936
  320.5 13.9 %collective-permute-start.6 = (f32[4,4352]{1,0:T(4,128)S(1)}, f32[4,4352]{1,0:T(4,128)S(1)}, u32[]{:S(2)}, u32[]{:S(2)}) collective-permute-start(f32[4,4352]{1,0:T(4,128)S(1)} %pad_maximum_fusion.6), channel_id=1, source_target_pairs={{0,24},{8,0},{16,8},{24,16},{1,25},{9,1},{17,9},{25,17},{2,26},{10... | collective-permute-start | bytes 208904 | tf_op jit(solution)/shard_map/ppermute | solution.py:625
  333.3 267.1 %reduce-scatter.7.cloned.1.call-start = ((), (), s32[]{:S(2)}) async-start(), calls=%async_computation.9 | async-start | bytes 9437184 | tf_op jit(solution)/shard_map/reduce_scatter | solution.py:1046
  374.7 54.0 %collective-permute-start.10 = (bf16[640,1024]{1,0:T(8,128)(2,1)}, bf16[640,1024]{1,0:T(8,128)(2,1)}, u32[]{:S(2)}, u32[]{:S(2)}) collective-permute-start(bf16[640,1024]{1,0:T(8,128)(2,1)} %head_grad.1), channel_id=1, source_target_pairs={{8,0},{16,8},{24,16},{9,1},{17,9},{25,17},{10,2},{18,10},{26,18},{... | collective-permute-start | bytes 3932168 | tf_op jit(solution)/shard_map/ppermute | solution.py:634
  376.0 52.7 %collective-permute-start.9 = (bf16[640,1024]{1,0:T(8,128)(2,1)}, bf16[640,1024]{1,0:T(8,128)(2,1)}, u32[]{:S(2)}, u32[]{:S(2)}) collective-permute-start(bf16[640,1024]{1,0:T(8,128)(2,1)} %head_grad.1), channel_id=1, source_target_pairs={{0,8},{8,16},{16,24},{1,9},{9,17},{17,25},{2,10},{10,18},{18,26},{... | collective-permute-start | bytes 3932168 | tf_op jit(solution)/shard_map/ppermute | solution.py:633
  428.7 43.6 %collective-permute-start.11 = (bf16[64,3328]{1,0:T(8,128)(2,1)}, bf16[64,3328]{1,0:T(8,128)(2,1)}, u32[]{:S(2)}, u32[]{:S(2)}) collective-permute-start(bf16[64,3328]{1,0:T(8,128)(2,1)} %band_grad.3), channel_id=1, source_target_pairs={{0,8},{8,16},{16,24},{1,9},{9,17},{17,25},{2,10},{10,18},{18,26},{... | collective-permute-start | bytes 1277960 | tf_op jit(solution)/shard_map/ppermute | solution.py:633
  430.8 41.5 %collective-permute-start.12 = (bf16[64,3328]{1,0:T(8,128)(2,1)}, bf16[64,3328]{1,0:T(8,128)(2,1)}, u32[]{:S(2)}, u32[]{:S(2)}) collective-permute-start(bf16[64,3328]{1,0:T(8,128)(2,1)} %band_grad.3), channel_id=1, source_target_pairs={{8,0},{16,8},{24,16},{9,1},{17,9},{25,17},{10,2},{18,10},{26,18},{... | collective-permute-start | bytes 1277960 | tf_op jit(solution)/shard_map/ppermute | solution.py:634
  432.1 34.1 %collective-permute-start.13 = (bf16[640,1024]{1,0:T(8,128)(2,1)}, bf16[640,1024]{1,0:T(8,128)(2,1)}, u32[]{:S(2)}, u32[]{:S(2)}) collective-permute-start(bf16[640,1024]{1,0:T(8,128)(2,1)} %collective-permute-done.9), channel_id=1, source_target_pairs={{8,16},{16,24},{9,17},{17,25},{10,18},{18,26},{11,19},{19,27},{12,... | collective-permute-start | bytes 3932168 | tf_op jit(solution)/shard_map/ppermute | solution.py:633
  433.8 38.5 %collective-permute-start.14 = (bf16[640,1024]{1,0:T(8,128)(2,1)}, bf16[640,1024]{1,0:T(8,128)(2,1)}, u32[]{:S(2)}, u32[]{:S(2)}) collective-permute-start(bf16[640,1024]{1,0:T(8,128)(2,1)} %collective-permute-done.10), channel_id=1, source_target_pairs={{8,0},{16,8},{9,1},{17,9},{10,2},{18,10},{11,3},{19,11},{12,4},{20... | collective-permute-start | bytes 3932168 | tf_op jit(solution)/shard_map/ppermute | solution.py:634
  490.8 216.0 %reduce-scatter.9.cloned.1.call-start = ((), (), s32[]{:S(2)}) async-start(), calls=%async_computation.10 | async-start | bytes 10321920 | tf_op jit(solution)/shard_map/reduce_scatter | solution.py:1115
  492.0 46.9 %collective-permute-start.15 = (bf16[64,3328]{1,0:T(8,128)(2,1)}, bf16[64,3328]{1,0:T(8,128)(2,1)S(1)}, u32[]{:S(2)}, u32[]{:S(2)}) collective-permute-start(bf16[64,3328]{1,0:T(8,128)(2,1)} %band_grad.4), channel_id=1, source_target_pairs={{0,8},{8,16},{16,24},{1,9},{9,17},{17,25},{2,10},{10,18},{18,26},{... | collective-permute-start | bytes 1277960 | tf_op jit(solution)/shard_map/ppermute | solution.py:633
  495.8 43.1 %collective-permute-start.16 = (bf16[64,3328]{1,0:T(8,128)(2,1)}, bf16[64,3328]{1,0:T(8,128)(2,1)S(1)}, u32[]{:S(2)}, u32[]{:S(2)}) collective-permute-start(bf16[64,3328]{1,0:T(8,128)(2,1)} %band_grad.4), channel_id=1, source_target_pairs={{8,0},{16,8},{24,16},{9,1},{17,9},{25,17},{10,2},{18,10},{26,18},{... | collective-permute-start | bytes 1277960 | tf_op jit(solution)/shard_map/ppermute | solution.py:634
  497.1 15.9 %collective-permute-start.17 = (bf16[640,1024]{1,0:T(8,128)(2,1)}, bf16[640,1024]{1,0:T(8,128)(2,1)}, u32[]{:S(2)}, u32[]{:S(2)}) collective-permute-start(bf16[640,1024]{1,0:T(8,128)(2,1)} %collective-permute-done.13), channel_id=1, source_target_pairs={{16,24},{17,25},{18,26},{19,27},{20,28},{21,29},{22,30},{23,31}} | collective-permute-start | bytes 3932168 | tf_op jit(solution)/shard_map/ppermute | solution.py:633
  498.9 40.1 %collective-permute-start.18 = (bf16[640,1024]{1,0:T(8,128)(2,1)}, bf16[640,1024]{1,0:T(8,128)(2,1)S(1)}, u32[]{:S(2)}, u32[]{:S(2)}) collective-permute-start(bf16[640,1024]{1,0:T(8,128)(2,1)} %collective-permute-done.14), channel_id=1, source_target_pairs={{8,0},{9,1},{10,2},{11,3},{12,4},{13,5},{14,6},{15,7}} | collective-permute-start | bytes 3932168 | tf_op jit(solution)/shard_map/ppermute | solution.py:634
  500.2 67.3 %collective-permute-start.21 = (bf16[64,3328]{1,0:T(8,128)(2,1)}, bf16[64,3328]{1,0:T(8,128)(2,1)S(1)}, u32[]{:S(2)}, u32[]{:S(2)}) collective-permute-start(bf16[64,3328]{1,0:T(8,128)(2,1)} %collective-permute-done.11), channel_id=1, source_target_pairs={{8,16},{16,24},{9,17},{17,25},{10,18},{18,26},{11,19},{19,27},{12,... | collective-permute-start | bytes 1277960 | tf_op jit(solution)/shard_map/ppermute | solution.py:633
  513.0 54.4 %collective-permute-start.22 = (bf16[64,3328]{1,0:T(8,128)(2,1)}, bf16[64,3328]{1,0:T(8,128)(2,1)S(1)}, u32[]{:S(2)}, u32[]{:S(2)}) collective-permute-start(bf16[64,3328]{1,0:T(8,128)(2,1)} %collective-permute-done.12), channel_id=1, source_target_pairs={{8,0},{16,8},{9,1},{17,9},{10,2},{18,10},{11,3},{19,11},{12,4},{20... | collective-permute-start | bytes 1277960 | tf_op jit(solution)/shard_map/ppermute | solution.py:634
  539.0 28.5 %collective-permute-start.19 = (bf16[64,3328]{1,0:T(8,128)(2,1)S(1)}, bf16[64,3328]{1,0:T(8,128)(2,1)}, u32[]{:S(2)}, u32[]{:S(2)}) collective-permute-start(bf16[64,3328]{1,0:T(8,128)(2,1)S(1)} %collective-permute-done.15), channel_id=1, source_target_pairs={{8,16},{16,24},{9,17},{17,25},{10,18},{18,26},{11,19},{19,27},{12,... | collective-permute-start | bytes 1277960 | tf_op jit(solution)/shard_map/ppermute | solution.py:633
  540.5 27.0 %collective-permute-start.20 = (bf16[64,3328]{1,0:T(8,128)(2,1)S(1)}, bf16[64,3328]{1,0:T(8,128)(2,1)}, u32[]{:S(2)}, u32[]{:S(2)}) collective-permute-start(bf16[64,3328]{1,0:T(8,128)(2,1)S(1)} %collective-permute-done.16), channel_id=1, source_target_pairs={{8,0},{16,8},{9,1},{17,9},{10,2},{18,10},{11,3},{19,11},{12,4},{20... | collective-permute-start | bytes 1277960 | tf_op jit(solution)/shard_map/ppermute | solution.py:634
  600.4 150.2 %reduce-scatter.11.cloned.1.call-start = ((), (), s32[]{:S(2)}) async-start(), calls=%async_computation.11 | async-start | bytes 9437184 | tf_op jit(solution)/shard_map/reduce_scatter | solution.py:1040
  610.4 249.4 %all-reduce.10.cloned.1.call-start = ((), (), s32[]{:S(2)}) async-start(), calls=%async_computation.12 | async-start | bytes 2293760 | tf_op jit(solution)/shard_map/psum | solution.py:1161
  625.0 60.1 %collective-permute-start.30 = (bf16[256,1024]{1,0:T(8,128)(2,1)}, bf16[256,1024]{1,0:T(8,128)(2,1)}, u32[]{:S(2)}, u32[]{:S(2)}) collective-permute-start(bf16[256,1024]{1,0:T(8,128)(2,1)} %get-tuple-element.221), channel_id=1, source_target_pairs={{8,0},{16,8},{24,16},{9,1},{17,9},{25,17},{10,2},{18,10},{26,18},{... | collective-permute-start | bytes 1572872 | tf_op jit(solution)/shard_map/ppermute | solution.py:696
  626.3 60.1 %collective-permute-start.31 = (bf16[256,1024]{1,0:T(8,128)(2,1)}, bf16[256,1024]{1,0:T(8,128)(2,1)}, u32[]{:S(2)}, u32[]{:S(2)}) collective-permute-start(bf16[256,1024]{1,0:T(8,128)(2,1)} %get-tuple-element.223), channel_id=1, source_target_pairs={{16,0},{24,8},{17,1},{25,9},{18,2},{26,10},{19,3},{27,11},{20,4},{... | collective-permute-start | bytes 1572872 | tf_op jit(solution)/shard_map/ppermute | solution.py:696
  628.5 41.0 %collective-permute-start.27 = (bf16[32,4096]{1,0:T(8,128)(2,1)}, bf16[32,4096]{1,0:T(8,128)(2,1)S(1)}, u32[]{:S(2)}, u32[]{:S(2)}) collective-permute-start(bf16[32,4096]{1,0:T(8,128)(2,1)} %get-tuple-element.228), channel_id=1, source_target_pairs={{0,24},{8,0},{16,8},{24,16},{1,25},{9,1},{17,9},{25,17},{2,26},{10... | collective-permute-start | bytes 786440 | tf_op jit(solution)/shard_map/ppermute | solution.py:696
  635.4 46.9 %collective-permute-start.28 = (bf16[32,4096]{1,0:T(8,128)(2,1)}, bf16[32,4096]{1,0:T(8,128)(2,1)}, u32[]{:S(2)}, u32[]{:S(2)}) collective-permute-start(bf16[32,4096]{1,0:T(8,128)(2,1)} %get-tuple-element.230), channel_id=1, source_target_pairs={{0,16},{8,24},{16,0},{24,8},{1,17},{9,25},{17,1},{25,9},{2,18},{10... | collective-permute-start | bytes 786440 | tf_op jit(solution)/shard_map/ppermute | solution.py:696
  635.4 48.2 %collective-permute-start.29 = (bf16[32,4096]{1,0:T(8,128)(2,1)}, bf16[32,4096]{1,0:T(8,128)(2,1)}, u32[]{:S(2)}, u32[]{:S(2)}) collective-permute-start(bf16[32,4096]{1,0:T(8,128)(2,1)} %get-tuple-element.229), channel_id=1, source_target_pairs={{0,8},{8,16},{16,24},{24,0},{1,9},{9,17},{17,25},{25,1},{2,10},{10... | collective-permute-start | bytes 786440 | tf_op jit(solution)/shard_map/ppermute | solution.py:696
  669.5 32.4 %collective-permute-start.25 = (bf16[64,3328]{1,0:T(8,128)(2,1)S(1)}, bf16[64,3328]{1,0:T(8,128)(2,1)S(1)}, u32[]{:S(2)}, u32[]{:S(2)}) collective-permute-start(bf16[64,3328]{1,0:T(8,128)(2,1)S(1)} %copy-done.41), channel_id=1, source_target_pairs={{16,24},{17,25},{18,26},{19,27},{20,28},{21,29},{22,30},{23,31}} | collective-permute-start | bytes 1277960 | tf_op jit(solution)/shard_map/ppermute | solution.py:633
  682.4 24.4 %collective-permute-start.26 = (bf16[64,3328]{1,0:T(8,128)(2,1)S(1)}, bf16[64,3328]{1,0:T(8,128)(2,1)}, u32[]{:S(2)}, u32[]{:S(2)}) collective-permute-start(bf16[64,3328]{1,0:T(8,128)(2,1)S(1)} %copy-done.44), channel_id=1, source_target_pairs={{8,0},{9,1},{10,2},{11,3},{12,4},{13,5},{14,6},{15,7}} | collective-permute-start | bytes 1277960 | tf_op jit(solution)/shard_map/ppermute | solution.py:634
  683.7 23.1 %collective-permute-start.23 = (bf16[64,3328]{1,0:T(8,128)(2,1)}, bf16[64,3328]{1,0:T(8,128)(2,1)}, u32[]{:S(2)}, u32[]{:S(2)}) collective-permute-start(bf16[64,3328]{1,0:T(8,128)(2,1)} %collective-permute-done.19), channel_id=1, source_target_pairs={{16,24},{17,25},{18,26},{19,27},{20,28},{21,29},{22,30},{23,31}} | collective-permute-start | bytes 1277960 | tf_op jit(solution)/shard_map/ppermute | solution.py:633
  685.1 26.7 %collective-permute-start.24 = (bf16[64,3328]{1,0:T(8,128)(2,1)}, bf16[64,3328]{1,0:T(8,128)(2,1)}, u32[]{:S(2)}, u32[]{:S(2)}) collective-permute-start(bf16[64,3328]{1,0:T(8,128)(2,1)} %collective-permute-done.20), channel_id=1, source_target_pairs={{8,0},{9,1},{10,2},{11,3},{12,4},{13,5},{14,6},{15,7}} | collective-permute-start | bytes 1277960 | tf_op jit(solution)/shard_map/ppermute | solution.py:634
  686.4 13.0 %collective-permute-start.32 = (bf16[256,1024]{1,0:T(8,128)(2,1)S(1)}, bf16[256,1024]{1,0:T(8,128)(2,1)S(1)}, u32[]{:S(2)}, u32[]{:S(2)}) collective-permute-start(bf16[256,1024]{1,0:T(8,128)(2,1)S(1)} %get-tuple-element.222), channel_id=1, source_target_pairs={{24,0},{25,1},{26,2},{27,3},{28,4},{29,5},{30,6},{31,7}} | collective-permute-start | bytes 1572872 | tf_op jit(solution)/shard_map/ppermute | solution.py:696
  750.7 68.3 %collective-permute-start.33 = (bf16[32,4096]{1,0:T(8,128)(2,1)S(1)}, bf16[32,4096]{1,0:T(8,128)(2,1)}, u32[]{:S(2)}, u32[]{:S(2)}) collective-permute-start(bf16[32,4096]{1,0:T(8,128)(2,1)S(1)} %fusion.41), channel_id=1, source_target_pairs={{0,24},{8,0},{16,8},{24,16},{1,25},{9,1},{17,9},{25,17},{2,26},{10... | collective-permute-start | bytes 786440 | tf_op jit(solution)/shard_map/ppermute | solution.py:625
  754.1 68.5 %collective-permute-start.34 = (bf16[32,4096]{1,0:T(8,128)(2,1)S(1)}, bf16[32,4096]{1,0:T(8,128)(2,1)}, u32[]{:S(2)}, u32[]{:S(2)}) collective-permute-start(bf16[32,4096]{1,0:T(8,128)(2,1)S(1)} %fusion.41), channel_id=1, source_target_pairs={{0,16},{8,24},{16,0},{24,8},{1,17},{9,25},{17,1},{25,9},{2,18},{10... | collective-permute-start | bytes 786440 | tf_op jit(solution)/shard_map/ppermute | solution.py:625
  766.2 51.1 %collective-permute-start.37 = (bf16[128,1024]{1,0:T(8,128)(2,1)}, bf16[128,1024]{1,0:T(8,128)(2,1)}, u32[]{:S(2)}, u32[]{:S(2)}) collective-permute-start(bf16[128,1024]{1,0:T(8,128)(2,1)} %get-tuple-element.227), channel_id=1, source_target_pairs={{0,16},{8,24},{16,0},{24,8},{1,17},{9,25},{17,1},{25,9},{2,18},{10... | collective-permute-start | bytes 786440 | tf_op jit(solution)/shard_map/ppermute | solution.py:696
  767.4 49.9 %collective-permute-start.38 = (bf16[128,1024]{1,0:T(8,128)(2,1)}, bf16[128,1024]{1,0:T(8,128)(2,1)}, u32[]{:S(2)}, u32[]{:S(2)}) collective-permute-start(bf16[128,1024]{1,0:T(8,128)(2,1)} %get-tuple-element.226), channel_id=1, source_target_pairs={{0,8},{8,16},{16,24},{24,0},{1,9},{9,17},{17,25},{25,1},{2,10},{10... | collective-permute-start | bytes 786440 | tf_op jit(solution)/shard_map/ppermute | solution.py:696
  776.7 47.6 %collective-permute-start.35 = (bf16[32,4096]{1,0:T(8,128)(2,1)S(1)}, bf16[32,4096]{1,0:T(8,128)(2,1)S(1)}, u32[]{:S(2)}, u32[]{:S(2)}) collective-permute-start(bf16[32,4096]{1,0:T(8,128)(2,1)S(1)} %fusion.41), channel_id=1, source_target_pairs={{0,8},{8,16},{16,24},{24,0},{1,9},{9,17},{17,25},{25,1},{2,10},{10... | collective-permute-start | bytes 786440 | tf_op jit(solution)/shard_map/ppermute | solution.py:625
  818.8 14.0 %collective-permute-start.39 = (bf16[128,1024]{1,0:T(8,128)(2,1)S(1)}, bf16[128,1024]{1,0:T(8,128)(2,1)S(1)}, u32[]{:S(2)}, u32[]{:S(2)}) collective-permute-start(bf16[128,1024]{1,0:T(8,128)(2,1)S(1)} %get-tuple-element.190), channel_id=1, source_target_pairs={{0,24},{8,0},{16,8},{24,16},{1,25},{9,1},{17,9},{25,17},{2,26},{10... | collective-permute-start | bytes 786440 | tf_op jit(solution)/shard_map/ppermute | solution.py:625
  818.9 39.2 %collective-permute-start.40 = (bf16[128,1024]{1,0:T(8,128)(2,1)S(1)}, bf16[128,1024]{1,0:T(8,128)(2,1)S(1)}, u32[]{:S(2)}, u32[]{:S(2)}) collective-permute-start(bf16[128,1024]{1,0:T(8,128)(2,1)S(1)} %get-tuple-element.190), channel_id=1, source_target_pairs={{0,16},{8,24},{16,0},{24,8},{1,17},{9,25},{17,1},{25,9},{2,18},{10... | collective-permute-start | bytes 786440 | tf_op jit(solution)/shard_map/ppermute | solution.py:625
  819.0 39.1 %collective-permute-start.41 = (bf16[128,1024]{1,0:T(8,128)(2,1)S(1)}, bf16[128,1024]{1,0:T(8,128)(2,1)S(1)}, u32[]{:S(2)}, u32[]{:S(2)}) collective-permute-start(bf16[128,1024]{1,0:T(8,128)(2,1)S(1)} %get-tuple-element.190), channel_id=1, source_target_pairs={{0,8},{8,16},{16,24},{24,0},{1,9},{9,17},{17,25},{25,1},{2,10},{10... | collective-permute-start | bytes 786440 | tf_op jit(solution)/shard_map/ppermute | solution.py:625
  (107 other events, 1431.5 us)
Sparse Core Ops, SparseCore 0:
  119.7 33.9 all-gather.5
  162.2 43.1 all-gather.7
  214.1 69.5 all-gather.9
  285.4 39.8 all-gather.11
  333.4 55.4 reduce-scatter.4
  490.9 71.5 reduce-scatter.6
  600.6 74.9 reduce-scatter.8
  679.4 71.2 reduce-scatter.10
  771.6 87.1 all-reduce.9

commit v9 on v7

--- a/solution.py
+++ b/solution.py
@@ -1108,16 +1108,17 @@
     ]
     rest = jnp.concatenate([lowered(column) for column in columns], 1)
     spread_low = lowered(spread)
-    inner_low = lowered(line_scatter(inner_part))
-    rest, facts, spread_low, inner_low = lax.optimization_barrier(
-        (rest, facts, spread_low, inner_low)
+    rest, facts, spread_low, inner_part = lax.optimization_barrier(
+        (rest, facts, spread_low, inner_part)
     )
     if split:
         for unused in range(nz - 3):
-            rest, facts, spread_low = first_advance(rest, facts, spread_low)
-            rest, facts, spread_low = second_advance(rest, facts, spread_low)
+            rest, facts, spread_low, inner_part = first_advance(rest, facts, spread_low, inner_part)
+            rest, facts, spread_low, inner_part = second_advance(
+                rest, facts, spread_low, inner_part
+            )
     rest_part = lax.psum_scatter(rest, "batch", scatter_dimension=0, tiled=True)
-    inner_pieces = line_turns(inner_low)
+    inner_low = lowered(line_scatter(inner_part))
     spread_sum = line_scatter(spread_low, False)
     middle_result = jax.ShapeDtypeStruct(
         (sizes[1], middle_width) if split else (middle_padded, middle_width),
@@ -1137,11 +1138,12 @@
         middle_result,
         False,
     )
-    middle_part, inner_pieces, spread_sum, outer_part = lax.optimization_barrier(
-        (middle_part, inner_pieces, spread_sum, outer_part)
-    )
+    middle_part, inner_low, outer_part = lax.optimization_barrier(
+        (middle_part, inner_low, outer_part)
+    )
+    rest_part, spread_sum = lax.optimization_barrier((rest_part, spread_sum))
+    inner_pieces = line_turns(inner_low)
     outer_low = lowered(line_scatter(outer_part))
-    rest_part, outer_low = lax.optimization_barrier((rest_part, outer_low))
     if split:
         middle_table_grad = middle_part
         head_table_grad = jnp.concatenate(line_ordered(head_found), 0)

time: 855 us -> 863 us (level)
  waiting for transfers between devices: 136 us -> 148 us
    ppermute x9, waiting for transfers between devices: 15.9 us -> 50.9 us  [line_scatter(): lax.ppermute(part(place + size - k), 'seq', pairs).astype(jnp.float32)]
    ppermute x12, waiting for transfers between devices: 46.4 us -> 23.6 us  [line_turns(): lax.ppermute(value, 'seq', [(d, (d - k) % size) for d in range(size)])]
    psum x1, waiting for transfers between devices: 30.9 us -> 48.3 us  [on_device(): rest_low = lax.psum(rest_part, 'seq')]
    reduce_scatter x1, waiting for transfers between devices: 9.74 us -> 0.01 us  [on_device(): rest_part = lax.psum_scatter(rest, 'batch', scatter_dimension=0, tiled=True)]
    ppermute x9, waiting for transfers between devices: 31 us -> 21.7 us  [line_step(): lax.ppermute(behind, 'seq', [(d, d - 1) for d in range(1, size - step + 1)])]
  transfers between devices with their start and end apart: 51 -> 51, of which waited for: 13 -> 10; matrix products, arithmetic and copies ran while one was open for 30% -> 29% of each run, Pallas kernels for 30% -> 29%
where the time goes in v9:
time: 863 us; the launch traced here: 849 us
  Pallas kernels  263 us (30%)
  waiting for transfers between devices  148 us (17%)
  other arithmetic  123 us (14%)
  local copies, waits for them, and re-layouts  102 us (12%)
  starting transfers between devices  88.5 us (10%)
  matrix products  84.4 us (10%)
  blocking collectives  21.7 us (3%)
  between operations  18.7 us (2%)
    pallas_call x3, Pallas kernels, band_forward(): pl.pallas_call(functools.partial(band_kernel, chunk, per, words, sum_colu...  80.8 us
    pallas_call x3, Pallas kernels, band_grad(): pl.pallas_call(functools.partial(band_grad_kernel, chunk // 2 if chunk >...  80.7 us
    ppermute x9, waiting for transfers between devices, line_scatter(): lax.ppermute(part(place + size - k), 'seq', pairs).astype(jnp.float32)  50.9 us
    psum x1, waiting for transfers between devices, on_device(): rest_low = lax.psum(rest_part, 'seq')  48.3 us
    gather x3, local copies, waits for them, and re-layouts, on_device(): jnp.take(table, jnp.clip(local, 0, size - 1), axis=0, mode='clip')  34.3 us
    pallas_call x1, Pallas kernels, head_grad(): pl.pallas_call(functools.partial(head_grad_kernel, chunk, len(lists)), gr...  32.7 us
    dot_general x10, matrix products, product_nt(): lax.dot_general(former, latter, (((1,), (1,)), ((), ())), preferred_eleme...  30.4 us
    dot_general x9, matrix products, product_tn(): lax.dot_general(former, latter, (((0,), (0,)), ((), ())), preferred_eleme...  27.2 us
  transfers between devices with their start and end apart: 51, of which 10 were waited for; matrix products, arithmetic and copies ran while one was open for 29% of the time, Pallas kernels for 29%

profile of v9, /device:TPU:0, one launch (start us, length us, event | category | flops | bytes accessed | tf_op | source)
XLA Modules:
  0.0 848.7 jit_solution(14830260748582454059)
XLA Ops:
  12.6 7.8 collective-permute-start
  26.7 9.1 %all_gather.21 = f32[3,2048]{1,0:T(4,128)S(1)} all-gather(f32[3,256]{1,0:T(4,128)S(1)} %pad_maximum_fusion.9), channel_id=1, replica_groups=mesh['seq'=4,'batch'=8] {'batch'}, dimensions={1}, use_global_device_ids=true | all-gather | bytes 27648 | tf_op jit(solution)/shard_map/all_gather | solution.py:765
  46.7 7.4 copy.119
  55.3 5.5 pad.29.table_ref
  73.9 15.2 %attend.1 = bf16[256,1024]{1,0:T(8,128)(2,1)} custom-call(s32[1]{0:T(128)} %bitcast.6.start_ref, bf16[256,1024]{1,0:T(8,128)(2,1)} %fusion.21.query_ref, bf16[1024,1024]{1,0:T(8,128)(2,1)} %convolution_convert_fusion.2.key_ref, bf16[1024,1024]{1,0:T(8,128)(2,1)} %add_convert_fusion.value_ref), custom_call_target="tpu_custom_call" | custom-call | flops 1073741824 | bytes 5242880 | tf_op jit(solution)/shard_map/attend/pallas_call | solution.py:92
  91.5 6.0 convolution_add_fusion
  103.3 11.9 %fusion.6.table_ref = bf16[26624,128]{1,0:T(8,128)(2,1)} fusion(bf16[64,25967]{0,1:T(8,128)(2,1)} %bitcast.211, bf16[1,26624]{0,1:T(8,128)(2,1)} %select_convert_fusion, bf16[128]{0:T(256)(128)(2,1)S(1)} %copy-done.84, bf16[128]{0:T(256)(128)(2,1)S(1)} %copy-done.85), kind=kLoop, calls=%fused_computation.17 | loop fusion | flops 34078720 | bytes 10193280 | tf_op jit(solution)/shard_map/transpose | solution.py:816
  115.2 11.5 %gather_fusion = bf16[2048,128]{1,0:T(8,128)(2,1)} fusion(bf16[26624,128]{1,0:T(8,128)(2,1)} %fusion.6.table_ref, s32[2048]{0:T(1024)S(1)} %copy-done.54), kind=kCustom, calls=%fused_computation | custom fusion | bytes 1056768 | tf_op jit(solution)/shard_map/jit(_take)/gather | solution.py:829
  126.7 14.1 %gather_fusion.1 = bf16[2048,1024]{1,0:T(8,128)(2,1)} fusion(bf16[2560,1024]{1,0:T(8,128)(2,1)} %pad.29.table_ref, s32[2048]{0:T(1024)S(1)} %broadcast_clamp_fusion.1), kind=kCustom, calls=%fused_computation.1 | custom fusion | bytes 8396800 | tf_op jit(solution)/shard_map/jit(_take)/gather | solution.py:829
  140.8 8.7 %gather_fusion.2 = bf16[2048,256]{1,0:T(8,128)(2,1)S(1)} fusion(bf16[5120,256]{1,0:T(8,128)(2,1)} %pad.30.table_ref, s32[2048]{0:T(1024)S(1)} %broadcast_clamp_fusion), kind=kCustom, calls=%fused_computation.2 | custom fusion | bytes 2105344 | tf_op jit(solution)/shard_map/jit(_take)/gather | solution.py:829
  150.7 5.2 convert_reduce_fusion
  160.6 3.9 broadcast_select_fusion.head_hit_ref
  164.6 5.7 add_convert_fusion.1.rows_ref
  170.3 8.8 %pick_rows.1 = bf16[2304,384]{1,0:T(8,128)(2,1)} custom-call(s32[1,2048]{1,0:T(1,128)} %bitcast.230, bf16[2048,384]{1,0:T(8,128)(2,1)} %add_convert_fusion.1.rows_ref), custom_call_target="tpu_custom_call" | custom-call | flops 3623878656 | bytes 5111808 | tf_op jit(solution)/shard_map/pick_rows/pallas_call | solution.py:188
  182.5 29.8 %band_forward.3 = (f32[8,2048]{1,0:T(8,128)}, bf16[2048,1024]{1,0:T(8,128)(2,1)}) custom-call(s32[2]{0:T(128)} %iota_multiply_fusion.1.span_ref, bf16[2048,1024]{1,0:T(8,128)(2,1)} %all-gather.6.cloned.1.call-done.rows_ref.refs_0_, bf16[2560,1024]{1,0:T(8,128)(2,1)} %pad.29.table_ref), custom_call_target="tpu_custom_call" | custom-call | flops 21474836480 | bytes 17825792 | tf_op jit(solution)/shard_map/band_forward/pallas_call | solution.py:279
  228.8 4.6 multiply_reduce_fusion
  233.5 10.6 %band_forward.5 = (f32[8,2304]{1,0:T(8,128)}, bf16[2304,256]{1,0:T(8,128)(2,1)}) custom-call(s32[2]{0:T(128)} %pad_add_fusion.4.span_ref, bf16[2304,256]{1,0:T(8,128)(2,1)} %copy-done.19, bf16[5120,256]{1,0:T(8,128)(2,1)} %pad.30.table_ref), custom_call_target="tpu_custom_call" | custom-call | flops 3019898880 | bytes 6160384 | tf_op jit(solution)/shard_map/band_forward/pallas_call | solution.py:279
  244.1 40.3 %band_forward.4 = (f32[8,2304]{1,0:T(8,128)}, bf16[2304,128]{1,0:T(8,128)(2,1)}) custom-call(s32[2]{0:T(128)} %pad_add_fusion.3.span_ref, bf16[2304,256]{1,0:T(8,128)(2,1)} %copy-done.19, bf16[26624,128]{1,0:T(8,128)(2,1)} %fusion.6.table_ref), custom_call_target="tpu_custom_call" | custom-call | flops 31406948352 | bytes 8585216 | tf_op jit(solution)/shard_map/band_forward/pallas_call | solution.py:279
  295.6 12.6 %all-gather = f32[64,2304]{1,0:T(8,128)} all-gather(f32[8,2304]{1,0:T(8,128)S(1)} %maximum_maximum_fusion), channel_id=2, replica_groups=mesh['seq'=4,'batch'=8] {'batch'}, dimensions={0}, use_global_device_ids=true | all-gather | bytes 663552 | tf_op jit(solution)/shard_map/all_gather | solution.py:919
  308.2 17.4 %settle.1 = (bf16[2048,1280]{1,0:T(8,128)(2,1)}, f32[8,2048]{1,0:T(8,128)}, f32[16,2304]{1,0:T(8,128)}) custom-call(s32[1]{0:T(128)} %bitcast.member_ref, f32[8,8,2304]{2,1,0:T(8,128)} %bitcast.224, f32[8,2048]{1,0:T(8,128)} %concatenate.73.fact_ref, bf16[2048,1024]{1,0:T(8,128)(2,1)} %get-tuple-element.119.head_mix_ref, ...), custom_call_target="tpu_custom_call" | custom-call | flops 9663676416 | bytes 28114944 | tf_op jit(solution)/shard_map/settle/pallas_call | solution.py:594
  335.5 5.6 collective-permute-done.7
  344.6 32.7 %head_grad.1 = bf16[640,1024]{1,0:T(8,128)(2,1)} custom-call(s32[2]{0:T(128)} %pad_add_fusion.5.base_ref, bf16[2560,1024]{1,0:T(8,128)(2,1)} %pad.29.table_ref, bf16[2048,1024]{1,0:T(8,128)(2,1)} %all-gather.6.cloned.1.call-done.rows_ref.refs_0_, f32[4,2048]{1,0:T(4,128)} %copy-done.42, bf16[6144,1024]{1,0:T(8,128)(2,1)} %all-gather.10.cloned.1.call-done.refs_2_, ...), custom_call_target="tpu_custom_call" | custom-call | flops 21474836480 | bytes 18087936 | tf_op jit(solution)/shard_map/head_grad/pallas_call | solution.py:344
  378.6 5.6 collective-permute-start.9
  393.7 8.3 pad_maximum_fusion.3.rows_ref
  402.0 26.9 %band_grad.3 = bf16[64,3328]{1,0:T(8,128)(2,1)} custom-call(s32[113]{0:T(128)} %concatenate.78.plan_ref, bf16[26624,128]{1,0:T(8,128)(2,1)} %fusion.6.table_ref, bf16[9216,256]{1,0:T(8,128)(2,1)} %pad_maximum_fusion.3.rows_ref, f32[4,9216]{1,0:T(4,128)} %fusion.46.fact_ref), custom_call_target="tpu_custom_call" | custom-call | flops 15703474176 | bytes 4063232 | tf_op jit(solution)/shard_map/band_grad/pallas_call | solution.py:442
  435.3 27.2 %band_grad.4 = bf16[64,3328]{1,0:T(8,128)(2,1)} custom-call(s32[113]{0:T(128)} %concatenate.82.plan_ref, bf16[26624,128]{1,0:T(8,128)(2,1)} %fusion.6.table_ref, bf16[9216,256]{1,0:T(8,128)(2,1)} %pad_maximum_fusion.3.rows_ref, f32[4,9216]{1,0:T(4,128)} %fusion.46.fact_ref), custom_call_target="tpu_custom_call" | custom-call | flops 15703474176 | bytes 4063232 | tf_op jit(solution)/shard_map/band_grad/pallas_call | solution.py:442
  463.9 8.4 collective-permute-done.14
  476.4 7.1 convert_reduce_fusion.2
  484.9 5.9 convolution_convert_fusion.1
  496.6 4.0 collective-permute-start.15
  506.7 9.0 %convolution_convert_fusion = bf16[4096,1024]{1,0:T(8,128)(2,1)} fusion(f32[256,1024]{1,0:T(8,128)} %copy-done.22, f32[256]{0:T(256)S(1)} %negate_multiply_fusion.2, f32[256,4096]{1,0:T(8,128)} %copy-done.92), kind=kOutput, calls=%fused_computation.12 | convolution fusion | flops 2161639424 | bytes 13632512 | tf_op jit(solution)/shard_map/dot_general | solution.py:47
  515.8 7.5 multiply_reduce_fusion.5
  530.4 13.3 %collective-permute-done.18 = bf16[640,1024]{1,0:T(8,128)(2,1)} collective-permute-done((bf16[640,1024]{1,0:T(8,128)(2,1)}, bf16[640,1024]{1,0:T(8,128)(2,1)}, u32[]{:S(2)}, u32[]{:S(2)}) %collective-permute-start.18) | collective-permute-done | bytes 1310752 | tf_op jit(solution)/shard_map/ppermute | solution.py:634
  543.7 23.9 %attend_back.1 = (bf16[256,1024]{1,0:T(8,128)(2,1)}, bf16[1024,1024]{1,0:T(8,128)(2,1)}, bf16[1024,1024]{1,0:T(8,128)(2,1)}) custom-call(s32[1]{0:T(128)} %bitcast.6.start_ref, bf16[256,1024]{1,0:T(8,128)(2,1)} %fusion.21.query_ref, bf16[1024,1024]{1,0:T(8,128)(2,1)} %convolution_convert_fusion.2.key_ref, bf16[1024,1024]{1,0:T(8,128)(2,1)} %add_convert_fusion.value_ref, ...), custom_call_target="tpu_custom_call" | custom-call | flops 2684354560 | bytes 7864320 | tf_op jit(solution)/shard_map/attend_back/pallas_call | solution.py:141
  573.0 4.3 select_select_fusion.3
  577.4 4.7 fusion.7
  593.1 4.0 copy-done.13
  601.4 4.2 fusion.64
  618.4 5.1 collective-permute-start.31
  642.7 5.2 convert_bitcast_fusion
  647.9 26.6 %band_grad.5 = f32[5000,256]{1,0:T(8,128)} custom-call(s32[187]{0:T(256)} %concatenate.86.plan_ref, bf16[5120,256]{1,0:T(8,128)(2,1)} %pad.30.table_ref, bf16[9216,256]{1,0:T(8,128)(2,1)} %pad_maximum_fusion.3.rows_ref, f32[4,9216]{1,0:T(4,128)} %fusion.46.fact_ref), custom_call_target="tpu_custom_call" | custom-call | flops 24159191040 | bytes 9961472 | tf_op jit(solution)/shard_map/band_grad/pallas_call | solution.py:442
  687.2 10.2 %collective-permute-start.38 = (bf16[128,1024]{1,0:T(8,128)(2,1)S(1)}, bf16[128,1024]{1,0:T(8,128)(2,1)S(1)}, u32[]{:S(2)}, u32[]{:S(2)}) collective-permute-start(bf16[128,1024]{1,0:T(8,128)(2,1)S(1)} %get-tuple-element.236), channel_id=1, source_target_pairs={{0,8},{8,16},{16,24},{24,0},{1,9},{9,17},{17,25},{25,1},{2,10},{10... | collective-permute-start | bytes 786440 | tf_op jit(solution)/shard_map/ppermute | solution.py:696
  698.7 45.9 %collective-permute-done.37 = bf16[128,1024]{1,0:T(8,128)(2,1)S(1)} collective-permute-done((bf16[128,1024]{1,0:T(8,128)(2,1)S(1)}, bf16[128,1024]{1,0:T(8,128)(2,1)S(1)}, u32[]{:S(2)}, u32[]{:S(2)}) %collective-permute-start.37) | collective-permute-done | bytes 262176 | tf_op jit(solution)/shard_map/ppermute | solution.py:696
  747.3 4.5 collective-permute-start.39
  751.8 8.6 %collective-permute-done.35 = bf16[32,4096]{1,0:T(8,128)(2,1)S(1)} collective-permute-done((bf16[32,4096]{1,0:T(8,128)(2,1)S(1)}, bf16[32,4096]{1,0:T(8,128)(2,1)S(1)}, u32[]{:S(2)}, u32[]{:S(2)}) %collective-permute-start.35) | collective-permute-done | bytes 262176 | tf_op jit(solution)/shard_map/ppermute | solution.py:625
  762.1 5.0 collective-permute-done.28
  769.6 6.8 collective-permute-done.40
  781.9 48.3 %all-reduce.10.cloned.1.call-done = bf16[128,4480]{1,0:T(8,128)(2,1)} async-done(((bf16[128,4480]{1,0:T(8,128)(2,1)}), bf16[128,4480]{1,0:T(8,128)(2,1)}) %all-reduce.10.cloned.1.call-update) | async-done | bytes 1146896 | tf_op jit(solution)/shard_map/psum | solution.py:1163
  (509 shorter events, 224.9 us)
Async XLA Ops:
  7.2 157.3 %all-gather.6.cloned.1.call-start = ((), (), s32[]{:S(2)}) async-start(), calls=%async_computation.4 | async-start | bytes 4718592 | tf_op jit(solution)/shard_map/all_gather | solution.py:845
  12.6 50.1 %collective-permute-start = (bf16[256,1024]{1,0:T(8,128)(2,1)}, bf16[256,1024]{1,0:T(8,128)(2,1)}, u32[]{:S(2)}, u32[]{:S(2)}) collective-permute-start(bf16[256,1024]{1,0:T(8,128)(2,1)} %add_convert_fusion.5), channel_id=1, source_target_pairs={{0,24},{1,25},{2,26},{3,27},{4,28},{5,29},{6,30},{7,31}} | collective-permute-start | bytes 1572872 | tf_op jit(solution)/shard_map/ppermute | solution.py:673
  20.4 43.7 %collective-permute-start.1 = (bf16[256,1024]{1,0:T(8,128)(2,1)}, bf16[256,1024]{1,0:T(8,128)(2,1)}, u32[]{:S(2)}, u32[]{:S(2)}) collective-permute-start(bf16[256,1024]{1,0:T(8,128)(2,1)} %add_convert_fusion.5), channel_id=1, source_target_pairs={{0,16},{8,24},{1,17},{9,25},{2,18},{10,26},{3,19},{11,27},{4,20},{... | collective-permute-start | bytes 1572872 | tf_op jit(solution)/shard_map/ppermute | solution.py:673
  22.5 42.7 %collective-permute-start.2 = (bf16[256,1024]{1,0:T(8,128)(2,1)}, bf16[256,1024]{1,0:T(8,128)(2,1)}, u32[]{:S(2)}, u32[]{:S(2)}) collective-permute-start(bf16[256,1024]{1,0:T(8,128)(2,1)} %add_convert_fusion.5), channel_id=1, source_target_pairs={{0,8},{8,16},{16,24},{1,9},{9,17},{17,25},{2,10},{10,18},{18,26},{... | collective-permute-start | bytes 1572872 | tf_op jit(solution)/shard_map/ppermute | solution.py:673
  103.2 109.1 %all-gather.8.cloned.1.call-start = ((), (), s32[]{:S(2)}) async-start(), calls=%async_computation.5 | async-start | bytes 2621440 | tf_op jit(solution)/shard_map/all_gather | solution.py:848
  164.5 124.7 %all-gather.10.cloned.1.call-start = ((), (), s32[]{:S(2)}) async-start(), calls=%async_computation.6 | async-start | bytes 14155776 | tf_op jit(solution)/shard_map/all_gather | solution.py:887
  216.2 175.2 %all-gather.12.cloned.1.call-start = ((), (), s32[]{:S(2)}) async-start(), calls=%async_computation.7 | async-start | bytes 3981312 | tf_op jit(solution)/shard_map/all_gather | solution.py:918
  218.8 66.7 %collective-permute-start.3 = (bf16[288,256]{1,0:T(8,128)(2,1)S(1)}, bf16[288,256]{1,0:T(8,128)(2,1)S(1)}, u32[]{:S(2)}, u32[]{:S(2)}) collective-permute-start(bf16[288,256]{1,0:T(8,128)(2,1)S(1)} %constant_dynamic-slice_fusion.1), channel_id=1, source_target_pairs={{0,24},{8,0},{16,8},{24,16},{1,25},{9,1},{17,9},{25,17},{2,26},{10... | collective-permute-start | bytes 442376 | tf_op jit(solution)/shard_map/ppermute | solution.py:625
  219.0 66.5 %collective-permute-start.4 = (bf16[288,256]{1,0:T(8,128)(2,1)S(1)}, bf16[288,256]{1,0:T(8,128)(2,1)S(1)}, u32[]{:S(2)}, u32[]{:S(2)}) collective-permute-start(bf16[288,256]{1,0:T(8,128)(2,1)S(1)} %constant_dynamic-slice_fusion.1), channel_id=1, source_target_pairs={{0,16},{8,24},{16,0},{24,8},{1,17},{9,25},{17,1},{25,9},{2,18},{10... | collective-permute-start | bytes 442376 | tf_op jit(solution)/shard_map/ppermute | solution.py:625
  222.0 63.5 %collective-permute-start.5 = (bf16[288,256]{1,0:T(8,128)(2,1)S(1)}, bf16[288,256]{1,0:T(8,128)(2,1)S(1)}, u32[]{:S(2)}, u32[]{:S(2)}) collective-permute-start(bf16[288,256]{1,0:T(8,128)(2,1)S(1)} %constant_dynamic-slice_fusion.1), channel_id=1, source_target_pairs={{0,8},{8,16},{16,24},{24,0},{1,9},{9,17},{17,25},{25,1},{2,10},{10... | collective-permute-start | bytes 442376 | tf_op jit(solution)/shard_map/ppermute | solution.py:625
  289.3 173.3 %reduce-scatter.5.cloned.1.call-start = ((), (), s32[]{:S(2)}) async-start(), calls=%async_computation.8 | async-start | bytes 5898240 | tf_op jit(solution)/shard_map/reduce_scatter | solution.py:935
  334.3 281.7 %reduce-scatter.7.cloned.1.call-start = ((), (), s32[]{:S(2)}) async-start(), calls=%async_computation.9 | async-start | bytes 9437184 | tf_op jit(solution)/shard_map/reduce_scatter | solution.py:1045
  377.3 51.6 %collective-permute-start.10 = (bf16[640,1024]{1,0:T(8,128)(2,1)}, bf16[640,1024]{1,0:T(8,128)(2,1)}, u32[]{:S(2)}, u32[]{:S(2)}) collective-permute-start(bf16[640,1024]{1,0:T(8,128)(2,1)} %head_grad.1), channel_id=1, source_target_pairs={{8,0},{16,8},{24,16},{9,1},{17,9},{25,17},{10,2},{18,10},{26,18},{... | collective-permute-start | bytes 3932168 | tf_op jit(solution)/shard_map/ppermute | solution.py:634
  378.6 50.4 %collective-permute-start.9 = (bf16[640,1024]{1,0:T(8,128)(2,1)}, bf16[640,1024]{1,0:T(8,128)(2,1)}, u32[]{:S(2)}, u32[]{:S(2)}) collective-permute-start(bf16[640,1024]{1,0:T(8,128)(2,1)} %head_grad.1), channel_id=1, source_target_pairs={{0,8},{8,16},{16,24},{1,9},{9,17},{17,25},{2,10},{10,18},{18,26},{... | collective-permute-start | bytes 3932168 | tf_op jit(solution)/shard_map/ppermute | solution.py:633
  429.0 43.3 %collective-permute-start.11 = (bf16[64,3328]{1,0:T(8,128)(2,1)}, bf16[64,3328]{1,0:T(8,128)(2,1)}, u32[]{:S(2)}, u32[]{:S(2)}) collective-permute-start(bf16[64,3328]{1,0:T(8,128)(2,1)} %band_grad.3), channel_id=1, source_target_pairs={{0,8},{8,16},{16,24},{1,9},{9,17},{17,25},{2,10},{10,18},{18,26},{... | collective-permute-start | bytes 1277960 | tf_op jit(solution)/shard_map/ppermute | solution.py:633
  431.0 41.3 %collective-permute-start.12 = (bf16[64,3328]{1,0:T(8,128)(2,1)}, bf16[64,3328]{1,0:T(8,128)(2,1)}, u32[]{:S(2)}, u32[]{:S(2)}) collective-permute-start(bf16[64,3328]{1,0:T(8,128)(2,1)} %band_grad.3), channel_id=1, source_target_pairs={{8,0},{16,8},{24,16},{9,1},{17,9},{25,17},{10,2},{18,10},{26,18},{... | collective-permute-start | bytes 1277960 | tf_op jit(solution)/shard_map/ppermute | solution.py:634
  432.3 31.6 %collective-permute-start.13 = (bf16[640,1024]{1,0:T(8,128)(2,1)}, bf16[640,1024]{1,0:T(8,128)(2,1)}, u32[]{:S(2)}, u32[]{:S(2)}) collective-permute-start(bf16[640,1024]{1,0:T(8,128)(2,1)} %collective-permute-done.9), channel_id=1, source_target_pairs={{8,16},{16,24},{9,17},{17,25},{10,18},{18,26},{11,19},{19,27},{12,... | collective-permute-start | bytes 3932168 | tf_op jit(solution)/shard_map/ppermute | solution.py:633
  434.1 38.2 %collective-permute-start.14 = (bf16[640,1024]{1,0:T(8,128)(2,1)}, bf16[640,1024]{1,0:T(8,128)(2,1)}, u32[]{:S(2)}, u32[]{:S(2)}) collective-permute-start(bf16[640,1024]{1,0:T(8,128)(2,1)} %collective-permute-done.10), channel_id=1, source_target_pairs={{8,0},{16,8},{9,1},{17,9},{10,2},{18,10},{11,3},{19,11},{12,4},{20... | collective-permute-start | bytes 3932168 | tf_op jit(solution)/shard_map/ppermute | solution.py:634
  490.7 185.9 %reduce-scatter.11.cloned.1.call-start = ((), (), s32[]{:S(2)}) async-start(), calls=%async_computation.12 | async-start | bytes 9437184 | tf_op jit(solution)/shard_map/reduce_scatter | solution.py:1039
  496.6 47.0 %collective-permute-start.15 = (bf16[64,3328]{1,0:T(8,128)(2,1)}, bf16[64,3328]{1,0:T(8,128)(2,1)}, u32[]{:S(2)}, u32[]{:S(2)}) collective-permute-start(bf16[64,3328]{1,0:T(8,128)(2,1)} %band_grad.4), channel_id=1, source_target_pairs={{0,8},{8,16},{16,24},{1,9},{9,17},{17,25},{2,10},{10,18},{18,26},{... | collective-permute-start | bytes 1277960 | tf_op jit(solution)/shard_map/ppermute | solution.py:633
  500.6 43.0 %collective-permute-start.16 = (bf16[64,3328]{1,0:T(8,128)(2,1)}, bf16[64,3328]{1,0:T(8,128)(2,1)}, u32[]{:S(2)}, u32[]{:S(2)}) collective-permute-start(bf16[64,3328]{1,0:T(8,128)(2,1)} %band_grad.4), channel_id=1, source_target_pairs={{8,0},{16,8},{24,16},{9,1},{17,9},{25,17},{10,2},{18,10},{26,18},{... | collective-permute-start | bytes 1277960 | tf_op jit(solution)/shard_map/ppermute | solution.py:634
  501.9 25.9 %collective-permute-start.17 = (bf16[640,1024]{1,0:T(8,128)(2,1)}, bf16[640,1024]{1,0:T(8,128)(2,1)}, u32[]{:S(2)}, u32[]{:S(2)}) collective-permute-start(bf16[640,1024]{1,0:T(8,128)(2,1)} %collective-permute-done.13), channel_id=1, source_target_pairs={{16,24},{17,25},{18,26},{19,27},{20,28},{21,29},{22,30},{23,31}} | collective-permute-start | bytes 3932168 | tf_op jit(solution)/shard_map/ppermute | solution.py:633
  503.6 40.0 %collective-permute-start.18 = (bf16[640,1024]{1,0:T(8,128)(2,1)}, bf16[640,1024]{1,0:T(8,128)(2,1)}, u32[]{:S(2)}, u32[]{:S(2)}) collective-permute-start(bf16[640,1024]{1,0:T(8,128)(2,1)} %collective-permute-done.14), channel_id=1, source_target_pairs={{8,0},{9,1},{10,2},{11,3},{12,4},{13,5},{14,6},{15,7}} | collective-permute-start | bytes 3932168 | tf_op jit(solution)/shard_map/ppermute | solution.py:634
  504.9 62.6 %collective-permute-start.21 = (bf16[64,3328]{1,0:T(8,128)(2,1)}, bf16[64,3328]{1,0:T(8,128)(2,1)}, u32[]{:S(2)}, u32[]{:S(2)}) collective-permute-start(bf16[64,3328]{1,0:T(8,128)(2,1)} %collective-permute-done.11), channel_id=1, source_target_pairs={{8,16},{16,24},{9,17},{17,25},{10,18},{18,26},{11,19},{19,27},{12,... | collective-permute-start | bytes 1277960 | tf_op jit(solution)/shard_map/ppermute | solution.py:633
  523.3 254.8 %reduce-scatter.9.cloned.1.call-start = ((), (), s32[]{:S(2)}) async-start(), calls=%async_computation.10 | async-start | bytes 10321920 | tf_op jit(solution)/shard_map/reduce_scatter | solution.py:1120
  527.8 39.7 %collective-permute-start.22 = (bf16[64,3328]{1,0:T(8,128)(2,1)}, bf16[64,3328]{1,0:T(8,128)(2,1)}, u32[]{:S(2)}, u32[]{:S(2)}) collective-permute-start(bf16[64,3328]{1,0:T(8,128)(2,1)} %collective-permute-done.12), channel_id=1, source_target_pairs={{8,0},{16,8},{9,1},{17,9},{10,2},{18,10},{11,3},{19,11},{12,4},{20... | collective-permute-start | bytes 1277960 | tf_op jit(solution)/shard_map/ppermute | solution.py:634
  567.6 14.5 %collective-permute-start.19 = (bf16[64,3328]{1,0:T(8,128)(2,1)}, bf16[64,3328]{1,0:T(8,128)(2,1)}, u32[]{:S(2)}, u32[]{:S(2)}) collective-permute-start(bf16[64,3328]{1,0:T(8,128)(2,1)} %collective-permute-done.15), channel_id=1, source_target_pairs={{8,16},{16,24},{9,17},{17,25},{10,18},{18,26},{11,19},{19,27},{12,... | collective-permute-start | bytes 1277960 | tf_op jit(solution)/shard_map/ppermute | solution.py:633
  569.0 13.1 %collective-permute-start.20 = (bf16[64,3328]{1,0:T(8,128)(2,1)}, bf16[64,3328]{1,0:T(8,128)(2,1)}, u32[]{:S(2)}, u32[]{:S(2)}) collective-permute-start(bf16[64,3328]{1,0:T(8,128)(2,1)} %collective-permute-done.16), channel_id=1, source_target_pairs={{8,0},{16,8},{9,1},{17,9},{10,2},{18,10},{11,3},{19,11},{12,4},{20... | collective-permute-start | bytes 1277960 | tf_op jit(solution)/shard_map/ppermute | solution.py:634
  570.3 45.8 %collective-permute-start.25 = (bf16[64,3328]{1,0:T(8,128)(2,1)}, bf16[64,3328]{1,0:T(8,128)(2,1)}, u32[]{:S(2)}, u32[]{:S(2)}) collective-permute-start(bf16[64,3328]{1,0:T(8,128)(2,1)} %collective-permute-done.21), channel_id=1, source_target_pairs={{16,24},{17,25},{18,26},{19,27},{20,28},{21,29},{22,30},{23,31}} | collective-permute-start | bytes 1277960 | tf_op jit(solution)/shard_map/ppermute | solution.py:633
  571.7 44.3 %collective-permute-start.26 = (bf16[64,3328]{1,0:T(8,128)(2,1)}, bf16[64,3328]{1,0:T(8,128)(2,1)}, u32[]{:S(2)}, u32[]{:S(2)}) collective-permute-start(bf16[64,3328]{1,0:T(8,128)(2,1)} %collective-permute-done.22), channel_id=1, source_target_pairs={{8,0},{9,1},{10,2},{11,3},{12,4},{13,5},{14,6},{15,7}} | collective-permute-start | bytes 1277960 | tf_op jit(solution)/shard_map/ppermute | solution.py:634
  584.0 32.0 %collective-permute-start.23 = (bf16[64,3328]{1,0:T(8,128)(2,1)}, bf16[64,3328]{1,0:T(8,128)(2,1)}, u32[]{:S(2)}, u32[]{:S(2)}) collective-permute-start(bf16[64,3328]{1,0:T(8,128)(2,1)} %collective-permute-done.19), channel_id=1, source_target_pairs={{16,24},{17,25},{18,26},{19,27},{20,28},{21,29},{22,30},{23,31}} | collective-permute-start | bytes 1277960 | tf_op jit(solution)/shard_map/ppermute | solution.py:633
  585.6 30.5 %collective-permute-start.24 = (bf16[64,3328]{1,0:T(8,128)(2,1)}, bf16[64,3328]{1,0:T(8,128)(2,1)}, u32[]{:S(2)}, u32[]{:S(2)}) collective-permute-start(bf16[64,3328]{1,0:T(8,128)(2,1)} %collective-permute-done.20), channel_id=1, source_target_pairs={{8,0},{9,1},{10,2},{11,3},{12,4},{13,5},{14,6},{15,7}} | collective-permute-start | bytes 1277960 | tf_op jit(solution)/shard_map/ppermute | solution.py:634
  618.2 56.3 %collective-permute-start.30 = (bf16[32,4096]{1,0:T(8,128)(2,1)}, bf16[32,4096]{1,0:T(8,128)(2,1)S(1)}, u32[]{:S(2)}, u32[]{:S(2)}) collective-permute-start(bf16[32,4096]{1,0:T(8,128)(2,1)} %get-tuple-element.238), channel_id=1, source_target_pairs={{0,24},{8,0},{16,8},{24,16},{1,25},{9,1},{17,9},{25,17},{2,26},{10... | collective-permute-start | bytes 786440 | tf_op jit(solution)/shard_map/ppermute | solution.py:696
  618.4 56.0 %collective-permute-start.31 = (bf16[32,4096]{1,0:T(8,128)(2,1)}, bf16[32,4096]{1,0:T(8,128)(2,1)}, u32[]{:S(2)}, u32[]{:S(2)}) collective-permute-start(bf16[32,4096]{1,0:T(8,128)(2,1)} %get-tuple-element.240), channel_id=1, source_target_pairs={{0,16},{8,24},{16,0},{24,8},{1,17},{9,25},{17,1},{25,9},{2,18},{10... | collective-permute-start | bytes 786440 | tf_op jit(solution)/shard_map/ppermute | solution.py:696
  623.5 51.6 %collective-permute-start.32 = (bf16[32,4096]{1,0:T(8,128)(2,1)}, bf16[32,4096]{1,0:T(8,128)(2,1)}, u32[]{:S(2)}, u32[]{:S(2)}) collective-permute-start(bf16[32,4096]{1,0:T(8,128)(2,1)} %get-tuple-element.239), channel_id=1, source_target_pairs={{0,8},{8,16},{16,24},{24,0},{1,9},{9,17},{17,25},{25,1},{2,10},{10... | collective-permute-start | bytes 786440 | tf_op jit(solution)/shard_map/ppermute | solution.py:696
  627.1 135.0 %collective-permute-start.27 = (bf16[256,1024]{1,0:T(8,128)(2,1)}, bf16[256,1024]{1,0:T(8,128)(2,1)}, u32[]{:S(2)}, u32[]{:S(2)}) collective-permute-start(bf16[256,1024]{1,0:T(8,128)(2,1)} %get-tuple-element.231), channel_id=1, source_target_pairs={{8,0},{16,8},{24,16},{9,1},{17,9},{25,17},{10,2},{18,10},{26,18},{... | collective-permute-start | bytes 1572872 | tf_op jit(solution)/shard_map/ppermute | solution.py:696
  642.6 187.7 %all-reduce.10.cloned.1.call-start = ((), (), s32[]{:S(2)}) async-start(), calls=%async_computation.11 | async-start | bytes 2293760 | tf_op jit(solution)/shard_map/psum | solution.py:1163
  676.7 10.5 %collective-permute-start.33 = (bf16[32,4096]{1,0:T(8,128)(2,1)S(1)}, bf16[32,4096]{1,0:T(8,128)(2,1)S(1)}, u32[]{:S(2)}, u32[]{:S(2)}) collective-permute-start(bf16[32,4096]{1,0:T(8,128)(2,1)S(1)} %fusion.41), channel_id=1, source_target_pairs={{0,24},{8,0},{16,8},{24,16},{1,25},{9,1},{17,9},{25,17},{2,26},{10... | collective-permute-start | bytes 786440 | tf_op jit(solution)/shard_map/ppermute | solution.py:625
  680.3 66.9 %collective-permute-start.34 = (bf16[32,4096]{1,0:T(8,128)(2,1)S(1)}, bf16[32,4096]{1,0:T(8,128)(2,1)S(1)}, u32[]{:S(2)}, u32[]{:S(2)}) collective-permute-start(bf16[32,4096]{1,0:T(8,128)(2,1)S(1)} %fusion.41), channel_id=1, source_target_pairs={{0,16},{8,24},{16,0},{24,8},{1,17},{9,25},{17,1},{25,9},{2,18},{10... | collective-permute-start | bytes 786440 | tf_op jit(solution)/shard_map/ppermute | solution.py:625
  682.5 15.0 %collective-permute-start.36 = (bf16[128,1024]{1,0:T(8,128)(2,1)S(1)}, bf16[128,1024]{1,0:T(8,128)(2,1)S(1)}, u32[]{:S(2)}, u32[]{:S(2)}) collective-permute-start(bf16[128,1024]{1,0:T(8,128)(2,1)S(1)} %get-tuple-element.235), channel_id=1, source_target_pairs={{0,24},{8,0},{16,8},{24,16},{1,25},{9,1},{17,9},{25,17},{2,26},{10... | collective-permute-start | bytes 786440 | tf_op jit(solution)/shard_map/ppermute | solution.py:696
  683.4 61.2 %collective-permute-start.37 = (bf16[128,1024]{1,0:T(8,128)(2,1)S(1)}, bf16[128,1024]{1,0:T(8,128)(2,1)S(1)}, u32[]{:S(2)}, u32[]{:S(2)}) collective-permute-start(bf16[128,1024]{1,0:T(8,128)(2,1)S(1)} %get-tuple-element.237), channel_id=1, source_target_pairs={{0,16},{8,24},{16,0},{24,8},{1,17},{9,25},{17,1},{25,9},{2,18},{10... | collective-permute-start | bytes 786440 | tf_op jit(solution)/shard_map/ppermute | solution.py:696
  687.2 58.8 %collective-permute-start.38 = (bf16[128,1024]{1,0:T(8,128)(2,1)S(1)}, bf16[128,1024]{1,0:T(8,128)(2,1)S(1)}, u32[]{:S(2)}, u32[]{:S(2)}) collective-permute-start(bf16[128,1024]{1,0:T(8,128)(2,1)S(1)} %get-tuple-element.236), channel_id=1, source_target_pairs={{0,8},{8,16},{16,24},{24,0},{1,9},{9,17},{17,25},{25,1},{2,10},{10... | collective-permute-start | bytes 786440 | tf_op jit(solution)/shard_map/ppermute | solution.py:696
  697.4 69.7 %collective-permute-start.28 = (bf16[256,1024]{1,0:T(8,128)(2,1)S(1)}, bf16[256,1024]{1,0:T(8,128)(2,1)S(1)}, u32[]{:S(2)}, u32[]{:S(2)}) collective-permute-start(bf16[256,1024]{1,0:T(8,128)(2,1)S(1)} %copy-done.35), channel_id=1, source_target_pairs={{16,0},{24,8},{17,1},{25,9},{18,2},{26,10},{19,3},{27,11},{20,4},{... | collective-permute-start | bytes 1572872 | tf_op jit(solution)/shard_map/ppermute | solution.py:696
  744.6 22.5 %collective-permute-start.29 = (bf16[256,1024]{1,0:T(8,128)(2,1)S(1)}, bf16[256,1024]{1,0:T(8,128)(2,1)S(1)}, u32[]{:S(2)}, u32[]{:S(2)}) collective-permute-start(bf16[256,1024]{1,0:T(8,128)(2,1)S(1)} %copy-done.34), channel_id=1, source_target_pairs={{24,0},{25,1},{26,2},{27,3},{28,4},{29,5},{30,6},{31,7}} | collective-permute-start | bytes 1572872 | tf_op jit(solution)/shard_map/ppermute | solution.py:696
  745.9 14.5 %collective-permute-start.35 = (bf16[32,4096]{1,0:T(8,128)(2,1)S(1)}, bf16[32,4096]{1,0:T(8,128)(2,1)S(1)}, u32[]{:S(2)}, u32[]{:S(2)}) collective-permute-start(bf16[32,4096]{1,0:T(8,128)(2,1)S(1)} %fusion.41), channel_id=1, source_target_pairs={{0,8},{8,16},{16,24},{24,0},{1,9},{9,17},{17,25},{25,1},{2,10},{10... | collective-permute-start | bytes 786440 | tf_op jit(solution)/shard_map/ppermute | solution.py:625
  747.3 22.3 %collective-permute-start.39 = (bf16[128,1024]{1,0:T(8,128)(2,1)S(1)}, bf16[128,1024]{1,0:T(8,128)(2,1)S(1)}, u32[]{:S(2)}, u32[]{:S(2)}) collective-permute-start(bf16[128,1024]{1,0:T(8,128)(2,1)S(1)} %get-tuple-element.200), channel_id=1, source_target_pairs={{0,24},{8,0},{16,8},{24,16},{1,25},{9,1},{17,9},{25,17},{2,26},{10... | collective-permute-start | bytes 786440 | tf_op jit(solution)/shard_map/ppermute | solution.py:625
  760.5 16.0 %collective-permute-start.40 = (bf16[128,1024]{1,0:T(8,128)(2,1)S(1)}, bf16[128,1024]{1,0:T(8,128)(2,1)S(1)}, u32[]{:S(2)}, u32[]{:S(2)}) collective-permute-start(bf16[128,1024]{1,0:T(8,128)(2,1)S(1)} %get-tuple-element.200), channel_id=1, source_target_pairs={{0,16},{8,24},{16,0},{24,8},{1,17},{9,25},{17,1},{25,9},{2,18},{10... | collective-permute-start | bytes 786440 | tf_op jit(solution)/shard_map/ppermute | solution.py:625
  762.1 14.3 %collective-permute-start.41 = (bf16[128,1024]{1,0:T(8,128)(2,1)S(1)}, bf16[128,1024]{1,0:T(8,128)(2,1)S(1)}, u32[]{:S(2)}, u32[]{:S(2)}) collective-permute-start(bf16[128,1024]{1,0:T(8,128)(2,1)S(1)} %get-tuple-element.200), channel_id=1, source_target_pairs={{0,8},{8,16},{16,24},{24,0},{1,9},{9,17},{17,25},{25,1},{2,10},{10... | collective-permute-start | bytes 786440 | tf_op jit(solution)/shard_map/ppermute | solution.py:625
  (101 other events, 1120.1 us)
Sparse Core Ops, SparseCore 0:
  103.3 37.3 all-gather.5
  164.6 46.6 all-gather.7
  216.3 72.8 all-gather.9
  291.0 36.6 all-gather.11
  334.5 57.0 reduce-scatter.4
  490.9 69.4 reduce-scatter.6
  563.8 71.2 reduce-scatter.10
  642.7 75.6 reduce-scatter.8
  778.3 51.9 all-reduce.9

commit v10 on v9

--- a/solution.py
+++ b/solution.py
@@ -1142,8 +1142,12 @@
         (middle_part, inner_low, outer_part)
     )
     rest_part, spread_sum = lax.optimization_barrier((rest_part, spread_sum))
+    rest_low = lax.psum(rest_part, "seq")
     inner_pieces = line_turns(inner_low)
     outer_low = lowered(line_scatter(outer_part))
+    rest_low, inner_pieces, outer_low = lax.optimization_barrier(
+        (rest_low, inner_pieces, outer_low)
+    )
     if split:
         middle_table_grad = middle_part
         head_table_grad = jnp.concatenate(line_ordered(head_found), 0)
@@ -1160,7 +1164,6 @@
     input_grad = mixed_grad + first_in_grad
     inner_sum = in_order(inner_pieces).astype(jnp.float32)
     outer_sum = in_order(line_turns(outer_low)).astype(jnp.float32)
-    rest_low = lax.psum(rest_part, "seq")
     rest_sum = rest_low[:, : 4 * feature_count + middle_width].astype(jnp.float32)
     cut = [rest_sum[:, i * feature_count : (i + 1) * feature_count] for i in range(4)]
     middle_map_sum = rest_sum[:, 4 * feature_count : 4 * feature_count + middle_width]

time: 863 us -> 853 us (0.988)
  waiting for transfers between devices: 148 us -> 117 us
  starting transfers between devices: 88.5 us -> 99.5 us
  Pallas kernels: 263 us -> 272 us
    ppermute x9, waiting for transfers between devices: 50.9 us -> 3.74 us  [line_scatter(): lax.ppermute(part(place + size - k), 'seq', pairs).astype(jnp.float32)]
    ppermute x9, waiting for transfers between devices: 21.7 us -> 42.9 us  [line_step(): lax.ppermute(behind, 'seq', [(d, d - 1) for d in range(1, size - step + 1)])]
    ppermute x9, starting transfers between devices: 22.8 us -> 34.4 us  [line_scatter(): lax.ppermute(part(place + size - k), 'seq', pairs).astype(jnp.float32)]
    unnamed x196 -> x214, local copies, waits for them, and re-layouts: 17.1 us -> 17.8 us
  transfers between devices with their start and end apart: 51 -> 51, of which waited for: 10 -> 11; matrix products, arithmetic and copies ran while one was open for 29% -> 30% of each run, Pallas kernels for 29% -> 31%
where the time goes in v10:
time: 853 us; the launch traced here: 841 us
  Pallas kernels  272 us (32%)
  other arithmetic  123 us (14%)
  waiting for transfers between devices  117 us (14%)
  local copies, waits for them, and re-layouts  105 us (12%)
  starting transfers between devices  99.5 us (12%)
  matrix products  84.5 us (10%)
  blocking collectives  21.5 us (3%)
  between operations  18.8 us (2%)
    pallas_call x3, Pallas kernels, band_grad(): pl.pallas_call(functools.partial(band_grad_kernel, chunk // 2 if chunk >...  88.4 us
    pallas_call x3, Pallas kernels, band_forward(): pl.pallas_call(functools.partial(band_kernel, chunk, per, words, sum_colu...  82.1 us
    ppermute x9, waiting for transfers between devices, line_step(): lax.ppermute(behind, 'seq', [(d, d - 1) for d in range(1, size - step + 1)])  42.9 us
    psum x1, waiting for transfers between devices, on_device(): rest_low = lax.psum(rest_part, 'seq')  40.7 us
    ppermute x9, starting transfers between devices, line_scatter(): lax.ppermute(part(place + size - k), 'seq', pairs).astype(jnp.float32)  34.4 us
    gather x3, local copies, waits for them, and re-layouts, on_device(): jnp.take(table, jnp.clip(local, 0, size - 1), axis=0, mode='clip')  34.4 us
    pallas_call x1, Pallas kernels, head_grad(): pl.pallas_call(functools.partial(head_grad_kernel, chunk, len(lists)), gr...  32.7 us
    dot_general x10, matrix products, product_nt(): lax.dot_general(former, latter, (((1,), (1,)), ((), ())), preferred_eleme...  29.8 us
  transfers between devices with their start and end apart: 51, of which 11 were waited for; matrix products, arithmetic and copies ran while one was open for 30% of the time, Pallas kernels for 31%

profile of v10, /device:TPU:0, one launch (start us, length us, event | category | flops | bytes accessed | tf_op | source)
XLA Modules:
  0.0 841.5 jit_solution(6961283816056867371)
XLA Ops:
  12.6 7.8 collective-permute-start
  26.7 9.1 %all_gather.21 = f32[3,2048]{1,0:T(4,128)S(1)} all-gather(f32[3,256]{1,0:T(4,128)S(1)} %pad_maximum_fusion.9), channel_id=1, replica_groups=mesh['seq'=4,'batch'=8] {'batch'}, dimensions={1}, use_global_device_ids=true | all-gather | bytes 27648 | tf_op jit(solution)/shard_map/all_gather | solution.py:765
  36.4 3.9 select_convert_fusion
  46.7 7.4 copy.119
  55.3 5.5 pad.29.table_ref
  70.2 3.7 add_convert_fusion.value_ref
  73.9 15.1 %attend.1 = bf16[256,1024]{1,0:T(8,128)(2,1)} custom-call(s32[1]{0:T(128)} %bitcast.6.start_ref, bf16[256,1024]{1,0:T(8,128)(2,1)} %fusion.21.query_ref, bf16[1024,1024]{1,0:T(8,128)(2,1)} %convolution_convert_fusion.2.key_ref, bf16[1024,1024]{1,0:T(8,128)(2,1)} %add_convert_fusion.value_ref), custom_call_target="tpu_custom_call" | custom-call | flops 1073741824 | bytes 5242880 | tf_op jit(solution)/shard_map/attend/pallas_call | solution.py:92
  91.4 6.0 convolution_add_fusion
  103.2 11.7 %fusion.6.table_ref = bf16[26624,128]{1,0:T(8,128)(2,1)} fusion(bf16[64,25967]{0,1:T(8,128)(2,1)} %bitcast.210, bf16[1,26624]{0,1:T(8,128)(2,1)} %select_convert_fusion, bf16[128]{0:T(256)(128)(2,1)S(1)} %copy-done.93, bf16[128]{0:T(256)(128)(2,1)S(1)} %copy-done.94), kind=kLoop, calls=%fused_computation.17 | loop fusion | flops 34078720 | bytes 10193280 | tf_op jit(solution)/shard_map/transpose | solution.py:816
  114.9 11.5 %gather_fusion = bf16[2048,128]{1,0:T(8,128)(2,1)} fusion(bf16[26624,128]{1,0:T(8,128)(2,1)} %fusion.6.table_ref, s32[2048]{0:T(1024)S(1)} %copy-done.63), kind=kCustom, calls=%fused_computation | custom fusion | bytes 1056768 | tf_op jit(solution)/shard_map/jit(_take)/gather | solution.py:829
  126.5 14.1 %gather_fusion.1 = bf16[2048,1024]{1,0:T(8,128)(2,1)} fusion(bf16[2560,1024]{1,0:T(8,128)(2,1)} %pad.29.table_ref, s32[2048]{0:T(1024)S(1)} %broadcast_clamp_fusion.1), kind=kCustom, calls=%fused_computation.1 | custom fusion | bytes 8396800 | tf_op jit(solution)/shard_map/jit(_take)/gather | solution.py:829
  140.6 8.7 %gather_fusion.2 = bf16[2048,256]{1,0:T(8,128)(2,1)S(1)} fusion(bf16[5120,256]{1,0:T(8,128)(2,1)} %pad.30.table_ref, s32[2048]{0:T(1024)S(1)} %broadcast_clamp_fusion), kind=kCustom, calls=%fused_computation.2 | custom fusion | bytes 2105344 | tf_op jit(solution)/shard_map/jit(_take)/gather | solution.py:829
  150.5 5.2 convert_reduce_fusion
  160.4 3.9 broadcast_select_fusion.head_hit_ref
  164.4 5.7 add_convert_fusion.1.rows_ref
  170.1 8.8 %pick_rows.1 = bf16[2304,384]{1,0:T(8,128)(2,1)} custom-call(s32[1,2048]{1,0:T(1,128)} %bitcast.229, bf16[2048,384]{1,0:T(8,128)(2,1)} %add_convert_fusion.1.rows_ref), custom_call_target="tpu_custom_call" | custom-call | flops 3623878656 | bytes 5111808 | tf_op jit(solution)/shard_map/pick_rows/pallas_call | solution.py:188
  182.3 29.8 %band_forward.3 = (f32[8,2048]{1,0:T(8,128)}, bf16[2048,1024]{1,0:T(8,128)(2,1)}) custom-call(s32[2]{0:T(128)} %iota_multiply_fusion.1.span_ref, bf16[2048,1024]{1,0:T(8,128)(2,1)} %all-gather.6.cloned.1.call-done.rows_ref.refs_0_, bf16[2560,1024]{1,0:T(8,128)(2,1)} %pad.29.table_ref), custom_call_target="tpu_custom_call" | custom-call | flops 21474836480 | bytes 17825792 | tf_op jit(solution)/shard_map/band_forward/pallas_call | solution.py:279
  212.1 3.9 fusion.15
  228.6 4.6 multiply_reduce_fusion
  233.3 11.9 %band_forward.5 = (f32[8,2304]{1,0:T(8,128)}, bf16[2304,256]{1,0:T(8,128)(2,1)}) custom-call(s32[2]{0:T(128)} %pad_add_fusion.4.span_ref, bf16[2304,256]{1,0:T(8,128)(2,1)} %copy-done.22, bf16[5120,256]{1,0:T(8,128)(2,1)} %pad.30.table_ref), custom_call_target="tpu_custom_call" | custom-call | flops 3019898880 | bytes 6160384 | tf_op jit(solution)/shard_map/band_forward/pallas_call | solution.py:279
  245.2 40.4 %band_forward.4 = (f32[8,2304]{1,0:T(8,128)}, bf16[2304,128]{1,0:T(8,128)(2,1)}) custom-call(s32[2]{0:T(128)} %pad_add_fusion.3.span_ref, bf16[2304,256]{1,0:T(8,128)(2,1)} %copy-done.22, bf16[26624,128]{1,0:T(8,128)(2,1)} %fusion.6.table_ref), custom_call_target="tpu_custom_call" | custom-call | flops 31406948352 | bytes 8585216 | tf_op jit(solution)/shard_map/band_forward/pallas_call | solution.py:279
  295.3 12.5 %all-gather = f32[64,2304]{1,0:T(8,128)} all-gather(f32[8,2304]{1,0:T(8,128)S(1)} %maximum_maximum_fusion), channel_id=2, replica_groups=mesh['seq'=4,'batch'=8] {'batch'}, dimensions={0}, use_global_device_ids=true | all-gather | bytes 663552 | tf_op jit(solution)/shard_map/all_gather | solution.py:919
  307.8 17.4 %settle.1 = (bf16[2048,1280]{1,0:T(8,128)(2,1)}, f32[8,2048]{1,0:T(8,128)}, f32[16,2304]{1,0:T(8,128)}) custom-call(s32[1]{0:T(128)} %bitcast.member_ref, f32[8,8,2304]{2,1,0:T(8,128)} %bitcast.223, f32[8,2048]{1,0:T(8,128)} %concatenate.73.fact_ref, bf16[2048,1024]{1,0:T(8,128)(2,1)} %get-tuple-element.125.head_mix_ref, ...), custom_call_target="tpu_custom_call" | custom-call | flops 9663676416 | bytes 28114944 | tf_op jit(solution)/shard_map/settle/pallas_call | solution.py:594
  328.2 7.8 collective-permute-start.6
  338.6 4.6 collective-permute-done.7
  346.6 32.7 %head_grad.1 = bf16[640,1024]{1,0:T(8,128)(2,1)} custom-call(s32[2]{0:T(128)} %pad_add_fusion.5.base_ref, bf16[2560,1024]{1,0:T(8,128)(2,1)} %pad.29.table_ref, bf16[2048,1024]{1,0:T(8,128)(2,1)} %all-gather.6.cloned.1.call-done.rows_ref.refs_0_, f32[4,2048]{1,0:T(4,128)} %copy-done.51, bf16[6144,1024]{1,0:T(8,128)(2,1)} %all-gather.10.cloned.1.call-done.refs_2_, ...), custom_call_target="tpu_custom_call" | custom-call | flops 21474836480 | bytes 18087936 | tf_op jit(solution)/shard_map/head_grad/pallas_call | solution.py:344
  380.5 5.6 collective-permute-start.9
  395.6 8.2 pad_maximum_fusion.3.rows_ref
  403.8 29.3 %band_grad.3 = bf16[64,3328]{1,0:T(8,128)(2,1)} custom-call(s32[113]{0:T(128)} %concatenate.78.plan_ref, bf16[26624,128]{1,0:T(8,128)(2,1)} %fusion.6.table_ref, bf16[9216,256]{1,0:T(8,128)(2,1)} %pad_maximum_fusion.3.rows_ref, f32[4,9216]{1,0:T(4,128)} %fusion.46.fact_ref), custom_call_target="tpu_custom_call" | custom-call | flops 15703474176 | bytes 4063232 | tf_op jit(solution)/shard_map/band_grad/pallas_call | solution.py:442
  439.8 29.5 %band_grad.4 = bf16[64,3328]{1,0:T(8,128)(2,1)} custom-call(s32[113]{0:T(128)} %concatenate.82.plan_ref, bf16[26624,128]{1,0:T(8,128)(2,1)} %fusion.6.table_ref, bf16[9216,256]{1,0:T(8,128)(2,1)} %pad_maximum_fusion.3.rows_ref, f32[4,9216]{1,0:T(4,128)} %fusion.46.fact_ref), custom_call_target="tpu_custom_call" | custom-call | flops 15703474176 | bytes 4063232 | tf_op jit(solution)/shard_map/band_grad/pallas_call | solution.py:442
  470.6 6.3 collective-permute-done.14
  481.0 7.1 convert_reduce_fusion.2
  489.5 5.9 convolution_convert_fusion.1
  501.7 10.1 %convolution_convert_fusion = bf16[4096,1024]{1,0:T(8,128)(2,1)} fusion(f32[256,1024]{1,0:T(8,128)} %copy-done.25, f32[256]{0:T(256)S(1)} %negate_multiply_fusion.2, f32[256,4096]{1,0:T(8,128)} %copy-done.101), kind=kOutput, calls=%fused_computation.12 | convolution fusion | flops 2161639424 | bytes 13632512 | tf_op jit(solution)/shard_map/dot_general | solution.py:47
  511.9 6.9 multiply_reduce_fusion.5
  518.8 4.0 collective-permute-start.15
  532.4 33.4 %collective-permute-done.18 = bf16[640,1024]{1,0:T(8,128)(2,1)S(1)} collective-permute-done((bf16[640,1024]{1,0:T(8,128)(2,1)}, bf16[640,1024]{1,0:T(8,128)(2,1)S(1)}, u32[]{:S(2)}, u32[]{:S(2)}) %collective-permute-start.18) | collective-permute-done | bytes 1310752 | tf_op jit(solution)/shard_map/ppermute | solution.py:634
  567.7 24.1 %attend_back.1 = (bf16[256,1024]{1,0:T(8,128)(2,1)}, bf16[1024,1024]{1,0:T(8,128)(2,1)}, bf16[1024,1024]{1,0:T(8,128)(2,1)}) custom-call(s32[1]{0:T(128)} %bitcast.6.start_ref, bf16[256,1024]{1,0:T(8,128)(2,1)} %fusion.21.query_ref, bf16[1024,1024]{1,0:T(8,128)(2,1)} %convolution_convert_fusion.2.key_ref, bf16[1024,1024]{1,0:T(8,128)(2,1)} %add_convert_fusion.value_ref, ...), custom_call_target="tpu_custom_call" | custom-call | flops 2684354560 | bytes 7864320 | tf_op jit(solution)/shard_map/attend_back/pallas_call | solution.py:141
  600.1 4.7 fusion.7
  618.8 4.1 copy-done.13
  627.1 4.2 fusion.64
  644.4 4.5 collective-permute-start.31
  665.6 29.6 %band_grad.5 = f32[5000,256]{1,0:T(8,128)} custom-call(s32[187]{0:T(256)} %concatenate.86.plan_ref, bf16[5120,256]{1,0:T(8,128)(2,1)} %pad.30.table_ref, bf16[9216,256]{1,0:T(8,128)(2,1)} %pad_maximum_fusion.3.rows_ref, f32[4,9216]{1,0:T(4,128)} %fusion.46.fact_ref), custom_call_target="tpu_custom_call" | custom-call | flops 24159191040 | bytes 9961472 | tf_op jit(solution)/shard_map/band_grad/pallas_call | solution.py:442
  701.2 8.6 %collective-permute-start.36 = (bf16[128,1024]{1,0:T(8,128)(2,1)S(1)}, bf16[128,1024]{1,0:T(8,128)(2,1)S(1)}, u32[]{:S(2)}, u32[]{:S(2)}) collective-permute-start(bf16[128,1024]{1,0:T(8,128)(2,1)S(1)} %get-tuple-element.245), channel_id=1, source_target_pairs={{0,24},{8,0},{16,8},{24,16},{1,25},{9,1},{17,9},{25,17},{2,26},{10... | collective-permute-start | bytes 786440 | tf_op jit(solution)/shard_map/ppermute | solution.py:696
  715.3 15.9 %collective-permute-start.38 = (bf16[128,1024]{1,0:T(8,128)(2,1)S(1)}, bf16[128,1024]{1,0:T(8,128)(2,1)S(1)}, u32[]{:S(2)}, u32[]{:S(2)}) collective-permute-start(bf16[128,1024]{1,0:T(8,128)(2,1)S(1)} %get-tuple-element.246), channel_id=1, source_target_pairs={{0,8},{8,16},{16,24},{24,0},{1,9},{9,17},{17,25},{25,1},{2,10},{10... | collective-permute-start | bytes 786440 | tf_op jit(solution)/shard_map/ppermute | solution.py:696
  731.1 5.3 convert_bitcast_fusion
  747.9 18.7 %collective-permute-done.34 = bf16[32,4096]{1,0:T(8,128)(2,1)} collective-permute-done((bf16[32,4096]{1,0:T(8,128)(2,1)S(1)}, bf16[32,4096]{1,0:T(8,128)(2,1)}, u32[]{:S(2)}, u32[]{:S(2)}) %collective-permute-start.34) | collective-permute-done | bytes 262176 | tf_op jit(solution)/shard_map/ppermute | solution.py:625
  766.5 40.7 %all-reduce.10.cloned.1.call-done = bf16[128,4480]{1,0:T(8,128)(2,1)} async-done(((bf16[128,4480]{1,0:T(8,128)(2,1)}), bf16[128,4480]{1,0:T(8,128)(2,1)}) %all-reduce.10.cloned.1.call-update) | async-done | bytes 1146896 | tf_op jit(solution)/shard_map/psum | solution.py:1145
  (528 shorter events, 222.7 us)
Async XLA Ops:
  7.2 157.1 %all-gather.6.cloned.1.call-start = ((), (), s32[]{:S(2)}) async-start(), calls=%async_computation.4 | async-start | bytes 4718592 | tf_op jit(solution)/shard_map/all_gather | solution.py:845
  12.6 50.0 %collective-permute-start = (bf16[256,1024]{1,0:T(8,128)(2,1)}, bf16[256,1024]{1,0:T(8,128)(2,1)}, u32[]{:S(2)}, u32[]{:S(2)}) collective-permute-start(bf16[256,1024]{1,0:T(8,128)(2,1)} %add_convert_fusion.5), channel_id=1, source_target_pairs={{0,24},{1,25},{2,26},{3,27},{4,28},{5,29},{6,30},{7,31}} | collective-permute-start | bytes 1572872 | tf_op jit(solution)/shard_map/ppermute | solution.py:673
  20.4 43.6 %collective-permute-start.1 = (bf16[256,1024]{1,0:T(8,128)(2,1)}, bf16[256,1024]{1,0:T(8,128)(2,1)}, u32[]{:S(2)}, u32[]{:S(2)}) collective-permute-start(bf16[256,1024]{1,0:T(8,128)(2,1)} %add_convert_fusion.5), channel_id=1, source_target_pairs={{0,16},{8,24},{1,17},{9,25},{2,18},{10,26},{3,19},{11,27},{4,20},{... | collective-permute-start | bytes 1572872 | tf_op jit(solution)/shard_map/ppermute | solution.py:673
  22.5 42.7 %collective-permute-start.2 = (bf16[256,1024]{1,0:T(8,128)(2,1)}, bf16[256,1024]{1,0:T(8,128)(2,1)}, u32[]{:S(2)}, u32[]{:S(2)}) collective-permute-start(bf16[256,1024]{1,0:T(8,128)(2,1)} %add_convert_fusion.5), channel_id=1, source_target_pairs={{0,8},{8,16},{16,24},{1,9},{9,17},{17,25},{2,10},{10,18},{18,26},{... | collective-permute-start | bytes 1572872 | tf_op jit(solution)/shard_map/ppermute | solution.py:673
  103.1 109.0 %all-gather.8.cloned.1.call-start = ((), (), s32[]{:S(2)}) async-start(), calls=%async_computation.5 | async-start | bytes 2621440 | tf_op jit(solution)/shard_map/all_gather | solution.py:848
  164.3 124.7 %all-gather.10.cloned.1.call-start = ((), (), s32[]{:S(2)}) async-start(), calls=%async_computation.6 | async-start | bytes 14155776 | tf_op jit(solution)/shard_map/all_gather | solution.py:887
  216.0 177.3 %all-gather.12.cloned.1.call-start = ((), (), s32[]{:S(2)}) async-start(), calls=%async_computation.7 | async-start | bytes 3981312 | tf_op jit(solution)/shard_map/all_gather | solution.py:918
  218.6 68.1 %collective-permute-start.3 = (bf16[288,256]{1,0:T(8,128)(2,1)S(1)}, bf16[288,256]{1,0:T(8,128)(2,1)S(1)}, u32[]{:S(2)}, u32[]{:S(2)}) collective-permute-start(bf16[288,256]{1,0:T(8,128)(2,1)S(1)} %constant_dynamic-slice_fusion.1), channel_id=1, source_target_pairs={{0,24},{8,0},{16,8},{24,16},{1,25},{9,1},{17,9},{25,17},{2,26},{10... | collective-permute-start | bytes 442376 | tf_op jit(solution)/shard_map/ppermute | solution.py:625
  218.9 67.8 %collective-permute-start.4 = (bf16[288,256]{1,0:T(8,128)(2,1)S(1)}, bf16[288,256]{1,0:T(8,128)(2,1)S(1)}, u32[]{:S(2)}, u32[]{:S(2)}) collective-permute-start(bf16[288,256]{1,0:T(8,128)(2,1)S(1)} %constant_dynamic-slice_fusion.1), channel_id=1, source_target_pairs={{0,16},{8,24},{16,0},{24,8},{1,17},{9,25},{17,1},{25,9},{2,18},{10... | collective-permute-start | bytes 442376 | tf_op jit(solution)/shard_map/ppermute | solution.py:625
  221.9 64.8 %collective-permute-start.5 = (bf16[288,256]{1,0:T(8,128)(2,1)S(1)}, bf16[288,256]{1,0:T(8,128)(2,1)S(1)}, u32[]{:S(2)}, u32[]{:S(2)}) collective-permute-start(bf16[288,256]{1,0:T(8,128)(2,1)S(1)} %constant_dynamic-slice_fusion.1), channel_id=1, source_target_pairs={{0,8},{8,16},{16,24},{24,0},{1,9},{9,17},{17,25},{25,1},{2,10},{10... | collective-permute-start | bytes 442376 | tf_op jit(solution)/shard_map/ppermute | solution.py:625
  289.0 180.3 %reduce-scatter.5.cloned.1.call-start = ((), (), s32[]{:S(2)}) async-start(), calls=%async_computation.8 | async-start | bytes 5898240 | tf_op jit(solution)/shard_map/reduce_scatter | solution.py:935
  328.2 10.4 %collective-permute-start.6 = (f32[4,4352]{1,0:T(4,128)S(1)}, f32[4,4352]{1,0:T(4,128)S(1)}, u32[]{:S(2)}, u32[]{:S(2)}) collective-permute-start(f32[4,4352]{1,0:T(4,128)S(1)} %pad_maximum_fusion.6), channel_id=1, source_target_pairs={{0,24},{8,0},{16,8},{24,16},{1,25},{9,1},{17,9},{25,17},{2,26},{10... | collective-permute-start | bytes 208904 | tf_op jit(solution)/shard_map/ppermute | solution.py:625
  336.7 305.0 %reduce-scatter.7.cloned.1.call-start = ((), (), s32[]{:S(2)}) async-start(), calls=%async_computation.9 | async-start | bytes 9437184 | tf_op jit(solution)/shard_map/reduce_scatter | solution.py:1045
  379.2 53.9 %collective-permute-start.10 = (bf16[640,1024]{1,0:T(8,128)(2,1)}, bf16[640,1024]{1,0:T(8,128)(2,1)}, u32[]{:S(2)}, u32[]{:S(2)}) collective-permute-start(bf16[640,1024]{1,0:T(8,128)(2,1)} %head_grad.1), channel_id=1, source_target_pairs={{8,0},{16,8},{24,16},{9,1},{17,9},{25,17},{10,2},{18,10},{26,18},{... | collective-permute-start | bytes 3932168 | tf_op jit(solution)/shard_map/ppermute | solution.py:634
  380.5 52.6 %collective-permute-start.9 = (bf16[640,1024]{1,0:T(8,128)(2,1)}, bf16[640,1024]{1,0:T(8,128)(2,1)}, u32[]{:S(2)}, u32[]{:S(2)}) collective-permute-start(bf16[640,1024]{1,0:T(8,128)(2,1)} %head_grad.1), channel_id=1, source_target_pairs={{0,8},{8,16},{16,24},{1,9},{9,17},{17,25},{2,10},{10,18},{18,26},{... | collective-permute-start | bytes 3932168 | tf_op jit(solution)/shard_map/ppermute | solution.py:633
  433.1 43.8 %collective-permute-start.11 = (bf16[64,3328]{1,0:T(8,128)(2,1)}, bf16[64,3328]{1,0:T(8,128)(2,1)}, u32[]{:S(2)}, u32[]{:S(2)}) collective-permute-start(bf16[64,3328]{1,0:T(8,128)(2,1)} %band_grad.3), channel_id=1, source_target_pairs={{0,8},{8,16},{16,24},{1,9},{9,17},{17,25},{2,10},{10,18},{18,26},{... | collective-permute-start | bytes 1277960 | tf_op jit(solution)/shard_map/ppermute | solution.py:633
  435.5 41.5 %collective-permute-start.12 = (bf16[64,3328]{1,0:T(8,128)(2,1)}, bf16[64,3328]{1,0:T(8,128)(2,1)}, u32[]{:S(2)}, u32[]{:S(2)}) collective-permute-start(bf16[64,3328]{1,0:T(8,128)(2,1)} %band_grad.3), channel_id=1, source_target_pairs={{8,0},{16,8},{24,16},{9,1},{17,9},{25,17},{10,2},{18,10},{26,18},{... | collective-permute-start | bytes 1277960 | tf_op jit(solution)/shard_map/ppermute | solution.py:634
  436.8 33.9 %collective-permute-start.13 = (bf16[640,1024]{1,0:T(8,128)(2,1)}, bf16[640,1024]{1,0:T(8,128)(2,1)}, u32[]{:S(2)}, u32[]{:S(2)}) collective-permute-start(bf16[640,1024]{1,0:T(8,128)(2,1)} %collective-permute-done.9), channel_id=1, source_target_pairs={{8,16},{16,24},{9,17},{17,25},{10,18},{18,26},{11,19},{19,27},{12,... | collective-permute-start | bytes 3932168 | tf_op jit(solution)/shard_map/ppermute | solution.py:633
  438.5 38.4 %collective-permute-start.14 = (bf16[640,1024]{1,0:T(8,128)(2,1)}, bf16[640,1024]{1,0:T(8,128)(2,1)}, u32[]{:S(2)}, u32[]{:S(2)}) collective-permute-start(bf16[640,1024]{1,0:T(8,128)(2,1)} %collective-permute-done.10), channel_id=1, source_target_pairs={{8,0},{16,8},{9,1},{17,9},{10,2},{18,10},{11,3},{19,11},{12,4},{20... | collective-permute-start | bytes 3932168 | tf_op jit(solution)/shard_map/ppermute | solution.py:634
  495.4 204.7 %reduce-scatter.11.cloned.1.call-start = ((), (), s32[]{:S(2)}) async-start(), calls=%async_computation.12 | async-start | bytes 9437184 | tf_op jit(solution)/shard_map/reduce_scatter | solution.py:1039
  511.8 232.3 %reduce-scatter.9.cloned.1.call-start = ((), (), s32[]{:S(2)}) async-start(), calls=%async_computation.10 | async-start | bytes 10321920 | tf_op jit(solution)/shard_map/reduce_scatter | solution.py:1120
  518.8 47.0 %collective-permute-start.15 = (bf16[64,3328]{1,0:T(8,128)(2,1)S(1)}, bf16[64,3328]{1,0:T(8,128)(2,1)S(1)}, u32[]{:S(2)}, u32[]{:S(2)}) collective-permute-start(bf16[64,3328]{1,0:T(8,128)(2,1)S(1)} %copy-done.17), channel_id=1, source_target_pairs={{0,8},{8,16},{16,24},{1,9},{9,17},{17,25},{2,10},{10,18},{18,26},{... | collective-permute-start | bytes 1277960 | tf_op jit(solution)/shard_map/ppermute | solution.py:633
  522.8 44.9 %collective-permute-start.16 = (bf16[64,3328]{1,0:T(8,128)(2,1)S(1)}, bf16[64,3328]{1,0:T(8,128)(2,1)}, u32[]{:S(2)}, u32[]{:S(2)}) collective-permute-start(bf16[64,3328]{1,0:T(8,128)(2,1)S(1)} %copy-done.17), channel_id=1, source_target_pairs={{8,0},{16,8},{24,16},{9,1},{17,9},{25,17},{10,2},{18,10},{26,18},{... | collective-permute-start | bytes 1277960 | tf_op jit(solution)/shard_map/ppermute | solution.py:634
  524.8 40.9 %collective-permute-start.18 = (bf16[640,1024]{1,0:T(8,128)(2,1)}, bf16[640,1024]{1,0:T(8,128)(2,1)S(1)}, u32[]{:S(2)}, u32[]{:S(2)}) collective-permute-start(bf16[640,1024]{1,0:T(8,128)(2,1)} %collective-permute-done.14), channel_id=1, source_target_pairs={{8,0},{9,1},{10,2},{11,3},{12,4},{13,5},{14,6},{15,7}} | collective-permute-start | bytes 3932168 | tf_op jit(solution)/shard_map/ppermute | solution.py:634
  526.1 65.7 %collective-permute-start.21 = (bf16[64,3328]{1,0:T(8,128)(2,1)}, bf16[64,3328]{1,0:T(8,128)(2,1)}, u32[]{:S(2)}, u32[]{:S(2)}) collective-permute-start(bf16[64,3328]{1,0:T(8,128)(2,1)} %collective-permute-done.11), channel_id=1, source_target_pairs={{8,16},{16,24},{9,17},{17,25},{10,18},{18,26},{11,19},{19,27},{12,... | collective-permute-start | bytes 1277960 | tf_op jit(solution)/shard_map/ppermute | solution.py:633
  529.9 61.9 %collective-permute-start.22 = (bf16[64,3328]{1,0:T(8,128)(2,1)}, bf16[64,3328]{1,0:T(8,128)(2,1)}, u32[]{:S(2)}, u32[]{:S(2)}) collective-permute-start(bf16[64,3328]{1,0:T(8,128)(2,1)} %collective-permute-done.12), channel_id=1, source_target_pairs={{8,0},{16,8},{9,1},{17,9},{10,2},{18,10},{11,3},{19,11},{12,4},{20... | collective-permute-start | bytes 1277960 | tf_op jit(solution)/shard_map/ppermute | solution.py:634
  591.8 12.9 %collective-permute-start.19 = (bf16[64,3328]{1,0:T(8,128)(2,1)S(1)}, bf16[64,3328]{1,0:T(8,128)(2,1)}, u32[]{:S(2)}, u32[]{:S(2)}) collective-permute-start(bf16[64,3328]{1,0:T(8,128)(2,1)S(1)} %copy-done.28), channel_id=1, source_target_pairs={{8,16},{16,24},{9,17},{17,25},{10,18},{18,26},{11,19},{19,27},{12,... | collective-permute-start | bytes 1277960 | tf_op jit(solution)/shard_map/ppermute | solution.py:633
  593.2 14.8 %collective-permute-start.20 = (bf16[64,3328]{1,0:T(8,128)(2,1)}, bf16[64,3328]{1,0:T(8,128)(2,1)}, u32[]{:S(2)}, u32[]{:S(2)}) collective-permute-start(bf16[64,3328]{1,0:T(8,128)(2,1)} %collective-permute-done.16), channel_id=1, source_target_pairs={{8,0},{16,8},{9,1},{17,9},{10,2},{18,10},{11,3},{19,11},{12,4},{20... | collective-permute-start | bytes 1277960 | tf_op jit(solution)/shard_map/ppermute | solution.py:634
  594.5 47.2 %collective-permute-start.25 = (bf16[64,3328]{1,0:T(8,128)(2,1)}, bf16[64,3328]{1,0:T(8,128)(2,1)}, u32[]{:S(2)}, u32[]{:S(2)}) collective-permute-start(bf16[64,3328]{1,0:T(8,128)(2,1)} %collective-permute-done.21), channel_id=1, source_target_pairs={{16,24},{17,25},{18,26},{19,27},{20,28},{21,29},{22,30},{23,31}} | collective-permute-start | bytes 1277960 | tf_op jit(solution)/shard_map/ppermute | solution.py:633
  595.9 45.8 %collective-permute-start.26 = (bf16[64,3328]{1,0:T(8,128)(2,1)}, bf16[64,3328]{1,0:T(8,128)(2,1)}, u32[]{:S(2)}, u32[]{:S(2)}) collective-permute-start(bf16[64,3328]{1,0:T(8,128)(2,1)} %collective-permute-done.22), channel_id=1, source_target_pairs={{8,0},{9,1},{10,2},{11,3},{12,4},{13,5},{14,6},{15,7}} | collective-permute-start | bytes 1277960 | tf_op jit(solution)/shard_map/ppermute | solution.py:634
  608.0 33.7 %collective-permute-start.23 = (bf16[64,3328]{1,0:T(8,128)(2,1)}, bf16[64,3328]{1,0:T(8,128)(2,1)}, u32[]{:S(2)}, u32[]{:S(2)}) collective-permute-start(bf16[64,3328]{1,0:T(8,128)(2,1)} %collective-permute-done.19), channel_id=1, source_target_pairs={{16,24},{17,25},{18,26},{19,27},{20,28},{21,29},{22,30},{23,31}} | collective-permute-start | bytes 1277960 | tf_op jit(solution)/shard_map/ppermute | solution.py:633
  609.5 32.3 %collective-permute-start.24 = (bf16[64,3328]{1,0:T(8,128)(2,1)}, bf16[64,3328]{1,0:T(8,128)(2,1)}, u32[]{:S(2)}, u32[]{:S(2)}) collective-permute-start(bf16[64,3328]{1,0:T(8,128)(2,1)} %collective-permute-done.20), channel_id=1, source_target_pairs={{8,0},{9,1},{10,2},{11,3},{12,4},{13,5},{14,6},{15,7}} | collective-permute-start | bytes 1277960 | tf_op jit(solution)/shard_map/ppermute | solution.py:634
  643.9 53.3 %collective-permute-start.30 = (bf16[32,4096]{1,0:T(8,128)(2,1)}, bf16[32,4096]{1,0:T(8,128)(2,1)S(1)}, u32[]{:S(2)}, u32[]{:S(2)}) collective-permute-start(bf16[32,4096]{1,0:T(8,128)(2,1)} %get-tuple-element.248), channel_id=1, source_target_pairs={{0,24},{8,0},{16,8},{24,16},{1,25},{9,1},{17,9},{25,17},{2,26},{10... | collective-permute-start | bytes 786440 | tf_op jit(solution)/shard_map/ppermute | solution.py:696
  644.4 54.1 %collective-permute-start.31 = (bf16[32,4096]{1,0:T(8,128)(2,1)}, bf16[32,4096]{1,0:T(8,128)(2,1)}, u32[]{:S(2)}, u32[]{:S(2)}) collective-permute-start(bf16[32,4096]{1,0:T(8,128)(2,1)} %get-tuple-element.250), channel_id=1, source_target_pairs={{0,16},{8,24},{16,0},{24,8},{1,17},{9,25},{17,1},{25,9},{2,18},{10... | collective-permute-start | bytes 786440 | tf_op jit(solution)/shard_map/ppermute | solution.py:696
  648.9 49.7 %collective-permute-start.32 = (bf16[32,4096]{1,0:T(8,128)(2,1)}, bf16[32,4096]{1,0:T(8,128)(2,1)}, u32[]{:S(2)}, u32[]{:S(2)}) collective-permute-start(bf16[32,4096]{1,0:T(8,128)(2,1)} %get-tuple-element.249), channel_id=1, source_target_pairs={{0,8},{8,16},{16,24},{24,0},{1,9},{9,17},{17,25},{25,1},{2,10},{10... | collective-permute-start | bytes 786440 | tf_op jit(solution)/shard_map/ppermute | solution.py:696
  652.5 87.1 %collective-permute-start.27 = (bf16[256,1024]{1,0:T(8,128)(2,1)}, bf16[256,1024]{1,0:T(8,128)(2,1)}, u32[]{:S(2)}, u32[]{:S(2)}) collective-permute-start(bf16[256,1024]{1,0:T(8,128)(2,1)} %get-tuple-element.241), channel_id=1, source_target_pairs={{8,0},{16,8},{24,16},{9,1},{17,9},{25,17},{10,2},{18,10},{26,18},{... | collective-permute-start | bytes 1572872 | tf_op jit(solution)/shard_map/ppermute | solution.py:696
  653.8 87.4 %collective-permute-start.28 = (bf16[256,1024]{1,0:T(8,128)(2,1)}, bf16[256,1024]{1,0:T(8,128)(2,1)}, u32[]{:S(2)}, u32[]{:S(2)}) collective-permute-start(bf16[256,1024]{1,0:T(8,128)(2,1)} %get-tuple-element.243), channel_id=1, source_target_pairs={{16,0},{24,8},{17,1},{25,9},{18,2},{26,10},{19,3},{27,11},{20,4},{... | collective-permute-start | bytes 1572872 | tf_op jit(solution)/shard_map/ppermute | solution.py:696
  661.3 146.0 %all-reduce.10.cloned.1.call-start = ((), (), s32[]{:S(2)}) async-start(), calls=%async_computation.11 | async-start | bytes 2293760 | tf_op jit(solution)/shard_map/psum | solution.py:1145
  697.2 44.0 %collective-permute-start.29 = (bf16[256,1024]{1,0:T(8,128)(2,1)}, bf16[256,1024]{1,0:T(8,128)(2,1)}, u32[]{:S(2)}, u32[]{:S(2)}) collective-permute-start(bf16[256,1024]{1,0:T(8,128)(2,1)} %get-tuple-element.242), channel_id=1, source_target_pairs={{24,0},{25,1},{26,2},{27,3},{28,4},{29,5},{30,6},{31,7}} | collective-permute-start | bytes 1572872 | tf_op jit(solution)/shard_map/ppermute | solution.py:696
  701.2 14.1 %collective-permute-start.36 = (bf16[128,1024]{1,0:T(8,128)(2,1)S(1)}, bf16[128,1024]{1,0:T(8,128)(2,1)S(1)}, u32[]{:S(2)}, u32[]{:S(2)}) collective-permute-start(bf16[128,1024]{1,0:T(8,128)(2,1)S(1)} %get-tuple-element.245), channel_id=1, source_target_pairs={{0,24},{8,0},{16,8},{24,16},{1,25},{9,1},{17,9},{25,17},{2,26},{10... | collective-permute-start | bytes 786440 | tf_op jit(solution)/shard_map/ppermute | solution.py:696
  712.0 24.4 %collective-permute-start.37 = (bf16[128,1024]{1,0:T(8,128)(2,1)S(1)}, bf16[128,1024]{1,0:T(8,128)(2,1)S(1)}, u32[]{:S(2)}, u32[]{:S(2)}) collective-permute-start(bf16[128,1024]{1,0:T(8,128)(2,1)S(1)} %get-tuple-element.247), channel_id=1, source_target_pairs={{0,16},{8,24},{16,0},{24,8},{1,17},{9,25},{17,1},{25,9},{2,18},{10... | collective-permute-start | bytes 786440 | tf_op jit(solution)/shard_map/ppermute | solution.py:696
  715.3 21.6 %collective-permute-start.38 = (bf16[128,1024]{1,0:T(8,128)(2,1)S(1)}, bf16[128,1024]{1,0:T(8,128)(2,1)S(1)}, u32[]{:S(2)}, u32[]{:S(2)}) collective-permute-start(bf16[128,1024]{1,0:T(8,128)(2,1)S(1)} %get-tuple-element.246), channel_id=1, source_target_pairs={{0,8},{8,16},{16,24},{24,0},{1,9},{9,17},{17,25},{25,1},{2,10},{10... | collective-permute-start | bytes 786440 | tf_op jit(solution)/shard_map/ppermute | solution.py:696
  736.4 11.5 %collective-permute-start.33 = (bf16[32,4096]{1,0:T(8,128)(2,1)S(1)}, bf16[32,4096]{1,0:T(8,128)(2,1)}, u32[]{:S(2)}, u32[]{:S(2)}) collective-permute-start(bf16[32,4096]{1,0:T(8,128)(2,1)S(1)} %fusion.41), channel_id=1, source_target_pairs={{0,24},{8,0},{16,8},{24,16},{1,25},{9,1},{17,9},{25,17},{2,26},{10... | collective-permute-start | bytes 786440 | tf_op jit(solution)/shard_map/ppermute | solution.py:625
  736.9 29.7 %collective-permute-start.34 = (bf16[32,4096]{1,0:T(8,128)(2,1)S(1)}, bf16[32,4096]{1,0:T(8,128)(2,1)}, u32[]{:S(2)}, u32[]{:S(2)}) collective-permute-start(bf16[32,4096]{1,0:T(8,128)(2,1)S(1)} %fusion.41), channel_id=1, source_target_pairs={{0,16},{8,24},{16,0},{24,8},{1,17},{9,25},{17,1},{25,9},{2,18},{10... | collective-permute-start | bytes 786440 | tf_op jit(solution)/shard_map/ppermute | solution.py:625
  739.6 26.9 %collective-permute-start.35 = (bf16[32,4096]{1,0:T(8,128)(2,1)S(1)}, bf16[32,4096]{1,0:T(8,128)(2,1)}, u32[]{:S(2)}, u32[]{:S(2)}) collective-permute-start(bf16[32,4096]{1,0:T(8,128)(2,1)S(1)} %fusion.41), channel_id=1, source_target_pairs={{0,8},{8,16},{16,24},{24,0},{1,9},{9,17},{17,25},{25,1},{2,10},{10... | collective-permute-start | bytes 786440 | tf_op jit(solution)/shard_map/ppermute | solution.py:625
  807.3 22.0 %collective-permute-start.39 = (bf16[128,1024]{1,0:T(8,128)(2,1)}, bf16[128,1024]{1,0:T(8,128)(2,1)S(1)}, u32[]{:S(2)}, u32[]{:S(2)}) collective-permute-start(bf16[128,1024]{1,0:T(8,128)(2,1)} %fusion.38), channel_id=1, source_target_pairs={{0,24},{8,0},{16,8},{24,16},{1,25},{9,1},{17,9},{25,17},{2,26},{10... | collective-permute-start | bytes 786440 | tf_op jit(solution)/shard_map/ppermute | solution.py:625
  809.2 23.8 %collective-permute-start.40 = (bf16[128,1024]{1,0:T(8,128)(2,1)}, bf16[128,1024]{1,0:T(8,128)(2,1)S(1)}, u32[]{:S(2)}, u32[]{:S(2)}) collective-permute-start(bf16[128,1024]{1,0:T(8,128)(2,1)} %fusion.38), channel_id=1, source_target_pairs={{0,16},{8,24},{16,0},{24,8},{1,17},{9,25},{17,1},{25,9},{2,18},{10... | collective-permute-start | bytes 786440 | tf_op jit(solution)/shard_map/ppermute | solution.py:625
  810.1 22.9 %collective-permute-start.41 = (bf16[128,1024]{1,0:T(8,128)(2,1)}, bf16[128,1024]{1,0:T(8,128)(2,1)S(1)}, u32[]{:S(2)}, u32[]{:S(2)}) collective-permute-start(bf16[128,1024]{1,0:T(8,128)(2,1)} %fusion.38), channel_id=1, source_target_pairs={{0,8},{8,16},{16,24},{24,0},{1,9},{9,17},{17,25},{25,1},{2,10},{10... | collective-permute-start | bytes 786440 | tf_op jit(solution)/shard_map/ppermute | solution.py:625
  (110 other events, 1361.5 us)
Sparse Core Ops, SparseCore 0:
  103.2 37.4 all-gather.5
  164.4 46.6 all-gather.7
  216.1 72.8 all-gather.9
  290.7 39.0 all-gather.11
  336.8 56.4 reduce-scatter.4
  495.5 71.6 reduce-scatter.6
  570.6 71.2 reduce-scatter.10
  661.4 80.2 reduce-scatter.8
  744.2 63.0 all-reduce.9
